TPU v7x, 32 devices: a whole 2x2x4 slice. The times are simulated.
32 devices in a mesh: groups: 2 (over y), ctx: 4 (over x, core), head: 4 (over z).
Axes of the slice: x: 2, y: 2, z: 4, core: 2. Of those that a mesh axis runs over, the one named last changes fastest.
Arguments:
- queries: bfloat16 [12288, 512], P(('groups', 'ctx', 'head')), parts along dimension 0, may hold values from -8 to 8
- keys: bfloat16 [12288, 512], P(('groups', 'ctx', 'head')), parts along dimension 0, may hold values from -8 to 8
- values: bfloat16 [12288, 512], P(('groups', 'ctx', 'head')), parts along dimension 0, may hold values from -6 to 6
- tile_lists: int32 [96, 16], P(('groups', 'ctx')), parts along dimension 0, may hold values from -8 to 54, as said below
- live_counts: int32 [96], P(('groups', 'ctx')), parts along dimension 0, may hold values from 8 to 16
Outputs:
- attended: bfloat16 [12288, 512], P(('groups', 'ctx', 'head')), parts along dimension 0
There are 2 independent parts, one for each index of `groups`. A program takes and returns all parts, laid end to end along the dimension named above; each array names one. Nothing has to cross between parts.
Inputs may be any that keep to these rules, and one draw needn't show every extreme that they name: `tile_lists`: row t holds t + o for each offset o from -8 to 7 exactly once, the first entry being t itself; entries outside 0 to 47 occur only near the ends of the video.
All inputs are finite; a program needn't handle non-finite values.
Results may differ from a plain program's by a relative error of at most 0.0047.
Values may be sent and summed in bfloat16 or wider, within the bound.
No kernel may reach another device: no remote copies, remote signals or barrier semaphores. Data moves between devices by JAX's collectives and lax.ppermute only.
A program may use at most 64 MiB of HBM per device.

v0:
```python
import jax
import jax.numpy as jnp
from jax import lax
from jax.sharding import PartitionSpec as P

HDIM = 128
TILE = 128
EDGE = 8
CTX_TILES = 12
LIST = 16


def with_halo(block, sides, width):
    for axis, dim in sides:
        count = lax.axis_size(axis)
        forward = [(i, i + 1) for i in range(count - 1)]
        backward = [(target, source) for source, target in forward]
        low = lax.ppermute(
            lax.slice_in_dim(block, block.shape[dim] - width, None, axis=dim), axis, forward
        )
        high = lax.ppermute(lax.slice_in_dim(block, 0, width, axis=dim), axis, backward)
        block = jnp.concatenate([low, block, high], axis=dim)
    return block


def block_tiles():
    for candidate in (4, 2, 1):
        return candidate
    return 1


def edge_tiles(kv_pair):
    return with_halo(kv_pair, (("ctx", 1),), EDGE * TILE)


def attend(q_rows, row_lists, row_counts, kv_tiles, query_first, kv_first, total_tiles):
    tile_count = row_lists.shape[0]
    per_block = block_tiles()
    block_count = tile_count // per_block
    window_span = per_block + 2 * EDGE - 1
    score_scale = HDIM ** (-0.5)
    q_blocks = q_rows.reshape(block_count, per_block, TILE, HDIM)
    block_list_entries = row_lists.reshape(block_count, per_block, LIST)
    count_blocks = row_counts.reshape(block_count, per_block)
    block_numbers = jnp.arange(block_count, dtype=jnp.int32)
    positions = jnp.arange(LIST)
    window_steps = jnp.arange(window_span, dtype=jnp.int32)

    def one_block(inputs):
        query_portion, list_part, count_part, block_number = inputs
        block_first = query_first + block_number * per_block
        window_first = block_first - EDGE
        window = lax.dynamic_slice_in_dim(kv_tiles, window_first - kv_first, window_span, 1)
        key_window_tiles = window[0].reshape(window_span * TILE, HDIM)
        value_window_tiles = window[1].reshape(window_span * TILE, HDIM)
        window_ids = window_first + window_steps
        in_range = (window_ids >= 0) & (window_ids < total_tiles)
        live = positions[None, :] < count_part[:, None]
        matched = (list_part[:, :, None] == window_ids[None, None, :]) & live[:, :, None]
        usable = jnp.any(matched, axis=1) & in_range[None, :]
        visible = jnp.repeat(usable, TILE, axis=1)[:, None, :]
        scores = (
            jnp.einsum(
                "tfy,vy->tfv", query_portion, key_window_tiles, preferred_element_type=jnp.float32
            )
            * score_scale
        )
        scores = jnp.where(visible, scores, -1e30)
        highest = jnp.max(scores, axis=-1, keepdims=True)
        weights = jnp.where(visible, jnp.exp(scores - highest), 0.0)
        softmax_divisor = jnp.sum(weights, axis=-1, keepdims=True)
        attention_probs = weights.astype(jnp.bfloat16)
        mixed = jnp.einsum(
            "jzn,nw->jzw", attention_probs, value_window_tiles, preferred_element_type=jnp.float32
        )
        return (mixed / softmax_divisor).astype(jnp.bfloat16)

    results = lax.map(one_block, (q_blocks, block_list_entries, count_blocks, block_numbers))
    return results.reshape(tile_count * TILE, HDIM)


def on_device(queries, keys, values, tile_lists, live_counts):
    ctx_count = lax.axis_size("ctx")
    total_tiles = CTX_TILES * ctx_count
    first_tile = lax.axis_index("ctx") * CTX_TILES
    kv_pair = lax.all_to_all(
        jnp.stack([keys, values]), "head", split_axis=2, concat_axis=1, tiled=True
    )
    padded = edge_tiles(kv_pair)
    local_q = lax.all_to_all(queries, "head", split_axis=1, concat_axis=0, tiled=True)
    padded_count = CTX_TILES + 2 * EDGE
    padded_tiles = padded.reshape(2, padded_count, TILE, HDIM)
    head_out = attend(
        local_q, tile_lists, live_counts, padded_tiles, first_tile, first_tile - EDGE, total_tiles
    )
    return lax.all_to_all(head_out, "head", split_axis=0, concat_axis=1, tiled=True)


def solution(mesh):
    return jax.shard_map(
        on_device,
        mesh=mesh,
        in_specs=(
            P(("groups", "ctx", "head"), None),
            P(("groups", "ctx", "head"), None),
            P(("groups", "ctx", "head"), None),
            P(("groups", "ctx"), None),
            P(("groups", "ctx")),
        ),
        out_specs=P(("groups", "ctx", "head"), None),
        check_vma=False,
    )
```

profile of v0, /device:TPU:0, one launch (start us, length us, event | category | flops | bytes accessed | tf_op | source)
XLA Modules:
  0.0 94.4 jit_solution(12368793994641363082)
XLA Ops:
  0.0 0.0 copy-start
  0.0 1.2 %pad_maximum_fusion.1 = bf16[2,384,512]{2,1,0:T(8,128)(2,1)S(1)} fusion(bf16[1,384,512]{2,1,0:T(8,128)(2,1)} %bitcast.91, bf16[1,384,512]{2,1,0:T(8,128)(2,1)} %bitcast.92), kind=kLoop, calls=%fused_computation.40 | loop fusion | flops 393216 | bytes 1572864 | tf_op jit(solution)/shard_map/stack | solution.py:87
  1.2 1.1 %copy.26 = bf16[2,384,512]{1,0,2:T(2,128)(2,1)S(1)} copy(bf16[2,384,512]{2,1,0:T(8,128)(2,1)S(1)} %pad_maximum_fusion.1) | data formatting | bytes 1572864 | tf_op jit(solution)/shard_map/stack | solution.py:87
  2.4 26.2 %all_to_all.53 = bf16[2,384,512]{1,0,2:T(2,128)(2,1)S(1)} all-to-all(bf16[2,384,512]{1,0,2:T(2,128)(2,1)S(1)} %copy.26), channel_id=1, replica_groups=mesh['groups'=2,'ctx'=4,'head'=4] {'head'}, dimensions={2} | all-to-all | bytes 1572864 | tf_op jit(solution)/shard_map/all_to_all | solution.py:86
  28.6 0.1 copy.27
  28.7 0.4 copy.28
  29.1 0.0 copy-start.1
  29.1 0.0 copy-start.2
  29.1 0.1 fusion.52
  29.2 1.3 %collective-permute-start = (bf16[2,1024,128]{2,1,0:T(8,128)(2,1)S(1)}, bf16[2,1024,128]{2,1,0:T(8,128)(2,1)S(1)}, u32[]{:S(2)}, u32[]{:S(2)}) collective-permute-start(bf16[2,1024,128]{2,1,0:T(8,128)(2,1)S(1)} %get-tuple-element.184), channel_id=1, source_target_pairs={{0,4},{4,8},{8,12},{1,5},{5,9},{9,13},{2,6},{6,10},{10,14},{3,7},{... | collective-permute-start | bytes 1572872 | tf_op jit(solution)/shard_map/ppermute | solution.py:18
  30.5 1.3 %collective-permute-start.1 = (bf16[2,1024,128]{2,1,0:T(8,128)(2,1)S(1)}, bf16[2,1024,128]{2,1,0:T(8,128)(2,1)}, u32[]{:S(2)}, u32[]{:S(2)}) collective-permute-start(bf16[2,1024,128]{2,1,0:T(8,128)(2,1)S(1)} %get-tuple-element.185), channel_id=1, source_target_pairs={{4,0},{8,4},{12,8},{5,1},{9,5},{13,9},{6,2},{10,6},{14,10},{7,3},{... | collective-permute-start | bytes 1572872 | tf_op jit(solution)/shard_map/ppermute | solution.py:21
  31.8 0.0 copy-done
  31.8 0.8 copy_bitcast_fusion.1
  32.7 4.1 %all-to-all-start = ((bf16[384,4,128]{2,0,1:T(8,128)(2,1)}), bf16[384,4,128]{2,0,1:T(8,128)(2,1)}, u32[]{:S(2)}, u32[]{:S(2)}) async-start(bf16[384,4,128]{2,0,1:T(8,128)(2,1)} %copy_bitcast_fusion.1), calls=%async_computation | async-start | bytes 786432 | tf_op jit(solution)/shard_map/all_to_all | solution.py:90
  36.8 0.0 copy-done.1
  36.8 0.0 copy-done.2
  36.8 0.1 reshape.75
  36.9 0.0 collective-permute-done
  36.9 0.0 collective-permute-done.1
  36.9 1.2 %pad_maximum_fusion = bf16[2,3584,128]{2,1,0:T(8,128)(2,1)S(1)} fusion(bf16[2,1024,128]{2,1,0:T(8,128)(2,1)} %collective-permute-done.1, bf16[2,1536,128]{2,1,0:T(8,128)(2,1)S(1)} %bitcast.87, bf16[2,1024,128]{2,1,0:T(8,128)(2,1)S(1)} %collective-permute-done), kind=kLoop, calls=%fused_computation.39 | loop fusion | flops 5505024 | bytes 3670016 | tf_op jit(solution)/shard_map/concatenate | solution.py:22
  38.1 9.7 %all-to-all-done = bf16[384,4,128]{2,0,1:T(8,128)(2,1)} async-done(((bf16[384,4,128]{2,0,1:T(8,128)(2,1)}), bf16[384,4,128]{2,0,1:T(8,128)(2,1)}, u32[]{:S(2)}, u32[]{:S(2)}) %all-to-all-start) | async-done | bytes 393248 | tf_op jit(solution)/shard_map/all_to_all | solution.py:90
  47.8 28.5 %while.13 = (s32[]{:T(128)}, bf16[3,4,128,128]{3,2,1,0:T(8,128)(2,1)}, s32[3,4,16]{2,1,0:T(4,128)S(1)}, s32[3]{0:T(128)S(1)}, s32[]{:T(128)}, /*index=5*/s32[3,4...) while((s32[]{:T(128)}, ...), condition=%wide.region_4.5_spmd.clone, body=%wide.region_0.4_spmd.clone.sunk | while | flops 968893440 | bytes 4826797 | solution.py:78
  47.8 0.6 dynamic_slice.67
  49.1 0.1 constant_dynamic-slice_fusion.4
  49.3 0.1 iota_compare_fusion.2
  49.3 0.1 and_reduce_fusion.2
  49.5 0.1 broadcast_bitcast_fusion.2
  49.6 3.1 %fusion.73 = f32[4,128]{1,0:T(4,128)S(1)} fusion(bf16[2432,128,1]{1,0,2:T(8,128)(2,1)S(1)} %bitcast.83, pred[4,2432]{1,0:T(4,128)(4,1)S(1)} %bitcast.93, bf16[3,4,128,128]{3,2,1,0:T(8,128)(2,1)} %get-tuple-element.281, s32[]{:T(128)} %get-tuple-element.260), kind=kOutput, calls=%fused_computation.42.clone.1 | convolution fusion | flops 324995456 | bytes 775680 | tf_op jit(solution)/shard_map/while/body/eval_jaxpr/sub | solution.py:70
  52.7 4.6 %fusion.74 = bf16[3,4,128,128]{3,2,1,0:T(8,128)(2,1)} fusion(bf16[3,4,128,128]{3,2,1,0:T(8,128)(2,1)} %get-tuple-element.261, s32[]{:T(128)} %get-tuple-element.260, bf16[2432,128,1]{1,0,2:T(8,128)(2,1)S(1)} %bitcast.85, f32[4,128]{1,0:T(4,128)S(1)} %fusion.73, pred[4,2432]{1,0:T(4,128)(4,1)S(1)} %bitcast.94, ...), kind=kOutput, calls=%fused_computation.12.clone.1 | convolution fusion | flops 643894144 | bytes 1529856 | tf_op jit(solution)/shard_map/while/body/eval_jaxpr/jzn,nw->jzw/dot_general | solution.py:73
  57.3 0.6 dynamic_slice.67
  58.6 0.1 constant_dynamic-slice_fusion.4
  58.7 0.1 iota_compare_fusion.2
  58.8 0.1 and_reduce_fusion.2
  58.9 0.1 broadcast_bitcast_fusion.2
  59.0 3.2 %fusion.73 = f32[4,128]{1,0:T(4,128)S(1)} fusion(bf16[2432,128,1]{1,0,2:T(8,128)(2,1)S(1)} %bitcast.83, pred[4,2432]{1,0:T(4,128)(4,1)S(1)} %bitcast.93, bf16[3,4,128,128]{3,2,1,0:T(8,128)(2,1)} %get-tuple-element.281, s32[]{:T(128)} %get-tuple-element.260), kind=kOutput, calls=%fused_computation.42.clone.1 | convolution fusion | flops 324995456 | bytes 775680 | tf_op jit(solution)/shard_map/while/body/eval_jaxpr/sub | solution.py:70
  62.2 4.6 %fusion.74 = bf16[3,4,128,128]{3,2,1,0:T(8,128)(2,1)} fusion(bf16[3,4,128,128]{3,2,1,0:T(8,128)(2,1)} %get-tuple-element.261, s32[]{:T(128)} %get-tuple-element.260, bf16[2432,128,1]{1,0,2:T(8,128)(2,1)S(1)} %bitcast.85, f32[4,128]{1,0:T(4,128)S(1)} %fusion.73, pred[4,2432]{1,0:T(4,128)(4,1)S(1)} %bitcast.94, ...), kind=kOutput, calls=%fused_computation.12.clone.1 | convolution fusion | flops 643894144 | bytes 1529856 | tf_op jit(solution)/shard_map/while/body/eval_jaxpr/jzn,nw->jzw/dot_general | solution.py:73
  66.8 0.6 dynamic_slice.67
  68.0 0.1 constant_dynamic-slice_fusion.4
  68.2 0.1 iota_compare_fusion.2
  68.3 0.1 and_reduce_fusion.2
  68.4 0.1 broadcast_bitcast_fusion.2
  68.5 3.2 %fusion.73 = f32[4,128]{1,0:T(4,128)S(1)} fusion(bf16[2432,128,1]{1,0,2:T(8,128)(2,1)S(1)} %bitcast.83, pred[4,2432]{1,0:T(4,128)(4,1)S(1)} %bitcast.93, bf16[3,4,128,128]{3,2,1,0:T(8,128)(2,1)} %get-tuple-element.281, s32[]{:T(128)} %get-tuple-element.260), kind=kOutput, calls=%fused_computation.42.clone.1 | convolution fusion | flops 324995456 | bytes 775680 | tf_op jit(solution)/shard_map/while/body/eval_jaxpr/sub | solution.py:70
  71.7 4.6 %fusion.74 = bf16[3,4,128,128]{3,2,1,0:T(8,128)(2,1)} fusion(bf16[3,4,128,128]{3,2,1,0:T(8,128)(2,1)} %get-tuple-element.261, s32[]{:T(128)} %get-tuple-element.260, bf16[2432,128,1]{1,0,2:T(8,128)(2,1)S(1)} %bitcast.85, f32[4,128]{1,0:T(4,128)S(1)} %fusion.73, pred[4,2432]{1,0:T(4,128)(4,1)S(1)} %bitcast.94, ...), kind=kOutput, calls=%fused_computation.12.clone.1 | convolution fusion | flops 643894144 | bytes 1529856 | tf_op jit(solution)/shard_map/while/body/eval_jaxpr/jzn,nw->jzw/dot_general | solution.py:73
  76.3 16.9 %all_to_all.54 = bf16[4,384,128]{2,1,0:T(8,128)(2,1)S(1)} all-to-all(bf16[4,384,128]{2,1,0:T(8,128)(2,1)} %bitcast.90), channel_id=1, replica_groups=mesh['groups'=2,'ctx'=4,'head'=4] {'head'}, dimensions={0} | all-to-all | bytes 786432 | tf_op jit(solution)/shard_map/all_to_all | solution.py:96
  93.2 0.2 copy.29
  93.5 0.9 copy.30
  (21 shorter events, 0.2 us)
Async XLA Ops:
  0.0 31.8 %copy-start = (bf16[384,512]{1,0:T(8,128)(2,1)S(1)}, bf16[384,512]{1,0:T(8,128)(2,1)}, u32[]{:S(2)}) copy-start(bf16[384,512]{1,0:T(8,128)(2,1)} %param.7) | copy-start | bytes 1179652
  29.1 7.7 %copy-start.1 = (s32[12,16]{1,0:T(8,128)S(1)}, s32[12,16]{1,0:T(8,128)}, u32[]{:S(2)}) copy-start(s32[12,16]{1,0:T(8,128)} %param.10) | copy-start | bytes 2308
  29.1 7.7 %copy-start.2 = (s32[12]{0:T(128)S(1)}, s32[12]{0:T(128)}, u32[]{:S(2)}) copy-start(s32[12]{0:T(128)} %param.11) | copy-start | bytes 148
  29.2 7.7 %collective-permute-start = (bf16[2,1024,128]{2,1,0:T(8,128)(2,1)S(1)}, bf16[2,1024,128]{2,1,0:T(8,128)(2,1)S(1)}, u32[]{:S(2)}, u32[]{:S(2)}) collective-permute-start(bf16[2,1024,128]{2,1,0:T(8,128)(2,1)S(1)} %get-tuple-element.184), channel_id=1, source_target_pairs={{0,4},{4,8},{8,12},{1,5},{5,9},{9,13},{2,6},{6,10},{10,14},{3,7},{... | collective-permute-start | bytes 1572872 | tf_op jit(solution)/shard_map/ppermute | solution.py:18
  30.5 6.4 %collective-permute-start.1 = (bf16[2,1024,128]{2,1,0:T(8,128)(2,1)S(1)}, bf16[2,1024,128]{2,1,0:T(8,128)(2,1)}, u32[]{:S(2)}, u32[]{:S(2)}) collective-permute-start(bf16[2,1024,128]{2,1,0:T(8,128)(2,1)S(1)} %get-tuple-element.185), channel_id=1, source_target_pairs={{4,0},{8,4},{12,8},{5,1},{9,5},{13,9},{6,2},{10,6},{14,10},{7,3},{... | collective-permute-start | bytes 1572872 | tf_op jit(solution)/shard_map/ppermute | solution.py:21
  32.7 15.2 %all-to-all-start = ((bf16[384,4,128]{2,0,1:T(8,128)(2,1)}), bf16[384,4,128]{2,0,1:T(8,128)(2,1)}, u32[]{:S(2)}, u32[]{:S(2)}) async-start(bf16[384,4,128]{2,0,1:T(8,128)(2,1)} %copy_bitcast_fusion.1), calls=%async_computation | async-start | bytes 786432 | tf_op jit(solution)/shard_map/all_to_all | solution.py:90
where the time goes:
time: 94.9 us; the launch traced here: 94.4 us
  blocking collectives  43.2 us (46%)
  matrix products  23.3 us (25%)
  waiting for transfers between devices  9.74 us (10%)
  starting transfers between devices  6.73 us (7%)
  local copies, waits for them, and re-layouts  6.34 us (7%)
  other arithmetic  2.97 us (3%)
  loops' own time  2.05 us (2%)
    all_to_all x1, blocking collectives, on_device(): lax.all_to_all(jnp.stack([keys, values]), 'head', split_axis=2, concat_ax...  26.2 us
    all_to_all x1, blocking collectives, on_device(): lax.all_to_all(head_out, 'head', split_axis=0, concat_axis=1, tiled=True)  16.9 us
    dot_general x3, matrix products, one_block(): jnp.einsum('jzn,nw->jzw', attention_probs, value_window_tiles, preferred_...  13.8 us
    all_to_all x1, waiting for transfers between devices, on_device(): lax.all_to_all(queries, 'head', split_axis=1, concat_axis=0, tiled=True)  9.74 us
    sub x3, matrix products, one_block(): weights = jnp.where(visible, jnp.exp(scores - highest), 0.0)  9.46 us
    all_to_all x1, starting transfers between devices, on_device(): lax.all_to_all(queries, 'head', split_axis=1, concat_axis=0, tiled=True)  4.11 us
    another operation x1, loops' own time, attend(): lax.map(one_block, (q_blocks, block_list_entries, count_blocks, block_num...  2.05 us
  transfers between devices with their start and end apart: 3, of which 1 were waited for; matrix products, arithmetic and copies ran while one was open for 2% of the time, Pallas kernels for 0%

commit v1 on v0

v1 whole, which is shorter than its diff:
```python
import functools
import math

import jax
import jax.numpy as jnp
from jax import lax
from jax.experimental import pallas as pl
from jax.experimental.pallas import tpu as pltpu
from jax.sharding import PartitionSpec as P

HDIM = 128
TILE = 128
EDGE = 8
LIST = 16
BLOCK = 3
WINDOW = BLOCK + LIST - 1
HIDDEN = -1e30
EXPONENT_SCALE = HDIM ** (-0.5) * math.log2(math.e)
SMEM = pl.BlockSpec(memory_space=pltpu.SMEM)
VMEM = pl.BlockSpec(memory_space=pltpu.VMEM)


def pack_kernel(heads, q_ref, k_ref, v_ref, q_out, k_out, v_out):
    for source, target in ((k_ref, k_out), (v_ref, v_out), (q_ref, q_out)):
        for head in range(heads):
            target[head] = source[:, head * HDIM : (head + 1) * HDIM]


def pack(queries, keys, values):
    rows, columns = queries.shape
    heads = columns // HDIM
    shape = jax.ShapeDtypeStruct((heads, rows, HDIM), queries.dtype)
    return pl.pallas_call(
        functools.partial(pack_kernel, heads),
        out_shape=[shape] * 3,
        in_specs=[VMEM] * 3,
        out_specs=[VMEM] * 3,
        compiler_params=pltpu.CompilerParams(vmem_limit_bytes=8 << 20),
        name="pack",
    )(queries, keys, values)


def unpack_kernel(heads, parts_ref, out_ref):
    for head in range(heads):
        out_ref[:, head * HDIM : (head + 1) * HDIM] = parts_ref[head]


def unpack(parts):
    heads, rows, _ = parts.shape
    return pl.pallas_call(
        functools.partial(unpack_kernel, heads),
        out_shape=jax.ShapeDtypeStruct((rows, heads * HDIM), parts.dtype),
        in_specs=[VMEM],
        out_specs=VMEM,
        compiler_params=pltpu.CompilerParams(vmem_limit_bytes=8 << 20),
        name="unpack",
    )(parts)


def attend_block(first, total_tiles, lists_ref, counts_ref, q_ref, kbuf, vbuf, bias, scores, probs):
    for tile in range(BLOCK):
        row = first + tile
        own = lists_ref[row, 0]
        count = counts_ref[row]
        for entry in range(LIST):
            listed = lists_ref[row, entry]
            live = (entry < count) & (listed >= 0) & (listed < total_tiles)
            bias[tile * LIST + listed - own + EDGE] = jnp.where(live, 0.0, HIDDEN)

    base = pl.multiple_of(first * TILE, TILE)
    for pair in range(WINDOW // 2):
        low = max(0, 2 * pair - LIST + 1)
        high = min(BLOCK - 1, 2 * pair + 1)
        part = lax.dot_general(
            q_ref[low * TILE : (high + 1) * TILE, :],
            kbuf[pl.ds(base + pair * 2 * TILE, 2 * TILE), :],
            (((1,), (1,)), ((), ())),
            preferred_element_type=jnp.float32,
        )
        for tile in range(low, high + 1):
            for half in range(2):
                place = 2 * pair + half
                if 0 <= place - tile < LIST:
                    rows = slice((tile - low) * TILE, (tile - low + 1) * TILE)
                    scores[tile * TILE : (tile + 1) * TILE, place * TILE : (place + 1) * TILE] = (
                        part[rows, half * TILE : (half + 1) * TILE] + bias[tile * LIST + place - tile]
                    )
    divisors = []
    for tile in range(BLOCK):
        rows = slice(tile * TILE, (tile + 1) * TILE)
        highest = scores[rows, tile * TILE : (tile + 1) * TILE]
        for place in range(tile + 1, tile + LIST):
            highest = jnp.maximum(highest, scores[rows, place * TILE : (place + 1) * TILE])
        highest = jnp.broadcast_to(jnp.max(highest, axis=1, keepdims=True), (TILE, TILE))
        total = jnp.zeros((TILE, TILE), jnp.float32)
        for place in range(WINDOW):
            columns = slice(place * TILE, (place + 1) * TILE)
            if 0 <= place - tile < LIST:
                weights = jnp.exp2((scores[rows, columns] - highest) * EXPONENT_SCALE)
                total += weights
                probs[rows, columns] = weights.astype(jnp.bfloat16)
            else:
                probs[rows, columns] = jnp.zeros((TILE, TILE), jnp.bfloat16)
        divisors.append(jnp.sum(total, axis=1, keepdims=True))
    mixed = jnp.dot(
        probs[...], vbuf[pl.ds(base, WINDOW * TILE), :], preferred_element_type=jnp.float32
    )
    return (mixed / jnp.concatenate(divisors, axis=0)).astype(jnp.bfloat16)


def attend_kernel(
    total_tiles, lists_ref, counts_ref, q_ref, k_own, v_own, k_low, v_low, k_high, v_high, out_ref,
    kbuf, vbuf, bias, scores, probs,
):
    rows = k_own.shape[0]
    for low, own, high, buffer in ((k_low, k_own, k_high, kbuf), (v_low, v_own, v_high, vbuf)):
        buffer[: EDGE * TILE, :] = low[...]
        buffer[EDGE * TILE : EDGE * TILE + rows, :] = own[...]
        buffer[EDGE * TILE + rows :, :] = high[...]

    @pl.loop(0, q_ref.shape[0] // (BLOCK * TILE))
    def _(block):
        place = pl.ds(pl.multiple_of(block * BLOCK * TILE, TILE), BLOCK * TILE)
        out_ref[place, :] = attend_block(
            block * BLOCK, total_tiles, lists_ref, counts_ref, q_ref.at[place, :],
            kbuf, vbuf, bias, scores, probs,
        )


def attend(queries, own, low, high, tile_lists, live_counts, total_tiles):
    rows = queries.shape[0]
    padded = rows + (LIST - 1) * TILE
    block_rows = BLOCK * TILE
    return pl.pallas_call(
        functools.partial(attend_kernel, total_tiles),
        out_shape=jax.ShapeDtypeStruct(queries.shape, queries.dtype),
        in_specs=[SMEM, SMEM] + [VMEM] * 7,
        out_specs=VMEM,
        scratch_shapes=[
            pltpu.VMEM((padded, HDIM), jnp.bfloat16),
            pltpu.VMEM((padded, HDIM), jnp.bfloat16),
            pltpu.SMEM((BLOCK * LIST,), jnp.float32),
            pltpu.VMEM((block_rows, WINDOW * TILE), jnp.float32),
            pltpu.VMEM((block_rows, WINDOW * TILE), jnp.bfloat16),
        ],
        compiler_params=pltpu.CompilerParams(vmem_limit_bytes=24 << 20),
        name="attend",
    )(tile_lists, live_counts, queries, own[0], own[1], low[0], low[1], high[0], high[1])


def to_heads(array):
    heads, rows, _ = array.shape
    return lax.all_to_all(array, "head", split_axis=0, concat_axis=0, tiled=True).reshape(heads * rows, HDIM)


def on_device(queries, keys, values, tile_lists, live_counts):
    ctx = lax.axis_size("ctx")
    total_tiles = tile_lists.shape[0] * ctx
    forward = [(i, i + 1) for i in range(ctx - 1)]
    backward = [(i + 1, i) for i in range(ctx - 1)]
    q_parts, k_parts, v_parts = pack(queries, keys, values)
    own = to_heads(k_parts), to_heads(v_parts)
    low = [lax.ppermute(array[-EDGE * TILE :], "ctx", forward) for array in own]
    high = [lax.ppermute(array[: (EDGE - 1) * TILE], "ctx", backward) for array in own]
    local_q = to_heads(q_parts)
    head_out = attend(local_q, own, low, high, tile_lists, live_counts, total_tiles)
    back = lax.all_to_all(
        head_out.reshape(q_parts.shape), "head", split_axis=0, concat_axis=0, tiled=True
    )
    return unpack(back)


def solution(mesh):
    return jax.shard_map(
        on_device,
        mesh=mesh,
        in_specs=(
            P(("groups", "ctx", "head"), None),
            P(("groups", "ctx", "head"), None),
            P(("groups", "ctx", "head"), None),
            P(("groups", "ctx"), None),
            P(("groups", "ctx")),
        ),
        out_specs=P(("groups", "ctx", "head"), None),
        check_vma=False,
    )
```

time: 94.9 us -> 79.5 us (0.84)
  the two profiles are of different devices: /device:TPU:0 before, /device:TPU:1 now
where the time goes in v1:
time: 79.5 us; the launch traced here: 79 us
  blocking collectives  42.6 us (54%)
  starting transfers between devices  15 us (19%)
  Pallas kernels  12.8 us (16%)
  waiting for transfers between devices  5.44 us (7%)
  local copies, waits for them, and re-layouts  3.07 us (4%)
    all_to_all x2, blocking collectives, to_heads(): lax.all_to_all(array, 'head', split_axis=0, concat_axis=0, tiled=True)  29.3 us
    all_to_all x1, blocking collectives, on_device(): lax.all_to_all(head_out.reshape(q_parts.shape), 'head', split_axis=0, con...  13.3 us
    pallas_call x1, Pallas kernels, attend(): pl.pallas_call(functools.partial(attend_kernel, total_tiles), out_shape=j...  11 us
    ppermute x2, starting transfers between devices, on_device(): low = [lax.ppermute(array[-EDGE * TILE:], 'ctx', forward) for array in own]  7.08 us
    ppermute x2, waiting for transfers between devices, on_device(): lax.ppermute(array[:(EDGE - 1) * TILE], 'ctx', backward)  5.43 us
    ppermute x2, starting transfers between devices, on_device(): lax.ppermute(array[:(EDGE - 1) * TILE], 'ctx', backward)  4.34 us
    all_to_all x1, starting transfers between devices, to_heads(): lax.all_to_all(array, 'head', split_axis=0, concat_axis=0, tiled=True)  3.56 us
    unnamed x10, local copies, waits for them, and re-layouts  3 us
  transfers between devices with their start and end apart: 5, of which 2 were waited for; matrix products, arithmetic and copies ran while one was open for 0% of the time, Pallas kernels for 0%

profile of v1, /device:TPU:1, one launch (start us, length us, event | category | flops | bytes accessed | tf_op | source)
XLA Modules:
  0.0 79.0 jit_solution(16642348798733619918)
XLA Ops:
  0.0 0.0 copy-start
  0.0 1.0 %copy-done = bf16[384,512]{1,0:T(8,128)(2,1)S(1)} copy-done((bf16[384,512]{1,0:T(8,128)(2,1)S(1)}, bf16[384,512]{1,0:T(8,128)(2,1)}, u32[]{:S(2)}) %copy-start) | copy-done | bytes 393240
  1.0 0.0 copy-start.1
  1.0 1.0 %copy-done.1 = bf16[384,512]{1,0:T(8,128)(2,1)S(1)} copy-done((bf16[384,512]{1,0:T(8,128)(2,1)S(1)}, bf16[384,512]{1,0:T(8,128)(2,1)}, u32[]{:S(2)}) %copy-start.1) | copy-done | bytes 393240
  2.0 0.0 copy-start.2
  2.0 1.0 %copy-done.2 = bf16[384,512]{1,0:T(8,128)(2,1)S(1)} copy-done((bf16[384,512]{1,0:T(8,128)(2,1)S(1)}, bf16[384,512]{1,0:T(8,128)(2,1)}, u32[]{:S(2)}) %copy-start.2) | copy-done | bytes 393240
  3.0 0.9 %pack.1 = (bf16[4,384,128]{2,1,0:T(8,128)(2,1)}, bf16[4,384,128]{2,1,0:T(8,128)(2,1)S(1)}, bf16[4,384,128]{2,1,0:T(8,128)(2,1)S(1)}) custom-call(bf16[384,512]{1,0:T(8,128)(2,1)S(1)} %copy-done, bf16[384,512]{1,0:T(8,128)(2,1)S(1)} %copy-done.1, bf16[384,512]{1,0:T(8,128)(2,1)S(1)} %copy-done.2), custom_call_target="tpu_custom_call" | custom-call | tf_op jit(solution)/shard_map/pack/pallas_call | solution.py:33
  3.9 16.0 %all_to_all.20 = bf16[4,384,128]{2,1,0:T(8,128)(2,1)S(1)} all-to-all(bf16[4,384,128]{2,1,0:T(8,128)(2,1)S(1)} %get-tuple-element.9), channel_id=1, replica_groups=mesh['groups'=2,'ctx'=4,'head'=4] {'head'}, dimensions={0} | all-to-all | bytes 786432 | tf_op jit(solution)/shard_map/all_to_all | solution.py:153
  20.0 13.3 %all_to_all.21 = bf16[4,384,128]{2,1,0:T(8,128)(2,1)S(1)} all-to-all(bf16[4,384,128]{2,1,0:T(8,128)(2,1)S(1)} %get-tuple-element.10), channel_id=1, replica_groups=mesh['groups'=2,'ctx'=4,'head'=4] {'head'}, dimensions={0} | all-to-all | bytes 786432 | tf_op jit(solution)/shard_map/all_to_all | solution.py:153
  33.3 3.6 %all-to-all-start = ((bf16[4,384,128]{2,1,0:T(8,128)(2,1)}), bf16[4,384,128]{2,1,0:T(8,128)(2,1)S(1)}, u32[]{:S(2)}, u32[]{:S(2)}) async-start(bf16[4,384,128]{2,1,0:T(8,128)(2,1)} %get-tuple-element.8), calls=%async_computation | async-start | bytes 786432 | tf_op jit(solution)/shard_map/all_to_all | solution.py:153
  36.9 5.2 %collective-permute-start = (bf16[1024,128]{1,0:T(8,128)(2,1)S(1)}, bf16[1024,128]{1,0:T(8,128)(2,1)S(1)}, u32[]{:S(2)}, u32[]{:S(2)}) collective-permute-start(bf16[1024,128]{1,0:T(8,128)(2,1)S(1)} %slice.16), channel_id=1, source_target_pairs={{0,4},{4,8},{8,12},{1,5},{5,9},{9,13},{2,6},{6,10},{10,14},{3,7},{... | collective-permute-start | bytes 786440 | tf_op jit(solution)/shard_map/ppermute | solution.py:163
  42.0 1.9 %collective-permute-start.1 = (bf16[1024,128]{1,0:T(8,128)(2,1)S(1)}, bf16[1024,128]{1,0:T(8,128)(2,1)S(1)}, u32[]{:S(2)}, u32[]{:S(2)}) collective-permute-start(bf16[1024,128]{1,0:T(8,128)(2,1)S(1)} %slice.17), channel_id=1, source_target_pairs={{0,4},{4,8},{8,12},{1,5},{5,9},{9,13},{2,6},{6,10},{10,14},{3,7},{... | collective-permute-start | bytes 786440 | tf_op jit(solution)/shard_map/ppermute | solution.py:163
  44.0 0.0 copy-start.3
  44.0 0.0 copy-start.4
  44.0 2.4 %collective-permute-start.2 = (bf16[896,128]{1,0:T(8,128)(2,1)S(1)}, bf16[896,128]{1,0:T(8,128)(2,1)S(1)}, u32[]{:S(2)}, u32[]{:S(2)}) collective-permute-start(bf16[896,128]{1,0:T(8,128)(2,1)S(1)} %slice.18), channel_id=1, source_target_pairs={{4,0},{8,4},{12,8},{5,1},{9,5},{13,9},{6,2},{10,6},{14,10},{7,3},{... | collective-permute-start | bytes 688136 | tf_op jit(solution)/shard_map/ppermute | solution.py:164
  46.5 1.9 %collective-permute-start.3 = (bf16[896,128]{1,0:T(8,128)(2,1)S(1)}, bf16[896,128]{1,0:T(8,128)(2,1)S(1)}, u32[]{:S(2)}, u32[]{:S(2)}) collective-permute-start(bf16[896,128]{1,0:T(8,128)(2,1)S(1)} %slice.19), channel_id=1, source_target_pairs={{4,0},{8,4},{12,8},{5,1},{9,5},{13,9},{6,2},{10,6},{14,10},{7,3},{... | collective-permute-start | bytes 688136 | tf_op jit(solution)/shard_map/ppermute | solution.py:164
  48.4 0.0 all-to-all-done
  48.4 3.0 %collective-permute-done.2.k_high = bf16[896,128]{1,0:T(8,128)(2,1)S(1)} collective-permute-done((bf16[896,128]{1,0:T(8,128)(2,1)S(1)}, bf16[896,128]{1,0:T(8,128)(2,1)S(1)}, u32[]{:S(2)}, u32[]{:S(2)}) %collective-permute-start.2) | collective-permute-done | bytes 229408 | tf_op jit(solution)/shard_map/ppermute | solution.py:164
  51.4 2.5 %collective-permute-done.3.v_high = bf16[896,128]{1,0:T(8,128)(2,1)S(1)} collective-permute-done((bf16[896,128]{1,0:T(8,128)(2,1)S(1)}, bf16[896,128]{1,0:T(8,128)(2,1)S(1)}, u32[]{:S(2)}, u32[]{:S(2)}) %collective-permute-start.3) | collective-permute-done | bytes 229408 | tf_op jit(solution)/shard_map/ppermute | solution.py:164
  53.8 0.0 collective-permute-done.k_low
  53.9 0.0 collective-permute-done.1.v_low
  53.9 0.0 copy-done.3
  53.9 0.0 copy-done.4
  53.9 11.0 %attend.1 = bf16[1536,128]{1,0:T(8,128)(2,1)S(1)} custom-call(s32[12,16]{1,0:T(8,128)S(1)} %copy-done.3, s32[12]{0:T(128)S(1)} %copy-done.4, bf16[1536,128]{1,0:T(8,128)(2,1)S(1)} %bitcast.10, bf16[1536,128]{1,0:T(8,128)(2,1)S(1)} %bitcast.6, bf16[1536,128]{1,0:T(8,128)(2,1)S(1)} %bitcast.9, bf16[1024,128]{1,0:T(8,128)(2,1)S(1)} %collective-permute-done.k_low, ...), custom_call_target="tpu_custom_call" | custom-call | tf_op jit(solution)/shard_map/attend/pallas_call | solution.py:134
  64.9 13.3 %all_to_all.22.parts_ref = bf16[4,384,128]{2,1,0:T(8,128)(2,1)S(1)} all-to-all(bf16[4,384,128]{2,1,0:T(8,128)(2,1)S(1)} %bitcast.11), channel_id=1, replica_groups=mesh['groups'=2,'ctx'=4,'head'=4] {'head'}, dimensions={0} | all-to-all | bytes 786432 | tf_op jit(solution)/shard_map/all_to_all | solution.py:167
  78.2 0.8 %unpack.1 = bf16[384,512]{1,0:T(8,128)(2,1)} custom-call(bf16[4,384,128]{2,1,0:T(8,128)(2,1)S(1)} %all_to_all.22.parts_ref), custom_call_target="tpu_custom_call" | custom-call | tf_op jit(solution)/shard_map/unpack/pallas_call | solution.py:50
  (4 shorter events, 0.1 us)
Async XLA Ops:
  0.0 1.0 %copy-start = (bf16[384,512]{1,0:T(8,128)(2,1)S(1)}, bf16[384,512]{1,0:T(8,128)(2,1)}, u32[]{:S(2)}) copy-start(bf16[384,512]{1,0:T(8,128)(2,1)} %q_ref.1) | copy-start | bytes 1179652
  1.0 1.0 %copy-start.1 = (bf16[384,512]{1,0:T(8,128)(2,1)S(1)}, bf16[384,512]{1,0:T(8,128)(2,1)}, u32[]{:S(2)}) copy-start(bf16[384,512]{1,0:T(8,128)(2,1)} %k_ref.1) | copy-start | bytes 1179652
  2.0 1.0 %copy-start.2 = (bf16[384,512]{1,0:T(8,128)(2,1)S(1)}, bf16[384,512]{1,0:T(8,128)(2,1)}, u32[]{:S(2)}) copy-start(bf16[384,512]{1,0:T(8,128)(2,1)} %v_ref.1) | copy-start | bytes 1179652
  33.3 15.1 %all-to-all-start = ((bf16[4,384,128]{2,1,0:T(8,128)(2,1)}), bf16[4,384,128]{2,1,0:T(8,128)(2,1)S(1)}, u32[]{:S(2)}, u32[]{:S(2)}) async-start(bf16[4,384,128]{2,1,0:T(8,128)(2,1)} %get-tuple-element.8), calls=%async_computation | async-start | bytes 786432 | tf_op jit(solution)/shard_map/all_to_all | solution.py:153
  36.9 17.0 %collective-permute-start = (bf16[1024,128]{1,0:T(8,128)(2,1)S(1)}, bf16[1024,128]{1,0:T(8,128)(2,1)S(1)}, u32[]{:S(2)}, u32[]{:S(2)}) collective-permute-start(bf16[1024,128]{1,0:T(8,128)(2,1)S(1)} %slice.16), channel_id=1, source_target_pairs={{0,4},{4,8},{8,12},{1,5},{5,9},{9,13},{2,6},{6,10},{10,14},{3,7},{... | collective-permute-start | bytes 786440 | tf_op jit(solution)/shard_map/ppermute | solution.py:163
  42.0 11.8 %collective-permute-start.1 = (bf16[1024,128]{1,0:T(8,128)(2,1)S(1)}, bf16[1024,128]{1,0:T(8,128)(2,1)S(1)}, u32[]{:S(2)}, u32[]{:S(2)}) collective-permute-start(bf16[1024,128]{1,0:T(8,128)(2,1)S(1)} %slice.17), channel_id=1, source_target_pairs={{0,4},{4,8},{8,12},{1,5},{5,9},{9,13},{2,6},{6,10},{10,14},{3,7},{... | collective-permute-start | bytes 786440 | tf_op jit(solution)/shard_map/ppermute | solution.py:163
  44.0 9.9 %copy-start.3 = (s32[12,16]{1,0:T(8,128)S(1)}, s32[12,16]{1,0:T(8,128)}, u32[]{:S(2)}) copy-start(s32[12,16]{1,0:T(8,128)} %lists_ref.1) | copy-start | bytes 2308
  44.0 9.8 %copy-start.4 = (s32[12]{0:T(128)S(1)}, s32[12]{0:T(128)}, u32[]{:S(2)}) copy-start(s32[12]{0:T(128)} %counts_ref.1) | copy-start | bytes 148
  44.0 7.3 %collective-permute-start.2 = (bf16[896,128]{1,0:T(8,128)(2,1)S(1)}, bf16[896,128]{1,0:T(8,128)(2,1)S(1)}, u32[]{:S(2)}, u32[]{:S(2)}) collective-permute-start(bf16[896,128]{1,0:T(8,128)(2,1)S(1)} %slice.18), channel_id=1, source_target_pairs={{4,0},{8,4},{12,8},{5,1},{9,5},{13,9},{6,2},{10,6},{14,10},{7,3},{... | collective-permute-start | bytes 688136 | tf_op jit(solution)/shard_map/ppermute | solution.py:164
  46.5 7.4 %collective-permute-start.3 = (bf16[896,128]{1,0:T(8,128)(2,1)S(1)}, bf16[896,128]{1,0:T(8,128)(2,1)S(1)}, u32[]{:S(2)}, u32[]{:S(2)}) collective-permute-start(bf16[896,128]{1,0:T(8,128)(2,1)S(1)} %slice.19), channel_id=1, source_target_pairs={{4,0},{8,4},{12,8},{5,1},{9,5},{13,9},{6,2},{10,6},{14,10},{7,3},{... | collective-permute-start | bytes 688136 | tf_op jit(solution)/shard_map/ppermute | solution.py:164

commit v2 on v1

--- a/solution.py
+++ b/solution.py
@@ -153,21 +153,178 @@
     return lax.all_to_all(array, "head", split_axis=0, concat_axis=0, tiled=True).reshape(heads * rows, HDIM)
 
 
-def on_device(queries, keys, values, tile_lists, live_counts):
+def halo(array, dim):
     ctx = lax.axis_size("ctx")
-    total_tiles = tile_lists.shape[0] * ctx
-    forward = [(i, i + 1) for i in range(ctx - 1)]
-    backward = [(i + 1, i) for i in range(ctx - 1)]
+    count = array.shape[dim]
+    tail = lax.slice_in_dim(array, count - EDGE * TILE, count, axis=dim)
+    head = lax.slice_in_dim(array, 0, (EDGE - 1) * TILE, axis=dim)
+    low = lax.ppermute(tail, "ctx", [(i, i + 1) for i in range(ctx - 1)])
+    high = lax.ppermute(head, "ctx", [(i + 1, i) for i in range(ctx - 1)])
+    return low, high
+
+
+def whole_range(queries, keys, values, tile_lists, live_counts, total_tiles):
     q_parts, k_parts, v_parts = pack(queries, keys, values)
     own = to_heads(k_parts), to_heads(v_parts)
-    low = [lax.ppermute(array[-EDGE * TILE :], "ctx", forward) for array in own]
-    high = [lax.ppermute(array[: (EDGE - 1) * TILE], "ctx", backward) for array in own]
+    low, high = zip(*(halo(array, 0) for array in own))
     local_q = to_heads(q_parts)
     head_out = attend(local_q, own, low, high, tile_lists, live_counts, total_tiles)
     back = lax.all_to_all(
         head_out.reshape(q_parts.shape), "head", split_axis=0, concat_axis=0, tiled=True
     )
     return unpack(back)
+
+
+def column_of(head):
+    return pl.ds(pl.multiple_of(head * HDIM, HDIM), HDIM)
+
+
+def shift_pack_kernel(heads, q_ref, k_ref, v_ref, *out_refs):
+    me = lax.axis_index("head")
+    for shift in range(heads):
+        columns = column_of(lax.rem(me + shift, heads))
+        kv_out, q_out = out_refs[2 * shift], out_refs[2 * shift + 1]
+        kv_out[0] = k_ref[:, columns]
+        kv_out[1] = v_ref[:, columns]
+        q_out[...] = q_ref[:, columns]
+
+
+def shift_pack(queries, keys, values, heads):
+    rows = queries.shape[0]
+    kv = jax.ShapeDtypeStruct((2, rows, HDIM), keys.dtype)
+    q = jax.ShapeDtypeStruct((rows, HDIM), queries.dtype)
+    parts = pl.pallas_call(
+        functools.partial(shift_pack_kernel, heads),
+        out_shape=[kv, q] * heads,
+        in_specs=[VMEM] * 3,
+        out_specs=[VMEM] * 2 * heads,
+        compiler_params=pltpu.CompilerParams(vmem_limit_bytes=8 << 20),
+        name="shift_pack",
+    )(queries, keys, values)
+    return list(parts[0::2]), list(parts[1::2])
+
+
+def gather_kernel(heads, *refs):
+    out_ref = refs[-1]
+    me = lax.axis_index("head")
+    for shift in range(heads):
+        rows = refs[shift].shape[1]
+        source = lax.rem(me + heads - shift, heads)
+        out_ref[:, pl.ds(pl.multiple_of(source * rows, TILE), rows), :] = refs[shift][...]
+
+
+def gather(parts):
+    heads, (_, rows, _) = len(parts), parts[0].shape
+    return pl.pallas_call(
+        functools.partial(gather_kernel, heads),
+        out_shape=jax.ShapeDtypeStruct((2, heads * rows, HDIM), parts[0].dtype),
+        in_specs=[VMEM] * heads,
+        out_specs=VMEM,
+        compiler_params=pltpu.CompilerParams(vmem_limit_bytes=8 << 20),
+        name="gather",
+    )(*parts)
+
+
+def pad_kernel(low_ref, own_ref, high_ref, out_ref):
+    at = 0
+    for ref in (low_ref, own_ref, high_ref):
+        rows = ref.shape[1]
+        out_ref[:, at : at + rows, :] = ref[...]
+        at += rows
+
+
+def pad(low, own, high):
+    rows = low.shape[1] + own.shape[1] + high.shape[1]
+    return pl.pallas_call(
+        pad_kernel,
+        out_shape=jax.ShapeDtypeStruct((2, rows, HDIM), own.dtype),
+        in_specs=[VMEM] * 3,
+        out_specs=VMEM,
+        compiler_params=pltpu.CompilerParams(vmem_limit_bytes=8 << 20),
+        name="pad",
+    )(low, own, high)
+
+
+def attend_chunk_kernel(
+    shift, heads, total_tiles, lists_ref, counts_ref, q_ref, kv_ref, out_ref, bias, scores, probs
+):
+    source = lax.rem(lax.axis_index("head") + heads - shift, heads)
+    out_ref[...] = attend_block(
+        source * BLOCK, total_tiles, lists_ref, counts_ref, q_ref, kv_ref.at[0], kv_ref.at[1],
+        bias, scores, probs,
+    )
+
+
+def attend_chunk(shift, heads, queries, padded, tile_lists, live_counts, total_tiles):
+    rows = queries.shape[0]
+    pairs = BLOCK * LIST * TILE * TILE
+    return pl.pallas_call(
+        functools.partial(attend_chunk_kernel, shift, heads, total_tiles),
+        out_shape=jax.ShapeDtypeStruct(queries.shape, queries.dtype),
+        in_specs=[SMEM, SMEM, VMEM, VMEM],
+        out_specs=VMEM,
+        scratch_shapes=[
+            pltpu.SMEM((BLOCK * LIST,), jnp.float32),
+            pltpu.VMEM((rows, WINDOW * TILE), jnp.float32),
+            pltpu.VMEM((rows, WINDOW * TILE), jnp.bfloat16),
+        ],
+        compiler_params=pltpu.CompilerParams(vmem_limit_bytes=16 << 20),
+        cost_estimate=pl.CostEstimate(
+            flops=4 * pairs * HDIM, bytes_accessed=padded.size * 2, transcendentals=pairs
+        ),
+        name="attend_chunk",
+    )(tile_lists, live_counts, queries, padded)
+
+
+def shift_unpack_kernel(heads, *refs):
+    out_ref = refs[-1]
+    me = lax.axis_index("head")
+    for shift in range(heads):
+        out_ref[:, column_of(lax.rem(me + shift, heads))] = refs[shift][...]
+
+
+def shift_unpack(parts):
+    heads, (rows, _) = len(parts), parts[0].shape
+    return pl.pallas_call(
+        functools.partial(shift_unpack_kernel, heads),
+        out_shape=jax.ShapeDtypeStruct((rows, heads * HDIM), parts[0].dtype),
+        in_specs=[VMEM] * heads,
+        out_specs=VMEM,
+        compiler_params=pltpu.CompilerParams(vmem_limit_bytes=8 << 20),
+        name="shift_unpack",
+    )(*parts)
+
+
+def by_shifts(queries, keys, values, tile_lists, live_counts, total_tiles):
+    heads = lax.axis_size("head")
+    order = sorted(range(1, heads), key=lambda shift: -min(shift, heads - shift))
+
+    def send(array, shift):
+        return lax.ppermute(array, "head", [(i, (i + shift) % heads) for i in range(heads)])
+
+    kv_parts, q_parts = shift_pack(queries, keys, values, heads)
+    for shift in order:
+        kv_parts[shift] = send(kv_parts[shift], shift)
+    for shift in order:
+        q_parts[shift] = send(q_parts[shift], shift)
+    own = gather(kv_parts)
+    low, high = halo(own, 1)
+    padded = pad(low, own, high)
+    outs = [None] * heads
+    for shift in order + [0]:
+        outs[shift] = attend_chunk(
+            shift, heads, q_parts[shift], padded, tile_lists, live_counts, total_tiles
+        )
+        if shift:
+            outs[shift] = send(outs[shift], -shift)
+    return shift_unpack(outs)
+
+
+def on_device(queries, keys, values, tile_lists, live_counts):
+    total_tiles = tile_lists.shape[0] * lax.axis_size("ctx")
+    one_block = queries.shape[0] == BLOCK * TILE
+    form = by_shifts if one_block and lax.axis_size("head") <= 8 else whole_range
+    return form(queries, keys, values, tile_lists, live_counts, total_tiles)
 
 
 def solution(mesh):

time: 79.5 us -> 57.1 us (0.72)
  blocking collectives: 42.6 us -> 0 us
  waiting for transfers between devices: 5.44 us -> 16.3 us
  starting transfers between devices: 15 us -> 23.1 us
  Pallas kernels: 12.8 us -> 14.2 us
    all_to_all x3 -> x0, blocking collectives: 42.6 us -> none  [the longest x2 29.3 us: to_heads(): lax.all_to_all(array, 'head', split_axis=0, concat_axis=0, tiled=True)]
    ppermute x4 -> x11, starting transfers between devices: 11.4 us -> 23.1 us  [the longest x9 17.6 us: send(): lax.ppermute(array, 'head', [(i, (i + shift) % heads) for i in range(head...]
    ppermute x4 -> x11, waiting for transfers between devices: 5.44 us -> 16.3 us  [the longest x9 14.8 us: send(): lax.ppermute(array, 'head', [(i, (i + shift) % heads) for i in range(head...]
    all_to_all x1 -> x0, starting transfers between devices: 3.56 us -> none  [to_heads(): lax.all_to_all(array, 'head', split_axis=0, concat_axis=0, tiled=True)]
    pallas_call x3 -> x8, Pallas kernels: 12.8 us -> 14.2 us  [the longest x4 13 us: attend_chunk(): pl.pallas_call(functools.partial(attend_chunk_kernel, shift, heads, total...]
  transfers between devices with their start and end apart: 5 -> 11, of which waited for: 2 -> 5; matrix products, arithmetic and copies ran while one was open for 0% -> 0% of each run, Pallas kernels for 0% -> 23%
where the time goes in v2:
time: 57.1 us; the launch traced here: 56.8 us
  starting transfers between devices  23.1 us (40%)
  waiting for transfers between devices  16.3 us (29%)
  Pallas kernels  14.2 us (25%)
  local copies, waits for them, and re-layouts  3.06 us (5%)
    ppermute x9, starting transfers between devices, send(): lax.ppermute(array, 'head', [(i, (i + shift) % heads) for i in range(head...  17.6 us
    ppermute x9, waiting for transfers between devices, send(): lax.ppermute(array, 'head', [(i, (i + shift) % heads) for i in range(head...  14.8 us
    pallas_call x4, Pallas kernels, attend_chunk(): pl.pallas_call(functools.partial(attend_chunk_kernel, shift, heads, total...  13 us
    ppermute x1, starting transfers between devices, halo(): low = lax.ppermute(tail, 'ctx', [(i, i + 1) for i in range(ctx - 1)])  3.56 us
    unnamed x10, local copies, waits for them, and re-layouts  2.99 us
    ppermute x1, starting transfers between devices, halo(): high = lax.ppermute(head, 'ctx', [(i + 1, i) for i in range(ctx - 1)])  1.92 us
    ppermute x1, waiting for transfers between devices, halo(): high = lax.ppermute(head, 'ctx', [(i + 1, i) for i in range(ctx - 1)])  1.55 us
  transfers between devices with their start and end apart: 11, of which 5 were waited for; matrix products, arithmetic and copies ran while one was open for 0% of the time, Pallas kernels for 23%

profile of v2, /device:TPU:1, one launch (start us, length us, event | category | flops | bytes accessed | tf_op | source)
XLA Modules:
  0.0 56.8 jit_solution(5994839804675091868)
XLA Ops:
  0.0 0.0 copy-start
  0.0 1.0 %copy-done = bf16[384,512]{1,0:T(8,128)(2,1)S(1)} copy-done((bf16[384,512]{1,0:T(8,128)(2,1)S(1)}, bf16[384,512]{1,0:T(8,128)(2,1)}, u32[]{:S(2)}) %copy-start) | copy-done | bytes 393240
  1.0 0.0 copy-start.1
  1.0 1.0 %copy-done.1 = bf16[384,512]{1,0:T(8,128)(2,1)S(1)} copy-done((bf16[384,512]{1,0:T(8,128)(2,1)S(1)}, bf16[384,512]{1,0:T(8,128)(2,1)}, u32[]{:S(2)}) %copy-start.1) | copy-done | bytes 393240
  2.0 0.0 copy-start.2
  2.0 1.0 %copy-done.2 = bf16[384,512]{1,0:T(8,128)(2,1)S(1)} copy-done((bf16[384,512]{1,0:T(8,128)(2,1)S(1)}, bf16[384,512]{1,0:T(8,128)(2,1)}, u32[]{:S(2)}) %copy-start.2) | copy-done | bytes 393240
  3.0 0.2 shift_pack.1
  3.2 2.2 %collective-permute-start = (bf16[2,384,128]{2,1,0:T(8,128)(2,1)S(1)}, bf16[2,384,128]{2,1,0:T(8,128)(2,1)S(1)}, u32[]{:S(2)}, u32[]{:S(2)}) collective-permute-start(bf16[2,384,128]{2,1,0:T(8,128)(2,1)S(1)} %get-tuple-element.15), channel_id=1, source_target_pairs={{0,1},{1,2},{2,3},{3,0},{4,5},{5,6},{6,7},{7,4},{8,9},{9,10},{10,1... | collective-permute-start | bytes 589832 | tf_op jit(solution)/shard_map/ppermute | solution.py:303
  5.4 2.3 %collective-permute-start.1 = (bf16[2,384,128]{2,1,0:T(8,128)(2,1)S(1)}, bf16[2,384,128]{2,1,0:T(8,128)(2,1)S(1)}, u32[]{:S(2)}, u32[]{:S(2)}) collective-permute-start(bf16[2,384,128]{2,1,0:T(8,128)(2,1)S(1)} %get-tuple-element.16), channel_id=1, source_target_pairs={{0,2},{1,3},{2,0},{3,1},{4,6},{5,7},{6,4},{7,5},{8,10},{9,11},{10,... | collective-permute-start | bytes 589832 | tf_op jit(solution)/shard_map/ppermute | solution.py:303
  7.7 1.1 %collective-permute-start.2 = (bf16[2,384,128]{2,1,0:T(8,128)(2,1)S(1)}, bf16[2,384,128]{2,1,0:T(8,128)(2,1)S(1)}, u32[]{:S(2)}, u32[]{:S(2)}) collective-permute-start(bf16[2,384,128]{2,1,0:T(8,128)(2,1)S(1)} %get-tuple-element.17), channel_id=1, source_target_pairs={{0,3},{1,0},{2,1},{3,2},{4,7},{5,4},{6,5},{7,6},{8,11},{9,8},{10,9... | collective-permute-start | bytes 589832 | tf_op jit(solution)/shard_map/ppermute | solution.py:303
  8.8 3.3 %collective-permute-done.refs_1_ = bf16[2,384,128]{2,1,0:T(8,128)(2,1)S(1)} collective-permute-done((bf16[2,384,128]{2,1,0:T(8,128)(2,1)S(1)}, bf16[2,384,128]{2,1,0:T(8,128)(2,1)S(1)}, u32[]{:S(2)}, u32[]{:S(2)}) %collective-permute-start) | collective-permute-done | bytes 196640 | tf_op jit(solution)/shard_map/ppermute | solution.py:303
  12.1 9.1 %collective-permute-done.1.refs_2_ = bf16[2,384,128]{2,1,0:T(8,128)(2,1)S(1)} collective-permute-done((bf16[2,384,128]{2,1,0:T(8,128)(2,1)S(1)}, bf16[2,384,128]{2,1,0:T(8,128)(2,1)S(1)}, u32[]{:S(2)}, u32[]{:S(2)}) %collective-permute-start.1) | collective-permute-done | bytes 196640 | tf_op jit(solution)/shard_map/ppermute | solution.py:303
  21.2 0.0 collective-permute-done.2.refs_3_
  21.2 0.1 gather.1.own_ref
  21.3 3.6 %collective-permute-start.3 = (bf16[2,1024,128]{2,1,0:T(8,128)(2,1)S(1)}, bf16[2,1024,128]{2,1,0:T(8,128)(2,1)S(1)}, u32[]{:S(2)}, u32[]{:S(2)}) collective-permute-start(bf16[2,1024,128]{2,1,0:T(8,128)(2,1)S(1)} %slice.8), channel_id=1, source_target_pairs={{0,4},{4,8},{8,12},{1,5},{5,9},{9,13},{2,6},{6,10},{10,14},{3,7},{... | collective-permute-start | bytes 1572872 | tf_op jit(solution)/shard_map/ppermute | solution.py:161
  25.0 1.9 %collective-permute-start.4 = (bf16[2,896,128]{2,1,0:T(8,128)(2,1)S(1)}, bf16[2,896,128]{2,1,0:T(8,128)(2,1)S(1)}, u32[]{:S(2)}, u32[]{:S(2)}) collective-permute-start(bf16[2,896,128]{2,1,0:T(8,128)(2,1)S(1)} %slice.9), channel_id=1, source_target_pairs={{4,0},{8,4},{12,8},{5,1},{9,5},{13,9},{6,2},{10,6},{14,10},{7,3},{... | collective-permute-start | bytes 1376264 | tf_op jit(solution)/shard_map/ppermute | solution.py:162
  26.9 4.5 %collective-permute-start.5 = (bf16[384,128]{1,0:T(8,128)(2,1)S(1)}, bf16[384,128]{1,0:T(8,128)(2,1)S(1)}, u32[]{:S(2)}, u32[]{:S(2)}) collective-permute-start(bf16[384,128]{1,0:T(8,128)(2,1)S(1)} %get-tuple-element.18), channel_id=1, source_target_pairs={{0,1},{1,2},{2,3},{3,0},{4,5},{5,6},{6,7},{7,4},{8,9},{9,10},{10,1... | collective-permute-start | bytes 294920 | tf_op jit(solution)/shard_map/ppermute | solution.py:303
  31.3 1.4 %collective-permute-start.7 = (bf16[384,128]{1,0:T(8,128)(2,1)S(1)}, bf16[384,128]{1,0:T(8,128)(2,1)S(1)}, u32[]{:S(2)}, u32[]{:S(2)}) collective-permute-start(bf16[384,128]{1,0:T(8,128)(2,1)S(1)} %get-tuple-element.19), channel_id=1, source_target_pairs={{0,2},{1,3},{2,0},{3,1},{4,6},{5,7},{6,4},{7,5},{8,10},{9,11},{10,... | collective-permute-start | bytes 294920 | tf_op jit(solution)/shard_map/ppermute | solution.py:303
  32.7 0.0 copy-start.3
  32.7 0.0 copy-start.4
  32.7 0.8 %collective-permute-start.9 = (bf16[384,128]{1,0:T(8,128)(2,1)S(1)}, bf16[384,128]{1,0:T(8,128)(2,1)S(1)}, u32[]{:S(2)}, u32[]{:S(2)}) collective-permute-start(bf16[384,128]{1,0:T(8,128)(2,1)S(1)} %get-tuple-element.20), channel_id=1, source_target_pairs={{0,3},{1,0},{2,1},{3,2},{4,7},{5,4},{6,5},{7,6},{8,11},{9,8},{10,9... | collective-permute-start | bytes 294920 | tf_op jit(solution)/shard_map/ppermute | solution.py:303
  33.5 1.5 %collective-permute-done.4.high_ref = bf16[2,896,128]{2,1,0:T(8,128)(2,1)S(1)} collective-permute-done((bf16[2,896,128]{2,1,0:T(8,128)(2,1)S(1)}, bf16[2,896,128]{2,1,0:T(8,128)(2,1)S(1)}, u32[]{:S(2)}, u32[]{:S(2)}) %collective-permute-start.4) | collective-permute-done | bytes 458784 | tf_op jit(solution)/shard_map/ppermute | solution.py:162
  35.0 0.0 collective-permute-done.3.low_ref
  35.0 0.1 pad.1.kv_ref
  35.2 0.3 collective-permute-done.5.q_ref
  35.5 0.0 copy-done.3
  35.5 0.0 copy-done.4
  35.5 3.2 %attend_chunk.5 = bf16[384,128]{1,0:T(8,128)(2,1)S(1)} custom-call(s32[12,16]{1,0:T(8,128)S(1)} %copy-done.3, s32[12]{0:T(128)S(1)} %copy-done.4, bf16[384,128]{1,0:T(8,128)(2,1)S(1)} %collective-permute-done.5.q_ref, bf16[2,3456,128]{2,1,0:T(8,128)(2,1)S(1)} %pad.1.kv_ref), custom_call_target="tpu_custom_call" | custom-call | flops 402653184 | bytes 1769472 | tf_op jit(solution)/shard_map/attend_chunk/pallas_call | solution.py:261
  38.7 4.9 %collective-permute-start.6 = (bf16[384,128]{1,0:T(8,128)(2,1)S(1)}, bf16[384,128]{1,0:T(8,128)(2,1)S(1)}, u32[]{:S(2)}, u32[]{:S(2)}) collective-permute-start(bf16[384,128]{1,0:T(8,128)(2,1)S(1)} %attend_chunk.5), channel_id=1, source_target_pairs={{0,3},{1,0},{2,1},{3,2},{4,7},{5,4},{6,5},{7,6},{8,11},{9,8},{10,9... | collective-permute-start | bytes 294920 | tf_op jit(solution)/shard_map/ppermute | solution.py:303
  43.7 0.0 collective-permute-done.7.q_ref
  43.7 3.2 %attend_chunk.6 = bf16[384,128]{1,0:T(8,128)(2,1)S(1)} custom-call(s32[12,16]{1,0:T(8,128)S(1)} %copy-done.3, s32[12]{0:T(128)S(1)} %copy-done.4, bf16[384,128]{1,0:T(8,128)(2,1)S(1)} %collective-permute-done.7.q_ref, bf16[2,3456,128]{2,1,0:T(8,128)(2,1)S(1)} %pad.1.kv_ref), custom_call_target="tpu_custom_call" | custom-call | flops 402653184 | bytes 1769472 | tf_op jit(solution)/shard_map/attend_chunk/pallas_call | solution.py:261
  46.9 0.5 collective-permute-start.8
  47.4 0.0 collective-permute-done.9.q_ref
  47.4 3.2 %attend_chunk.7 = bf16[384,128]{1,0:T(8,128)(2,1)S(1)} custom-call(s32[12,16]{1,0:T(8,128)S(1)} %copy-done.3, s32[12]{0:T(128)S(1)} %copy-done.4, bf16[384,128]{1,0:T(8,128)(2,1)S(1)} %collective-permute-done.9.q_ref, bf16[2,3456,128]{2,1,0:T(8,128)(2,1)S(1)} %pad.1.kv_ref), custom_call_target="tpu_custom_call" | custom-call | flops 402653184 | bytes 1769472 | tf_op jit(solution)/shard_map/attend_chunk/pallas_call | solution.py:261
  50.7 0.1 collective-permute-start.10
  50.7 3.2 %attend_chunk.4.refs_0_ = bf16[384,128]{1,0:T(8,128)(2,1)S(1)} custom-call(s32[12,16]{1,0:T(8,128)S(1)} %copy-done.3, s32[12]{0:T(128)S(1)} %copy-done.4, bf16[384,128]{1,0:T(8,128)(2,1)S(1)} %get-tuple-element.13.q_ref, bf16[2,3456,128]{2,1,0:T(8,128)(2,1)S(1)} %pad.1.kv_ref), custom_call_target="tpu_custom_call" | custom-call | flops 402653184 | bytes 1769472 | tf_op jit(solution)/shard_map/attend_chunk/pallas_call | solution.py:261
  54.0 0.0 collective-permute-done.6.refs_1_
  54.0 0.0 collective-permute-done.8.refs_2_
  54.0 2.0 %collective-permute-done.10.refs_3_ = bf16[384,128]{1,0:T(8,128)(2,1)S(1)} collective-permute-done((bf16[384,128]{1,0:T(8,128)(2,1)S(1)}, bf16[384,128]{1,0:T(8,128)(2,1)S(1)}, u32[]{:S(2)}, u32[]{:S(2)}) %collective-permute-start.10) | collective-permute-done | bytes 98336 | tf_op jit(solution)/shard_map/ppermute | solution.py:303
  56.0 0.9 %shift_unpack.1 = bf16[384,512]{1,0:T(8,128)(2,1)} custom-call(bf16[384,128]{1,0:T(8,128)(2,1)S(1)} %attend_chunk.4.refs_0_, bf16[384,128]{1,0:T(8,128)(2,1)S(1)} %collective-permute-done.6.refs_1_, bf16[384,128]{1,0:T(8,128)(2,1)S(1)} %collective-permute-done.8.refs_2_, bf16[384,128]{1,0:T(8,128)(2,1)S(1)} %collective-permute-done.10.refs_3_), custom_call_target="tpu_custom_call" | custom-call | tf_op jit(solution)/shard_map/shift_unpack/pallas_call | solution.py:288
  (2 shorter events, 0.1 us)
Async XLA Ops:
  0.0 1.0 %copy-start = (bf16[384,512]{1,0:T(8,128)(2,1)S(1)}, bf16[384,512]{1,0:T(8,128)(2,1)}, u32[]{:S(2)}) copy-start(bf16[384,512]{1,0:T(8,128)(2,1)} %q_ref.1) | copy-start | bytes 1179652
  1.0 1.0 %copy-start.1 = (bf16[384,512]{1,0:T(8,128)(2,1)S(1)}, bf16[384,512]{1,0:T(8,128)(2,1)}, u32[]{:S(2)}) copy-start(bf16[384,512]{1,0:T(8,128)(2,1)} %k_ref.1) | copy-start | bytes 1179652
  2.0 1.0 %copy-start.2 = (bf16[384,512]{1,0:T(8,128)(2,1)S(1)}, bf16[384,512]{1,0:T(8,128)(2,1)}, u32[]{:S(2)}) copy-start(bf16[384,512]{1,0:T(8,128)(2,1)} %v_ref.1) | copy-start | bytes 1179652
  3.2 8.9 %collective-permute-start = (bf16[2,384,128]{2,1,0:T(8,128)(2,1)S(1)}, bf16[2,384,128]{2,1,0:T(8,128)(2,1)S(1)}, u32[]{:S(2)}, u32[]{:S(2)}) collective-permute-start(bf16[2,384,128]{2,1,0:T(8,128)(2,1)S(1)} %get-tuple-element.15), channel_id=1, source_target_pairs={{0,1},{1,2},{2,3},{3,0},{4,5},{5,6},{6,7},{7,4},{8,9},{9,10},{10,1... | collective-permute-start | bytes 589832 | tf_op jit(solution)/shard_map/ppermute | solution.py:303
  5.4 15.8 %collective-permute-start.1 = (bf16[2,384,128]{2,1,0:T(8,128)(2,1)S(1)}, bf16[2,384,128]{2,1,0:T(8,128)(2,1)S(1)}, u32[]{:S(2)}, u32[]{:S(2)}) collective-permute-start(bf16[2,384,128]{2,1,0:T(8,128)(2,1)S(1)} %get-tuple-element.16), channel_id=1, source_target_pairs={{0,2},{1,3},{2,0},{3,1},{4,6},{5,7},{6,4},{7,5},{8,10},{9,11},{10,... | collective-permute-start | bytes 589832 | tf_op jit(solution)/shard_map/ppermute | solution.py:303
  7.7 13.5 %collective-permute-start.2 = (bf16[2,384,128]{2,1,0:T(8,128)(2,1)S(1)}, bf16[2,384,128]{2,1,0:T(8,128)(2,1)S(1)}, u32[]{:S(2)}, u32[]{:S(2)}) collective-permute-start(bf16[2,384,128]{2,1,0:T(8,128)(2,1)S(1)} %get-tuple-element.17), channel_id=1, source_target_pairs={{0,3},{1,0},{2,1},{3,2},{4,7},{5,4},{6,5},{7,6},{8,11},{9,8},{10,9... | collective-permute-start | bytes 589832 | tf_op jit(solution)/shard_map/ppermute | solution.py:303
  21.3 13.7 %collective-permute-start.3 = (bf16[2,1024,128]{2,1,0:T(8,128)(2,1)S(1)}, bf16[2,1024,128]{2,1,0:T(8,128)(2,1)S(1)}, u32[]{:S(2)}, u32[]{:S(2)}) collective-permute-start(bf16[2,1024,128]{2,1,0:T(8,128)(2,1)S(1)} %slice.8), channel_id=1, source_target_pairs={{0,4},{4,8},{8,12},{1,5},{5,9},{9,13},{2,6},{6,10},{10,14},{3,7},{... | collective-permute-start | bytes 1572872 | tf_op jit(solution)/shard_map/ppermute | solution.py:161
  25.0 10.1 %collective-permute-start.4 = (bf16[2,896,128]{2,1,0:T(8,128)(2,1)S(1)}, bf16[2,896,128]{2,1,0:T(8,128)(2,1)S(1)}, u32[]{:S(2)}, u32[]{:S(2)}) collective-permute-start(bf16[2,896,128]{2,1,0:T(8,128)(2,1)S(1)} %slice.9), channel_id=1, source_target_pairs={{4,0},{8,4},{12,8},{5,1},{9,5},{13,9},{6,2},{10,6},{14,10},{7,3},{... | collective-permute-start | bytes 1376264 | tf_op jit(solution)/shard_map/ppermute | solution.py:162
  26.9 8.6 %collective-permute-start.5 = (bf16[384,128]{1,0:T(8,128)(2,1)S(1)}, bf16[384,128]{1,0:T(8,128)(2,1)S(1)}, u32[]{:S(2)}, u32[]{:S(2)}) collective-permute-start(bf16[384,128]{1,0:T(8,128)(2,1)S(1)} %get-tuple-element.18), channel_id=1, source_target_pairs={{0,1},{1,2},{2,3},{3,0},{4,5},{5,6},{6,7},{7,4},{8,9},{9,10},{10,1... | collective-permute-start | bytes 294920 | tf_op jit(solution)/shard_map/ppermute | solution.py:303
  31.3 12.3 %collective-permute-start.7 = (bf16[384,128]{1,0:T(8,128)(2,1)S(1)}, bf16[384,128]{1,0:T(8,128)(2,1)S(1)}, u32[]{:S(2)}, u32[]{:S(2)}) collective-permute-start(bf16[384,128]{1,0:T(8,128)(2,1)S(1)} %get-tuple-element.19), channel_id=1, source_target_pairs={{0,2},{1,3},{2,0},{3,1},{4,6},{5,7},{6,4},{7,5},{8,10},{9,11},{10,... | collective-permute-start | bytes 294920 | tf_op jit(solution)/shard_map/ppermute | solution.py:303
  32.7 2.8 %copy-start.3 = (s32[12,16]{1,0:T(8,128)S(1)}, s32[12,16]{1,0:T(8,128)}, u32[]{:S(2)}) copy-start(s32[12,16]{1,0:T(8,128)} %lists_ref.7) | copy-start | bytes 2308
  32.7 2.8 %copy-start.4 = (s32[12]{0:T(128)S(1)}, s32[12]{0:T(128)}, u32[]{:S(2)}) copy-start(s32[12]{0:T(128)} %counts_ref.7) | copy-start | bytes 148
  32.7 14.7 %collective-permute-start.9 = (bf16[384,128]{1,0:T(8,128)(2,1)S(1)}, bf16[384,128]{1,0:T(8,128)(2,1)S(1)}, u32[]{:S(2)}, u32[]{:S(2)}) collective-permute-start(bf16[384,128]{1,0:T(8,128)(2,1)S(1)} %get-tuple-element.20), channel_id=1, source_target_pairs={{0,3},{1,0},{2,1},{3,2},{4,7},{5,4},{6,5},{7,6},{8,11},{9,8},{10,9... | collective-permute-start | bytes 294920 | tf_op jit(solution)/shard_map/ppermute | solution.py:303
  38.7 15.3 %collective-permute-start.6 = (bf16[384,128]{1,0:T(8,128)(2,1)S(1)}, bf16[384,128]{1,0:T(8,128)(2,1)S(1)}, u32[]{:S(2)}, u32[]{:S(2)}) collective-permute-start(bf16[384,128]{1,0:T(8,128)(2,1)S(1)} %attend_chunk.5), channel_id=1, source_target_pairs={{0,3},{1,0},{2,1},{3,2},{4,7},{5,4},{6,5},{7,6},{8,11},{9,8},{10,9... | collective-permute-start | bytes 294920 | tf_op jit(solution)/shard_map/ppermute | solution.py:303
  46.9 7.1 %collective-permute-start.8 = (bf16[384,128]{1,0:T(8,128)(2,1)S(1)}, bf16[384,128]{1,0:T(8,128)(2,1)S(1)}, u32[]{:S(2)}, u32[]{:S(2)}) collective-permute-start(bf16[384,128]{1,0:T(8,128)(2,1)S(1)} %attend_chunk.6), channel_id=1, source_target_pairs={{0,2},{1,3},{2,0},{3,1},{4,6},{5,7},{6,4},{7,5},{8,10},{9,11},{10,... | collective-permute-start | bytes 294920 | tf_op jit(solution)/shard_map/ppermute | solution.py:303
  50.7 5.3 %collective-permute-start.10 = (bf16[384,128]{1,0:T(8,128)(2,1)S(1)}, bf16[384,128]{1,0:T(8,128)(2,1)S(1)}, u32[]{:S(2)}, u32[]{:S(2)}) collective-permute-start(bf16[384,128]{1,0:T(8,128)(2,1)S(1)} %attend_chunk.7), channel_id=1, source_target_pairs={{0,1},{1,2},{2,3},{3,0},{4,5},{5,6},{6,7},{7,4},{8,9},{9,10},{10,1... | collective-permute-start | bytes 294920 | tf_op jit(solution)/shard_map/ppermute | solution.py:303

commit v3 on v1

v3 whole, which is shorter than its diff:
```python
import functools
import math

import jax
import jax.numpy as jnp
from jax import lax
from jax.experimental import pallas as pl
from jax.experimental.pallas import tpu as pltpu
from jax.sharding import PartitionSpec as P

HDIM = 128
TILE = 128
EDGE = 8
LIST = 16
BLOCK = 3
WINDOW = BLOCK + LIST - 1
HIDDEN = -1e30
EXPONENT_SCALE = HDIM ** (-0.5) * math.log2(math.e)
SMEM = pl.BlockSpec(memory_space=pltpu.SMEM)
VMEM = pl.BlockSpec(memory_space=pltpu.VMEM)


def call(kernel, name, operands, in_specs, shapes, scratch=(), limit=8, cost=None):
    out_shape = jax.tree.map(
        lambda shape: shape if hasattr(shape, "dtype") else jax.ShapeDtypeStruct(shape, jnp.bfloat16),
        shapes,
        is_leaf=lambda node: isinstance(node, tuple) or hasattr(node, "dtype"),
    )
    return pl.pallas_call(
        kernel,
        out_shape=out_shape,
        in_specs=in_specs,
        out_specs=jax.tree.map(lambda _: VMEM, out_shape),
        scratch_shapes=scratch,
        compiler_params=pltpu.CompilerParams(vmem_limit_bytes=limit << 20),
        cost_estimate=cost,
        name=name,
    )(*operands)


def column_of(head):
    return pl.ds(pl.multiple_of(head * HDIM, HDIM), HDIM)


def bias_kernel(total_tiles, lists_ref, counts_ref, bias_ref):
    @pl.loop(0, lists_ref.shape[0])
    def _(row):
        own = lists_ref[row, 0]
        count = counts_ref[row]
        for entry in range(LIST):
            listed = lists_ref[row, entry]
            live = (entry < count) & (listed >= 0) & (listed < total_tiles)
            value = jnp.where(live, 0.0, HIDDEN)
            bias_ref[row, pl.ds(listed - own + EDGE, 1), :] = jnp.full((1, TILE), value, jnp.float32)


def mask_bias(tile_lists, live_counts, total_tiles):
    shape = jax.ShapeDtypeStruct((tile_lists.shape[0], LIST, TILE), jnp.float32)
    kernel = functools.partial(bias_kernel, total_tiles)
    return call(kernel, "mask_bias", (tile_lists, live_counts), [SMEM, SMEM], shape)


def attend_block(first, q_ref, kt_ref, v_ref, bias_ref, scores, probs):
    base = pl.multiple_of(first * TILE, TILE)
    for pair in range(WINDOW // 2):
        low = max(0, 2 * pair - LIST + 1)
        high = min(BLOCK - 1, 2 * pair + 1)
        part = jnp.dot(
            q_ref[low * TILE : (high + 1) * TILE, :],
            kt_ref[:, pl.ds(base + pair * 2 * TILE, 2 * TILE)],
            preferred_element_type=jnp.float32,
        )
        for tile in range(low, high + 1):
            for half in range(2):
                place = 2 * pair + half
                offset = place - tile
                if 0 <= offset < LIST:
                    rows = slice((tile - low) * TILE, (tile - low + 1) * TILE)
                    scores[tile * TILE : (tile + 1) * TILE, place * TILE : (place + 1) * TILE] = (
                        part[rows, half * TILE : (half + 1) * TILE]
                        + bias_ref[first + tile, offset : offset + 1, :]
                    )
    divisors = []
    for tile in range(BLOCK):
        rows = slice(tile * TILE, (tile + 1) * TILE)
        highest = scores[rows, tile * TILE : (tile + 1) * TILE]
        for place in range(tile + 1, tile + LIST):
            highest = jnp.maximum(highest, scores[rows, place * TILE : (place + 1) * TILE])
        highest = jnp.broadcast_to(jnp.max(highest, axis=1, keepdims=True), (TILE, TILE))
        total = jnp.zeros((TILE, TILE), jnp.float32)
        for place in range(WINDOW):
            columns = slice(place * TILE, (place + 1) * TILE)
            if 0 <= place - tile < LIST:
                weights = jnp.exp2((scores[rows, columns] - highest) * EXPONENT_SCALE)
                total += weights
                probs[rows, columns] = weights.astype(jnp.bfloat16)
            else:
                probs[rows, columns] = jnp.zeros((TILE, TILE), jnp.bfloat16)
        divisors.append(jnp.sum(total, axis=1, keepdims=True))
    mixed = jnp.dot(
        probs[...], v_ref[pl.ds(base, WINDOW * TILE), :], preferred_element_type=jnp.float32
    )
    return (mixed / jnp.concatenate(divisors, axis=0)).astype(jnp.bfloat16)


def block_scratch():
    rows = BLOCK * TILE
    return [
        pltpu.VMEM((rows, WINDOW * TILE), jnp.float32),
        pltpu.VMEM((rows, WINDOW * TILE), jnp.bfloat16),
    ]


def halo(array, dim):
    ctx = lax.axis_size("ctx")
    count = array.shape[dim]
    tail = lax.slice_in_dim(array, count - EDGE * TILE, count, axis=dim)
    head = lax.slice_in_dim(array, 0, (EDGE - 1) * TILE, axis=dim)
    low = lax.ppermute(tail, "ctx", [(i, i + 1) for i in range(ctx - 1)])
    high = lax.ppermute(head, "ctx", [(i + 1, i) for i in range(ctx - 1)])
    return low, array, high


def pack_kernel(heads, q_ref, k_ref, v_ref, q_out, k_out, v_out):
    for source, target in ((k_ref, k_out), (v_ref, v_out), (q_ref, q_out)):
        for head in range(heads):
            target[head] = source[:, head * HDIM : (head + 1) * HDIM]


def unpack_kernel(heads, parts_ref, out_ref):
    for head in range(heads):
        out_ref[:, head * HDIM : (head + 1) * HDIM] = parts_ref[head]


def attend_range_kernel(q_ref, k_low, k_own, k_high, v_low, v_own, v_high, bias_ref, out_ref, kt, v, *scratch):
    at = 0
    for k_part, v_part in ((k_low, v_low), (k_own, v_own), (k_high, v_high)):
        rows = k_part.shape[0]
        kt[:, at : at + rows] = k_part[...].T
        v[at : at + rows, :] = v_part[...]
        at += rows

    @pl.loop(0, q_ref.shape[0] // (BLOCK * TILE))
    def _(block):
        place = pl.ds(pl.multiple_of(block * BLOCK * TILE, TILE), BLOCK * TILE)
        out_ref[place, :] = attend_block(block * BLOCK, q_ref.at[place, :], kt, v, bias_ref, *scratch)


def to_heads(array):
    heads, rows, _ = array.shape
    return lax.all_to_all(array, "head", split_axis=0, concat_axis=0, tiled=True).reshape(heads * rows, HDIM)


def whole_range(queries, keys, values, bias):
    rows, columns = queries.shape
    heads = columns // HDIM
    parts = (heads, rows, HDIM)
    q_parts, k_parts, v_parts = call(
        functools.partial(pack_kernel, heads), "pack", (queries, keys, values), [VMEM] * 3, [parts] * 3
    )
    k_own, v_own = to_heads(k_parts), to_heads(v_parts)
    local_q = to_heads(q_parts)
    padded = heads * rows + (LIST - 1) * TILE
    head_out = call(
        attend_range_kernel,
        "attend_range",
        (local_q, *halo(k_own, 0), *halo(v_own, 0), bias),
        [VMEM] * 8,
        (heads * rows, HDIM),
        [pltpu.VMEM((HDIM, padded), jnp.bfloat16), pltpu.VMEM((padded, HDIM), jnp.bfloat16)] + block_scratch(),
        24,
    )
    back = lax.all_to_all(head_out.reshape(parts), "head", split_axis=0, concat_axis=0, tiled=True)
    return call(functools.partial(unpack_kernel, heads), "unpack", (back,), [VMEM], (rows, columns))


def load_kernel(heads, array_ref, *out_refs):
    me = lax.axis_index("head")
    for shift in range(heads):
        out_refs[shift][...] = array_ref[:, column_of(lax.rem(me + shift, heads))]


def load(array, heads):
    shapes = [(array.shape[0], HDIM)] * heads
    return list(call(functools.partial(load_kernel, heads), "load", (array,), [VMEM], shapes))


def turn_kernel(array_ref, *refs):
    refs[-1][...] = array_ref[...].T


def pass_kernel(array_ref, *refs):
    refs[-1][...] = array_ref[...]


def turned(array, *after):
    operands = (array, *after)
    return call(turn_kernel, "turned", operands, [VMEM] * len(operands), array.shape[::-1])


def passed(array, *after):
    operands = (array, *after)
    return call(pass_kernel, "passed", operands, [VMEM] * len(operands), array.shape)


def gather_kernel(dim, *refs):
    heads, out_ref = len(refs) - 1, refs[-1]
    me = lax.axis_index("head")
    for shift in range(heads):
        count = refs[shift].shape[dim]
        source = lax.rem(me + heads - shift, heads)
        place = pl.ds(pl.multiple_of(source * count, TILE), count)
        if dim == 0:
            out_ref[place, :] = refs[shift][...]
        else:
            out_ref[:, place] = refs[shift][...]


def gathered(parts, dim):
    shape = list(parts[0].shape)
    shape[dim] *= len(parts)
    kernel = functools.partial(gather_kernel, dim)
    return call(kernel, "gathered", parts, [VMEM] * len(parts), tuple(shape))


def pad_kernel(dim, low_ref, own_ref, high_ref, out_ref):
    at = 0
    for ref in (low_ref, own_ref, high_ref):
        count = ref.shape[dim]
        if dim == 0:
            out_ref[at : at + count, :] = ref[...]
        else:
            out_ref[:, at : at + count] = ref[...]
        at += count


def padded_range(parts, dim):
    parts = halo(gathered(parts, dim), dim)
    shape = list(parts[1].shape)
    shape[dim] += (LIST - 1) * TILE
    return call(functools.partial(pad_kernel, dim), "padded", parts, [VMEM] * 3, tuple(shape))


def attend_chunk_kernel(shift, heads, q_ref, kt_ref, v_ref, bias_ref, out_ref, *scratch):
    source = lax.rem(lax.axis_index("head") + heads - shift, heads)
    out_ref[...] = attend_block(source * BLOCK, q_ref, kt_ref, v_ref, bias_ref, *scratch)


def attend_chunk(shift, heads, queries, keys, values, bias):
    pairs = BLOCK * LIST * TILE * TILE
    return call(
        functools.partial(attend_chunk_kernel, shift, heads),
        "attend_chunk",
        (queries, keys, values, bias),
        [VMEM] * 4,
        queries.shape,
        block_scratch(),
        16,
        pl.CostEstimate(flops=4 * pairs * HDIM, bytes_accessed=1 << 20, transcendentals=pairs),
    )


def spread_kernel(heads, *refs):
    out_ref = refs[-1]
    me = lax.axis_index("head")
    for shift in range(heads):
        out_ref[:, column_of(lax.rem(me + shift, heads))] = refs[shift][...]


def by_shifts(queries, keys, values, bias):
    heads = lax.axis_size("head")
    order = sorted(range(1, heads), key=lambda shift: -min(shift, heads - shift))

    def send(array, shift):
        return lax.ppermute(array, "head", [(i, (i + shift) % heads) for i in range(heads)])

    v_parts, k_parts, q_parts = (load(array, heads) for array in (values, keys, queries))
    k_parts[0] = turned(k_parts[0])
    for shift in order:
        v_parts[shift] = send(v_parts[shift], shift)
    for shift in order:
        k_parts[shift] = send(turned(k_parts[shift], v_parts[shift]), shift)
    all_values = padded_range(v_parts, 0)
    for shift in order:
        q_parts[shift] = send(passed(q_parts[shift], k_parts[shift]), shift)
    all_keys = padded_range(k_parts, 1)
    outs = [None] * heads
    for shift in order + [0]:
        outs[shift] = attend_chunk(shift, heads, q_parts[shift], all_keys, all_values, bias)
        if shift:
            outs[shift] = send(outs[shift], -shift)
    return call(functools.partial(spread_kernel, heads), "spread", outs, [VMEM] * heads, queries.shape)


def on_device(queries, keys, values, tile_lists, live_counts):
    bias = mask_bias(tile_lists, live_counts, tile_lists.shape[0] * lax.axis_size("ctx"))
    one_block = queries.shape[0] == BLOCK * TILE
    form = by_shifts if one_block and lax.axis_size("head") <= 8 else whole_range
    return form(queries, keys, values, bias)


def solution(mesh):
    return jax.shard_map(
        on_device,
        mesh=mesh,
        in_specs=(
            P(("groups", "ctx", "head"), None),
            P(("groups", "ctx", "head"), None),
            P(("groups", "ctx", "head"), None),
            P(("groups", "ctx"), None),
            P(("groups", "ctx")),
        ),
        out_specs=P(("groups", "ctx", "head"), None),
        check_vma=False,
    )
```

time: 79.5 us -> 51.9 us (0.65)
  the two profiles are of different devices: /device:TPU:1 before, /device:TPU:0 now
where the time goes in v3:
time: 51.9 us; the launch traced here: 51 us
  starting transfers between devices  31.8 us (61%)
  Pallas kernels  12.3 us (24%)
  waiting for transfers between devices  5.56 us (11%)
  local copies, waits for them, and re-layouts  1.09 us (2%)
    ppermute x12, starting transfers between devices, send(): lax.ppermute(array, 'head', [(i, (i + shift) % heads) for i in range(head...  23 us
    pallas_call x20, Pallas kernels, call(): pl.pallas_call(kernel, out_shape=out_shape, in_specs=in_specs, out_specs=...  12.3 us
    ppermute x2, starting transfers between devices, halo(): low = lax.ppermute(tail, 'ctx', [(i, i + 1) for i in range(ctx - 1)])  6.19 us
    ppermute x12, waiting for transfers between devices, send(): lax.ppermute(array, 'head', [(i, (i + shift) % heads) for i in range(head...  5.55 us
    ppermute x2, starting transfers between devices, halo(): high = lax.ppermute(head, 'ctx', [(i + 1, i) for i in range(ctx - 1)])  2.58 us
  transfers between devices with their start and end apart: 16, of which 3 were waited for; matrix products, arithmetic and copies ran while one was open for 0% of the time, Pallas kernels for 22%

profile of v3, /device:TPU:0, one launch (start us, length us, event | category | flops | bytes accessed | tf_op | source)
XLA Modules:
  0.0 51.0 jit_solution(1325601835723921623)
XLA Ops:
  0.0 1.0 %copy-done = bf16[384,512]{1,0:T(8,128)(2,1)S(1)} copy-done((bf16[384,512]{1,0:T(8,128)(2,1)S(1)}, bf16[384,512]{1,0:T(8,128)(2,1)}, u32[]{:S(2)}) %copy-start) | copy-done | bytes 393240
  1.0 0.1 load.5
  1.1 3.1 %collective-permute-start = (bf16[384,128]{1,0:T(8,128)(2,1)S(1)}, bf16[384,128]{1,0:T(8,128)(2,1)S(1)}, u32[]{:S(2)}, u32[]{:S(2)}) collective-permute-start(bf16[384,128]{1,0:T(8,128)(2,1)S(1)} %get-tuple-element.20), channel_id=1, source_target_pairs={{0,1},{1,2},{2,3},{3,0},{4,5},{5,6},{6,7},{7,4},{8,9},{9,10},{10,1... | collective-permute-start | bytes 294920 | tf_op jit(solution)/shard_map/ppermute | solution.py:275
  4.2 2.6 %collective-permute-start.2 = (bf16[384,128]{1,0:T(8,128)(2,1)S(1)}, bf16[384,128]{1,0:T(8,128)(2,1)S(1)}, u32[]{:S(2)}, u32[]{:S(2)}) collective-permute-start(bf16[384,128]{1,0:T(8,128)(2,1)S(1)} %get-tuple-element.22), channel_id=1, source_target_pairs={{0,2},{1,3},{2,0},{3,1},{4,6},{5,7},{6,4},{7,5},{8,10},{9,11},{10,... | collective-permute-start | bytes 294920 | tf_op jit(solution)/shard_map/ppermute | solution.py:275
  6.7 1.3 %collective-permute-start.4 = (bf16[384,128]{1,0:T(8,128)(2,1)S(1)}, bf16[384,128]{1,0:T(8,128)(2,1)S(1)}, u32[]{:S(2)}, u32[]{:S(2)}) collective-permute-start(bf16[384,128]{1,0:T(8,128)(2,1)S(1)} %get-tuple-element.24), channel_id=1, source_target_pairs={{0,3},{1,0},{2,1},{3,2},{4,7},{5,4},{6,5},{7,6},{8,11},{9,8},{10,9... | collective-permute-start | bytes 294920 | tf_op jit(solution)/shard_map/ppermute | solution.py:275
  8.1 0.1 load.4
  8.2 1.7 %collective-permute-done.refs_0_.refs_1_ = bf16[384,128]{1,0:T(8,128)(2,1)S(1)} collective-permute-done((bf16[384,128]{1,0:T(8,128)(2,1)S(1)}, bf16[384,128]{1,0:T(8,128)(2,1)S(1)}, u32[]{:S(2)}, u32[]{:S(2)}) %collective-permute-start) | collective-permute-done | bytes 98336 | tf_op jit(solution)/shard_map/ppermute | solution.py:275
  9.8 0.1 turned.5
  9.9 2.7 %collective-permute-start.1 = (bf16[128,384]{1,0:T(8,128)(2,1)S(1)}, bf16[128,384]{1,0:T(8,128)(2,1)S(1)}, u32[]{:S(2)}, u32[]{:S(2)}) collective-permute-start(bf16[128,384]{1,0:T(8,128)(2,1)S(1)} %turned.5), channel_id=1, source_target_pairs={{0,1},{1,2},{2,3},{3,0},{4,5},{5,6},{6,7},{7,4},{8,9},{9,10},{10,1... | collective-permute-start | bytes 294920 | tf_op jit(solution)/shard_map/ppermute | solution.py:275
  12.6 1.8 %collective-permute-done.2.refs_0_.refs_2_ = bf16[384,128]{1,0:T(8,128)(2,1)S(1)} collective-permute-done((bf16[384,128]{1,0:T(8,128)(2,1)S(1)}, bf16[384,128]{1,0:T(8,128)(2,1)S(1)}, u32[]{:S(2)}, u32[]{:S(2)}) %collective-permute-start.2) | collective-permute-done | bytes 98336 | tf_op jit(solution)/shard_map/ppermute | solution.py:275
  14.4 0.1 turned.6
  14.5 0.5 collective-permute-start.3
  14.9 0.0 collective-permute-done.4.refs_0_.refs_3_
  14.9 0.1 turned.7
  15.0 3.4 %collective-permute-start.5 = (bf16[128,384]{1,0:T(8,128)(2,1)S(1)}, bf16[128,384]{1,0:T(8,128)(2,1)S(1)}, u32[]{:S(2)}, u32[]{:S(2)}) collective-permute-start(bf16[128,384]{1,0:T(8,128)(2,1)S(1)} %turned.7), channel_id=1, source_target_pairs={{0,3},{1,0},{2,1},{3,2},{4,7},{5,4},{6,5},{7,6},{8,11},{9,8},{10,9... | collective-permute-start | bytes 294920 | tf_op jit(solution)/shard_map/ppermute | solution.py:275
  18.5 1.3 %collective-permute-start.9 = (bf16[896,128]{1,0:T(8,128)(2,1)S(1)}, bf16[896,128]{1,0:T(8,128)(2,1)S(1)}, u32[]{:S(2)}, u32[]{:S(2)}) collective-permute-start(bf16[896,128]{1,0:T(8,128)(2,1)S(1)} %slice.19), channel_id=1, source_target_pairs={{4,0},{8,4},{12,8},{5,1},{9,5},{13,9},{6,2},{10,6},{14,10},{7,3},{... | collective-permute-start | bytes 688136 | tf_op jit(solution)/shard_map/ppermute | solution.py:120
  19.8 3.0 %collective-permute-start.8 = (bf16[1024,128]{1,0:T(8,128)(2,1)S(1)}, bf16[1024,128]{1,0:T(8,128)(2,1)S(1)}, u32[]{:S(2)}, u32[]{:S(2)}) collective-permute-start(bf16[1024,128]{1,0:T(8,128)(2,1)S(1)} %slice.18), channel_id=1, source_target_pairs={{0,4},{4,8},{8,12},{1,5},{5,9},{9,13},{2,6},{6,10},{10,14},{3,7},{... | collective-permute-start | bytes 786440 | tf_op jit(solution)/shard_map/ppermute | solution.py:119
  22.9 0.1 turned.4.refs_0_
  23.0 0.0 collective-permute-done.1.refs_1_.refs_0_
  23.0 0.0 collective-permute-done.3.refs_2_.refs_0_
  23.0 0.0 collective-permute-done.5.refs_3_.refs_0_
  23.1 0.0 copy-start.2
  23.1 3.1 %collective-permute-start.6 = (bf16[128,1024]{1,0:T(8,128)(2,1)S(1)}, bf16[128,1024]{1,0:T(8,128)(2,1)S(1)}, u32[]{:S(2)}, u32[]{:S(2)}) collective-permute-start(bf16[128,1024]{1,0:T(8,128)(2,1)S(1)} %slice.16), channel_id=1, source_target_pairs={{0,4},{4,8},{8,12},{1,5},{5,9},{9,13},{2,6},{6,10},{10,14},{3,7},{... | collective-permute-start | bytes 786440 | tf_op jit(solution)/shard_map/ppermute | solution.py:119
  26.3 1.3 %collective-permute-start.7 = (bf16[128,896]{1,0:T(8,128)(2,1)S(1)}, bf16[128,896]{1,0:T(8,128)(2,1)S(1)}, u32[]{:S(2)}, u32[]{:S(2)}) collective-permute-start(bf16[128,896]{1,0:T(8,128)(2,1)S(1)} %slice.17), channel_id=1, source_target_pairs={{4,0},{8,4},{12,8},{5,1},{9,5},{13,9},{6,2},{10,6},{14,10},{7,3},{... | collective-permute-start | bytes 688136 | tf_op jit(solution)/shard_map/ppermute | solution.py:120
  27.6 0.1 load.3
  27.7 1.4 %collective-permute-start.14 = (bf16[384,128]{1,0:T(8,128)(2,1)S(1)}, bf16[384,128]{1,0:T(8,128)(2,1)S(1)}, u32[]{:S(2)}, u32[]{:S(2)}) collective-permute-start(bf16[384,128]{1,0:T(8,128)(2,1)S(1)} %passed.5), channel_id=1, source_target_pairs={{0,3},{1,0},{2,1},{3,2},{4,7},{5,4},{6,5},{7,6},{8,11},{9,8},{10,9... | collective-permute-start | bytes 294920 | tf_op jit(solution)/shard_map/ppermute | solution.py:275
  29.1 0.0 collective-permute-done.9.high_ref
  29.1 1.1 %collective-permute-start.12 = (bf16[384,128]{1,0:T(8,128)(2,1)S(1)}, bf16[384,128]{1,0:T(8,128)(2,1)S(1)}, u32[]{:S(2)}, u32[]{:S(2)}) collective-permute-start(bf16[384,128]{1,0:T(8,128)(2,1)S(1)} %passed.4), channel_id=1, source_target_pairs={{0,2},{1,3},{2,0},{3,1},{4,6},{5,7},{6,4},{7,5},{8,10},{9,11},{10,... | collective-permute-start | bytes 294920 | tf_op jit(solution)/shard_map/ppermute | solution.py:275
  30.2 0.0 collective-permute-done.8.low_ref
  30.2 2.0 %collective-permute-start.10 = (bf16[384,128]{1,0:T(8,128)(2,1)S(1)}, bf16[384,128]{1,0:T(8,128)(2,1)S(1)}, u32[]{:S(2)}, u32[]{:S(2)}) collective-permute-start(bf16[384,128]{1,0:T(8,128)(2,1)S(1)} %passed.3), channel_id=1, source_target_pairs={{0,1},{1,2},{2,3},{3,0},{4,5},{5,6},{6,7},{7,4},{8,9},{9,10},{10,1... | collective-permute-start | bytes 294920 | tf_op jit(solution)/shard_map/ppermute | solution.py:275
  32.3 1.4 %mask_bias.1.bias_ref = f32[12,16,128]{2,1,0:T(8,128)S(1)} custom-call(s32[12,16]{1,0:T(8,128)S(1)} %copy-done.3, s32[12]{0:T(128)S(1)} %copy-done.4), custom_call_target="tpu_custom_call" | custom-call | tf_op jit(solution)/shard_map/mask_bias/pallas_call | solution.py:29
  33.7 0.1 padded.3.v_ref
  33.7 0.0 collective-permute-done.7.high_ref
  33.7 0.0 collective-permute-done.6.low_ref
  33.7 0.1 padded.2.kt_ref
  33.8 0.0 collective-permute-done.14.q_ref
  33.8 2.3 %attend_chunk.7 = bf16[384,128]{1,0:T(8,128)(2,1)S(1)} custom-call(bf16[384,128]{1,0:T(8,128)(2,1)S(1)} %collective-permute-done.14.q_ref, bf16[128,3456]{1,0:T(8,128)(2,1)S(1)} %padded.2.kt_ref, bf16[3456,128]{1,0:T(8,128)(2,1)S(1)} %padded.3.v_ref, f32[12,16,128]{2,1,0:T(8,128)S(1)} %mask_bias.1.bias_ref), custom_call_target="tpu_custom_call" | custom-call | flops 402653184 | bytes 1048576 | tf_op jit(solution)/shard_map/attend_chunk/pallas_call | solution.py:29
  36.1 0.7 %collective-permute-start.15 = (bf16[384,128]{1,0:T(8,128)(2,1)S(1)}, bf16[384,128]{1,0:T(8,128)(2,1)S(1)}, u32[]{:S(2)}, u32[]{:S(2)}) collective-permute-start(bf16[384,128]{1,0:T(8,128)(2,1)S(1)} %attend_chunk.7), channel_id=1, source_target_pairs={{0,1},{1,2},{2,3},{3,0},{4,5},{5,6},{6,7},{7,4},{8,9},{9,10},{10,1... | collective-permute-start | bytes 294920 | tf_op jit(solution)/shard_map/ppermute | solution.py:275
  36.8 0.0 collective-permute-done.12.q_ref
  36.8 2.3 %attend_chunk.6 = bf16[384,128]{1,0:T(8,128)(2,1)S(1)} custom-call(bf16[384,128]{1,0:T(8,128)(2,1)S(1)} %collective-permute-done.12.q_ref, bf16[128,3456]{1,0:T(8,128)(2,1)S(1)} %padded.2.kt_ref, bf16[3456,128]{1,0:T(8,128)(2,1)S(1)} %padded.3.v_ref, f32[12,16,128]{2,1,0:T(8,128)S(1)} %mask_bias.1.bias_ref), custom_call_target="tpu_custom_call" | custom-call | flops 402653184 | bytes 1048576 | tf_op jit(solution)/shard_map/attend_chunk/pallas_call | solution.py:29
  39.1 1.9 %collective-permute-start.13 = (bf16[384,128]{1,0:T(8,128)(2,1)S(1)}, bf16[384,128]{1,0:T(8,128)(2,1)S(1)}, u32[]{:S(2)}, u32[]{:S(2)}) collective-permute-start(bf16[384,128]{1,0:T(8,128)(2,1)S(1)} %attend_chunk.6), channel_id=1, source_target_pairs={{0,2},{1,3},{2,0},{3,1},{4,6},{5,7},{6,4},{7,5},{8,10},{9,11},{10,... | collective-permute-start | bytes 294920 | tf_op jit(solution)/shard_map/ppermute | solution.py:275
  41.0 0.0 collective-permute-done.10.q_ref
  41.0 2.3 %attend_chunk.5 = bf16[384,128]{1,0:T(8,128)(2,1)S(1)} custom-call(bf16[384,128]{1,0:T(8,128)(2,1)S(1)} %collective-permute-done.10.q_ref, bf16[128,3456]{1,0:T(8,128)(2,1)S(1)} %padded.2.kt_ref, bf16[3456,128]{1,0:T(8,128)(2,1)S(1)} %padded.3.v_ref, f32[12,16,128]{2,1,0:T(8,128)S(1)} %mask_bias.1.bias_ref), custom_call_target="tpu_custom_call" | custom-call | flops 402653184 | bytes 1048576 | tf_op jit(solution)/shard_map/attend_chunk/pallas_call | solution.py:29
  43.3 2.4 %collective-permute-start.11 = (bf16[384,128]{1,0:T(8,128)(2,1)S(1)}, bf16[384,128]{1,0:T(8,128)(2,1)S(1)}, u32[]{:S(2)}, u32[]{:S(2)}) collective-permute-start(bf16[384,128]{1,0:T(8,128)(2,1)S(1)} %attend_chunk.5), channel_id=1, source_target_pairs={{0,3},{1,0},{2,1},{3,2},{4,7},{5,4},{6,5},{7,6},{8,11},{9,8},{10,9... | collective-permute-start | bytes 294920 | tf_op jit(solution)/shard_map/ppermute | solution.py:275
  45.7 2.3 %attend_chunk.4.refs_0_ = bf16[384,128]{1,0:T(8,128)(2,1)S(1)} custom-call(bf16[384,128]{1,0:T(8,128)(2,1)S(1)} %get-tuple-element.17.q_ref, bf16[128,3456]{1,0:T(8,128)(2,1)S(1)} %padded.2.kt_ref, bf16[3456,128]{1,0:T(8,128)(2,1)S(1)} %padded.3.v_ref, f32[12,16,128]{2,1,0:T(8,128)S(1)} %mask_bias.1.bias_ref), custom_call_target="tpu_custom_call" | custom-call | flops 402653184 | bytes 1048576 | tf_op jit(solution)/shard_map/attend_chunk/pallas_call | solution.py:29
  48.0 0.0 collective-permute-done.15.refs_3_
  48.0 2.1 %collective-permute-done.11.refs_1_ = bf16[384,128]{1,0:T(8,128)(2,1)S(1)} collective-permute-done((bf16[384,128]{1,0:T(8,128)(2,1)S(1)}, bf16[384,128]{1,0:T(8,128)(2,1)S(1)}, u32[]{:S(2)}, u32[]{:S(2)}) %collective-permute-start.11) | collective-permute-done | bytes 98336 | tf_op jit(solution)/shard_map/ppermute | solution.py:275
  50.1 0.9 %spread.1 = bf16[384,512]{1,0:T(8,128)(2,1)} custom-call(bf16[384,128]{1,0:T(8,128)(2,1)S(1)} %attend_chunk.4.refs_0_, bf16[384,128]{1,0:T(8,128)(2,1)S(1)} %collective-permute-done.11.refs_1_, bf16[384,128]{1,0:T(8,128)(2,1)S(1)} %collective-permute-done.13.refs_2_, bf16[384,128]{1,0:T(8,128)(2,1)S(1)} %collective-permute-done.15.refs_3_), custom_call_target="tpu_custom_call" | custom-call | tf_op jit(solution)/shard_map/spread/pallas_call | solution.py:29
  (18 shorter events, 0.2 us)
Async XLA Ops:
  0.0 1.0 %copy-start = (bf16[384,512]{1,0:T(8,128)(2,1)S(1)}, bf16[384,512]{1,0:T(8,128)(2,1)}, u32[]{:S(2)}) copy-start(bf16[384,512]{1,0:T(8,128)(2,1)} %array_ref.5) | copy-start | bytes 1179652
  1.0 7.1 %copy-start.1 = (bf16[384,512]{1,0:T(8,128)(2,1)S(1)}, bf16[384,512]{1,0:T(8,128)(2,1)}, u32[]{:S(2)}) copy-start(bf16[384,512]{1,0:T(8,128)(2,1)} %array_ref.4) | copy-start | bytes 1179652
  1.1 8.8 %collective-permute-start = (bf16[384,128]{1,0:T(8,128)(2,1)S(1)}, bf16[384,128]{1,0:T(8,128)(2,1)S(1)}, u32[]{:S(2)}, u32[]{:S(2)}) collective-permute-start(bf16[384,128]{1,0:T(8,128)(2,1)S(1)} %get-tuple-element.20), channel_id=1, source_target_pairs={{0,1},{1,2},{2,3},{3,0},{4,5},{5,6},{6,7},{7,4},{8,9},{9,10},{10,1... | collective-permute-start | bytes 294920 | tf_op jit(solution)/shard_map/ppermute | solution.py:275
  4.2 10.2 %collective-permute-start.2 = (bf16[384,128]{1,0:T(8,128)(2,1)S(1)}, bf16[384,128]{1,0:T(8,128)(2,1)S(1)}, u32[]{:S(2)}, u32[]{:S(2)}) collective-permute-start(bf16[384,128]{1,0:T(8,128)(2,1)S(1)} %get-tuple-element.22), channel_id=1, source_target_pairs={{0,2},{1,3},{2,0},{3,1},{4,6},{5,7},{6,4},{7,5},{8,10},{9,11},{10,... | collective-permute-start | bytes 294920 | tf_op jit(solution)/shard_map/ppermute | solution.py:275
  6.7 8.2 %collective-permute-start.4 = (bf16[384,128]{1,0:T(8,128)(2,1)S(1)}, bf16[384,128]{1,0:T(8,128)(2,1)S(1)}, u32[]{:S(2)}, u32[]{:S(2)}) collective-permute-start(bf16[384,128]{1,0:T(8,128)(2,1)S(1)} %get-tuple-element.24), channel_id=1, source_target_pairs={{0,3},{1,0},{2,1},{3,2},{4,7},{5,4},{6,5},{7,6},{8,11},{9,8},{10,9... | collective-permute-start | bytes 294920 | tf_op jit(solution)/shard_map/ppermute | solution.py:275
  9.9 13.1 %collective-permute-start.1 = (bf16[128,384]{1,0:T(8,128)(2,1)S(1)}, bf16[128,384]{1,0:T(8,128)(2,1)S(1)}, u32[]{:S(2)}, u32[]{:S(2)}) collective-permute-start(bf16[128,384]{1,0:T(8,128)(2,1)S(1)} %turned.5), channel_id=1, source_target_pairs={{0,1},{1,2},{2,3},{3,0},{4,5},{5,6},{6,7},{7,4},{8,9},{9,10},{10,1... | collective-permute-start | bytes 294920 | tf_op jit(solution)/shard_map/ppermute | solution.py:275
  14.5 8.5 %collective-permute-start.3 = (bf16[128,384]{1,0:T(8,128)(2,1)S(1)}, bf16[128,384]{1,0:T(8,128)(2,1)S(1)}, u32[]{:S(2)}, u32[]{:S(2)}) collective-permute-start(bf16[128,384]{1,0:T(8,128)(2,1)S(1)} %turned.6), channel_id=1, source_target_pairs={{0,2},{1,3},{2,0},{3,1},{4,6},{5,7},{6,4},{7,5},{8,10},{9,11},{10,... | collective-permute-start | bytes 294920 | tf_op jit(solution)/shard_map/ppermute | solution.py:275
  15.0 8.0 %collective-permute-start.5 = (bf16[128,384]{1,0:T(8,128)(2,1)S(1)}, bf16[128,384]{1,0:T(8,128)(2,1)S(1)}, u32[]{:S(2)}, u32[]{:S(2)}) collective-permute-start(bf16[128,384]{1,0:T(8,128)(2,1)S(1)} %turned.7), channel_id=1, source_target_pairs={{0,3},{1,0},{2,1},{3,2},{4,7},{5,4},{6,5},{7,6},{8,11},{9,8},{10,9... | collective-permute-start | bytes 294920 | tf_op jit(solution)/shard_map/ppermute | solution.py:275
  18.5 10.6 %collective-permute-start.9 = (bf16[896,128]{1,0:T(8,128)(2,1)S(1)}, bf16[896,128]{1,0:T(8,128)(2,1)S(1)}, u32[]{:S(2)}, u32[]{:S(2)}) collective-permute-start(bf16[896,128]{1,0:T(8,128)(2,1)S(1)} %slice.19), channel_id=1, source_target_pairs={{4,0},{8,4},{12,8},{5,1},{9,5},{13,9},{6,2},{10,6},{14,10},{7,3},{... | collective-permute-start | bytes 688136 | tf_op jit(solution)/shard_map/ppermute | solution.py:120
  19.8 10.4 %collective-permute-start.8 = (bf16[1024,128]{1,0:T(8,128)(2,1)S(1)}, bf16[1024,128]{1,0:T(8,128)(2,1)S(1)}, u32[]{:S(2)}, u32[]{:S(2)}) collective-permute-start(bf16[1024,128]{1,0:T(8,128)(2,1)S(1)} %slice.18), channel_id=1, source_target_pairs={{0,4},{4,8},{8,12},{1,5},{5,9},{9,13},{2,6},{6,10},{10,14},{3,7},{... | collective-permute-start | bytes 786440 | tf_op jit(solution)/shard_map/ppermute | solution.py:119
  23.1 4.5 %copy-start.2 = (bf16[384,512]{1,0:T(8,128)(2,1)S(1)}, bf16[384,512]{1,0:T(8,128)(2,1)}, u32[]{:S(2)}) copy-start(bf16[384,512]{1,0:T(8,128)(2,1)} %array_ref.3) | copy-start | bytes 1179652
  23.1 10.6 %collective-permute-start.6 = (bf16[128,1024]{1,0:T(8,128)(2,1)S(1)}, bf16[128,1024]{1,0:T(8,128)(2,1)S(1)}, u32[]{:S(2)}, u32[]{:S(2)}) collective-permute-start(bf16[128,1024]{1,0:T(8,128)(2,1)S(1)} %slice.16), channel_id=1, source_target_pairs={{0,4},{4,8},{8,12},{1,5},{5,9},{9,13},{2,6},{6,10},{10,14},{3,7},{... | collective-permute-start | bytes 786440 | tf_op jit(solution)/shard_map/ppermute | solution.py:119
  26.3 7.5 %collective-permute-start.7 = (bf16[128,896]{1,0:T(8,128)(2,1)S(1)}, bf16[128,896]{1,0:T(8,128)(2,1)S(1)}, u32[]{:S(2)}, u32[]{:S(2)}) collective-permute-start(bf16[128,896]{1,0:T(8,128)(2,1)S(1)} %slice.17), channel_id=1, source_target_pairs={{4,0},{8,4},{12,8},{5,1},{9,5},{13,9},{6,2},{10,6},{14,10},{7,3},{... | collective-permute-start | bytes 688136 | tf_op jit(solution)/shard_map/ppermute | solution.py:120
  27.7 6.1 %collective-permute-start.14 = (bf16[384,128]{1,0:T(8,128)(2,1)S(1)}, bf16[384,128]{1,0:T(8,128)(2,1)S(1)}, u32[]{:S(2)}, u32[]{:S(2)}) collective-permute-start(bf16[384,128]{1,0:T(8,128)(2,1)S(1)} %passed.5), channel_id=1, source_target_pairs={{0,3},{1,0},{2,1},{3,2},{4,7},{5,4},{6,5},{7,6},{8,11},{9,8},{10,9... | collective-permute-start | bytes 294920 | tf_op jit(solution)/shard_map/ppermute | solution.py:275
  29.1 7.7 %collective-permute-start.12 = (bf16[384,128]{1,0:T(8,128)(2,1)S(1)}, bf16[384,128]{1,0:T(8,128)(2,1)S(1)}, u32[]{:S(2)}, u32[]{:S(2)}) collective-permute-start(bf16[384,128]{1,0:T(8,128)(2,1)S(1)} %passed.4), channel_id=1, source_target_pairs={{0,2},{1,3},{2,0},{3,1},{4,6},{5,7},{6,4},{7,5},{8,10},{9,11},{10,... | collective-permute-start | bytes 294920 | tf_op jit(solution)/shard_map/ppermute | solution.py:275
  30.2 2.0 %copy-start.3 = (s32[12,16]{1,0:T(8,128)S(1)}, s32[12,16]{1,0:T(8,128)}, u32[]{:S(2)}) copy-start(s32[12,16]{1,0:T(8,128)} %lists_ref.1) | copy-start | bytes 2308
  30.2 2.0 %copy-start.4 = (s32[12]{0:T(128)S(1)}, s32[12]{0:T(128)}, u32[]{:S(2)}) copy-start(s32[12]{0:T(128)} %counts_ref.1) | copy-start | bytes 148
  30.2 10.8 %collective-permute-start.10 = (bf16[384,128]{1,0:T(8,128)(2,1)S(1)}, bf16[384,128]{1,0:T(8,128)(2,1)S(1)}, u32[]{:S(2)}, u32[]{:S(2)}) collective-permute-start(bf16[384,128]{1,0:T(8,128)(2,1)S(1)} %passed.3), channel_id=1, source_target_pairs={{0,1},{1,2},{2,3},{3,0},{4,5},{5,6},{6,7},{7,4},{8,9},{9,10},{10,1... | collective-permute-start | bytes 294920 | tf_op jit(solution)/shard_map/ppermute | solution.py:275
  36.1 11.8 %collective-permute-start.15 = (bf16[384,128]{1,0:T(8,128)(2,1)S(1)}, bf16[384,128]{1,0:T(8,128)(2,1)S(1)}, u32[]{:S(2)}, u32[]{:S(2)}) collective-permute-start(bf16[384,128]{1,0:T(8,128)(2,1)S(1)} %attend_chunk.7), channel_id=1, source_target_pairs={{0,1},{1,2},{2,3},{3,0},{4,5},{5,6},{6,7},{7,4},{8,9},{9,10},{10,1... | collective-permute-start | bytes 294920 | tf_op jit(solution)/shard_map/ppermute | solution.py:275
  39.1 8.9 %collective-permute-start.13 = (bf16[384,128]{1,0:T(8,128)(2,1)S(1)}, bf16[384,128]{1,0:T(8,128)(2,1)S(1)}, u32[]{:S(2)}, u32[]{:S(2)}) collective-permute-start(bf16[384,128]{1,0:T(8,128)(2,1)S(1)} %attend_chunk.6), channel_id=1, source_target_pairs={{0,2},{1,3},{2,0},{3,1},{4,6},{5,7},{6,4},{7,5},{8,10},{9,11},{10,... | collective-permute-start | bytes 294920 | tf_op jit(solution)/shard_map/ppermute | solution.py:275
  43.3 6.8 %collective-permute-start.11 = (bf16[384,128]{1,0:T(8,128)(2,1)S(1)}, bf16[384,128]{1,0:T(8,128)(2,1)S(1)}, u32[]{:S(2)}, u32[]{:S(2)}) collective-permute-start(bf16[384,128]{1,0:T(8,128)(2,1)S(1)} %attend_chunk.5), channel_id=1, source_target_pairs={{0,3},{1,0},{2,1},{3,2},{4,7},{5,4},{6,5},{7,6},{8,11},{9,8},{10,9... | collective-permute-start | bytes 294920 | tf_op jit(solution)/shard_map/ppermute | solution.py:275

commit v4 on v3

v4 whole, which is shorter than its diff:
```python
import functools
import math

import jax
import jax.numpy as jnp
from jax import lax
from jax.experimental import pallas as pl
from jax.experimental.pallas import tpu as pltpu
from jax.sharding import PartitionSpec as P

HDIM = 128
TILE = 128
EDGE = 8
LIST = 16
BLOCK = 3
WINDOW = BLOCK + LIST - 1
HIDDEN = -1e30
EXPONENT_SCALE = HDIM ** (-0.5) * math.log2(math.e)
SMEM = pl.BlockSpec(memory_space=pltpu.SMEM)
VMEM = pl.BlockSpec(memory_space=pltpu.VMEM)


def call(kernel, name, operands, in_specs, shapes, scratch=(), limit=8, cost=None):
    out_shape = jax.tree.map(
        lambda shape: shape if hasattr(shape, "dtype") else jax.ShapeDtypeStruct(shape, jnp.bfloat16),
        shapes,
        is_leaf=lambda node: isinstance(node, tuple) or hasattr(node, "dtype"),
    )
    return pl.pallas_call(
        kernel,
        out_shape=out_shape,
        in_specs=in_specs,
        out_specs=jax.tree.map(lambda _: VMEM, out_shape),
        scratch_shapes=scratch,
        compiler_params=pltpu.CompilerParams(vmem_limit_bytes=limit << 20),
        cost_estimate=cost,
        name=name,
    )(*operands)


def column_of(head):
    return pl.ds(pl.multiple_of(head * HDIM, HDIM), HDIM)


def rows_of(tile):
    return slice(tile * TILE, (tile + 1) * TILE)


def bias_kernel(total_tiles, lists_ref, counts_ref, bias_ref):
    bias_ref[...] = jnp.full(bias_ref.shape, HIDDEN, jnp.float32)

    @pl.loop(0, lists_ref.shape[0])
    def _(row):
        own = lists_ref[row, 0]
        count = counts_ref[row]
        for entry in range(LIST):
            listed = lists_ref[row, entry]
            live = (entry < count) & (listed >= 0) & (listed < total_tiles)
            value = jnp.where(live, 0.0, HIDDEN)
            bias_ref[row, pl.ds(row + listed - own + EDGE, 1), :] = jnp.full((1, TILE), value, jnp.float32)


def mask_bias(tile_lists, live_counts, total_tiles):
    tiles = tile_lists.shape[0]
    shape = jax.ShapeDtypeStruct((tiles, tiles + LIST - 1, TILE), jnp.float32)
    kernel = functools.partial(bias_kernel, total_tiles)
    return call(kernel, "mask_bias", (tile_lists, live_counts), [SMEM, SMEM], shape)


def attend_tiles(q_ref, kv_ref, at, count, bias_ref, row, place_of, scores, probs, before=None):
    for pair in range(count // 2):
        keys = jnp.concatenate([kv_ref[0, at + 2 * pair], kv_ref[0, at + 2 * pair + 1]], axis=1)
        part = jnp.dot(q_ref[...], keys, preferred_element_type=jnp.float32)
        for half in range(2):
            place = pl.ds(place_of(2 * pair + half), 1)
            columns = rows_of(2 * pair + half)
            for tile in range(BLOCK):
                scores[rows_of(tile), columns] = part[rows_of(tile), rows_of(half)] + bias_ref[row + tile, place, :]
    maxima, divisors, factors = [], [], []
    for tile in range(BLOCK):
        rows = rows_of(tile)
        highest = scores[rows, rows_of(0)]
        for key_tile in range(1, count):
            highest = jnp.maximum(highest, scores[rows, rows_of(key_tile)])
        highest = jnp.broadcast_to(jnp.max(highest, axis=1, keepdims=True), (TILE, TILE))
        if before:
            highest = jnp.maximum(highest, before[0][rows, :])
        total = jnp.zeros((TILE, TILE), jnp.float32)
        for key_tile in range(count):
            columns = rows_of(key_tile)
            weights = jnp.exp2((scores[rows, columns] - highest) * EXPONENT_SCALE)
            total += weights
            probs[rows, columns] = weights.astype(jnp.bfloat16)
        divisor = jnp.broadcast_to(jnp.sum(total, axis=1, keepdims=True), (TILE, TILE))
        if before:
            factors.append(jnp.exp2((before[0][rows, :] - highest) * EXPONENT_SCALE))
            divisor += before[1][rows, :] * factors[-1]
        maxima.append(highest)
        divisors.append(divisor)
    values = kv_ref[1, pl.ds(at, count)].reshape(count * TILE, HDIM)
    mixed = jnp.dot(probs[...], values, preferred_element_type=jnp.float32)
    if before:
        mixed += before[2][...] * jnp.concatenate(factors, axis=0)
    return jnp.concatenate(maxima, axis=0), jnp.concatenate(divisors, axis=0), mixed


def tile_scratch(count):
    shape = (BLOCK * TILE, count * TILE)
    return [pltpu.VMEM(shape, jnp.float32), pltpu.VMEM(shape, jnp.bfloat16)]


def attend_cost(count):
    pairs = BLOCK * count * TILE * TILE
    return pl.CostEstimate(flops=4 * pairs * HDIM, bytes_accessed=1 << 20, transcendentals=pairs)


def halo(array, dim, unit):
    ctx = lax.axis_size("ctx")
    count = array.shape[dim]
    tail = lax.slice_in_dim(array, count - EDGE * unit, count, axis=dim)
    head = lax.slice_in_dim(array, 0, (EDGE - 1) * unit, axis=dim)
    low = lax.ppermute(tail, "ctx", [(i, i + 1) for i in range(ctx - 1)])
    high = lax.ppermute(head, "ctx", [(i + 1, i) for i in range(ctx - 1)])
    return low, high


def pack_kernel(heads, q_ref, k_ref, v_ref, q_out, k_out, v_out):
    for source, target in ((k_ref, k_out), (v_ref, v_out), (q_ref, q_out)):
        for head in range(heads):
            target[head] = source[:, head * HDIM : (head + 1) * HDIM]


def unpack_kernel(heads, parts_ref, out_ref):
    for head in range(heads):
        out_ref[:, head * HDIM : (head + 1) * HDIM] = parts_ref[head]


def attend_range_kernel(q_ref, k_low, k_own, k_high, v_low, v_own, v_high, bias_ref, out_ref, kv, *scratch):
    at = 0
    for k_part, v_part in ((k_low, v_low), (k_own, v_own), (k_high, v_high)):
        for tile in range(k_part.shape[0] // TILE):
            kv[0, at] = k_part[rows_of(tile), :].T
            kv[1, at] = v_part[rows_of(tile), :]
            at += 1

    @pl.loop(0, q_ref.shape[0] // (BLOCK * TILE))
    def _(block):
        place = pl.ds(pl.multiple_of(block * BLOCK * TILE, TILE), BLOCK * TILE)
        first = block * BLOCK
        _, divisor, mixed = attend_tiles(
            q_ref.at[place, :], kv, first, WINDOW, bias_ref, first, lambda tile: first + tile, *scratch
        )
        out_ref[place, :] = (mixed / divisor).astype(jnp.bfloat16)


def to_heads(array):
    heads, rows, _ = array.shape
    return lax.all_to_all(array, "head", split_axis=0, concat_axis=0, tiled=True).reshape(heads * rows, HDIM)


def whole_range(queries, keys, values, bias):
    rows, columns = queries.shape
    heads = columns // HDIM
    parts = (heads, rows, HDIM)
    q_parts, k_parts, v_parts = call(
        functools.partial(pack_kernel, heads), "pack", (queries, keys, values), [VMEM] * 3, [parts] * 3
    )
    k_own, v_own = to_heads(k_parts), to_heads(v_parts)
    (k_low, k_high), (v_low, v_high) = halo(k_own, 0, TILE), halo(v_own, 0, TILE)
    local_q = to_heads(q_parts)
    padded = heads * rows // TILE + LIST - 1
    head_out = call(
        attend_range_kernel,
        "attend_range",
        (local_q, k_low, k_own, k_high, v_low, v_own, v_high, bias),
        [VMEM] * 8,
        (heads * rows, HDIM),
        [pltpu.VMEM((2, padded, TILE, HDIM), jnp.bfloat16)] + tile_scratch(WINDOW),
        24,
    )
    back = lax.all_to_all(head_out.reshape(parts), "head", split_axis=0, concat_axis=0, tiled=True)
    return call(functools.partial(unpack_kernel, heads), "unpack", (back,), [VMEM], (rows, columns))


def load_kv_kernel(heads, shift, k_ref, v_ref, out_ref):
    columns = column_of(lax.rem(lax.axis_index("head") + shift, heads))
    for tile in range(BLOCK):
        out_ref[0, tile] = k_ref[rows_of(tile), columns].T
        out_ref[1, tile] = v_ref[rows_of(tile), columns]


def load_q_kernel(heads, shift, q_ref, *refs):
    refs[-1][...] = q_ref[:, column_of(lax.rem(lax.axis_index("head") + shift, heads))]


def gather_kernel(*refs):
    heads, out_ref = len(refs) - 1, refs[-1]
    me = lax.axis_index("head")
    for shift in range(heads):
        out_ref[:, pl.ds(lax.rem(me + heads - shift, heads) * BLOCK, BLOCK)] = refs[shift][...]


def join_kernel(low_ref, high_ref, out_ref):
    out_ref[:, : low_ref.shape[1]] = low_ref[...]
    out_ref[:, low_ref.shape[1] :] = high_ref[...]


def first_row(shift, heads):
    return lax.rem(lax.axis_index("head") + heads - shift, heads) * BLOCK


def attend_own_kernel(shift, heads, q_ref, kv_ref, bias_ref, max_ref, divisor_ref, mixed_ref, *scratch):
    max_ref[...], divisor_ref[...], mixed_ref[...] = attend_tiles(
        q_ref, kv_ref, 0, kv_ref.shape[1], bias_ref, first_row(shift, heads), lambda tile: EDGE + tile, *scratch
    )


def attend_halo_kernel(shift, heads, own, q_ref, kv_ref, bias_ref, *refs):
    before, out_ref, scratch = refs[:3], refs[3], refs[4:]
    row = first_row(shift, heads)
    at = jnp.minimum(row, kv_ref.shape[1] - EDGE)

    def place_of(tile):
        return at + tile + jnp.where(at + tile < EDGE, 0, own)

    _, divisor, mixed = attend_tiles(
        q_ref, kv_ref, at, EDGE, bias_ref, row, place_of, *scratch, before=before
    )
    out_ref[...] = (mixed / divisor).astype(jnp.bfloat16)


def spread_kernel(heads, *refs):
    out_ref = refs[-1]
    me = lax.axis_index("head")
    for shift in range(heads):
        out_ref[:, column_of(lax.rem(me + shift, heads))] = refs[shift][...]


def by_shifts(queries, keys, values, bias):
    heads = lax.axis_size("head")
    tiles = heads * BLOCK
    order = sorted(range(1, heads), key=lambda shift: -min(shift, heads - shift))
    chunk = (queries.shape[0], HDIM)
    sums = jax.ShapeDtypeStruct(chunk, jnp.float32)

    def send(array, shift):
        return lax.ppermute(array, "head", [(i, (i + shift) % heads) for i in range(heads)])

    def kernel_of(kernel, *settings):
        return functools.partial(kernel, *settings)

    kv_parts, q_parts = [None] * heads, [None] * heads
    for shift in order + [0]:
        part = call(
            kernel_of(load_kv_kernel, heads, shift), "load_kv", (keys, values), [VMEM] * 2, (2, BLOCK, TILE, HDIM)
        )
        kv_parts[shift] = send(part, shift) if shift else part
    for shift in order + [0]:
        after = (kv_parts[shift],) if shift else ()
        part = call(
            kernel_of(load_q_kernel, heads, shift), "load_q", (queries, *after), [VMEM] * (1 + len(after)), chunk
        )
        q_parts[shift] = send(part, shift) if shift else part
    own = call(gather_kernel, "gather", kv_parts, [VMEM] * heads, (2, tiles, TILE, HDIM))
    low_high = halo(own, 1, 1)
    partial = [None] * heads
    for shift in order + [0]:
        partial[shift] = call(
            kernel_of(attend_own_kernel, shift, heads),
            "attend_own",
            (q_parts[shift], own, bias),
            [VMEM] * 3,
            [sums] * 3,
            tile_scratch(tiles),
            16,
            attend_cost(tiles),
        )
    around = call(join_kernel, "join", low_high, [VMEM] * 2, (2, LIST - 1, TILE, HDIM))
    outs = [None] * heads
    for shift in order + [0]:
        outs[shift] = call(
            kernel_of(attend_halo_kernel, shift, heads, tiles),
            "attend_halo",
            (q_parts[shift], around, bias, *partial[shift]),
            [VMEM] * 6,
            chunk,
            tile_scratch(EDGE),
            16,
            attend_cost(EDGE),
        )
        if shift:
            outs[shift] = send(outs[shift], -shift)
    return call(kernel_of(spread_kernel, heads), "spread", outs, [VMEM] * heads, queries.shape)


def on_device(queries, keys, values, tile_lists, live_counts):
    bias = mask_bias(tile_lists, live_counts, tile_lists.shape[0] * lax.axis_size("ctx"))
    heads = lax.axis_size("head")
    in_chunks = queries.shape[0] == BLOCK * TILE and heads <= 8 and heads % 2 == 0
    form = by_shifts if in_chunks and heads * BLOCK >= EDGE else whole_range
    return form(queries, keys, values, bias)


def solution(mesh):
    return jax.shard_map(
        on_device,
        mesh=mesh,
        in_specs=(
            P(("groups", "ctx", "head"), None),
            P(("groups", "ctx", "head"), None),
            P(("groups", "ctx", "head"), None),
            P(("groups", "ctx"), None),
            P(("groups", "ctx")),
        ),
        out_specs=P(("groups", "ctx", "head"), None),
        check_vma=False,
    )
```

time: 51.9 us -> 57 us (1.098); the launches traced: 51 us -> 56.8 us
  waiting for transfers between devices: 5.56 us -> 19.8 us
  starting transfers between devices: 31.8 us -> 20.8 us
  Pallas kernels: 12.3 us -> 13.9 us
  local copies, waits for them, and re-layouts: 1.09 us -> 2.08 us
    ppermute x12 -> x9, waiting for transfers between devices: 5.55 us -> 19.8 us  [send(): lax.ppermute(array, 'head', [(i, (i + shift) % heads) for i in range(head...]
    ppermute x12 -> x9, starting transfers between devices: 23 us -> 17.5 us  [send(): lax.ppermute(array, 'head', [(i, (i + shift) % heads) for i in range(head...]
    ppermute x2 -> x1, starting transfers between devices: 6.19 us -> 1.99 us  [halo(): low = lax.ppermute(tail, 'ctx', [(i, i + 1) for i in range(ctx - 1)])]
    pallas_call x20, Pallas kernels: 12.3 us -> 13.9 us  [call(): pl.pallas_call(kernel, out_shape=out_shape, in_specs=in_specs, out_specs=...]
    ppermute x2 -> x1, starting transfers between devices: 2.58 us -> 1.29 us  [halo(): high = lax.ppermute(head, 'ctx', [(i + 1, i) for i in range(ctx - 1)])]
    unnamed x10, local copies, waits for them, and re-layouts: 1.01 us -> 2.01 us
  transfers between devices with their start and end apart: 16 -> 11, of which waited for: 3 -> 5; matrix products, arithmetic and copies ran while one was open for 0% -> 0% of each run, Pallas kernels for 22% -> 21%
where the time goes in v4:
time: 57 us; the launch traced here: 56.8 us
  starting transfers between devices  20.8 us (36%)
  waiting for transfers between devices  19.8 us (35%)
  Pallas kernels  13.9 us (24%)
  local copies, waits for them, and re-layouts  2.08 us (4%)
    ppermute x9, waiting for transfers between devices, send(): lax.ppermute(array, 'head', [(i, (i + shift) % heads) for i in range(head...  19.8 us
    ppermute x9, starting transfers between devices, send(): lax.ppermute(array, 'head', [(i, (i + shift) % heads) for i in range(head...  17.5 us
    pallas_call x20, Pallas kernels, call(): pl.pallas_call(kernel, out_shape=out_shape, in_specs=in_specs, out_specs=...  13.9 us
    unnamed x10, local copies, waits for them, and re-layouts  2.01 us
    ppermute x1, starting transfers between devices, halo(): low = lax.ppermute(tail, 'ctx', [(i, i + 1) for i in range(ctx - 1)])  1.99 us
    ppermute x1, starting transfers between devices, halo(): high = lax.ppermute(head, 'ctx', [(i + 1, i) for i in range(ctx - 1)])  1.29 us
  transfers between devices with their start and end apart: 11, of which 5 were waited for; matrix products, arithmetic and copies ran while one was open for 0% of the time, Pallas kernels for 21%

profile of v4, /device:TPU:0, one launch (start us, length us, event | category | flops | bytes accessed | tf_op | source)
XLA Modules:
  0.0 56.8 jit_solution(17675038050296245899)
XLA Ops:
  0.0 0.0 copy-start
  0.0 1.0 %copy-done = bf16[384,512]{1,0:T(8,128)(2,1)S(1)} copy-done((bf16[384,512]{1,0:T(8,128)(2,1)S(1)}, bf16[384,512]{1,0:T(8,128)(2,1)}, u32[]{:S(2)}) %copy-start) | copy-done | bytes 393240
  1.0 0.0 copy-start.1
  1.0 1.0 %copy-done.1 = bf16[384,512]{1,0:T(8,128)(2,1)S(1)} copy-done((bf16[384,512]{1,0:T(8,128)(2,1)S(1)}, bf16[384,512]{1,0:T(8,128)(2,1)}, u32[]{:S(2)}) %copy-start.1) | copy-done | bytes 393240
  2.0 0.1 load_kv.5
  2.1 3.1 %collective-permute-start = (bf16[2,3,128,128]{3,2,1,0:T(8,128)(2,1)S(1)}, bf16[2,3,128,128]{3,2,1,0:T(8,128)(2,1)S(1)}, u32[]{:S(2)}, u32[]{:S(2)}) collective-permute-start(bf16[2,3,128,128]{3,2,1,0:T(8,128)(2,1)S(1)} %load_kv.5), channel_id=1, source_target_pairs={{0,1},{1,2},{2,3},{3,0},{4,5},{5,6},{6,7},{7,4},{8,9},{9,10},{10,1... | collective-permute-start | bytes 589832 | tf_op jit(solution)/shard_map/ppermute | solution.py:247
  5.2 0.1 load_kv.6
  5.3 2.7 %collective-permute-start.1 = (bf16[2,3,128,128]{3,2,1,0:T(8,128)(2,1)S(1)}, bf16[2,3,128,128]{3,2,1,0:T(8,128)(2,1)S(1)}, u32[]{:S(2)}, u32[]{:S(2)}) collective-permute-start(bf16[2,3,128,128]{3,2,1,0:T(8,128)(2,1)S(1)} %load_kv.6), channel_id=1, source_target_pairs={{0,2},{1,3},{2,0},{3,1},{4,6},{5,7},{6,4},{7,5},{8,10},{9,11},{10,... | collective-permute-start | bytes 589832 | tf_op jit(solution)/shard_map/ppermute | solution.py:247
  7.9 0.1 load_kv.7
  8.0 1.4 %collective-permute-start.2 = (bf16[2,3,128,128]{3,2,1,0:T(8,128)(2,1)S(1)}, bf16[2,3,128,128]{3,2,1,0:T(8,128)(2,1)S(1)}, u32[]{:S(2)}, u32[]{:S(2)}) collective-permute-start(bf16[2,3,128,128]{3,2,1,0:T(8,128)(2,1)S(1)} %load_kv.7), channel_id=1, source_target_pairs={{0,3},{1,0},{2,1},{3,2},{4,7},{5,4},{6,5},{7,6},{8,11},{9,8},{10,9... | collective-permute-start | bytes 589832 | tf_op jit(solution)/shard_map/ppermute | solution.py:247
  9.4 0.1 load_kv.4.refs_0_
  9.5 3.5 %collective-permute-done.refs_1_.refs_0_ = bf16[2,3,128,128]{3,2,1,0:T(8,128)(2,1)S(1)} collective-permute-done((bf16[2,3,128,128]{3,2,1,0:T(8,128)(2,1)S(1)}, bf16[2,3,128,128]{3,2,1,0:T(8,128)(2,1)S(1)}, u32[]{:S(2)}, u32[]{:S(2)}) %collective-permute-start) | collective-permute-done | bytes 196640 | tf_op jit(solution)/shard_map/ppermute | solution.py:247
  13.0 7.6 %collective-permute-done.1.refs_2_.refs_0_ = bf16[2,3,128,128]{3,2,1,0:T(8,128)(2,1)S(1)} collective-permute-done((bf16[2,3,128,128]{3,2,1,0:T(8,128)(2,1)S(1)}, bf16[2,3,128,128]{3,2,1,0:T(8,128)(2,1)S(1)}, u32[]{:S(2)}, u32[]{:S(2)}) %collective-permute-start.1) | collective-permute-done | bytes 196640 | tf_op jit(solution)/shard_map/ppermute | solution.py:247
  20.6 0.0 collective-permute-done.2.refs_3_.refs_0_
  20.6 0.1 gather.1.kv_ref
  20.7 0.0 copy-start.2
  20.8 2.0 %collective-permute-start.3 = (bf16[2,8,128,128]{3,2,1,0:T(8,128)(2,1)S(1)}, bf16[2,8,128,128]{3,2,1,0:T(8,128)(2,1)S(1)}, u32[]{:S(2)}, u32[]{:S(2)}) collective-permute-start(bf16[2,8,128,128]{3,2,1,0:T(8,128)(2,1)S(1)} %slice.8), channel_id=1, source_target_pairs={{0,4},{4,8},{8,12},{1,5},{5,9},{9,13},{2,6},{6,10},{10,14},{3,7},{... | collective-permute-start | bytes 1572872 | tf_op jit(solution)/shard_map/ppermute | solution.py:122
  22.8 1.3 %collective-permute-start.4 = (bf16[2,7,128,128]{3,2,1,0:T(8,128)(2,1)S(1)}, bf16[2,7,128,128]{3,2,1,0:T(8,128)(2,1)S(1)}, u32[]{:S(2)}, u32[]{:S(2)}) collective-permute-start(bf16[2,7,128,128]{3,2,1,0:T(8,128)(2,1)S(1)} %slice.9), channel_id=1, source_target_pairs={{4,0},{8,4},{12,8},{5,1},{9,5},{13,9},{6,2},{10,6},{14,10},{7,3},{... | collective-permute-start | bytes 1376264 | tf_op jit(solution)/shard_map/ppermute | solution.py:123
  24.1 0.0 copy-done.2
  24.1 5.3 %collective-permute-start.9 = (bf16[384,128]{1,0:T(8,128)(2,1)S(1)}, bf16[384,128]{1,0:T(8,128)(2,1)S(1)}, u32[]{:S(2)}, u32[]{:S(2)}) collective-permute-start(bf16[384,128]{1,0:T(8,128)(2,1)S(1)} %load_q.7), channel_id=1, source_target_pairs={{0,3},{1,0},{2,1},{3,2},{4,7},{5,4},{6,5},{7,6},{8,11},{9,8},{10,9... | collective-permute-start | bytes 294920 | tf_op jit(solution)/shard_map/ppermute | solution.py:247
  29.4 0.0 copy-start.3
  29.4 0.0 copy-start.4
  29.4 1.1 %collective-permute-start.7 = (bf16[384,128]{1,0:T(8,128)(2,1)S(1)}, bf16[384,128]{1,0:T(8,128)(2,1)S(1)}, u32[]{:S(2)}, u32[]{:S(2)}) collective-permute-start(bf16[384,128]{1,0:T(8,128)(2,1)S(1)} %load_q.6), channel_id=1, source_target_pairs={{0,2},{1,3},{2,0},{3,1},{4,6},{5,7},{6,4},{7,5},{8,10},{9,11},{10,... | collective-permute-start | bytes 294920 | tf_op jit(solution)/shard_map/ppermute | solution.py:247
  30.6 0.1 collective-permute-start.5
  30.6 0.0 copy-done.3
  30.6 0.0 copy-done.4
  30.6 1.4 %mask_bias.1.bias_ref = f32[12,27,128]{2,1,0:T(8,128)S(1)} custom-call(s32[12,16]{1,0:T(8,128)S(1)} %copy-done.3, s32[12]{0:T(128)S(1)} %copy-done.4), custom_call_target="tpu_custom_call" | custom-call | tf_op jit(solution)/shard_map/mask_bias/pallas_call | solution.py:29
  32.1 0.0 collective-permute-done.9.q_ref
  32.1 1.6 %attend_own.7 = (f32[384,128]{1,0:T(8,128)S(1)}, f32[384,128]{1,0:T(8,128)S(1)}, f32[384,128]{1,0:T(8,128)S(1)}) custom-call(bf16[384,128]{1,0:T(8,128)(2,1)S(1)} %collective-permute-done.9.q_ref, bf16[2,12,128,128]{3,2,1,0:T(8,128)(2,1)S(1)} %gather.1.kv_ref, f32[12,27,128]{2,1,0:T(8,128)S(1)} %mask_bias.1.bias_ref), custom_call_target="tpu_custom_call" | custom-call | flops 301989888 | bytes 1048576 | tf_op jit(solution)/shard_map/attend_own/pallas_call | solution.py:29
  33.7 6.0 %collective-permute-done.7.q_ref = bf16[384,128]{1,0:T(8,128)(2,1)S(1)} collective-permute-done((bf16[384,128]{1,0:T(8,128)(2,1)S(1)}, bf16[384,128]{1,0:T(8,128)(2,1)S(1)}, u32[]{:S(2)}, u32[]{:S(2)}) %collective-permute-start.7) | collective-permute-done | bytes 98336 | tf_op jit(solution)/shard_map/ppermute | solution.py:247
  39.7 1.6 %attend_own.6 = (f32[384,128]{1,0:T(8,128)S(1)}, f32[384,128]{1,0:T(8,128)S(1)}, f32[384,128]{1,0:T(8,128)S(1)}) custom-call(bf16[384,128]{1,0:T(8,128)(2,1)S(1)} %collective-permute-done.7.q_ref, bf16[2,12,128,128]{3,2,1,0:T(8,128)(2,1)S(1)} %gather.1.kv_ref, f32[12,27,128]{2,1,0:T(8,128)S(1)} %mask_bias.1.bias_ref), custom_call_target="tpu_custom_call" | custom-call | flops 301989888 | bytes 1048576 | tf_op jit(solution)/shard_map/attend_own/pallas_call | solution.py:29
  41.4 0.0 collective-permute-done.5.q_ref
  41.4 1.6 %attend_own.5 = (f32[384,128]{1,0:T(8,128)S(1)}, f32[384,128]{1,0:T(8,128)S(1)}, f32[384,128]{1,0:T(8,128)S(1)}) custom-call(bf16[384,128]{1,0:T(8,128)(2,1)S(1)} %collective-permute-done.5.q_ref, bf16[2,12,128,128]{3,2,1,0:T(8,128)(2,1)S(1)} %gather.1.kv_ref, f32[12,27,128]{2,1,0:T(8,128)S(1)} %mask_bias.1.bias_ref), custom_call_target="tpu_custom_call" | custom-call | flops 301989888 | bytes 1048576 | tf_op jit(solution)/shard_map/attend_own/pallas_call | solution.py:29
  43.0 0.0 collective-permute-done.4.high_ref
  43.0 0.0 collective-permute-done.3.low_ref
  43.0 0.1 join.1.kv_ref
  43.1 1.1 %attend_halo.7 = bf16[384,128]{1,0:T(8,128)(2,1)S(1)} custom-call(bf16[384,128]{1,0:T(8,128)(2,1)S(1)} %collective-permute-done.9.q_ref, bf16[2,15,128,128]{3,2,1,0:T(8,128)(2,1)S(1)} %join.1.kv_ref, f32[12,27,128]{2,1,0:T(8,128)S(1)} %mask_bias.1.bias_ref, f32[384,128]{1,0:T(8,128)S(1)} %get-tuple-element.26.refs_0_, ...), custom_call_target="tpu_custom_call" | custom-call | flops 201326592 | bytes 1048576 | tf_op jit(solution)/shard_map/attend_halo/pallas_call | solution.py:29
  44.2 0.1 collective-permute-start.10
  44.3 1.1 %attend_halo.6 = bf16[384,128]{1,0:T(8,128)(2,1)S(1)} custom-call(bf16[384,128]{1,0:T(8,128)(2,1)S(1)} %collective-permute-done.7.q_ref, bf16[2,15,128,128]{3,2,1,0:T(8,128)(2,1)S(1)} %join.1.kv_ref, f32[12,27,128]{2,1,0:T(8,128)S(1)} %mask_bias.1.bias_ref, f32[384,128]{1,0:T(8,128)S(1)} %get-tuple-element.23.refs_0_, ...), custom_call_target="tpu_custom_call" | custom-call | flops 201326592 | bytes 1048576 | tf_op jit(solution)/shard_map/attend_halo/pallas_call | solution.py:29
  45.4 0.1 collective-permute-start.8
  45.5 1.1 %attend_halo.5 = bf16[384,128]{1,0:T(8,128)(2,1)S(1)} custom-call(bf16[384,128]{1,0:T(8,128)(2,1)S(1)} %collective-permute-done.5.q_ref, bf16[2,15,128,128]{3,2,1,0:T(8,128)(2,1)S(1)} %join.1.kv_ref, f32[12,27,128]{2,1,0:T(8,128)S(1)} %mask_bias.1.bias_ref, f32[384,128]{1,0:T(8,128)S(1)} %get-tuple-element.20.refs_0_, ...), custom_call_target="tpu_custom_call" | custom-call | flops 201326592 | bytes 1048576 | tf_op jit(solution)/shard_map/attend_halo/pallas_call | solution.py:29
  46.6 3.9 %collective-permute-start.6 = (bf16[384,128]{1,0:T(8,128)(2,1)S(1)}, bf16[384,128]{1,0:T(8,128)(2,1)S(1)}, u32[]{:S(2)}, u32[]{:S(2)}) collective-permute-start(bf16[384,128]{1,0:T(8,128)(2,1)S(1)} %attend_halo.5), channel_id=1, source_target_pairs={{0,3},{1,0},{2,1},{3,2},{4,7},{5,4},{6,5},{7,6},{8,11},{9,8},{10,9... | collective-permute-start | bytes 294920 | tf_op jit(solution)/shard_map/ppermute | solution.py:247
  50.5 1.6 %attend_own.4 = (f32[384,128]{1,0:T(8,128)S(1)}, f32[384,128]{1,0:T(8,128)S(1)}, f32[384,128]{1,0:T(8,128)S(1)}) custom-call(bf16[384,128]{1,0:T(8,128)(2,1)S(1)} %load_q.4.q_ref, bf16[2,12,128,128]{3,2,1,0:T(8,128)(2,1)S(1)} %gather.1.kv_ref, f32[12,27,128]{2,1,0:T(8,128)S(1)} %mask_bias.1.bias_ref), custom_call_target="tpu_custom_call" | custom-call | flops 301989888 | bytes 1048576 | tf_op jit(solution)/shard_map/attend_own/pallas_call | solution.py:29
  52.1 1.1 %attend_halo.4.refs_0_ = bf16[384,128]{1,0:T(8,128)(2,1)S(1)} custom-call(bf16[384,128]{1,0:T(8,128)(2,1)S(1)} %load_q.4.q_ref, bf16[2,15,128,128]{3,2,1,0:T(8,128)(2,1)S(1)} %join.1.kv_ref, f32[12,27,128]{2,1,0:T(8,128)S(1)} %mask_bias.1.bias_ref, f32[384,128]{1,0:T(8,128)S(1)} %get-tuple-element.17.refs_0_, f32[384,128]{1,0:T(8,128)S(1)} %get-tuple-element.18.refs_1_, ...), custom_call_target="tpu_custom_call" | custom-call | flops 201326592 | bytes 1048576 | tf_op jit(solution)/shard_map/attend_halo/pallas_call | solution.py:29
  53.2 0.0 collective-permute-done.10.refs_3_
  53.3 2.4 %collective-permute-done.8.refs_2_ = bf16[384,128]{1,0:T(8,128)(2,1)S(1)} collective-permute-done((bf16[384,128]{1,0:T(8,128)(2,1)S(1)}, bf16[384,128]{1,0:T(8,128)(2,1)S(1)}, u32[]{:S(2)}, u32[]{:S(2)}) %collective-permute-start.8) | collective-permute-done | bytes 98336 | tf_op jit(solution)/shard_map/ppermute | solution.py:247
  55.6 0.3 collective-permute-done.6.refs_1_
  55.9 0.9 %spread.1 = bf16[384,512]{1,0:T(8,128)(2,1)} custom-call(bf16[384,128]{1,0:T(8,128)(2,1)S(1)} %attend_halo.4.refs_0_, bf16[384,128]{1,0:T(8,128)(2,1)S(1)} %collective-permute-done.6.refs_1_, bf16[384,128]{1,0:T(8,128)(2,1)S(1)} %collective-permute-done.8.refs_2_, bf16[384,128]{1,0:T(8,128)(2,1)S(1)} %collective-permute-done.10.refs_3_), custom_call_target="tpu_custom_call" | custom-call | tf_op jit(solution)/shard_map/spread/pallas_call | solution.py:29
  (6 shorter events, 0.2 us)
Async XLA Ops:
  0.0 1.0 %copy-start = (bf16[384,512]{1,0:T(8,128)(2,1)S(1)}, bf16[384,512]{1,0:T(8,128)(2,1)}, u32[]{:S(2)}) copy-start(bf16[384,512]{1,0:T(8,128)(2,1)} %k_ref.7) | copy-start | bytes 1179652
  1.0 1.0 %copy-start.1 = (bf16[384,512]{1,0:T(8,128)(2,1)S(1)}, bf16[384,512]{1,0:T(8,128)(2,1)}, u32[]{:S(2)}) copy-start(bf16[384,512]{1,0:T(8,128)(2,1)} %v_ref.7) | copy-start | bytes 1179652
  2.1 10.9 %collective-permute-start = (bf16[2,3,128,128]{3,2,1,0:T(8,128)(2,1)S(1)}, bf16[2,3,128,128]{3,2,1,0:T(8,128)(2,1)S(1)}, u32[]{:S(2)}, u32[]{:S(2)}) collective-permute-start(bf16[2,3,128,128]{3,2,1,0:T(8,128)(2,1)S(1)} %load_kv.5), channel_id=1, source_target_pairs={{0,1},{1,2},{2,3},{3,0},{4,5},{5,6},{6,7},{7,4},{8,9},{9,10},{10,1... | collective-permute-start | bytes 589832 | tf_op jit(solution)/shard_map/ppermute | solution.py:247
  5.3 15.3 %collective-permute-start.1 = (bf16[2,3,128,128]{3,2,1,0:T(8,128)(2,1)S(1)}, bf16[2,3,128,128]{3,2,1,0:T(8,128)(2,1)S(1)}, u32[]{:S(2)}, u32[]{:S(2)}) collective-permute-start(bf16[2,3,128,128]{3,2,1,0:T(8,128)(2,1)S(1)} %load_kv.6), channel_id=1, source_target_pairs={{0,2},{1,3},{2,0},{3,1},{4,6},{5,7},{6,4},{7,5},{8,10},{9,11},{10,... | collective-permute-start | bytes 589832 | tf_op jit(solution)/shard_map/ppermute | solution.py:247
  8.0 12.6 %collective-permute-start.2 = (bf16[2,3,128,128]{3,2,1,0:T(8,128)(2,1)S(1)}, bf16[2,3,128,128]{3,2,1,0:T(8,128)(2,1)S(1)}, u32[]{:S(2)}, u32[]{:S(2)}) collective-permute-start(bf16[2,3,128,128]{3,2,1,0:T(8,128)(2,1)S(1)} %load_kv.7), channel_id=1, source_target_pairs={{0,3},{1,0},{2,1},{3,2},{4,7},{5,4},{6,5},{7,6},{8,11},{9,8},{10,9... | collective-permute-start | bytes 589832 | tf_op jit(solution)/shard_map/ppermute | solution.py:247
  20.7 3.4 %copy-start.2 = (bf16[384,512]{1,0:T(8,128)(2,1)S(1)}, bf16[384,512]{1,0:T(8,128)(2,1)}, u32[]{:S(2)}) copy-start(bf16[384,512]{1,0:T(8,128)(2,1)} %q_ref.7) | copy-start | bytes 1179652
  20.8 22.3 %collective-permute-start.3 = (bf16[2,8,128,128]{3,2,1,0:T(8,128)(2,1)S(1)}, bf16[2,8,128,128]{3,2,1,0:T(8,128)(2,1)S(1)}, u32[]{:S(2)}, u32[]{:S(2)}) collective-permute-start(bf16[2,8,128,128]{3,2,1,0:T(8,128)(2,1)S(1)} %slice.8), channel_id=1, source_target_pairs={{0,4},{4,8},{8,12},{1,5},{5,9},{9,13},{2,6},{6,10},{10,14},{3,7},{... | collective-permute-start | bytes 1572872 | tf_op jit(solution)/shard_map/ppermute | solution.py:122
  22.8 20.2 %collective-permute-start.4 = (bf16[2,7,128,128]{3,2,1,0:T(8,128)(2,1)S(1)}, bf16[2,7,128,128]{3,2,1,0:T(8,128)(2,1)S(1)}, u32[]{:S(2)}, u32[]{:S(2)}) collective-permute-start(bf16[2,7,128,128]{3,2,1,0:T(8,128)(2,1)S(1)} %slice.9), channel_id=1, source_target_pairs={{4,0},{8,4},{12,8},{5,1},{9,5},{13,9},{6,2},{10,6},{14,10},{7,3},{... | collective-permute-start | bytes 1376264 | tf_op jit(solution)/shard_map/ppermute | solution.py:123
  24.1 8.0 %collective-permute-start.9 = (bf16[384,128]{1,0:T(8,128)(2,1)S(1)}, bf16[384,128]{1,0:T(8,128)(2,1)S(1)}, u32[]{:S(2)}, u32[]{:S(2)}) collective-permute-start(bf16[384,128]{1,0:T(8,128)(2,1)S(1)} %load_q.7), channel_id=1, source_target_pairs={{0,3},{1,0},{2,1},{3,2},{4,7},{5,4},{6,5},{7,6},{8,11},{9,8},{10,9... | collective-permute-start | bytes 294920 | tf_op jit(solution)/shard_map/ppermute | solution.py:247
  29.4 1.2 %copy-start.3 = (s32[12,16]{1,0:T(8,128)S(1)}, s32[12,16]{1,0:T(8,128)}, u32[]{:S(2)}) copy-start(s32[12,16]{1,0:T(8,128)} %lists_ref.1) | copy-start | bytes 2308
  29.4 1.2 %copy-start.4 = (s32[12]{0:T(128)S(1)}, s32[12]{0:T(128)}, u32[]{:S(2)}) copy-start(s32[12]{0:T(128)} %counts_ref.1) | copy-start | bytes 148
  29.4 10.3 %collective-permute-start.7 = (bf16[384,128]{1,0:T(8,128)(2,1)S(1)}, bf16[384,128]{1,0:T(8,128)(2,1)S(1)}, u32[]{:S(2)}, u32[]{:S(2)}) collective-permute-start(bf16[384,128]{1,0:T(8,128)(2,1)S(1)} %load_q.6), channel_id=1, source_target_pairs={{0,2},{1,3},{2,0},{3,1},{4,6},{5,7},{6,4},{7,5},{8,10},{9,11},{10,... | collective-permute-start | bytes 294920 | tf_op jit(solution)/shard_map/ppermute | solution.py:247
  30.6 10.8 %collective-permute-start.5 = (bf16[384,128]{1,0:T(8,128)(2,1)S(1)}, bf16[384,128]{1,0:T(8,128)(2,1)S(1)}, u32[]{:S(2)}, u32[]{:S(2)}) collective-permute-start(bf16[384,128]{1,0:T(8,128)(2,1)S(1)} %load_q.5), channel_id=1, source_target_pairs={{0,1},{1,2},{2,3},{3,0},{4,5},{5,6},{6,7},{7,4},{8,9},{9,10},{10,1... | collective-permute-start | bytes 294920 | tf_op jit(solution)/shard_map/ppermute | solution.py:247
  44.2 9.0 %collective-permute-start.10 = (bf16[384,128]{1,0:T(8,128)(2,1)S(1)}, bf16[384,128]{1,0:T(8,128)(2,1)S(1)}, u32[]{:S(2)}, u32[]{:S(2)}) collective-permute-start(bf16[384,128]{1,0:T(8,128)(2,1)S(1)} %attend_halo.7), channel_id=1, source_target_pairs={{0,1},{1,2},{2,3},{3,0},{4,5},{5,6},{6,7},{7,4},{8,9},{9,10},{10,1... | collective-permute-start | bytes 294920 | tf_op jit(solution)/shard_map/ppermute | solution.py:247
  45.4 10.2 %collective-permute-start.8 = (bf16[384,128]{1,0:T(8,128)(2,1)S(1)}, bf16[384,128]{1,0:T(8,128)(2,1)S(1)}, u32[]{:S(2)}, u32[]{:S(2)}) collective-permute-start(bf16[384,128]{1,0:T(8,128)(2,1)S(1)} %attend_halo.6), channel_id=1, source_target_pairs={{0,2},{1,3},{2,0},{3,1},{4,6},{5,7},{6,4},{7,5},{8,10},{9,11},{10,... | collective-permute-start | bytes 294920 | tf_op jit(solution)/shard_map/ppermute | solution.py:247
  46.6 9.3 %collective-permute-start.6 = (bf16[384,128]{1,0:T(8,128)(2,1)S(1)}, bf16[384,128]{1,0:T(8,128)(2,1)S(1)}, u32[]{:S(2)}, u32[]{:S(2)}) collective-permute-start(bf16[384,128]{1,0:T(8,128)(2,1)S(1)} %attend_halo.5), channel_id=1, source_target_pairs={{0,3},{1,0},{2,1},{3,2},{4,7},{5,4},{6,5},{7,6},{8,11},{9,8},{10,9... | collective-permute-start | bytes 294920 | tf_op jit(solution)/shard_map/ppermute | solution.py:247

commit v5 on v4

--- a/solution.py
+++ b/solution.py
@@ -109,9 +109,9 @@
     return [pltpu.VMEM(shape, jnp.float32), pltpu.VMEM(shape, jnp.bfloat16)]
 
 
-def attend_cost(count):
-    pairs = BLOCK * count * TILE * TILE
-    return pl.CostEstimate(flops=4 * pairs * HDIM, bytes_accessed=1 << 20, transcendentals=pairs)
+def attend_cost(count, weight=1):
+    pairs = BLOCK * count * TILE * TILE * weight
+    return pl.CostEstimate(flops=4 * pairs * HDIM, bytes_accessed=weight << 20, transcendentals=pairs)
 
 
 def halo(array, dim, unit):
@@ -209,7 +209,8 @@
     return lax.rem(lax.axis_index("head") + heads - shift, heads) * BLOCK
 
 
-def attend_own_kernel(shift, heads, q_ref, kv_ref, bias_ref, max_ref, divisor_ref, mixed_ref, *scratch):
+def attend_own_kernel(shift, heads, q_ref, kv_ref, bias_ref, *refs):
+    max_ref, divisor_ref, mixed_ref, *scratch = refs[-5:]
     max_ref[...], divisor_ref[...], mixed_ref[...] = attend_tiles(
         q_ref, kv_ref, 0, kv_ref.shape[1], bias_ref, first_row(shift, heads), lambda tile: EDGE + tile, *scratch
     )
@@ -256,7 +257,7 @@
         )
         kv_parts[shift] = send(part, shift) if shift else part
     for shift in order + [0]:
-        after = (kv_parts[shift],) if shift else ()
+        after = (kv_parts[order[0]],) if shift else ()
         part = call(
             kernel_of(load_q_kernel, heads, shift), "load_q", (queries, *after), [VMEM] * (1 + len(after)), chunk
         )
@@ -264,16 +265,20 @@
     own = call(gather_kernel, "gather", kv_parts, [VMEM] * heads, (2, tiles, TILE, HDIM))
     low_high = halo(own, 1, 1)
     partial = [None] * heads
-    for shift in order + [0]:
+    for shift in [0] + order:
+        after = (partial[last][0],) if shift else ()
+        if shift == order[0]:
+            after += tuple(q_parts[other] for other in order[1:])
+        last = shift
         partial[shift] = call(
             kernel_of(attend_own_kernel, shift, heads),
             "attend_own",
-            (q_parts[shift], own, bias),
-            [VMEM] * 3,
+            (q_parts[shift], own, bias, *after),
+            [VMEM] * (3 + len(after)),
             [sums] * 3,
             tile_scratch(tiles),
             16,
-            attend_cost(tiles),
+            attend_cost(tiles, 100 if shift else 1),
         )
     around = call(join_kernel, "join", low_high, [VMEM] * 2, (2, LIST - 1, TILE, HDIM))
     outs = [None] * heads

time: 57 us -> 53.6 us (0.940)
  waiting for transfers between devices: 19.8 us -> 14.5 us
  local copies, waits for them, and re-layouts: 2.08 us -> 3.55 us
    ppermute x9, waiting for transfers between devices: 19.8 us -> 14.5 us  [send(): lax.ppermute(array, 'head', [(i, (i + shift) % heads) for i in range(head...]
    unnamed x10 -> x12, local copies, waits for them, and re-layouts: 2.01 us -> 3.48 us
    ppermute x1, starting transfers between devices: 1.99 us -> 3.06 us  [halo(): low = lax.ppermute(tail, 'ctx', [(i, i + 1) for i in range(ctx - 1)])]
    ppermute x9, starting transfers between devices: 17.5 us -> 16.8 us  [send(): lax.ppermute(array, 'head', [(i, (i + shift) % heads) for i in range(head...]
  transfers between devices with their start and end apart: 11 -> 11, of which waited for: 5 -> 3; matrix products, arithmetic and copies ran while one was open for 0% -> 0% of each run, Pallas kernels for 21% -> 22%
where the time goes in v5:
time: 53.6 us; the launch traced here: 53.3 us
  starting transfers between devices  21.1 us (39%)
  waiting for transfers between devices  14.5 us (27%)
  Pallas kernels  13.9 us (26%)
  local copies, waits for them, and re-layouts  3.55 us (7%)
    ppermute x9, starting transfers between devices, send(): lax.ppermute(array, 'head', [(i, (i + shift) % heads) for i in range(head...  16.8 us
    ppermute x9, waiting for transfers between devices, send(): lax.ppermute(array, 'head', [(i, (i + shift) % heads) for i in range(head...  14.5 us
    pallas_call x20, Pallas kernels, call(): pl.pallas_call(kernel, out_shape=out_shape, in_specs=in_specs, out_specs=...  13.9 us
    unnamed x12, local copies, waits for them, and re-layouts  3.48 us
    ppermute x1, starting transfers between devices, halo(): low = lax.ppermute(tail, 'ctx', [(i, i + 1) for i in range(ctx - 1)])  3.06 us
    ppermute x1, starting transfers between devices, halo(): high = lax.ppermute(head, 'ctx', [(i + 1, i) for i in range(ctx - 1)])  1.29 us
  transfers between devices with their start and end apart: 11, of which 3 were waited for; matrix products, arithmetic and copies ran while one was open for 0% of the time, Pallas kernels for 22%

profile of v5, /device:TPU:0, one launch (start us, length us, event | category | flops | bytes accessed | tf_op | source)
XLA Modules:
  0.0 53.3 jit_solution(5501359902789765505)
XLA Ops:
  0.0 1.0 %copy-done.1 = bf16[384,512]{1,0:T(8,128)(2,1)S(1)} copy-done((bf16[384,512]{1,0:T(8,128)(2,1)S(1)}, bf16[384,512]{1,0:T(8,128)(2,1)}, u32[]{:S(2)}) %copy-start.1) | copy-done | bytes 393240
  1.0 0.0 copy-start.2
  1.0 1.0 %copy-done.2 = bf16[384,512]{1,0:T(8,128)(2,1)S(1)} copy-done((bf16[384,512]{1,0:T(8,128)(2,1)S(1)}, bf16[384,512]{1,0:T(8,128)(2,1)}, u32[]{:S(2)}) %copy-start.2) | copy-done | bytes 393240
  2.0 0.1 load_kv.6
  2.1 4.1 %collective-permute-start.1 = (bf16[2,3,128,128]{3,2,1,0:T(8,128)(2,1)S(1)}, bf16[2,3,128,128]{3,2,1,0:T(8,128)(2,1)S(1)}, u32[]{:S(2)}, u32[]{:S(2)}) collective-permute-start(bf16[2,3,128,128]{3,2,1,0:T(8,128)(2,1)S(1)} %load_kv.6), channel_id=1, source_target_pairs={{0,2},{1,3},{2,0},{3,1},{4,6},{5,7},{6,4},{7,5},{8,10},{9,11},{10,... | collective-permute-start | bytes 589832 | tf_op jit(solution)/shard_map/ppermute | solution.py:248
  6.2 0.1 load_kv.7
  6.3 0.0 copy-start
  6.3 1.4 %collective-permute-start.2 = (bf16[2,3,128,128]{3,2,1,0:T(8,128)(2,1)S(1)}, bf16[2,3,128,128]{3,2,1,0:T(8,128)(2,1)S(1)}, u32[]{:S(2)}, u32[]{:S(2)}) collective-permute-start(bf16[2,3,128,128]{3,2,1,0:T(8,128)(2,1)S(1)} %load_kv.7), channel_id=1, source_target_pairs={{0,3},{1,0},{2,1},{3,2},{4,7},{5,4},{6,5},{7,6},{8,11},{9,8},{10,9... | collective-permute-start | bytes 589832 | tf_op jit(solution)/shard_map/ppermute | solution.py:248
  7.7 0.1 load_kv.5
  7.8 0.7 %collective-permute-start = (bf16[2,3,128,128]{3,2,1,0:T(8,128)(2,1)S(1)}, bf16[2,3,128,128]{3,2,1,0:T(8,128)(2,1)S(1)}, u32[]{:S(2)}, u32[]{:S(2)}) collective-permute-start(bf16[2,3,128,128]{3,2,1,0:T(8,128)(2,1)S(1)} %load_kv.5), channel_id=1, source_target_pairs={{0,1},{1,2},{2,3},{3,0},{4,5},{5,6},{6,7},{7,4},{8,9},{9,10},{10,1... | collective-permute-start | bytes 589832 | tf_op jit(solution)/shard_map/ppermute | solution.py:248
  8.5 8.5 %collective-permute-done.1.refs_2_.refs_0_ = bf16[2,3,128,128]{3,2,1,0:T(8,128)(2,1)S(1)} collective-permute-done((bf16[2,3,128,128]{3,2,1,0:T(8,128)(2,1)S(1)}, bf16[2,3,128,128]{3,2,1,0:T(8,128)(2,1)S(1)}, u32[]{:S(2)}, u32[]{:S(2)}) %collective-permute-start.1) | collective-permute-done | bytes 196640 | tf_op jit(solution)/shard_map/ppermute | solution.py:248
  17.1 0.0 copy-done
  17.1 3.4 %collective-permute-start.5 = (bf16[384,128]{1,0:T(8,128)(2,1)S(1)}, bf16[384,128]{1,0:T(8,128)(2,1)S(1)}, u32[]{:S(2)}, u32[]{:S(2)}) collective-permute-start(bf16[384,128]{1,0:T(8,128)(2,1)S(1)} %load_q.5), channel_id=1, source_target_pairs={{0,1},{1,2},{2,3},{3,0},{4,5},{5,6},{6,7},{7,4},{8,9},{9,10},{10,1... | collective-permute-start | bytes 294920 | tf_op jit(solution)/shard_map/ppermute | solution.py:248
  20.5 3.4 %collective-permute-start.6 = (bf16[384,128]{1,0:T(8,128)(2,1)S(1)}, bf16[384,128]{1,0:T(8,128)(2,1)S(1)}, u32[]{:S(2)}, u32[]{:S(2)}) collective-permute-start(bf16[384,128]{1,0:T(8,128)(2,1)S(1)} %load_q.6), channel_id=1, source_target_pairs={{0,2},{1,3},{2,0},{3,1},{4,6},{5,7},{6,4},{7,5},{8,10},{9,11},{10,... | collective-permute-start | bytes 294920 | tf_op jit(solution)/shard_map/ppermute | solution.py:248
  24.0 0.0 copy-start.3
  24.0 0.1 collective-permute-start.7
  24.1 0.9 %copy-done.3 = bf16[384,512]{1,0:T(8,128)(2,1)S(1)} copy-done((bf16[384,512]{1,0:T(8,128)(2,1)S(1)}, bf16[384,512]{1,0:T(8,128)(2,1)}, u32[]{:S(2)}) %copy-start.3) | copy-done | bytes 393240
  25.0 0.0 copy-start.4
  25.0 0.1 load_kv.4.refs_0_
  25.1 0.6 %copy-done.4 = s32[12,16]{1,0:T(8,128)S(1)} copy-done((s32[12,16]{1,0:T(8,128)S(1)}, s32[12,16]{1,0:T(8,128)}, u32[]{:S(2)}) %copy-start.4) | copy-done | bytes 792
  25.6 0.0 copy-done.5
  25.7 1.4 %mask_bias.1.bias_ref = f32[12,27,128]{2,1,0:T(8,128)S(1)} custom-call(s32[12,16]{1,0:T(8,128)S(1)} %copy-done.4, s32[12]{0:T(128)S(1)} %copy-done.5), custom_call_target="tpu_custom_call" | custom-call | tf_op jit(solution)/shard_map/mask_bias/pallas_call | solution.py:29
  27.1 0.0 collective-permute-done.2.refs_3_
  27.1 0.0 collective-permute-done.refs_1_
  27.1 0.1 gather.1.kv_ref
  27.3 1.3 %collective-permute-start.4 = (bf16[2,7,128,128]{3,2,1,0:T(8,128)(2,1)S(1)}, bf16[2,7,128,128]{3,2,1,0:T(8,128)(2,1)S(1)}, u32[]{:S(2)}, u32[]{:S(2)}) collective-permute-start(bf16[2,7,128,128]{3,2,1,0:T(8,128)(2,1)S(1)} %slice.9), channel_id=1, source_target_pairs={{4,0},{8,4},{12,8},{5,1},{9,5},{13,9},{6,2},{10,6},{14,10},{7,3},{... | collective-permute-start | bytes 1376264 | tf_op jit(solution)/shard_map/ppermute | solution.py:123
  28.6 3.1 %collective-permute-start.3 = (bf16[2,8,128,128]{3,2,1,0:T(8,128)(2,1)S(1)}, bf16[2,8,128,128]{3,2,1,0:T(8,128)(2,1)S(1)}, u32[]{:S(2)}, u32[]{:S(2)}) collective-permute-start(bf16[2,8,128,128]{3,2,1,0:T(8,128)(2,1)S(1)} %slice.8), channel_id=1, source_target_pairs={{0,4},{4,8},{8,12},{1,5},{5,9},{9,13},{2,6},{6,10},{10,14},{3,7},{... | collective-permute-start | bytes 1572872 | tf_op jit(solution)/shard_map/ppermute | solution.py:122
  31.7 1.6 %attend_own.4 = (f32[384,128]{1,0:T(8,128)S(1)}, f32[384,128]{1,0:T(8,128)S(1)}, f32[384,128]{1,0:T(8,128)S(1)}) custom-call(bf16[384,128]{1,0:T(8,128)(2,1)S(1)} %load_q.4.q_ref, bf16[2,12,128,128]{3,2,1,0:T(8,128)(2,1)S(1)} %gather.1.kv_ref, f32[12,27,128]{2,1,0:T(8,128)S(1)} %mask_bias.1.bias_ref), custom_call_target="tpu_custom_call" | custom-call | flops 301989888 | bytes 1048576 | tf_op jit(solution)/shard_map/attend_own/pallas_call | solution.py:29
  33.3 0.0 collective-permute-done.5.refs_1_.q_ref
  33.3 0.0 collective-permute-done.6.q_ref
  33.3 0.0 collective-permute-done.7.refs_2_.q_ref
  33.3 1.6 %attend_own.5 = (f32[384,128]{1,0:T(8,128)S(1)}, f32[384,128]{1,0:T(8,128)S(1)}, f32[384,128]{1,0:T(8,128)S(1)}) custom-call(bf16[384,128]{1,0:T(8,128)(2,1)S(1)} %collective-permute-done.6.q_ref, bf16[2,12,128,128]{3,2,1,0:T(8,128)(2,1)S(1)} %gather.1.kv_ref, f32[12,27,128]{2,1,0:T(8,128)S(1)} %mask_bias.1.bias_ref, ...), custom_call_target="tpu_custom_call" | custom-call | flops 30198988800 | bytes 104857600 | tf_op jit(solution)/shard_map/attend_own/pallas_call | solution.py:29
  35.0 1.6 %attend_own.6 = (f32[384,128]{1,0:T(8,128)S(1)}, f32[384,128]{1,0:T(8,128)S(1)}, f32[384,128]{1,0:T(8,128)S(1)}) custom-call(bf16[384,128]{1,0:T(8,128)(2,1)S(1)} %collective-permute-done.5.refs_1_.q_ref, bf16[2,12,128,128]{3,2,1,0:T(8,128)(2,1)S(1)} %gather.1.kv_ref, f32[12,27,128]{2,1,0:T(8,128)S(1)} %mask_bias.1.bias_ref, ...), custom_call_target="tpu_custom_call" | custom-call | flops 30198988800 | bytes 104857600 | tf_op jit(solution)/shard_map/attend_own/pallas_call | solution.py:29
  36.6 1.6 %attend_own.7 = (f32[384,128]{1,0:T(8,128)S(1)}, f32[384,128]{1,0:T(8,128)S(1)}, f32[384,128]{1,0:T(8,128)S(1)}) custom-call(bf16[384,128]{1,0:T(8,128)(2,1)S(1)} %collective-permute-done.7.refs_2_.q_ref, bf16[2,12,128,128]{3,2,1,0:T(8,128)(2,1)S(1)} %gather.1.kv_ref, f32[12,27,128]{2,1,0:T(8,128)S(1)} %mask_bias.1.bias_ref, ...), custom_call_target="tpu_custom_call" | custom-call | flops 30198988800 | bytes 104857600 | tf_op jit(solution)/shard_map/attend_own/pallas_call | solution.py:29
  38.2 0.0 collective-permute-done.4.high_ref
  38.2 0.0 collective-permute-done.3.low_ref
  38.3 0.1 join.1.kv_ref
  38.3 1.1 %attend_halo.6 = bf16[384,128]{1,0:T(8,128)(2,1)S(1)} custom-call(bf16[384,128]{1,0:T(8,128)(2,1)S(1)} %collective-permute-done.6.q_ref, bf16[2,15,128,128]{3,2,1,0:T(8,128)(2,1)S(1)} %join.1.kv_ref, f32[12,27,128]{2,1,0:T(8,128)S(1)} %mask_bias.1.bias_ref, f32[384,128]{1,0:T(8,128)S(1)} %get-tuple-element.20.refs_0_, ...), custom_call_target="tpu_custom_call" | custom-call | flops 201326592 | bytes 1048576 | tf_op jit(solution)/shard_map/attend_halo/pallas_call | solution.py:29
  39.5 0.7 %collective-permute-start.9 = (bf16[384,128]{1,0:T(8,128)(2,1)S(1)}, bf16[384,128]{1,0:T(8,128)(2,1)S(1)}, u32[]{:S(2)}, u32[]{:S(2)}) collective-permute-start(bf16[384,128]{1,0:T(8,128)(2,1)S(1)} %attend_halo.6), channel_id=1, source_target_pairs={{0,2},{1,3},{2,0},{3,1},{4,6},{5,7},{6,4},{7,5},{8,10},{9,11},{10,... | collective-permute-start | bytes 294920 | tf_op jit(solution)/shard_map/ppermute | solution.py:248
  40.1 1.1 %attend_halo.5 = bf16[384,128]{1,0:T(8,128)(2,1)S(1)} custom-call(bf16[384,128]{1,0:T(8,128)(2,1)S(1)} %collective-permute-done.5.refs_1_.q_ref, bf16[2,15,128,128]{3,2,1,0:T(8,128)(2,1)S(1)} %join.1.kv_ref, f32[12,27,128]{2,1,0:T(8,128)S(1)} %mask_bias.1.bias_ref, f32[384,128]{1,0:T(8,128)S(1)} %get-tuple-element.21.refs_0_, ...), custom_call_target="tpu_custom_call" | custom-call | flops 201326592 | bytes 1048576 | tf_op jit(solution)/shard_map/attend_halo/pallas_call | solution.py:29
  41.2 3.0 %collective-permute-start.8 = (bf16[384,128]{1,0:T(8,128)(2,1)S(1)}, bf16[384,128]{1,0:T(8,128)(2,1)S(1)}, u32[]{:S(2)}, u32[]{:S(2)}) collective-permute-start(bf16[384,128]{1,0:T(8,128)(2,1)S(1)} %attend_halo.5), channel_id=1, source_target_pairs={{0,3},{1,0},{2,1},{3,2},{4,7},{5,4},{6,5},{7,6},{8,11},{9,8},{10,9... | collective-permute-start | bytes 294920 | tf_op jit(solution)/shard_map/ppermute | solution.py:248
  44.2 1.1 %attend_halo.7 = bf16[384,128]{1,0:T(8,128)(2,1)S(1)} custom-call(bf16[384,128]{1,0:T(8,128)(2,1)S(1)} %collective-permute-done.7.refs_2_.q_ref, bf16[2,15,128,128]{3,2,1,0:T(8,128)(2,1)S(1)} %join.1.kv_ref, f32[12,27,128]{2,1,0:T(8,128)S(1)} %mask_bias.1.bias_ref, f32[384,128]{1,0:T(8,128)S(1)} %get-tuple-element.26.refs_0_, ...), custom_call_target="tpu_custom_call" | custom-call | flops 201326592 | bytes 1048576 | tf_op jit(solution)/shard_map/attend_halo/pallas_call | solution.py:29
  45.3 0.1 collective-permute-start.10
  45.3 1.1 %attend_halo.4.refs_0_ = bf16[384,128]{1,0:T(8,128)(2,1)S(1)} custom-call(bf16[384,128]{1,0:T(8,128)(2,1)S(1)} %load_q.4.q_ref, bf16[2,15,128,128]{3,2,1,0:T(8,128)(2,1)S(1)} %join.1.kv_ref, f32[12,27,128]{2,1,0:T(8,128)S(1)} %mask_bias.1.bias_ref, f32[384,128]{1,0:T(8,128)S(1)} %get-tuple-element.17.refs_0_, f32[384,128]{1,0:T(8,128)S(1)} %get-tuple-element.18.refs_1_, ...), custom_call_target="tpu_custom_call" | custom-call | flops 201326592 | bytes 1048576 | tf_op jit(solution)/shard_map/attend_halo/pallas_call | solution.py:29
  46.5 1.6 %collective-permute-done.9.refs_2_ = bf16[384,128]{1,0:T(8,128)(2,1)S(1)} collective-permute-done((bf16[384,128]{1,0:T(8,128)(2,1)S(1)}, bf16[384,128]{1,0:T(8,128)(2,1)S(1)}, u32[]{:S(2)}, u32[]{:S(2)}) %collective-permute-start.9) | collective-permute-done | bytes 98336 | tf_op jit(solution)/shard_map/ppermute | solution.py:248
  48.1 0.0 collective-permute-done.8.refs_1_
  48.1 4.3 %collective-permute-done.10.refs_3_ = bf16[384,128]{1,0:T(8,128)(2,1)S(1)} collective-permute-done((bf16[384,128]{1,0:T(8,128)(2,1)S(1)}, bf16[384,128]{1,0:T(8,128)(2,1)S(1)}, u32[]{:S(2)}, u32[]{:S(2)}) %collective-permute-start.10) | collective-permute-done | bytes 98336 | tf_op jit(solution)/shard_map/ppermute | solution.py:248
  52.4 0.9 %spread.1 = bf16[384,512]{1,0:T(8,128)(2,1)} custom-call(bf16[384,128]{1,0:T(8,128)(2,1)S(1)} %attend_halo.4.refs_0_, bf16[384,128]{1,0:T(8,128)(2,1)S(1)} %collective-permute-done.8.refs_1_, bf16[384,128]{1,0:T(8,128)(2,1)S(1)} %collective-permute-done.9.refs_2_, bf16[384,128]{1,0:T(8,128)(2,1)S(1)} %collective-permute-done.10.refs_3_), custom_call_target="tpu_custom_call" | custom-call | tf_op jit(solution)/shard_map/spread/pallas_call | solution.py:29
  (8 shorter events, 0.2 us)
Async XLA Ops:
  0.0 1.0 %copy-start.1 = (bf16[384,512]{1,0:T(8,128)(2,1)S(1)}, bf16[384,512]{1,0:T(8,128)(2,1)}, u32[]{:S(2)}) copy-start(bf16[384,512]{1,0:T(8,128)(2,1)} %k_ref.7) | copy-start | bytes 1179652
  1.0 1.0 %copy-start.2 = (bf16[384,512]{1,0:T(8,128)(2,1)S(1)}, bf16[384,512]{1,0:T(8,128)(2,1)}, u32[]{:S(2)}) copy-start(bf16[384,512]{1,0:T(8,128)(2,1)} %v_ref.7) | copy-start | bytes 1179652
  2.1 15.0 %collective-permute-start.1 = (bf16[2,3,128,128]{3,2,1,0:T(8,128)(2,1)S(1)}, bf16[2,3,128,128]{3,2,1,0:T(8,128)(2,1)S(1)}, u32[]{:S(2)}, u32[]{:S(2)}) collective-permute-start(bf16[2,3,128,128]{3,2,1,0:T(8,128)(2,1)S(1)} %load_kv.6), channel_id=1, source_target_pairs={{0,2},{1,3},{2,0},{3,1},{4,6},{5,7},{6,4},{7,5},{8,10},{9,11},{10,... | collective-permute-start | bytes 589832 | tf_op jit(solution)/shard_map/ppermute | solution.py:248
  6.3 10.8 %copy-start = (bf16[384,512]{1,0:T(8,128)(2,1)S(1)}, bf16[384,512]{1,0:T(8,128)(2,1)}, u32[]{:S(2)}) copy-start(bf16[384,512]{1,0:T(8,128)(2,1)} %q_ref.7) | copy-start | bytes 1179652
  6.3 20.8 %collective-permute-start.2 = (bf16[2,3,128,128]{3,2,1,0:T(8,128)(2,1)S(1)}, bf16[2,3,128,128]{3,2,1,0:T(8,128)(2,1)S(1)}, u32[]{:S(2)}, u32[]{:S(2)}) collective-permute-start(bf16[2,3,128,128]{3,2,1,0:T(8,128)(2,1)S(1)} %load_kv.7), channel_id=1, source_target_pairs={{0,3},{1,0},{2,1},{3,2},{4,7},{5,4},{6,5},{7,6},{8,11},{9,8},{10,9... | collective-permute-start | bytes 589832 | tf_op jit(solution)/shard_map/ppermute | solution.py:248
  7.8 19.3 %collective-permute-start = (bf16[2,3,128,128]{3,2,1,0:T(8,128)(2,1)S(1)}, bf16[2,3,128,128]{3,2,1,0:T(8,128)(2,1)S(1)}, u32[]{:S(2)}, u32[]{:S(2)}) collective-permute-start(bf16[2,3,128,128]{3,2,1,0:T(8,128)(2,1)S(1)} %load_kv.5), channel_id=1, source_target_pairs={{0,1},{1,2},{2,3},{3,0},{4,5},{5,6},{6,7},{7,4},{8,9},{9,10},{10,1... | collective-permute-start | bytes 589832 | tf_op jit(solution)/shard_map/ppermute | solution.py:248
  17.1 16.2 %collective-permute-start.5 = (bf16[384,128]{1,0:T(8,128)(2,1)S(1)}, bf16[384,128]{1,0:T(8,128)(2,1)S(1)}, u32[]{:S(2)}, u32[]{:S(2)}) collective-permute-start(bf16[384,128]{1,0:T(8,128)(2,1)S(1)} %load_q.5), channel_id=1, source_target_pairs={{0,1},{1,2},{2,3},{3,0},{4,5},{5,6},{6,7},{7,4},{8,9},{9,10},{10,1... | collective-permute-start | bytes 294920 | tf_op jit(solution)/shard_map/ppermute | solution.py:248
  20.5 12.8 %collective-permute-start.6 = (bf16[384,128]{1,0:T(8,128)(2,1)S(1)}, bf16[384,128]{1,0:T(8,128)(2,1)S(1)}, u32[]{:S(2)}, u32[]{:S(2)}) collective-permute-start(bf16[384,128]{1,0:T(8,128)(2,1)S(1)} %load_q.6), channel_id=1, source_target_pairs={{0,2},{1,3},{2,0},{3,1},{4,6},{5,7},{6,4},{7,5},{8,10},{9,11},{10,... | collective-permute-start | bytes 294920 | tf_op jit(solution)/shard_map/ppermute | solution.py:248
  24.0 1.0 %copy-start.3 = (bf16[384,512]{1,0:T(8,128)(2,1)S(1)}, bf16[384,512]{1,0:T(8,128)(2,1)}, u32[]{:S(2)}) copy-start(bf16[384,512]{1,0:T(8,128)(2,1)} %v_ref.7) | copy-start | bytes 1179652
  24.0 9.3 %collective-permute-start.7 = (bf16[384,128]{1,0:T(8,128)(2,1)S(1)}, bf16[384,128]{1,0:T(8,128)(2,1)S(1)}, u32[]{:S(2)}, u32[]{:S(2)}) collective-permute-start(bf16[384,128]{1,0:T(8,128)(2,1)S(1)} %load_q.7), channel_id=1, source_target_pairs={{0,3},{1,0},{2,1},{3,2},{4,7},{5,4},{6,5},{7,6},{8,11},{9,8},{10,9... | collective-permute-start | bytes 294920 | tf_op jit(solution)/shard_map/ppermute | solution.py:248
  25.0 0.7 %copy-start.4 = (s32[12,16]{1,0:T(8,128)S(1)}, s32[12,16]{1,0:T(8,128)}, u32[]{:S(2)}) copy-start(s32[12,16]{1,0:T(8,128)} %lists_ref.1) | copy-start | bytes 2308
  25.0 0.7 %copy-start.5 = (s32[12]{0:T(128)S(1)}, s32[12]{0:T(128)}, u32[]{:S(2)}) copy-start(s32[12]{0:T(128)} %counts_ref.1) | copy-start | bytes 148
  27.3 11.0 %collective-permute-start.4 = (bf16[2,7,128,128]{3,2,1,0:T(8,128)(2,1)S(1)}, bf16[2,7,128,128]{3,2,1,0:T(8,128)(2,1)S(1)}, u32[]{:S(2)}, u32[]{:S(2)}) collective-permute-start(bf16[2,7,128,128]{3,2,1,0:T(8,128)(2,1)S(1)} %slice.9), channel_id=1, source_target_pairs={{4,0},{8,4},{12,8},{5,1},{9,5},{13,9},{6,2},{10,6},{14,10},{7,3},{... | collective-permute-start | bytes 1376264 | tf_op jit(solution)/shard_map/ppermute | solution.py:123
  28.6 9.7 %collective-permute-start.3 = (bf16[2,8,128,128]{3,2,1,0:T(8,128)(2,1)S(1)}, bf16[2,8,128,128]{3,2,1,0:T(8,128)(2,1)S(1)}, u32[]{:S(2)}, u32[]{:S(2)}) collective-permute-start(bf16[2,8,128,128]{3,2,1,0:T(8,128)(2,1)S(1)} %slice.8), channel_id=1, source_target_pairs={{0,4},{4,8},{8,12},{1,5},{5,9},{9,13},{2,6},{6,10},{10,14},{3,7},{... | collective-permute-start | bytes 1572872 | tf_op jit(solution)/shard_map/ppermute | solution.py:122
  39.5 8.7 %collective-permute-start.9 = (bf16[384,128]{1,0:T(8,128)(2,1)S(1)}, bf16[384,128]{1,0:T(8,128)(2,1)S(1)}, u32[]{:S(2)}, u32[]{:S(2)}) collective-permute-start(bf16[384,128]{1,0:T(8,128)(2,1)S(1)} %attend_halo.6), channel_id=1, source_target_pairs={{0,2},{1,3},{2,0},{3,1},{4,6},{5,7},{6,4},{7,5},{8,10},{9,11},{10,... | collective-permute-start | bytes 294920 | tf_op jit(solution)/shard_map/ppermute | solution.py:248
  41.2 6.9 %collective-permute-start.8 = (bf16[384,128]{1,0:T(8,128)(2,1)S(1)}, bf16[384,128]{1,0:T(8,128)(2,1)S(1)}, u32[]{:S(2)}, u32[]{:S(2)}) collective-permute-start(bf16[384,128]{1,0:T(8,128)(2,1)S(1)} %attend_halo.5), channel_id=1, source_target_pairs={{0,3},{1,0},{2,1},{3,2},{4,7},{5,4},{6,5},{7,6},{8,11},{9,8},{10,9... | collective-permute-start | bytes 294920 | tf_op jit(solution)/shard_map/ppermute | solution.py:248
  45.3 7.1 %collective-permute-start.10 = (bf16[384,128]{1,0:T(8,128)(2,1)S(1)}, bf16[384,128]{1,0:T(8,128)(2,1)S(1)}, u32[]{:S(2)}, u32[]{:S(2)}) collective-permute-start(bf16[384,128]{1,0:T(8,128)(2,1)S(1)} %attend_halo.7), channel_id=1, source_target_pairs={{0,1},{1,2},{2,3},{3,0},{4,5},{5,6},{6,7},{7,4},{8,9},{9,10},{10,1... | collective-permute-start | bytes 294920 | tf_op jit(solution)/shard_map/ppermute | solution.py:248

commit v6 on v4

v6 whole, which is shorter than its diff:
```python
import functools
import math

import jax
import jax.numpy as jnp
from jax import lax
from jax.experimental import pallas as pl
from jax.experimental.pallas import tpu as pltpu
from jax.sharding import PartitionSpec as P

HDIM = 128
TILE = 128
EDGE = 8
LIST = 16
BLOCK = 3
WINDOW = BLOCK + LIST - 1
HIDDEN = -1e30
EXPONENT_SCALE = HDIM ** (-0.5) * math.log2(math.e)
SMEM = pl.BlockSpec(memory_space=pltpu.SMEM)
VMEM = pl.BlockSpec(memory_space=pltpu.VMEM)


def call(kernel, name, operands, in_specs, shapes, scratch=(), limit=8, cost=None):
    out_shape = jax.tree.map(
        lambda shape: shape if hasattr(shape, "dtype") else jax.ShapeDtypeStruct(shape, jnp.bfloat16),
        shapes,
        is_leaf=lambda node: isinstance(node, tuple) or hasattr(node, "dtype"),
    )
    return pl.pallas_call(
        kernel,
        out_shape=out_shape,
        in_specs=in_specs,
        out_specs=jax.tree.map(lambda _: VMEM, out_shape),
        scratch_shapes=scratch,
        compiler_params=pltpu.CompilerParams(vmem_limit_bytes=limit << 20),
        cost_estimate=cost,
        name=name,
    )(*operands)


def column_of(head):
    return pl.ds(pl.multiple_of(head * HDIM, HDIM), HDIM)


def rows_of(tile):
    return slice(tile * TILE, (tile + 1) * TILE)


def bias_kernel(total_tiles, lists_ref, counts_ref, bias_ref):
    tiles, entries = lists_ref.shape
    lists = lists_ref[...]
    entry = lax.broadcasted_iota(jnp.int32, lists.shape, 1)
    row = lax.broadcasted_iota(jnp.int32, lists.shape, 0)
    live = (entry < counts_ref[...]) & (lists >= 0) & (lists < total_tiles)
    places = jnp.where(live, lists - lists[:, :1] + row + EDGE, -1)
    listed = [jnp.broadcast_to(places[:, at : at + 1], (tiles, TILE)) for at in range(entries)]
    for place in range(bias_ref.shape[0]):
        visible = listed[0] == place
        for at in range(1, entries):
            visible |= listed[at] == place
        bias_ref[place] = jnp.where(visible, 0.0, HIDDEN)


def mask_bias(tile_lists, live_counts, total_tiles):
    tiles = tile_lists.shape[0]
    shape = jax.ShapeDtypeStruct((tiles + LIST - 1, tiles, TILE), jnp.float32)
    kernel = functools.partial(bias_kernel, total_tiles)
    return call(kernel, "mask_bias", (tile_lists, live_counts[:, None]), [VMEM] * 2, shape)


def attend_block(first, q_ref, kv_ref, bias_ref, out_ref, scores, probs):
    for pair in range(WINDOW // 2):
        low = max(0, 2 * pair - LIST + 1)
        high = min(BLOCK - 1, 2 * pair + 1)
        at = first + 2 * pair
        keys = jnp.concatenate([kv_ref[0, at], kv_ref[0, at + 1]], axis=1)
        part = jnp.dot(
            q_ref[low * TILE : (high + 1) * TILE, :], keys, preferred_element_type=jnp.float32
        )
        for half in range(2):
            for tile in range(low, high + 1):
                offset = 2 * pair + half - tile
                if 0 <= offset < LIST:
                    bias = bias_ref[at + half, pl.ds(first + tile, 1), :]
                    scores[tile, :, rows_of(offset)] = part[rows_of(tile - low), rows_of(half)] + bias
    for tile in range(BLOCK):
        highest = scores[tile, :, rows_of(0)]
        for offset in range(1, LIST):
            highest = jnp.maximum(highest, scores[tile, :, rows_of(offset)])
        highest = jnp.broadcast_to(jnp.max(highest, axis=1, keepdims=True), (TILE, TILE))
        total = jnp.zeros((TILE, TILE), jnp.float32)
        for offset in range(LIST):
            weights = jnp.exp2((scores[tile, :, rows_of(offset)] - highest) * EXPONENT_SCALE)
            total += weights
            probs[tile, :, rows_of(offset)] = weights.astype(jnp.bfloat16)
        values = kv_ref[1, pl.ds(first + tile, LIST)].reshape(LIST * TILE, HDIM)
        mixed = jnp.dot(probs[tile], values, preferred_element_type=jnp.float32)
        out_ref[rows_of(tile), :] = (mixed / jnp.sum(total, axis=1, keepdims=True)).astype(jnp.bfloat16)


def block_scratch():
    shape = (BLOCK, TILE, LIST * TILE)
    return [pltpu.VMEM(shape, jnp.float32), pltpu.VMEM(shape, jnp.bfloat16)]


def cost(tile_pairs):
    pairs = tile_pairs * TILE * TILE
    return pl.CostEstimate(flops=4 * pairs * HDIM, bytes_accessed=pairs, transcendentals=pairs)


def halo(array, dim, unit):
    ctx = lax.axis_size("ctx")
    count = array.shape[dim]
    tail = lax.slice_in_dim(array, count - EDGE * unit, count, axis=dim)
    head = lax.slice_in_dim(array, 0, (EDGE - 1) * unit, axis=dim)
    low = lax.ppermute(tail, "ctx", [(i, i + 1) for i in range(ctx - 1)])
    high = lax.ppermute(head, "ctx", [(i + 1, i) for i in range(ctx - 1)])
    return low, high


def pack_kernel(heads, q_ref, k_ref, v_ref, q_out, k_out, v_out):
    for source, target in ((k_ref, k_out), (v_ref, v_out), (q_ref, q_out)):
        for head in range(heads):
            target[head] = source[:, head * HDIM : (head + 1) * HDIM]


def unpack_kernel(heads, parts_ref, out_ref):
    for head in range(heads):
        out_ref[:, head * HDIM : (head + 1) * HDIM] = parts_ref[head]


def attend_range_kernel(q_ref, k_low, k_own, k_high, v_low, v_own, v_high, bias_ref, out_ref, kv, *scratch):
    at = 0
    for k_part, v_part in ((k_low, v_low), (k_own, v_own), (k_high, v_high)):
        for tile in range(k_part.shape[0] // TILE):
            kv[0, at] = k_part[rows_of(tile), :].T
            kv[1, at] = v_part[rows_of(tile), :]
            at += 1

    @pl.loop(0, q_ref.shape[0] // (BLOCK * TILE))
    def _(block):
        place = pl.ds(pl.multiple_of(block * BLOCK * TILE, TILE), BLOCK * TILE)
        attend_block(block * BLOCK, q_ref.at[place, :], kv, bias_ref, out_ref.at[place, :], *scratch)


def to_heads(array):
    heads, rows, _ = array.shape
    return lax.all_to_all(array, "head", split_axis=0, concat_axis=0, tiled=True).reshape(heads * rows, HDIM)


def whole_range(queries, keys, values, bias):
    rows, columns = queries.shape
    heads = columns // HDIM
    parts = (heads, rows, HDIM)
    q_parts, k_parts, v_parts = call(
        functools.partial(pack_kernel, heads), "pack", (queries, keys, values), [VMEM] * 3, [parts] * 3
    )
    k_own, v_own = to_heads(k_parts), to_heads(v_parts)
    (k_low, k_high), (v_low, v_high) = halo(k_own, 0, TILE), halo(v_own, 0, TILE)
    local_q = to_heads(q_parts)
    padded = heads * rows // TILE + LIST - 1
    head_out = call(
        attend_range_kernel,
        "attend_range",
        (local_q, k_low, k_own, k_high, v_low, v_own, v_high, bias),
        [VMEM] * 8,
        (heads * rows, HDIM),
        [pltpu.VMEM((2, padded, TILE, HDIM), jnp.bfloat16)] + block_scratch(),
        24,
    )
    back = lax.all_to_all(head_out.reshape(parts), "head", split_axis=0, concat_axis=0, tiled=True)
    return call(functools.partial(unpack_kernel, heads), "unpack", (back,), [VMEM], (rows, columns))


def load_kv_kernel(heads, shift, k_ref, v_ref, out_ref):
    columns = column_of(lax.rem(lax.axis_index("head") + shift, heads))
    for tile in range(BLOCK):
        out_ref[0, tile] = k_ref[rows_of(tile), columns].T
        out_ref[1, tile] = v_ref[rows_of(tile), columns]


def load_q_kernel(heads, shift, q_ref, *refs):
    refs[-1][...] = q_ref[:, column_of(lax.rem(lax.axis_index("head") + shift, heads))]


def gather_kernel(*refs):
    heads, out_ref = len(refs) - 1, refs[-1]
    me = lax.axis_index("head")
    for shift in range(heads):
        out_ref[:, pl.ds(lax.rem(me + heads - shift, heads) * BLOCK, BLOCK)] = refs[shift][...]


def join_kernel(*refs):
    at = 0
    for ref in refs[:-1]:
        refs[-1][:, at : at + ref.shape[1]] = ref[...]
        at += ref.shape[1]


def pass_kernel(array_ref, *refs):
    refs[-1][...] = array_ref[...]


def stack_kernel(*refs):
    for at, ref in enumerate(refs[:-1]):
        refs[-1][at] = ref[...]


def attend_chunk_kernel(shift, heads, q_ref, kv_ref, bias_ref, *refs):
    out_ref, *scratch = refs[-3:]
    source = lax.rem(lax.axis_index("head") + heads - shift, heads)
    attend_block(source * BLOCK, q_ref.at[shift], kv_ref, bias_ref, out_ref, *scratch)


def spread_kernel(heads, *refs):
    out_ref = refs[-1]
    me = lax.axis_index("head")
    for shift in range(heads):
        out_ref[:, column_of(lax.rem(me + shift, heads))] = refs[shift][...]


def by_shifts(queries, keys, values, bias):
    heads = lax.axis_size("head")
    tiles = heads * BLOCK
    order = sorted(range(1, heads), key=lambda shift: -min(shift, heads - shift))
    chunk = (queries.shape[0], HDIM)

    def send(array, shift):
        return lax.ppermute(array, "head", [(i, (i + shift) % heads) for i in range(heads)])

    def kernel_of(kernel, *settings):
        return functools.partial(kernel, *settings)

    kv_parts, q_parts = [None] * heads, [None] * heads
    for shift in order + [0]:
        part = call(
            kernel_of(load_kv_kernel, heads, shift), "load_kv", (keys, values), [VMEM] * 2, (2, BLOCK, TILE, HDIM)
        )
        kv_parts[shift] = send(part, shift) if shift else part
    for shift in order + [0]:
        after = (kv_parts[order[0]],) if shift else ()
        part = call(
            kernel_of(load_q_kernel, heads, shift), "load_q", (queries, *after), [VMEM] * (1 + len(after)), chunk
        )
        q_parts[shift] = send(part, shift) if shift else part
    own = call(gather_kernel, "gather", kv_parts, [VMEM] * heads, (2, tiles, TILE, HDIM))
    low, high = halo(own, 1, 1)
    local_q = call(stack_kernel, "stack", q_parts, [VMEM] * heads, (heads, *chunk), cost=cost(1 << 14))
    padded = call(join_kernel, "join", (low, own, high), [VMEM] * 3, (2, tiles + LIST - 1, TILE, HDIM))
    outs = [None] * heads
    after = ()
    for shift in order + [0]:
        outs[shift] = call(
            kernel_of(attend_chunk_kernel, shift, heads),
            "attend_chunk",
            (local_q, padded, bias, *after),
            [VMEM] * (3 + len(after)),
            chunk,
            block_scratch(),
            16,
            cost(BLOCK * LIST // 2 if shift else 1),
        )
        after = (outs[shift],)
        if shift:
            outs[shift] = send(outs[shift], -shift)
    after = ()
    for shift in order:
        operands = (outs[shift], *after)
        outs[shift] = call(
            pass_kernel, "landed", operands, [VMEM] * len(operands), chunk, cost=cost(BLOCK * LIST // 2)
        )
        after = (outs[shift],)
    return call(kernel_of(spread_kernel, heads), "spread", outs, [VMEM] * heads, queries.shape)


def on_device(queries, keys, values, tile_lists, live_counts):
    bias = mask_bias(tile_lists, live_counts, tile_lists.shape[0] * lax.axis_size("ctx"))
    heads = lax.axis_size("head")
    in_chunks = queries.shape[0] == BLOCK * TILE and heads <= 8 and heads % 2 == 0
    form = by_shifts if in_chunks and heads * BLOCK >= EDGE else whole_range
    return form(queries, keys, values, bias)


def solution(mesh):
    return jax.shard_map(
        on_device,
        mesh=mesh,
        in_specs=(
            P(("groups", "ctx", "head"), None),
            P(("groups", "ctx", "head"), None),
            P(("groups", "ctx", "head"), None),
            P(("groups", "ctx"), None),
            P(("groups", "ctx")),
        ),
        out_specs=P(("groups", "ctx", "head"), None),
        check_vma=False,
    )
```

time: 57 us -> 56.7 us (level)
  the two profiles are of different devices: /device:TPU:0 before, /device:TPU:1 now
where the time goes in v6:
time: 56.7 us; the launch traced here: 56.5 us
  starting transfers between devices  24.5 us (43%)
  waiting for transfers between devices  20.5 us (36%)
  Pallas kernels  9.04 us (16%)
  local copies, waits for them, and re-layouts  2.19 us (4%)
    ppermute x9, starting transfers between devices, send(): lax.ppermute(array, 'head', [(i, (i + shift) % heads) for i in range(head...  16.6 us
    ppermute x9, waiting for transfers between devices, send(): lax.ppermute(array, 'head', [(i, (i + shift) % heads) for i in range(head...  12.7 us
    pallas_call x20, Pallas kernels, call(): pl.pallas_call(kernel, out_shape=out_shape, in_specs=in_specs, out_specs=...  9.04 us
    ppermute x1, waiting for transfers between devices, halo(): high = lax.ppermute(head, 'ctx', [(i + 1, i) for i in range(ctx - 1)])  7.8 us
    ppermute x1, starting transfers between devices, halo(): low = lax.ppermute(tail, 'ctx', [(i, i + 1) for i in range(ctx - 1)])  5.97 us
    unnamed x14, local copies, waits for them, and re-layouts  2.02 us
    ppermute x1, starting transfers between devices, halo(): high = lax.ppermute(head, 'ctx', [(i + 1, i) for i in range(ctx - 1)])  1.92 us
  transfers between devices with their start and end apart: 11, of which 3 were waited for; matrix products, arithmetic and copies ran while one was open for 0% of the time, Pallas kernels for 11%

profile of v6, /device:TPU:1, one launch (start us, length us, event | category | flops | bytes accessed | tf_op | source)
XLA Modules:
  0.0 56.5 jit_solution(2116081837878742576)
XLA Ops:
  0.0 0.0 copy-start
  0.0 1.0 %copy-done = bf16[384,512]{1,0:T(8,128)(2,1)S(1)} copy-done((bf16[384,512]{1,0:T(8,128)(2,1)S(1)}, bf16[384,512]{1,0:T(8,128)(2,1)}, u32[]{:S(2)}) %copy-start) | copy-done | bytes 393240
  1.0 0.0 copy-start.2
  1.0 1.0 %copy-done.2 = bf16[384,512]{1,0:T(8,128)(2,1)S(1)} copy-done((bf16[384,512]{1,0:T(8,128)(2,1)S(1)}, bf16[384,512]{1,0:T(8,128)(2,1)}, u32[]{:S(2)}) %copy-start.2) | copy-done | bytes 393240
  2.0 0.1 load_kv.4
  2.1 3.2 %collective-permute-start = (bf16[2,3,128,128]{3,2,1,0:T(8,128)(2,1)S(1)}, bf16[2,3,128,128]{3,2,1,0:T(8,128)(2,1)S(1)}, u32[]{:S(2)}, u32[]{:S(2)}) collective-permute-start(bf16[2,3,128,128]{3,2,1,0:T(8,128)(2,1)S(1)} %load_kv.4), channel_id=1, source_target_pairs={{0,2},{1,3},{2,0},{3,1},{4,6},{5,7},{6,4},{7,5},{8,10},{9,11},{10,... | collective-permute-start | bytes 589832 | tf_op jit(solution)/shard_map/ppermute | solution.py:229
  5.3 0.1 load_kv.6
  5.4 0.0 copy-start.1
  5.4 0.0 copy-start.3
  5.4 1.3 %collective-permute-start.4 = (bf16[2,3,128,128]{3,2,1,0:T(8,128)(2,1)S(1)}, bf16[2,3,128,128]{3,2,1,0:T(8,128)(2,1)S(1)}, u32[]{:S(2)}, u32[]{:S(2)}) collective-permute-start(bf16[2,3,128,128]{3,2,1,0:T(8,128)(2,1)S(1)} %load_kv.6), channel_id=1, source_target_pairs={{0,1},{1,2},{2,3},{3,0},{4,5},{5,6},{6,7},{7,4},{8,9},{9,10},{10,1... | collective-permute-start | bytes 589832 | tf_op jit(solution)/shard_map/ppermute | solution.py:229
  6.8 0.1 load_kv.7
  6.9 0.0 copy-start.6
  6.9 0.0 copy-start.5
  6.9 2.0 %collective-permute-start.5 = (bf16[2,3,128,128]{3,2,1,0:T(8,128)(2,1)S(1)}, bf16[2,3,128,128]{3,2,1,0:T(8,128)(2,1)S(1)}, u32[]{:S(2)}, u32[]{:S(2)}) collective-permute-start(bf16[2,3,128,128]{3,2,1,0:T(8,128)(2,1)S(1)} %load_kv.7), channel_id=1, source_target_pairs={{0,3},{1,0},{2,1},{3,2},{4,7},{5,4},{6,5},{7,6},{8,11},{9,8},{10,9... | collective-permute-start | bytes 589832 | tf_op jit(solution)/shard_map/ppermute | solution.py:229
  8.9 9.5 %collective-permute-done.refs_0_.refs_2_ = bf16[2,3,128,128]{3,2,1,0:T(8,128)(2,1)S(1)} collective-permute-done((bf16[2,3,128,128]{3,2,1,0:T(8,128)(2,1)S(1)}, bf16[2,3,128,128]{3,2,1,0:T(8,128)(2,1)S(1)}, u32[]{:S(2)}, u32[]{:S(2)}) %collective-permute-start) | collective-permute-done | bytes 196640 | tf_op jit(solution)/shard_map/ppermute | solution.py:229
  18.4 0.0 copy-done.4
  18.4 0.1 collective-permute-start.1
  18.5 1.1 %collective-permute-start.2 = (bf16[384,128]{1,0:T(8,128)(2,1)S(1)}, bf16[384,128]{1,0:T(8,128)(2,1)S(1)}, u32[]{:S(2)}, u32[]{:S(2)}) collective-permute-start(bf16[384,128]{1,0:T(8,128)(2,1)S(1)} %load_q.6), channel_id=1, source_target_pairs={{0,2},{1,3},{2,0},{3,1},{4,6},{5,7},{6,4},{7,5},{8,10},{9,11},{10,... | collective-permute-start | bytes 294920 | tf_op jit(solution)/shard_map/ppermute | solution.py:229
  19.6 2.3 %collective-permute-start.3 = (bf16[384,128]{1,0:T(8,128)(2,1)S(1)}, bf16[384,128]{1,0:T(8,128)(2,1)S(1)}, u32[]{:S(2)}, u32[]{:S(2)}) collective-permute-start(bf16[384,128]{1,0:T(8,128)(2,1)S(1)} %load_q.7), channel_id=1, source_target_pairs={{0,3},{1,0},{2,1},{3,2},{4,7},{5,4},{6,5},{7,6},{8,11},{9,8},{10,9... | collective-permute-start | bytes 294920 | tf_op jit(solution)/shard_map/ppermute | solution.py:229
  21.9 0.0 copy-done.1
  21.9 0.0 copy-done.3
  21.9 0.1 load_kv.5.refs_0_
  22.1 0.0 copy-done.6
  22.1 0.1 copy.6.counts_ref
  22.2 0.0 copy-done.5
  22.2 0.6 %mask_bias.1.bias_ref = f32[27,12,128]{2,1,0:T(8,128)S(1)} custom-call(s32[12,16]{1,0:T(8,128)S(1)} %copy-done.5, s32[12,1]{1,0:T(8,128)S(1)} %copy.6.counts_ref), custom_call_target="tpu_custom_call" | custom-call | tf_op jit(solution)/shard_map/mask_bias/pallas_call | solution.py:29
  22.8 0.0 collective-permute-done.4.refs_1_
  22.8 0.0 collective-permute-done.5.refs_3_
  22.8 0.1 gather.1.refs_1_
  22.9 6.0 %collective-permute-start.6 = (bf16[2,8,128,128]{3,2,1,0:T(8,128)(2,1)S(1)}, bf16[2,8,128,128]{3,2,1,0:T(8,128)(2,1)S(1)}, u32[]{:S(2)}, u32[]{:S(2)}) collective-permute-start(bf16[2,8,128,128]{3,2,1,0:T(8,128)(2,1)S(1)} %slice.8), channel_id=1, source_target_pairs={{0,4},{4,8},{8,12},{1,5},{5,9},{9,13},{2,6},{6,10},{10,14},{3,7},{... | collective-permute-start | bytes 1572872 | tf_op jit(solution)/shard_map/ppermute | solution.py:116
  28.9 1.9 %collective-permute-start.7 = (bf16[2,7,128,128]{3,2,1,0:T(8,128)(2,1)S(1)}, bf16[2,7,128,128]{3,2,1,0:T(8,128)(2,1)S(1)}, u32[]{:S(2)}, u32[]{:S(2)}) collective-permute-start(bf16[2,7,128,128]{3,2,1,0:T(8,128)(2,1)S(1)} %slice.9), channel_id=1, source_target_pairs={{4,0},{8,4},{12,8},{5,1},{9,5},{13,9},{6,2},{10,6},{14,10},{7,3},{... | collective-permute-start | bytes 1376264 | tf_op jit(solution)/shard_map/ppermute | solution.py:117
  30.9 0.0 collective-permute-done.1.refs_1_
  30.9 0.0 collective-permute-done.2.refs_2_
  30.9 0.0 collective-permute-done.3.refs_3_
  30.9 7.8 %collective-permute-done.7.refs_2_ = bf16[2,7,128,128]{3,2,1,0:T(8,128)(2,1)S(1)} collective-permute-done((bf16[2,7,128,128]{3,2,1,0:T(8,128)(2,1)S(1)}, bf16[2,7,128,128]{3,2,1,0:T(8,128)(2,1)S(1)}, u32[]{:S(2)}, u32[]{:S(2)}) %collective-permute-start.7) | collective-permute-done | bytes 458784 | tf_op jit(solution)/shard_map/ppermute | solution.py:117
  38.7 0.0 collective-permute-done.6.refs_0_
  38.7 0.1 join.1.kv_ref
  38.9 1.7 %attend_chunk.4.refs_0_ = bf16[384,128]{1,0:T(8,128)(2,1)S(1)} custom-call(bf16[4,384,128]{2,1,0:T(8,128)(2,1)S(1)} %stack.1.q_ref, bf16[2,27,128,128]{3,2,1,0:T(8,128)(2,1)S(1)} %join.1.kv_ref, f32[27,12,128]{2,1,0:T(8,128)S(1)} %mask_bias.1.bias_ref), custom_call_target="tpu_custom_call" | custom-call | flops 201326592 | bytes 393216 | tf_op jit(solution)/shard_map/attend_chunk/pallas_call | solution.py:29
  40.6 5.1 %collective-permute-start.9 = (bf16[384,128]{1,0:T(8,128)(2,1)S(1)}, bf16[384,128]{1,0:T(8,128)(2,1)S(1)}, u32[]{:S(2)}, u32[]{:S(2)}) collective-permute-start(bf16[384,128]{1,0:T(8,128)(2,1)S(1)} %attend_chunk.4.refs_0_), channel_id=1, source_target_pairs={{0,2},{1,3},{2,0},{3,1},{4,6},{5,7},{6,4},{7,5},{8,10},{9,11},{10,... | collective-permute-start | bytes 294920 | tf_op jit(solution)/shard_map/ppermute | solution.py:229
  45.7 1.7 %attend_chunk.5.refs_0_ = bf16[384,128]{1,0:T(8,128)(2,1)S(1)} custom-call(bf16[4,384,128]{2,1,0:T(8,128)(2,1)S(1)} %stack.1.q_ref, bf16[2,27,128,128]{3,2,1,0:T(8,128)(2,1)S(1)} %join.1.kv_ref, f32[27,12,128]{2,1,0:T(8,128)S(1)} %mask_bias.1.bias_ref, bf16[384,128]{1,0:T(8,128)(2,1)S(1)} %attend_chunk.4.refs_0_), custom_call_target="tpu_custom_call" | custom-call | flops 201326592 | bytes 393216 | tf_op jit(solution)/shard_map/attend_chunk/pallas_call | solution.py:29
  47.4 1.2 %collective-permute-start.8 = (bf16[384,128]{1,0:T(8,128)(2,1)S(1)}, bf16[384,128]{1,0:T(8,128)(2,1)S(1)}, u32[]{:S(2)}, u32[]{:S(2)}) collective-permute-start(bf16[384,128]{1,0:T(8,128)(2,1)S(1)} %attend_chunk.5.refs_0_), channel_id=1, source_target_pairs={{0,3},{1,0},{2,1},{3,2},{4,7},{5,4},{6,5},{7,6},{8,11},{9,8},{10,9... | collective-permute-start | bytes 294920 | tf_op jit(solution)/shard_map/ppermute | solution.py:229
  48.6 1.7 %attend_chunk.6.refs_0_ = bf16[384,128]{1,0:T(8,128)(2,1)S(1)} custom-call(bf16[4,384,128]{2,1,0:T(8,128)(2,1)S(1)} %stack.1.q_ref, bf16[2,27,128,128]{3,2,1,0:T(8,128)(2,1)S(1)} %join.1.kv_ref, f32[27,12,128]{2,1,0:T(8,128)S(1)} %mask_bias.1.bias_ref, bf16[384,128]{1,0:T(8,128)(2,1)S(1)} %attend_chunk.5.refs_0_), custom_call_target="tpu_custom_call" | custom-call | flops 201326592 | bytes 393216 | tf_op jit(solution)/shard_map/attend_chunk/pallas_call | solution.py:29
  50.3 0.4 collective-permute-start.10
  50.7 1.7 %attend_chunk.7.refs_0_ = bf16[384,128]{1,0:T(8,128)(2,1)S(1)} custom-call(bf16[4,384,128]{2,1,0:T(8,128)(2,1)S(1)} %stack.1.q_ref, bf16[2,27,128,128]{3,2,1,0:T(8,128)(2,1)S(1)} %join.1.kv_ref, f32[27,12,128]{2,1,0:T(8,128)S(1)} %mask_bias.1.bias_ref, bf16[384,128]{1,0:T(8,128)(2,1)S(1)} %attend_chunk.6.refs_0_), custom_call_target="tpu_custom_call" | custom-call | flops 8388608 | bytes 16384 | tf_op jit(solution)/shard_map/attend_chunk/pallas_call | solution.py:29
  52.4 0.0 collective-permute-done.9.array_ref
  52.4 0.0 collective-permute-done.8.array_ref
  52.5 3.2 %collective-permute-done.10.array_ref = bf16[384,128]{1,0:T(8,128)(2,1)S(1)} collective-permute-done((bf16[384,128]{1,0:T(8,128)(2,1)S(1)}, bf16[384,128]{1,0:T(8,128)(2,1)S(1)}, u32[]{:S(2)}, u32[]{:S(2)}) %collective-permute-start.10) | collective-permute-done | bytes 98336 | tf_op jit(solution)/shard_map/ppermute | solution.py:229
  55.6 0.9 %spread.1 = bf16[384,512]{1,0:T(8,128)(2,1)} custom-call(bf16[384,128]{1,0:T(8,128)(2,1)S(1)} %attend_chunk.7.refs_0_, bf16[384,128]{1,0:T(8,128)(2,1)S(1)} %landed.4.refs_0_.refs_1_, bf16[384,128]{1,0:T(8,128)(2,1)S(1)} %landed.3.refs_0_.refs_2_, bf16[384,128]{1,0:T(8,128)(2,1)S(1)} %landed.5.refs_3_), custom_call_target="tpu_custom_call" | custom-call | tf_op jit(solution)/shard_map/spread/pallas_call | solution.py:29
  (11 shorter events, 0.2 us)
Async XLA Ops:
  0.0 1.0 %copy-start = (bf16[384,512]{1,0:T(8,128)(2,1)S(1)}, bf16[384,512]{1,0:T(8,128)(2,1)}, u32[]{:S(2)}) copy-start(bf16[384,512]{1,0:T(8,128)(2,1)} %k_ref.7) | copy-start | bytes 1179652
  1.0 1.0 %copy-start.2 = (bf16[384,512]{1,0:T(8,128)(2,1)S(1)}, bf16[384,512]{1,0:T(8,128)(2,1)}, u32[]{:S(2)}) copy-start(bf16[384,512]{1,0:T(8,128)(2,1)} %v_ref.7) | copy-start | bytes 1179652
  2.0 16.4 %copy-start.4 = (bf16[384,512]{1,0:T(8,128)(2,1)S(1)}, bf16[384,512]{1,0:T(8,128)(2,1)}, u32[]{:S(2)}) copy-start(bf16[384,512]{1,0:T(8,128)(2,1)} %q_ref.7) | copy-start | bytes 1179652
  2.1 16.3 %collective-permute-start = (bf16[2,3,128,128]{3,2,1,0:T(8,128)(2,1)S(1)}, bf16[2,3,128,128]{3,2,1,0:T(8,128)(2,1)S(1)}, u32[]{:S(2)}, u32[]{:S(2)}) collective-permute-start(bf16[2,3,128,128]{3,2,1,0:T(8,128)(2,1)S(1)} %load_kv.4), channel_id=1, source_target_pairs={{0,2},{1,3},{2,0},{3,1},{4,6},{5,7},{6,4},{7,5},{8,10},{9,11},{10,... | collective-permute-start | bytes 589832 | tf_op jit(solution)/shard_map/ppermute | solution.py:229
  5.4 16.5 %copy-start.1 = (bf16[384,512]{1,0:T(8,128)(2,1)S(1)}, bf16[384,512]{1,0:T(8,128)(2,1)}, u32[]{:S(2)}) copy-start(bf16[384,512]{1,0:T(8,128)(2,1)} %k_ref.7) | copy-start | bytes 1179652
  5.4 16.5 %copy-start.3 = (bf16[384,512]{1,0:T(8,128)(2,1)S(1)}, bf16[384,512]{1,0:T(8,128)(2,1)}, u32[]{:S(2)}) copy-start(bf16[384,512]{1,0:T(8,128)(2,1)} %v_ref.7) | copy-start | bytes 1179652
  5.4 17.3 %collective-permute-start.4 = (bf16[2,3,128,128]{3,2,1,0:T(8,128)(2,1)S(1)}, bf16[2,3,128,128]{3,2,1,0:T(8,128)(2,1)S(1)}, u32[]{:S(2)}, u32[]{:S(2)}) collective-permute-start(bf16[2,3,128,128]{3,2,1,0:T(8,128)(2,1)S(1)} %load_kv.6), channel_id=1, source_target_pairs={{0,1},{1,2},{2,3},{3,0},{4,5},{5,6},{6,7},{7,4},{8,9},{9,10},{10,1... | collective-permute-start | bytes 589832 | tf_op jit(solution)/shard_map/ppermute | solution.py:229
  6.9 15.2 %copy-start.6 = (s32[12]{0:T(128)S(1)}, s32[12]{0:T(128)}, u32[]{:S(2)}) copy-start(s32[12]{0:T(128)} %param.9) | copy-start | bytes 148
  6.9 15.3 %copy-start.5 = (s32[12,16]{1,0:T(8,128)S(1)}, s32[12,16]{1,0:T(8,128)}, u32[]{:S(2)}) copy-start(s32[12,16]{1,0:T(8,128)} %lists_ref.1) | copy-start | bytes 2308
  6.9 15.9 %collective-permute-start.5 = (bf16[2,3,128,128]{3,2,1,0:T(8,128)(2,1)S(1)}, bf16[2,3,128,128]{3,2,1,0:T(8,128)(2,1)S(1)}, u32[]{:S(2)}, u32[]{:S(2)}) collective-permute-start(bf16[2,3,128,128]{3,2,1,0:T(8,128)(2,1)S(1)} %load_kv.7), channel_id=1, source_target_pairs={{0,3},{1,0},{2,1},{3,2},{4,7},{5,4},{6,5},{7,6},{8,11},{9,8},{10,9... | collective-permute-start | bytes 589832 | tf_op jit(solution)/shard_map/ppermute | solution.py:229
  18.4 12.4 %collective-permute-start.1 = (bf16[384,128]{1,0:T(8,128)(2,1)S(1)}, bf16[384,128]{1,0:T(8,128)(2,1)S(1)}, u32[]{:S(2)}, u32[]{:S(2)}) collective-permute-start(bf16[384,128]{1,0:T(8,128)(2,1)S(1)} %load_q.5), channel_id=1, source_target_pairs={{0,1},{1,2},{2,3},{3,0},{4,5},{5,6},{6,7},{7,4},{8,9},{9,10},{10,1... | collective-permute-start | bytes 294920 | tf_op jit(solution)/shard_map/ppermute | solution.py:229
  18.5 12.3 %collective-permute-start.2 = (bf16[384,128]{1,0:T(8,128)(2,1)S(1)}, bf16[384,128]{1,0:T(8,128)(2,1)S(1)}, u32[]{:S(2)}, u32[]{:S(2)}) collective-permute-start(bf16[384,128]{1,0:T(8,128)(2,1)S(1)} %load_q.6), channel_id=1, source_target_pairs={{0,2},{1,3},{2,0},{3,1},{4,6},{5,7},{6,4},{7,5},{8,10},{9,11},{10,... | collective-permute-start | bytes 294920 | tf_op jit(solution)/shard_map/ppermute | solution.py:229
  19.6 11.3 %collective-permute-start.3 = (bf16[384,128]{1,0:T(8,128)(2,1)S(1)}, bf16[384,128]{1,0:T(8,128)(2,1)S(1)}, u32[]{:S(2)}, u32[]{:S(2)}) collective-permute-start(bf16[384,128]{1,0:T(8,128)(2,1)S(1)} %load_q.7), channel_id=1, source_target_pairs={{0,3},{1,0},{2,1},{3,2},{4,7},{5,4},{6,5},{7,6},{8,11},{9,8},{10,9... | collective-permute-start | bytes 294920 | tf_op jit(solution)/shard_map/ppermute | solution.py:229
  22.9 15.8 %collective-permute-start.6 = (bf16[2,8,128,128]{3,2,1,0:T(8,128)(2,1)S(1)}, bf16[2,8,128,128]{3,2,1,0:T(8,128)(2,1)S(1)}, u32[]{:S(2)}, u32[]{:S(2)}) collective-permute-start(bf16[2,8,128,128]{3,2,1,0:T(8,128)(2,1)S(1)} %slice.8), channel_id=1, source_target_pairs={{0,4},{4,8},{8,12},{1,5},{5,9},{9,13},{2,6},{6,10},{10,14},{3,7},{... | collective-permute-start | bytes 1572872 | tf_op jit(solution)/shard_map/ppermute | solution.py:116
  28.9 9.8 %collective-permute-start.7 = (bf16[2,7,128,128]{3,2,1,0:T(8,128)(2,1)S(1)}, bf16[2,7,128,128]{3,2,1,0:T(8,128)(2,1)S(1)}, u32[]{:S(2)}, u32[]{:S(2)}) collective-permute-start(bf16[2,7,128,128]{3,2,1,0:T(8,128)(2,1)S(1)} %slice.9), channel_id=1, source_target_pairs={{4,0},{8,4},{12,8},{5,1},{9,5},{13,9},{6,2},{10,6},{14,10},{7,3},{... | collective-permute-start | bytes 1376264 | tf_op jit(solution)/shard_map/ppermute | solution.py:117
  40.6 11.8 %collective-permute-start.9 = (bf16[384,128]{1,0:T(8,128)(2,1)S(1)}, bf16[384,128]{1,0:T(8,128)(2,1)S(1)}, u32[]{:S(2)}, u32[]{:S(2)}) collective-permute-start(bf16[384,128]{1,0:T(8,128)(2,1)S(1)} %attend_chunk.4.refs_0_), channel_id=1, source_target_pairs={{0,2},{1,3},{2,0},{3,1},{4,6},{5,7},{6,4},{7,5},{8,10},{9,11},{10,... | collective-permute-start | bytes 294920 | tf_op jit(solution)/shard_map/ppermute | solution.py:229
  47.4 5.0 %collective-permute-start.8 = (bf16[384,128]{1,0:T(8,128)(2,1)S(1)}, bf16[384,128]{1,0:T(8,128)(2,1)S(1)}, u32[]{:S(2)}, u32[]{:S(2)}) collective-permute-start(bf16[384,128]{1,0:T(8,128)(2,1)S(1)} %attend_chunk.5.refs_0_), channel_id=1, source_target_pairs={{0,3},{1,0},{2,1},{3,2},{4,7},{5,4},{6,5},{7,6},{8,11},{9,8},{10,9... | collective-permute-start | bytes 294920 | tf_op jit(solution)/shard_map/ppermute | solution.py:229
  50.3 5.3 %collective-permute-start.10 = (bf16[384,128]{1,0:T(8,128)(2,1)S(1)}, bf16[384,128]{1,0:T(8,128)(2,1)S(1)}, u32[]{:S(2)}, u32[]{:S(2)}) collective-permute-start(bf16[384,128]{1,0:T(8,128)(2,1)S(1)} %attend_chunk.6.refs_0_), channel_id=1, source_target_pairs={{0,1},{1,2},{2,3},{3,0},{4,5},{5,6},{6,7},{7,4},{8,9},{9,10},{10,1... | collective-permute-start | bytes 294920 | tf_op jit(solution)/shard_map/ppermute | solution.py:229

commit v7 on v6

--- a/solution.py
+++ b/solution.py
@@ -68,12 +68,12 @@
     return call(kernel, "mask_bias", (tile_lists, live_counts[:, None]), [VMEM] * 2, shape)
 
 
-def attend_block(first, q_ref, kv_ref, bias_ref, out_ref, scores, probs):
+def attend_block(first, q_ref, kt_ref, v_ref, bias_ref, out_ref, scores, probs):
     for pair in range(WINDOW // 2):
         low = max(0, 2 * pair - LIST + 1)
         high = min(BLOCK - 1, 2 * pair + 1)
         at = first + 2 * pair
-        keys = jnp.concatenate([kv_ref[0, at], kv_ref[0, at + 1]], axis=1)
+        keys = jnp.concatenate([kt_ref[at], kt_ref[at + 1]], axis=1)
         part = jnp.dot(
             q_ref[low * TILE : (high + 1) * TILE, :], keys, preferred_element_type=jnp.float32
         )
@@ -93,7 +93,7 @@
             weights = jnp.exp2((scores[tile, :, rows_of(offset)] - highest) * EXPONENT_SCALE)
             total += weights
             probs[tile, :, rows_of(offset)] = weights.astype(jnp.bfloat16)
-        values = kv_ref[1, pl.ds(first + tile, LIST)].reshape(LIST * TILE, HDIM)
+        values = v_ref[pl.ds(first + tile, LIST)].reshape(LIST * TILE, HDIM)
         mixed = jnp.dot(probs[tile], values, preferred_element_type=jnp.float32)
         out_ref[rows_of(tile), :] = (mixed / jnp.sum(total, axis=1, keepdims=True)).astype(jnp.bfloat16)
 
@@ -129,18 +129,18 @@
         out_ref[:, head * HDIM : (head + 1) * HDIM] = parts_ref[head]
 
 
-def attend_range_kernel(q_ref, k_low, k_own, k_high, v_low, v_own, v_high, bias_ref, out_ref, kv, *scratch):
+def attend_range_kernel(q_ref, k_low, k_own, k_high, v_low, v_own, v_high, bias_ref, out_ref, kt, v, *scratch):
     at = 0
     for k_part, v_part in ((k_low, v_low), (k_own, v_own), (k_high, v_high)):
         for tile in range(k_part.shape[0] // TILE):
-            kv[0, at] = k_part[rows_of(tile), :].T
-            kv[1, at] = v_part[rows_of(tile), :]
+            kt[at] = k_part[rows_of(tile), :].T
+            v[at] = v_part[rows_of(tile), :]
             at += 1
 
     @pl.loop(0, q_ref.shape[0] // (BLOCK * TILE))
     def _(block):
         place = pl.ds(pl.multiple_of(block * BLOCK * TILE, TILE), BLOCK * TILE)
-        attend_block(block * BLOCK, q_ref.at[place, :], kv, bias_ref, out_ref.at[place, :], *scratch)
+        attend_block(block * BLOCK, q_ref.at[place, :], kt, v, bias_ref, out_ref.at[place, :], *scratch)
 
 
 def to_heads(array):
@@ -165,18 +165,18 @@
         (local_q, k_low, k_own, k_high, v_low, v_own, v_high, bias),
         [VMEM] * 8,
         (heads * rows, HDIM),
-        [pltpu.VMEM((2, padded, TILE, HDIM), jnp.bfloat16)] + block_scratch(),
+        [pltpu.VMEM((padded, TILE, HDIM), jnp.bfloat16)] * 2 + block_scratch(),
         24,
     )
     back = lax.all_to_all(head_out.reshape(parts), "head", split_axis=0, concat_axis=0, tiled=True)
     return call(functools.partial(unpack_kernel, heads), "unpack", (back,), [VMEM], (rows, columns))
 
 
-def load_kv_kernel(heads, shift, k_ref, v_ref, out_ref):
+def load_tiles_kernel(heads, shift, turn, array_ref, *refs):
     columns = column_of(lax.rem(lax.axis_index("head") + shift, heads))
     for tile in range(BLOCK):
-        out_ref[0, tile] = k_ref[rows_of(tile), columns].T
-        out_ref[1, tile] = v_ref[rows_of(tile), columns]
+        part = array_ref[rows_of(tile), columns]
+        refs[-1][tile] = part.T if turn else part
 
 
 def load_q_kernel(heads, shift, q_ref, *refs):
@@ -187,29 +187,32 @@
     heads, out_ref = len(refs) - 1, refs[-1]
     me = lax.axis_index("head")
     for shift in range(heads):
-        out_ref[:, pl.ds(lax.rem(me + heads - shift, heads) * BLOCK, BLOCK)] = refs[shift][...]
+        out_ref[pl.ds(lax.rem(me + heads - shift, heads) * BLOCK, BLOCK)] = refs[shift][...]
 
 
 def join_kernel(*refs):
     at = 0
     for ref in refs[:-1]:
-        refs[-1][:, at : at + ref.shape[1]] = ref[...]
-        at += ref.shape[1]
+        refs[-1][at : at + ref.shape[0]] = ref[...]
+        at += ref.shape[0]
+
+
+def with_halo(parts):
+    heads = len(parts)
+    tiles = heads * BLOCK
+    own = call(gather_kernel, "gather", parts, [VMEM] * heads, (tiles, TILE, HDIM))
+    low, high = halo(own, 0, 1)
+    return call(join_kernel, "join", (low, own, high), [VMEM] * 3, (tiles + LIST - 1, TILE, HDIM))
 
 
 def pass_kernel(array_ref, *refs):
     refs[-1][...] = array_ref[...]
 
 
-def stack_kernel(*refs):
-    for at, ref in enumerate(refs[:-1]):
-        refs[-1][at] = ref[...]
-
-
-def attend_chunk_kernel(shift, heads, q_ref, kv_ref, bias_ref, *refs):
+def attend_chunk_kernel(shift, heads, q_ref, kt_ref, v_ref, bias_ref, *refs):
     out_ref, *scratch = refs[-3:]
     source = lax.rem(lax.axis_index("head") + heads - shift, heads)
-    attend_block(source * BLOCK, q_ref.at[shift], kv_ref, bias_ref, out_ref, *scratch)
+    attend_block(source * BLOCK, q_ref, kt_ref, v_ref, bias_ref, out_ref, *scratch)
 
 
 def spread_kernel(heads, *refs):
@@ -221,40 +224,43 @@
 
 def by_shifts(queries, keys, values, bias):
     heads = lax.axis_size("head")
-    tiles = heads * BLOCK
     order = sorted(range(1, heads), key=lambda shift: -min(shift, heads - shift))
-    chunk = (queries.shape[0], HDIM)
+    chunk, tiles = (queries.shape[0], HDIM), (BLOCK, TILE, HDIM)
+
+    def kernel_of(kernel, *settings):
+        return functools.partial(kernel, *settings)
+
+    def call_after(kernel, name, operands, after, shape):
+        operands = (*operands, *after)
+        return call(kernel, name, operands, [VMEM] * len(operands), shape)
 
     def send(array, shift):
         return lax.ppermute(array, "head", [(i, (i + shift) % heads) for i in range(heads)])
 
-    def kernel_of(kernel, *settings):
-        return functools.partial(kernel, *settings)
-
-    kv_parts, q_parts = [None] * heads, [None] * heads
+    v_parts, k_parts, q_parts = [None] * heads, [None] * heads, [None] * heads
     for shift in order + [0]:
-        part = call(
-            kernel_of(load_kv_kernel, heads, shift), "load_kv", (keys, values), [VMEM] * 2, (2, BLOCK, TILE, HDIM)
-        )
-        kv_parts[shift] = send(part, shift) if shift else part
+        part = call_after(kernel_of(load_tiles_kernel, heads, shift, False), "load_v", (values,), (), tiles)
+        v_parts[shift] = send(part, shift) if shift else part
     for shift in order + [0]:
-        after = (kv_parts[order[0]],) if shift else ()
-        part = call(
-            kernel_of(load_q_kernel, heads, shift), "load_q", (queries, *after), [VMEM] * (1 + len(after)), chunk
-        )
+        after = [v_parts[shift]] if shift else []
+        if shift == order[-1]:
+            after.append(bias)
+        part = call_after(kernel_of(load_tiles_kernel, heads, shift, True), "load_k", (keys,), after, tiles)
+        k_parts[shift] = send(part, shift) if shift else part
+    for shift in order + [0]:
+        after = (k_parts[shift],) if shift else ()
+        part = call_after(kernel_of(load_q_kernel, heads, shift), "load_q", (queries,), after, chunk)
         q_parts[shift] = send(part, shift) if shift else part
-    own = call(gather_kernel, "gather", kv_parts, [VMEM] * heads, (2, tiles, TILE, HDIM))
-    low, high = halo(own, 1, 1)
-    local_q = call(stack_kernel, "stack", q_parts, [VMEM] * heads, (heads, *chunk), cost=cost(1 << 14))
-    padded = call(join_kernel, "join", (low, own, high), [VMEM] * 3, (2, tiles + LIST - 1, TILE, HDIM))
+    all_values, all_keys = with_halo(v_parts), with_halo(k_parts)
     outs = [None] * heads
     after = ()
     for shift in order + [0]:
+        operands = (q_parts[shift], all_keys, all_values, bias, *after)
         outs[shift] = call(
             kernel_of(attend_chunk_kernel, shift, heads),
             "attend_chunk",
-            (local_q, padded, bias, *after),
-            [VMEM] * (3 + len(after)),
+            operands,
+            [VMEM] * len(operands),
             chunk,
             block_scratch(),
             16,

time: 56.7 us -> 54.3 us (0.958)
  the two profiles are of different devices: /device:TPU:1 before, /device:TPU:2 now
where the time goes in v7:
time: 54.3 us; the launch traced here: 54.1 us
  starting transfers between devices  29.1 us (54%)
  waiting for transfers between devices  14.4 us (27%)
  Pallas kernels  9.08 us (17%)
  local copies, waits for them, and re-layouts  1.19 us (2%)
    ppermute x12, starting transfers between devices, send(): lax.ppermute(array, 'head', [(i, (i + shift) % heads) for i in range(head...  17.8 us
    ppermute x12, waiting for transfers between devices, send(): lax.ppermute(array, 'head', [(i, (i + shift) % heads) for i in range(head...  14.4 us
    pallas_call x25, Pallas kernels, call(): pl.pallas_call(kernel, out_shape=out_shape, in_specs=in_specs, out_specs=...  9.08 us
    ppermute x2, starting transfers between devices, halo(): high = lax.ppermute(head, 'ctx', [(i + 1, i) for i in range(ctx - 1)])  7.28 us
    ppermute x2, starting transfers between devices, halo(): low = lax.ppermute(tail, 'ctx', [(i, i + 1) for i in range(ctx - 1)])  3.97 us
  transfers between devices with their start and end apart: 16, of which 7 were waited for; matrix products, arithmetic and copies ran while one was open for 0% of the time, Pallas kernels for 15%

profile of v7, /device:TPU:2, one launch (start us, length us, event | category | flops | bytes accessed | tf_op | source)
XLA Modules:
  0.0 54.1 jit_solution(7595009823561318885)
XLA Ops:
  0.0 1.0 %copy-done.2 = bf16[384,512]{1,0:T(8,128)(2,1)S(1)} copy-done((bf16[384,512]{1,0:T(8,128)(2,1)S(1)}, bf16[384,512]{1,0:T(8,128)(2,1)}, u32[]{:S(2)}) %copy-start.2) | copy-done | bytes 393240
  1.0 3.7 %collective-permute-start.4 = (bf16[3,128,128]{2,1,0:T(8,128)(2,1)S(1)}, bf16[3,128,128]{2,1,0:T(8,128)(2,1)S(1)}, u32[]{:S(2)}, u32[]{:S(2)}) collective-permute-start(bf16[3,128,128]{2,1,0:T(8,128)(2,1)S(1)} %load_v.6), channel_id=1, source_target_pairs={{0,3},{1,0},{2,1},{3,2},{4,7},{5,4},{6,5},{7,6},{8,11},{9,8},{10,9... | collective-permute-start | bytes 294920 | tf_op jit(solution)/shard_map/ppermute | solution.py:238
  4.7 0.0 copy-start
  4.7 0.1 collective-permute-start
  4.8 0.0 copy-start.5
  4.8 0.0 copy-start.4
  4.8 1.0 %collective-permute-start.2 = (bf16[3,128,128]{2,1,0:T(8,128)(2,1)S(1)}, bf16[3,128,128]{2,1,0:T(8,128)(2,1)S(1)}, u32[]{:S(2)}, u32[]{:S(2)}) collective-permute-start(bf16[3,128,128]{2,1,0:T(8,128)(2,1)S(1)} %load_v.5), channel_id=1, source_target_pairs={{0,2},{1,3},{2,0},{3,1},{4,6},{5,7},{6,4},{7,5},{8,10},{9,11},{10,... | collective-permute-start | bytes 294920 | tf_op jit(solution)/shard_map/ppermute | solution.py:238
  5.9 0.1 copy.6.counts_ref
  6.0 0.6 %mask_bias.1.refs_1_.bias_ref = f32[27,12,128]{2,1,0:T(8,128)S(1)} custom-call(s32[12,16]{1,0:T(8,128)S(1)} %copy-done.4, s32[12,1]{1,0:T(8,128)S(1)} %copy.6.counts_ref), custom_call_target="tpu_custom_call" | custom-call | tf_op jit(solution)/shard_map/mask_bias/pallas_call | solution.py:29
  6.6 1.3 %collective-permute-done.4.refs_0_.refs_3_ = bf16[3,128,128]{2,1,0:T(8,128)(2,1)S(1)} collective-permute-done((bf16[3,128,128]{2,1,0:T(8,128)(2,1)S(1)}, bf16[3,128,128]{2,1,0:T(8,128)(2,1)S(1)}, u32[]{:S(2)}, u32[]{:S(2)}) %collective-permute-start.4) | collective-permute-done | bytes 98336 | tf_op jit(solution)/shard_map/ppermute | solution.py:238
  7.9 0.1 load_k.7
  8.0 4.3 %collective-permute-start.5 = (bf16[3,128,128]{2,1,0:T(8,128)(2,1)S(1)}, bf16[3,128,128]{2,1,0:T(8,128)(2,1)S(1)}, u32[]{:S(2)}, u32[]{:S(2)}) collective-permute-start(bf16[3,128,128]{2,1,0:T(8,128)(2,1)S(1)} %load_k.7), channel_id=1, source_target_pairs={{0,3},{1,0},{2,1},{3,2},{4,7},{5,4},{6,5},{7,6},{8,11},{9,8},{10,9... | collective-permute-start | bytes 294920 | tf_op jit(solution)/shard_map/ppermute | solution.py:238
  12.3 0.1 collective-permute-done.refs_0_.refs_1_
  12.4 0.1 load_k.5
  12.5 0.0 copy-start.3
  12.5 0.1 collective-permute-start.1
  12.6 4.7 %collective-permute-done.2.refs_0_.refs_2_ = bf16[3,128,128]{2,1,0:T(8,128)(2,1)S(1)} collective-permute-done((bf16[3,128,128]{2,1,0:T(8,128)(2,1)S(1)}, bf16[3,128,128]{2,1,0:T(8,128)(2,1)S(1)}, u32[]{:S(2)}, u32[]{:S(2)}) %collective-permute-start.2) | collective-permute-done | bytes 98336 | tf_op jit(solution)/shard_map/ppermute | solution.py:238
  17.3 0.1 load_k.6
  17.4 0.1 collective-permute-start.3
  17.6 1.9 %collective-permute-start.8 = (bf16[8,128,128]{2,1,0:T(8,128)(2,1)S(1)}, bf16[8,128,128]{2,1,0:T(8,128)(2,1)S(1)}, u32[]{:S(2)}, u32[]{:S(2)}) collective-permute-start(bf16[8,128,128]{2,1,0:T(8,128)(2,1)S(1)} %slice.18), channel_id=1, source_target_pairs={{0,4},{4,8},{8,12},{1,5},{5,9},{9,13},{2,6},{6,10},{10,14},{3,7},{... | collective-permute-start | bytes 786440 | tf_op jit(solution)/shard_map/ppermute | solution.py:116
  19.5 3.6 %collective-permute-start.9 = (bf16[7,128,128]{2,1,0:T(8,128)(2,1)S(1)}, bf16[7,128,128]{2,1,0:T(8,128)(2,1)S(1)}, u32[]{:S(2)}, u32[]{:S(2)}) collective-permute-start(bf16[7,128,128]{2,1,0:T(8,128)(2,1)S(1)} %slice.19), channel_id=1, source_target_pairs={{4,0},{8,4},{12,8},{5,1},{9,5},{13,9},{6,2},{10,6},{14,10},{7,3},{... | collective-permute-start | bytes 688136 | tf_op jit(solution)/shard_map/ppermute | solution.py:117
  23.2 0.1 load_k.4.refs_0_
  23.3 0.0 collective-permute-done.5.refs_3_.refs_0_
  23.3 0.5 %collective-permute-done.3.refs_2_.refs_0_ = bf16[3,128,128]{2,1,0:T(8,128)(2,1)S(1)} collective-permute-done((bf16[3,128,128]{2,1,0:T(8,128)(2,1)S(1)}, bf16[3,128,128]{2,1,0:T(8,128)(2,1)S(1)}, u32[]{:S(2)}, u32[]{:S(2)}) %collective-permute-start.3) | collective-permute-done | bytes 98336 | tf_op jit(solution)/shard_map/ppermute | solution.py:238
  23.9 0.0 copy-start.1
  23.9 2.1 %collective-permute-start.6 = (bf16[8,128,128]{2,1,0:T(8,128)(2,1)S(1)}, bf16[8,128,128]{2,1,0:T(8,128)(2,1)S(1)}, u32[]{:S(2)}, u32[]{:S(2)}) collective-permute-start(bf16[8,128,128]{2,1,0:T(8,128)(2,1)S(1)} %slice.16), channel_id=1, source_target_pairs={{0,4},{4,8},{8,12},{1,5},{5,9},{9,13},{2,6},{6,10},{10,14},{3,7},{... | collective-permute-start | bytes 786440 | tf_op jit(solution)/shard_map/ppermute | solution.py:116
  26.0 3.6 %collective-permute-start.7 = (bf16[7,128,128]{2,1,0:T(8,128)(2,1)S(1)}, bf16[7,128,128]{2,1,0:T(8,128)(2,1)S(1)}, u32[]{:S(2)}, u32[]{:S(2)}) collective-permute-start(bf16[7,128,128]{2,1,0:T(8,128)(2,1)S(1)} %slice.17), channel_id=1, source_target_pairs={{4,0},{8,4},{12,8},{5,1},{9,5},{13,9},{6,2},{10,6},{14,10},{7,3},{... | collective-permute-start | bytes 688136 | tf_op jit(solution)/shard_map/ppermute | solution.py:117
  29.7 2.4 %collective-permute-start.12 = (bf16[384,128]{1,0:T(8,128)(2,1)S(1)}, bf16[384,128]{1,0:T(8,128)(2,1)S(1)}, u32[]{:S(2)}, u32[]{:S(2)}) collective-permute-start(bf16[384,128]{1,0:T(8,128)(2,1)S(1)} %load_q.7), channel_id=1, source_target_pairs={{0,2},{1,3},{2,0},{3,1},{4,6},{5,7},{6,4},{7,5},{8,10},{9,11},{10,... | collective-permute-start | bytes 294920 | tf_op jit(solution)/shard_map/ppermute | solution.py:238
  32.2 0.0 collective-permute-done.9.refs_2_
  32.2 0.5 collective-permute-start.11
  32.7 0.0 collective-permute-done.8.refs_0_
  32.7 3.4 %collective-permute-start.10 = (bf16[384,128]{1,0:T(8,128)(2,1)S(1)}, bf16[384,128]{1,0:T(8,128)(2,1)S(1)}, u32[]{:S(2)}, u32[]{:S(2)}) collective-permute-start(bf16[384,128]{1,0:T(8,128)(2,1)S(1)} %load_q.5), channel_id=1, source_target_pairs={{0,3},{1,0},{2,1},{3,2},{4,7},{5,4},{6,5},{7,6},{8,11},{9,8},{10,9... | collective-permute-start | bytes 294920 | tf_op jit(solution)/shard_map/ppermute | solution.py:238
  36.1 0.1 join.3.v_ref
  36.2 0.0 collective-permute-done.7.refs_2_
  36.2 0.0 collective-permute-done.6.refs_0_
  36.2 0.1 join.2.kt_ref
  36.3 4.2 %collective-permute-done.12.q_ref = bf16[384,128]{1,0:T(8,128)(2,1)S(1)} collective-permute-done((bf16[384,128]{1,0:T(8,128)(2,1)S(1)}, bf16[384,128]{1,0:T(8,128)(2,1)S(1)}, u32[]{:S(2)}, u32[]{:S(2)}) %collective-permute-start.12) | collective-permute-done | bytes 98336 | tf_op jit(solution)/shard_map/ppermute | solution.py:238
  40.4 1.7 %attend_chunk.4.refs_0_ = bf16[384,128]{1,0:T(8,128)(2,1)S(1)} custom-call(bf16[384,128]{1,0:T(8,128)(2,1)S(1)} %collective-permute-done.12.q_ref, bf16[27,128,128]{2,1,0:T(8,128)(2,1)S(1)} %join.2.kt_ref, bf16[27,128,128]{2,1,0:T(8,128)(2,1)S(1)} %join.3.v_ref, f32[27,12,128]{2,1,0:T(8,128)S(1)} %mask_bias.1.refs_1_.bias_ref), custom_call_target="tpu_custom_call" | custom-call | flops 201326592 | bytes 393216 | tf_op jit(solution)/shard_map/attend_chunk/pallas_call | solution.py:29
  42.2 0.1 collective-permute-start.14
  42.3 0.0 collective-permute-done.11.q_ref
  42.3 1.7 %attend_chunk.5.refs_0_ = bf16[384,128]{1,0:T(8,128)(2,1)S(1)} custom-call(bf16[384,128]{1,0:T(8,128)(2,1)S(1)} %collective-permute-done.11.q_ref, bf16[27,128,128]{2,1,0:T(8,128)(2,1)S(1)} %join.2.kt_ref, bf16[27,128,128]{2,1,0:T(8,128)(2,1)S(1)} %join.3.v_ref, f32[27,12,128]{2,1,0:T(8,128)S(1)} %mask_bias.1.refs_1_.bias_ref, ...), custom_call_target="tpu_custom_call" | custom-call | flops 201326592 | bytes 393216 | tf_op jit(solution)/shard_map/attend_chunk/pallas_call | solution.py:29
  44.0 1.0 %collective-permute-start.13 = (bf16[384,128]{1,0:T(8,128)(2,1)S(1)}, bf16[384,128]{1,0:T(8,128)(2,1)S(1)}, u32[]{:S(2)}, u32[]{:S(2)}) collective-permute-start(bf16[384,128]{1,0:T(8,128)(2,1)S(1)} %attend_chunk.5.refs_0_), channel_id=1, source_target_pairs={{0,3},{1,0},{2,1},{3,2},{4,7},{5,4},{6,5},{7,6},{8,11},{9,8},{10,9... | collective-permute-start | bytes 294920 | tf_op jit(solution)/shard_map/ppermute | solution.py:238
  45.0 1.7 %attend_chunk.6.refs_0_ = bf16[384,128]{1,0:T(8,128)(2,1)S(1)} custom-call(bf16[384,128]{1,0:T(8,128)(2,1)S(1)} %collective-permute-done.10.q_ref, bf16[27,128,128]{2,1,0:T(8,128)(2,1)S(1)} %join.2.kt_ref, bf16[27,128,128]{2,1,0:T(8,128)(2,1)S(1)} %join.3.v_ref, f32[27,12,128]{2,1,0:T(8,128)S(1)} %mask_bias.1.refs_1_.bias_ref, ...), custom_call_target="tpu_custom_call" | custom-call | flops 201326592 | bytes 393216 | tf_op jit(solution)/shard_map/attend_chunk/pallas_call | solution.py:29
  46.7 1.1 %collective-permute-start.15 = (bf16[384,128]{1,0:T(8,128)(2,1)S(1)}, bf16[384,128]{1,0:T(8,128)(2,1)S(1)}, u32[]{:S(2)}, u32[]{:S(2)}) collective-permute-start(bf16[384,128]{1,0:T(8,128)(2,1)S(1)} %attend_chunk.6.refs_0_), channel_id=1, source_target_pairs={{0,1},{1,2},{2,3},{3,0},{4,5},{5,6},{6,7},{7,4},{8,9},{9,10},{10,1... | collective-permute-start | bytes 294920 | tf_op jit(solution)/shard_map/ppermute | solution.py:238
  47.9 1.7 %attend_chunk.7.refs_0_ = bf16[384,128]{1,0:T(8,128)(2,1)S(1)} custom-call(bf16[384,128]{1,0:T(8,128)(2,1)S(1)} %load_q.4.q_ref, bf16[27,128,128]{2,1,0:T(8,128)(2,1)S(1)} %join.2.kt_ref, bf16[27,128,128]{2,1,0:T(8,128)(2,1)S(1)} %join.3.v_ref, f32[27,12,128]{2,1,0:T(8,128)S(1)} %mask_bias.1.refs_1_.bias_ref, bf16[384,128]{1,0:T(8,128)(2,1)S(1)} %attend_chunk.6.refs_0_), custom_call_target="tpu_custom_call" | custom-call | flops 8388608 | bytes 16384 | tf_op jit(solution)/shard_map/attend_chunk/pallas_call | solution.py:29
  49.7 0.2 collective-permute-done.13.array_ref
  49.9 3.3 %collective-permute-done.15.array_ref = bf16[384,128]{1,0:T(8,128)(2,1)S(1)} collective-permute-done((bf16[384,128]{1,0:T(8,128)(2,1)S(1)}, bf16[384,128]{1,0:T(8,128)(2,1)S(1)}, u32[]{:S(2)}, u32[]{:S(2)}) %collective-permute-start.15) | collective-permute-done | bytes 98336 | tf_op jit(solution)/shard_map/ppermute | solution.py:238
  53.2 0.9 %spread.1 = bf16[384,512]{1,0:T(8,128)(2,1)} custom-call(bf16[384,128]{1,0:T(8,128)(2,1)S(1)} %attend_chunk.7.refs_0_, bf16[384,128]{1,0:T(8,128)(2,1)S(1)} %landed.4.refs_0_.refs_1_, bf16[384,128]{1,0:T(8,128)(2,1)S(1)} %landed.3.refs_0_.refs_2_, bf16[384,128]{1,0:T(8,128)(2,1)S(1)} %landed.5.refs_3_), custom_call_target="tpu_custom_call" | custom-call | tf_op jit(solution)/shard_map/spread/pallas_call | solution.py:29
  (26 shorter events, 0.4 us)
Async XLA Ops:
  0.0 1.0 %copy-start.2 = (bf16[384,512]{1,0:T(8,128)(2,1)S(1)}, bf16[384,512]{1,0:T(8,128)(2,1)}, u32[]{:S(2)}) copy-start(bf16[384,512]{1,0:T(8,128)(2,1)} %array_ref.15) | copy-start | bytes 1179652
  1.0 6.9 %collective-permute-start.4 = (bf16[3,128,128]{2,1,0:T(8,128)(2,1)S(1)}, bf16[3,128,128]{2,1,0:T(8,128)(2,1)S(1)}, u32[]{:S(2)}, u32[]{:S(2)}) collective-permute-start(bf16[3,128,128]{2,1,0:T(8,128)(2,1)S(1)} %load_v.6), channel_id=1, source_target_pairs={{0,3},{1,0},{2,1},{3,2},{4,7},{5,4},{6,5},{7,6},{8,11},{9,8},{10,9... | collective-permute-start | bytes 294920 | tf_op jit(solution)/shard_map/ppermute | solution.py:238
  4.7 3.2 %copy-start = (bf16[384,512]{1,0:T(8,128)(2,1)S(1)}, bf16[384,512]{1,0:T(8,128)(2,1)}, u32[]{:S(2)}) copy-start(bf16[384,512]{1,0:T(8,128)(2,1)} %array_ref.14) | copy-start | bytes 1179652
  4.7 7.7 %collective-permute-start = (bf16[3,128,128]{2,1,0:T(8,128)(2,1)S(1)}, bf16[3,128,128]{2,1,0:T(8,128)(2,1)S(1)}, u32[]{:S(2)}, u32[]{:S(2)}) collective-permute-start(bf16[3,128,128]{2,1,0:T(8,128)(2,1)S(1)} %load_v.4), channel_id=1, source_target_pairs={{0,1},{1,2},{2,3},{3,0},{4,5},{5,6},{6,7},{7,4},{8,9},{9,10},{10,1... | collective-permute-start | bytes 294920 | tf_op jit(solution)/shard_map/ppermute | solution.py:238
  4.8 1.1 %copy-start.5 = (s32[12]{0:T(128)S(1)}, s32[12]{0:T(128)}, u32[]{:S(2)}) copy-start(s32[12]{0:T(128)} %param.9) | copy-start | bytes 148
  4.8 1.1 %copy-start.4 = (s32[12,16]{1,0:T(8,128)S(1)}, s32[12,16]{1,0:T(8,128)}, u32[]{:S(2)}) copy-start(s32[12,16]{1,0:T(8,128)} %lists_ref.1) | copy-start | bytes 2308
  4.8 12.4 %collective-permute-start.2 = (bf16[3,128,128]{2,1,0:T(8,128)(2,1)S(1)}, bf16[3,128,128]{2,1,0:T(8,128)(2,1)S(1)}, u32[]{:S(2)}, u32[]{:S(2)}) collective-permute-start(bf16[3,128,128]{2,1,0:T(8,128)(2,1)S(1)} %load_v.5), channel_id=1, source_target_pairs={{0,2},{1,3},{2,0},{3,1},{4,6},{5,7},{6,4},{7,5},{8,10},{9,11},{10,... | collective-permute-start | bytes 294920 | tf_op jit(solution)/shard_map/ppermute | solution.py:238
  8.0 15.3 %collective-permute-start.5 = (bf16[3,128,128]{2,1,0:T(8,128)(2,1)S(1)}, bf16[3,128,128]{2,1,0:T(8,128)(2,1)S(1)}, u32[]{:S(2)}, u32[]{:S(2)}) collective-permute-start(bf16[3,128,128]{2,1,0:T(8,128)(2,1)S(1)} %load_k.7), channel_id=1, source_target_pairs={{0,3},{1,0},{2,1},{3,2},{4,7},{5,4},{6,5},{7,6},{8,11},{9,8},{10,9... | collective-permute-start | bytes 294920 | tf_op jit(solution)/shard_map/ppermute | solution.py:238
  12.5 5.0 %copy-start.3 = (bf16[384,512]{1,0:T(8,128)(2,1)S(1)}, bf16[384,512]{1,0:T(8,128)(2,1)}, u32[]{:S(2)}) copy-start(bf16[384,512]{1,0:T(8,128)(2,1)} %array_ref.15) | copy-start | bytes 1179652
  12.5 10.8 %collective-permute-start.1 = (bf16[3,128,128]{2,1,0:T(8,128)(2,1)S(1)}, bf16[3,128,128]{2,1,0:T(8,128)(2,1)S(1)}, u32[]{:S(2)}, u32[]{:S(2)}) collective-permute-start(bf16[3,128,128]{2,1,0:T(8,128)(2,1)S(1)} %load_k.5), channel_id=1, source_target_pairs={{0,1},{1,2},{2,3},{3,0},{4,5},{5,6},{6,7},{7,4},{8,9},{9,10},{10,1... | collective-permute-start | bytes 294920 | tf_op jit(solution)/shard_map/ppermute | solution.py:238
  17.4 6.5 %collective-permute-start.3 = (bf16[3,128,128]{2,1,0:T(8,128)(2,1)S(1)}, bf16[3,128,128]{2,1,0:T(8,128)(2,1)S(1)}, u32[]{:S(2)}, u32[]{:S(2)}) collective-permute-start(bf16[3,128,128]{2,1,0:T(8,128)(2,1)S(1)} %load_k.6), channel_id=1, source_target_pairs={{0,2},{1,3},{2,0},{3,1},{4,6},{5,7},{6,4},{7,5},{8,10},{9,11},{10,... | collective-permute-start | bytes 294920 | tf_op jit(solution)/shard_map/ppermute | solution.py:238
  17.6 15.1 %collective-permute-start.8 = (bf16[8,128,128]{2,1,0:T(8,128)(2,1)S(1)}, bf16[8,128,128]{2,1,0:T(8,128)(2,1)S(1)}, u32[]{:S(2)}, u32[]{:S(2)}) collective-permute-start(bf16[8,128,128]{2,1,0:T(8,128)(2,1)S(1)} %slice.18), channel_id=1, source_target_pairs={{0,4},{4,8},{8,12},{1,5},{5,9},{9,13},{2,6},{6,10},{10,14},{3,7},{... | collective-permute-start | bytes 786440 | tf_op jit(solution)/shard_map/ppermute | solution.py:116
  19.5 12.6 %collective-permute-start.9 = (bf16[7,128,128]{2,1,0:T(8,128)(2,1)S(1)}, bf16[7,128,128]{2,1,0:T(8,128)(2,1)S(1)}, u32[]{:S(2)}, u32[]{:S(2)}) collective-permute-start(bf16[7,128,128]{2,1,0:T(8,128)(2,1)S(1)} %slice.19), channel_id=1, source_target_pairs={{4,0},{8,4},{12,8},{5,1},{9,5},{13,9},{6,2},{10,6},{14,10},{7,3},{... | collective-permute-start | bytes 688136 | tf_op jit(solution)/shard_map/ppermute | solution.py:117
  23.9 5.8 %copy-start.1 = (bf16[384,512]{1,0:T(8,128)(2,1)S(1)}, bf16[384,512]{1,0:T(8,128)(2,1)}, u32[]{:S(2)}) copy-start(bf16[384,512]{1,0:T(8,128)(2,1)} %q_ref.7) | copy-start | bytes 1179652
  23.9 12.3 %collective-permute-start.6 = (bf16[8,128,128]{2,1,0:T(8,128)(2,1)S(1)}, bf16[8,128,128]{2,1,0:T(8,128)(2,1)S(1)}, u32[]{:S(2)}, u32[]{:S(2)}) collective-permute-start(bf16[8,128,128]{2,1,0:T(8,128)(2,1)S(1)} %slice.16), channel_id=1, source_target_pairs={{0,4},{4,8},{8,12},{1,5},{5,9},{9,13},{2,6},{6,10},{10,14},{3,7},{... | collective-permute-start | bytes 786440 | tf_op jit(solution)/shard_map/ppermute | solution.py:116
  26.0 10.2 %collective-permute-start.7 = (bf16[7,128,128]{2,1,0:T(8,128)(2,1)S(1)}, bf16[7,128,128]{2,1,0:T(8,128)(2,1)S(1)}, u32[]{:S(2)}, u32[]{:S(2)}) collective-permute-start(bf16[7,128,128]{2,1,0:T(8,128)(2,1)S(1)} %slice.17), channel_id=1, source_target_pairs={{4,0},{8,4},{12,8},{5,1},{9,5},{13,9},{6,2},{10,6},{14,10},{7,3},{... | collective-permute-start | bytes 688136 | tf_op jit(solution)/shard_map/ppermute | solution.py:117
  29.7 10.7 %collective-permute-start.12 = (bf16[384,128]{1,0:T(8,128)(2,1)S(1)}, bf16[384,128]{1,0:T(8,128)(2,1)S(1)}, u32[]{:S(2)}, u32[]{:S(2)}) collective-permute-start(bf16[384,128]{1,0:T(8,128)(2,1)S(1)} %load_q.7), channel_id=1, source_target_pairs={{0,2},{1,3},{2,0},{3,1},{4,6},{5,7},{6,4},{7,5},{8,10},{9,11},{10,... | collective-permute-start | bytes 294920 | tf_op jit(solution)/shard_map/ppermute | solution.py:238
  32.2 10.1 %collective-permute-start.11 = (bf16[384,128]{1,0:T(8,128)(2,1)S(1)}, bf16[384,128]{1,0:T(8,128)(2,1)S(1)}, u32[]{:S(2)}, u32[]{:S(2)}) collective-permute-start(bf16[384,128]{1,0:T(8,128)(2,1)S(1)} %load_q.6), channel_id=1, source_target_pairs={{0,1},{1,2},{2,3},{3,0},{4,5},{5,6},{6,7},{7,4},{8,9},{9,10},{10,1... | collective-permute-start | bytes 294920 | tf_op jit(solution)/shard_map/ppermute | solution.py:238
  32.7 12.3 %collective-permute-start.10 = (bf16[384,128]{1,0:T(8,128)(2,1)S(1)}, bf16[384,128]{1,0:T(8,128)(2,1)S(1)}, u32[]{:S(2)}, u32[]{:S(2)}) collective-permute-start(bf16[384,128]{1,0:T(8,128)(2,1)S(1)} %load_q.5), channel_id=1, source_target_pairs={{0,3},{1,0},{2,1},{3,2},{4,7},{5,4},{6,5},{7,6},{8,11},{9,8},{10,9... | collective-permute-start | bytes 294920 | tf_op jit(solution)/shard_map/ppermute | solution.py:238
  42.2 7.5 %collective-permute-start.14 = (bf16[384,128]{1,0:T(8,128)(2,1)S(1)}, bf16[384,128]{1,0:T(8,128)(2,1)S(1)}, u32[]{:S(2)}, u32[]{:S(2)}) collective-permute-start(bf16[384,128]{1,0:T(8,128)(2,1)S(1)} %attend_chunk.4.refs_0_), channel_id=1, source_target_pairs={{0,2},{1,3},{2,0},{3,1},{4,6},{5,7},{6,4},{7,5},{8,10},{9,11},{10,... | collective-permute-start | bytes 294920 | tf_op jit(solution)/shard_map/ppermute | solution.py:238
  44.0 5.9 %collective-permute-start.13 = (bf16[384,128]{1,0:T(8,128)(2,1)S(1)}, bf16[384,128]{1,0:T(8,128)(2,1)S(1)}, u32[]{:S(2)}, u32[]{:S(2)}) collective-permute-start(bf16[384,128]{1,0:T(8,128)(2,1)S(1)} %attend_chunk.5.refs_0_), channel_id=1, source_target_pairs={{0,3},{1,0},{2,1},{3,2},{4,7},{5,4},{6,5},{7,6},{8,11},{9,8},{10,9... | collective-permute-start | bytes 294920 | tf_op jit(solution)/shard_map/ppermute | solution.py:238
  46.7 6.5 %collective-permute-start.15 = (bf16[384,128]{1,0:T(8,128)(2,1)S(1)}, bf16[384,128]{1,0:T(8,128)(2,1)S(1)}, u32[]{:S(2)}, u32[]{:S(2)}) collective-permute-start(bf16[384,128]{1,0:T(8,128)(2,1)S(1)} %attend_chunk.6.refs_0_), channel_id=1, source_target_pairs={{0,1},{1,2},{2,3},{3,0},{4,5},{5,6},{6,7},{7,4},{8,9},{9,10},{10,1... | collective-permute-start | bytes 294920 | tf_op jit(solution)/shard_map/ppermute | solution.py:238

commit v8 on v7

--- a/solution.py
+++ b/solution.py
@@ -172,47 +172,41 @@
     return call(functools.partial(unpack_kernel, heads), "unpack", (back,), [VMEM], (rows, columns))
 
 
-def load_tiles_kernel(heads, shift, turn, array_ref, *refs):
+def load_kernel(heads, shift, k_ref, v_ref, q_ref, out_ref):
     columns = column_of(lax.rem(lax.axis_index("head") + shift, heads))
     for tile in range(BLOCK):
-        part = array_ref[rows_of(tile), columns]
-        refs[-1][tile] = part.T if turn else part
-
-
-def load_q_kernel(heads, shift, q_ref, *refs):
-    refs[-1][...] = q_ref[:, column_of(lax.rem(lax.axis_index("head") + shift, heads))]
+        out_ref[0, tile] = k_ref[rows_of(tile), columns].T
+        out_ref[1, tile] = v_ref[rows_of(tile), columns]
+        out_ref[2, tile] = q_ref[rows_of(tile), columns]
 
 
 def gather_kernel(*refs):
-    heads, out_ref = len(refs) - 1, refs[-1]
+    *parts, kv_out, q_out = refs
     me = lax.axis_index("head")
-    for shift in range(heads):
-        out_ref[pl.ds(lax.rem(me + heads - shift, heads) * BLOCK, BLOCK)] = refs[shift][...]
+    for shift, part in enumerate(parts):
+        place = pl.ds(lax.rem(me + len(parts) - shift, len(parts)) * BLOCK, BLOCK)
+        kv_out[:, place] = part[:2]
+        for tile in range(BLOCK):
+            q_out[shift, rows_of(tile), :] = part[2, tile]
 
 
 def join_kernel(*refs):
     at = 0
     for ref in refs[:-1]:
-        refs[-1][at : at + ref.shape[0]] = ref[...]
-        at += ref.shape[0]
-
-
-def with_halo(parts):
-    heads = len(parts)
-    tiles = heads * BLOCK
-    own = call(gather_kernel, "gather", parts, [VMEM] * heads, (tiles, TILE, HDIM))
-    low, high = halo(own, 0, 1)
-    return call(join_kernel, "join", (low, own, high), [VMEM] * 3, (tiles + LIST - 1, TILE, HDIM))
+        refs[-1][:, at : at + ref.shape[1]] = ref[...]
+        at += ref.shape[1]
 
 
 def pass_kernel(array_ref, *refs):
     refs[-1][...] = array_ref[...]
 
 
-def attend_chunk_kernel(shift, heads, q_ref, kt_ref, v_ref, bias_ref, *refs):
+def attend_chunk_kernel(shift, heads, q_ref, kv_ref, bias_ref, *refs):
     out_ref, *scratch = refs[-3:]
     source = lax.rem(lax.axis_index("head") + heads - shift, heads)
-    attend_block(source * BLOCK, q_ref, kt_ref, v_ref, bias_ref, out_ref, *scratch)
+    attend_block(
+        source * BLOCK, q_ref.at[shift], kv_ref.at[0], kv_ref.at[1], bias_ref, out_ref, *scratch
+    )
 
 
 def spread_kernel(heads, *refs):
@@ -225,37 +219,33 @@
 def by_shifts(queries, keys, values, bias):
     heads = lax.axis_size("head")
     order = sorted(range(1, heads), key=lambda shift: -min(shift, heads - shift))
-    chunk, tiles = (queries.shape[0], HDIM), (BLOCK, TILE, HDIM)
+    chunk, tiles = (queries.shape[0], HDIM), heads * BLOCK
 
     def kernel_of(kernel, *settings):
         return functools.partial(kernel, *settings)
 
-    def call_after(kernel, name, operands, after, shape):
-        operands = (*operands, *after)
-        return call(kernel, name, operands, [VMEM] * len(operands), shape)
-
     def send(array, shift):
         return lax.ppermute(array, "head", [(i, (i + shift) % heads) for i in range(heads)])
 
-    v_parts, k_parts, q_parts = [None] * heads, [None] * heads, [None] * heads
+    parts = [None] * heads
     for shift in order + [0]:
-        part = call_after(kernel_of(load_tiles_kernel, heads, shift, False), "load_v", (values,), (), tiles)
-        v_parts[shift] = send(part, shift) if shift else part
-    for shift in order + [0]:
-        after = [v_parts[shift]] if shift else []
-        if shift == order[-1]:
-            after.append(bias)
-        part = call_after(kernel_of(load_tiles_kernel, heads, shift, True), "load_k", (keys,), after, tiles)
-        k_parts[shift] = send(part, shift) if shift else part
-    for shift in order + [0]:
-        after = (k_parts[shift],) if shift else ()
-        part = call_after(kernel_of(load_q_kernel, heads, shift), "load_q", (queries,), after, chunk)
-        q_parts[shift] = send(part, shift) if shift else part
-    all_values, all_keys = with_halo(v_parts), with_halo(k_parts)
+        part = call(
+            kernel_of(load_kernel, heads, shift),
+            "load",
+            (keys, values, queries),
+            [VMEM] * 3,
+            (3, BLOCK, TILE, HDIM),
+        )
+        parts[shift] = send(part, shift) if shift else part
+    own, local_q = call(
+        gather_kernel, "gather", parts, [VMEM] * heads, [(2, tiles, TILE, HDIM), (heads, *chunk)]
+    )
+    low, high = halo(own, 1, 1)
+    padded = call(join_kernel, "join", (low, own, high), [VMEM] * 3, (2, tiles + LIST - 1, TILE, HDIM))
     outs = [None] * heads
     after = ()
     for shift in order + [0]:
-        operands = (q_parts[shift], all_keys, all_values, bias, *after)
+        operands = (local_q, padded, bias, *after)
         outs[shift] = call(
             kernel_of(attend_chunk_kernel, shift, heads),
             "attend_chunk",

time: 54.3 us -> 61.8 us (1.14)
  the two profiles are of different devices: /device:TPU:2 before, /device:TPU:1 now
where the time goes in v8:
time: 61.8 us; the launch traced here: 61.6 us
  waiting for transfers between devices  29 us (47%)
  starting transfers between devices  20.2 us (33%)
  Pallas kernels  9.03 us (15%)
  local copies, waits for them, and re-layouts  3.16 us (5%)
    ppermute x6, waiting for transfers between devices, send(): lax.ppermute(array, 'head', [(i, (i + shift) % heads) for i in range(head...  21.8 us
    ppermute x6, starting transfers between devices, send(): lax.ppermute(array, 'head', [(i, (i + shift) % heads) for i in range(head...  14.7 us
    pallas_call x15, Pallas kernels, call(): pl.pallas_call(kernel, out_shape=out_shape, in_specs=in_specs, out_specs=...  9.03 us
    ppermute x1, waiting for transfers between devices, halo(): high = lax.ppermute(head, 'ctx', [(i + 1, i) for i in range(ctx - 1)])  7.18 us
    ppermute x1, starting transfers between devices, halo(): low = lax.ppermute(tail, 'ctx', [(i, i + 1) for i in range(ctx - 1)])  3.59 us
    unnamed x10, local copies, waits for them, and re-layouts  3 us
    ppermute x1, starting transfers between devices, halo(): high = lax.ppermute(head, 'ctx', [(i + 1, i) for i in range(ctx - 1)])  1.92 us
  transfers between devices with their start and end apart: 8, of which 4 were waited for; matrix products, arithmetic and copies ran while one was open for 0% of the time, Pallas kernels for 10%

profile of v8, /device:TPU:1, one launch (start us, length us, event | category | flops | bytes accessed | tf_op | source)
XLA Modules:
  0.0 61.6 jit_solution(5081531861384374413)
XLA Ops:
  0.0 0.0 copy-start
  0.0 1.0 %copy-done = bf16[384,512]{1,0:T(8,128)(2,1)S(1)} copy-done((bf16[384,512]{1,0:T(8,128)(2,1)S(1)}, bf16[384,512]{1,0:T(8,128)(2,1)}, u32[]{:S(2)}) %copy-start) | copy-done | bytes 393240
  1.0 0.0 copy-start.1
  1.0 1.0 %copy-done.1 = bf16[384,512]{1,0:T(8,128)(2,1)S(1)} copy-done((bf16[384,512]{1,0:T(8,128)(2,1)S(1)}, bf16[384,512]{1,0:T(8,128)(2,1)}, u32[]{:S(2)}) %copy-start.1) | copy-done | bytes 393240
  2.0 0.0 copy-start.2
  2.0 1.0 %copy-done.2 = bf16[384,512]{1,0:T(8,128)(2,1)S(1)} copy-done((bf16[384,512]{1,0:T(8,128)(2,1)S(1)}, bf16[384,512]{1,0:T(8,128)(2,1)}, u32[]{:S(2)}) %copy-start.2) | copy-done | bytes 393240
  3.0 0.1 load.5
  3.1 2.2 %collective-permute-start = (bf16[3,3,128,128]{3,2,1,0:T(8,128)(2,1)S(1)}, bf16[3,3,128,128]{3,2,1,0:T(8,128)(2,1)S(1)}, u32[]{:S(2)}, u32[]{:S(2)}) collective-permute-start(bf16[3,3,128,128]{3,2,1,0:T(8,128)(2,1)S(1)} %load.5), channel_id=1, source_target_pairs={{0,1},{1,2},{2,3},{3,0},{4,5},{5,6},{6,7},{7,4},{8,9},{9,10},{10,1... | collective-permute-start | bytes 884744 | tf_op jit(solution)/shard_map/ppermute | solution.py:228
  5.3 0.1 load.6
  5.4 2.4 %collective-permute-start.1 = (bf16[3,3,128,128]{3,2,1,0:T(8,128)(2,1)S(1)}, bf16[3,3,128,128]{3,2,1,0:T(8,128)(2,1)S(1)}, u32[]{:S(2)}, u32[]{:S(2)}) collective-permute-start(bf16[3,3,128,128]{3,2,1,0:T(8,128)(2,1)S(1)} %load.6), channel_id=1, source_target_pairs={{0,2},{1,3},{2,0},{3,1},{4,6},{5,7},{6,4},{7,5},{8,10},{9,11},{10,... | collective-permute-start | bytes 884744 | tf_op jit(solution)/shard_map/ppermute | solution.py:228
  7.8 0.1 load.7
  7.9 1.1 %collective-permute-start.2 = (bf16[3,3,128,128]{3,2,1,0:T(8,128)(2,1)S(1)}, bf16[3,3,128,128]{3,2,1,0:T(8,128)(2,1)S(1)}, u32[]{:S(2)}, u32[]{:S(2)}) collective-permute-start(bf16[3,3,128,128]{3,2,1,0:T(8,128)(2,1)S(1)} %load.7), channel_id=1, source_target_pairs={{0,3},{1,0},{2,1},{3,2},{4,7},{5,4},{6,5},{7,6},{8,11},{9,8},{10,9... | collective-permute-start | bytes 884744 | tf_op jit(solution)/shard_map/ppermute | solution.py:228
  9.0 0.1 load.4.refs_0_
  9.1 0.0 copy-start.4
  9.2 0.0 copy-start.3
  9.2 5.0 %collective-permute-done.refs_1_ = bf16[3,3,128,128]{3,2,1,0:T(8,128)(2,1)S(1)} collective-permute-done((bf16[3,3,128,128]{3,2,1,0:T(8,128)(2,1)S(1)}, bf16[3,3,128,128]{3,2,1,0:T(8,128)(2,1)S(1)}, u32[]{:S(2)}, u32[]{:S(2)}) %collective-permute-start) | collective-permute-done | bytes 294944 | tf_op jit(solution)/shard_map/ppermute | solution.py:228
  14.1 13.3 %collective-permute-done.1.refs_2_ = bf16[3,3,128,128]{3,2,1,0:T(8,128)(2,1)S(1)} collective-permute-done((bf16[3,3,128,128]{3,2,1,0:T(8,128)(2,1)S(1)}, bf16[3,3,128,128]{3,2,1,0:T(8,128)(2,1)S(1)}, u32[]{:S(2)}, u32[]{:S(2)}) %collective-permute-start.1) | collective-permute-done | bytes 294944 | tf_op jit(solution)/shard_map/ppermute | solution.py:228
  27.5 0.0 collective-permute-done.2.refs_3_
  27.5 0.1 gather.1
  27.6 3.6 %collective-permute-start.3 = (bf16[2,8,128,128]{3,2,1,0:T(8,128)(2,1)S(1)}, bf16[2,8,128,128]{3,2,1,0:T(8,128)(2,1)S(1)}, u32[]{:S(2)}, u32[]{:S(2)}) collective-permute-start(bf16[2,8,128,128]{3,2,1,0:T(8,128)(2,1)S(1)} %slice.6), channel_id=1, source_target_pairs={{0,4},{4,8},{8,12},{1,5},{5,9},{9,13},{2,6},{6,10},{10,14},{3,7},{... | collective-permute-start | bytes 1572872 | tf_op jit(solution)/shard_map/ppermute | solution.py:116
  31.2 1.9 %collective-permute-start.4 = (bf16[2,7,128,128]{3,2,1,0:T(8,128)(2,1)S(1)}, bf16[2,7,128,128]{3,2,1,0:T(8,128)(2,1)S(1)}, u32[]{:S(2)}, u32[]{:S(2)}) collective-permute-start(bf16[2,7,128,128]{3,2,1,0:T(8,128)(2,1)S(1)} %slice.7), channel_id=1, source_target_pairs={{4,0},{8,4},{12,8},{5,1},{9,5},{13,9},{6,2},{10,6},{14,10},{7,3},{... | collective-permute-start | bytes 1376264 | tf_op jit(solution)/shard_map/ppermute | solution.py:117
  33.2 0.0 copy-done.4
  33.2 0.1 copy.6.counts_ref
  33.3 0.0 copy-done.3
  33.3 0.6 mask_bias.1.bias_ref
  33.9 7.2 %collective-permute-done.4.refs_2_ = bf16[2,7,128,128]{3,2,1,0:T(8,128)(2,1)S(1)} collective-permute-done((bf16[2,7,128,128]{3,2,1,0:T(8,128)(2,1)S(1)}, bf16[2,7,128,128]{3,2,1,0:T(8,128)(2,1)S(1)}, u32[]{:S(2)}, u32[]{:S(2)}) %collective-permute-start.4) | collective-permute-done | bytes 458784 | tf_op jit(solution)/shard_map/ppermute | solution.py:117
  41.0 0.0 collective-permute-done.3.refs_0_
  41.0 0.1 join.1.kv_ref
  41.2 1.7 %attend_chunk.4.refs_0_ = bf16[384,128]{1,0:T(8,128)(2,1)S(1)} custom-call(bf16[4,384,128]{2,1,0:T(8,128)(2,1)S(1)} %get-tuple-element.7.q_ref, bf16[2,27,128,128]{3,2,1,0:T(8,128)(2,1)S(1)} %join.1.kv_ref, f32[27,12,128]{2,1,0:T(8,128)S(1)} %mask_bias.1.bias_ref), custom_call_target="tpu_custom_call" | custom-call | flops 201326592 | bytes 393216 | tf_op jit(solution)/shard_map/attend_chunk/pallas_call | solution.py:29
  42.9 5.8 %collective-permute-start.6 = (bf16[384,128]{1,0:T(8,128)(2,1)S(1)}, bf16[384,128]{1,0:T(8,128)(2,1)S(1)}, u32[]{:S(2)}, u32[]{:S(2)}) collective-permute-start(bf16[384,128]{1,0:T(8,128)(2,1)S(1)} %attend_chunk.4.refs_0_), channel_id=1, source_target_pairs={{0,2},{1,3},{2,0},{3,1},{4,6},{5,7},{6,4},{7,5},{8,10},{9,11},{10,... | collective-permute-start | bytes 294920 | tf_op jit(solution)/shard_map/ppermute | solution.py:228
  48.7 1.7 %attend_chunk.5.refs_0_ = bf16[384,128]{1,0:T(8,128)(2,1)S(1)} custom-call(bf16[4,384,128]{2,1,0:T(8,128)(2,1)S(1)} %get-tuple-element.7.q_ref, bf16[2,27,128,128]{3,2,1,0:T(8,128)(2,1)S(1)} %join.1.kv_ref, f32[27,12,128]{2,1,0:T(8,128)S(1)} %mask_bias.1.bias_ref, bf16[384,128]{1,0:T(8,128)(2,1)S(1)} %attend_chunk.4.refs_0_), custom_call_target="tpu_custom_call" | custom-call | flops 201326592 | bytes 393216 | tf_op jit(solution)/shard_map/attend_chunk/pallas_call | solution.py:29
  50.5 3.2 %collective-permute-start.5 = (bf16[384,128]{1,0:T(8,128)(2,1)S(1)}, bf16[384,128]{1,0:T(8,128)(2,1)S(1)}, u32[]{:S(2)}, u32[]{:S(2)}) collective-permute-start(bf16[384,128]{1,0:T(8,128)(2,1)S(1)} %attend_chunk.5.refs_0_), channel_id=1, source_target_pairs={{0,3},{1,0},{2,1},{3,2},{4,7},{5,4},{6,5},{7,6},{8,11},{9,8},{10,9... | collective-permute-start | bytes 294920 | tf_op jit(solution)/shard_map/ppermute | solution.py:228
  53.6 1.7 %attend_chunk.6.refs_0_ = bf16[384,128]{1,0:T(8,128)(2,1)S(1)} custom-call(bf16[4,384,128]{2,1,0:T(8,128)(2,1)S(1)} %get-tuple-element.7.q_ref, bf16[2,27,128,128]{3,2,1,0:T(8,128)(2,1)S(1)} %join.1.kv_ref, f32[27,12,128]{2,1,0:T(8,128)S(1)} %mask_bias.1.bias_ref, bf16[384,128]{1,0:T(8,128)(2,1)S(1)} %attend_chunk.5.refs_0_), custom_call_target="tpu_custom_call" | custom-call | flops 201326592 | bytes 393216 | tf_op jit(solution)/shard_map/attend_chunk/pallas_call | solution.py:29
  55.4 0.1 collective-permute-start.7
  55.4 1.7 %attend_chunk.7.refs_0_ = bf16[384,128]{1,0:T(8,128)(2,1)S(1)} custom-call(bf16[4,384,128]{2,1,0:T(8,128)(2,1)S(1)} %get-tuple-element.7.q_ref, bf16[2,27,128,128]{3,2,1,0:T(8,128)(2,1)S(1)} %join.1.kv_ref, f32[27,12,128]{2,1,0:T(8,128)S(1)} %mask_bias.1.bias_ref, bf16[384,128]{1,0:T(8,128)(2,1)S(1)} %attend_chunk.6.refs_0_), custom_call_target="tpu_custom_call" | custom-call | flops 8388608 | bytes 16384 | tf_op jit(solution)/shard_map/attend_chunk/pallas_call | solution.py:29
  57.2 0.0 collective-permute-done.6.array_ref
  57.2 0.0 collective-permute-done.5.array_ref
  57.2 3.5 %collective-permute-done.7.array_ref = bf16[384,128]{1,0:T(8,128)(2,1)S(1)} collective-permute-done((bf16[384,128]{1,0:T(8,128)(2,1)S(1)}, bf16[384,128]{1,0:T(8,128)(2,1)S(1)}, u32[]{:S(2)}, u32[]{:S(2)}) %collective-permute-start.7) | collective-permute-done | bytes 98336 | tf_op jit(solution)/shard_map/ppermute | solution.py:228
  60.7 0.9 %spread.1 = bf16[384,512]{1,0:T(8,128)(2,1)} custom-call(bf16[384,128]{1,0:T(8,128)(2,1)S(1)} %attend_chunk.7.refs_0_, bf16[384,128]{1,0:T(8,128)(2,1)S(1)} %landed.4.refs_0_.refs_1_, bf16[384,128]{1,0:T(8,128)(2,1)S(1)} %landed.3.refs_0_.refs_2_, bf16[384,128]{1,0:T(8,128)(2,1)S(1)} %landed.5.refs_3_), custom_call_target="tpu_custom_call" | custom-call | tf_op jit(solution)/shard_map/spread/pallas_call | solution.py:29
  (5 shorter events, 0.1 us)
Async XLA Ops:
  0.0 1.0 %copy-start = (bf16[384,512]{1,0:T(8,128)(2,1)S(1)}, bf16[384,512]{1,0:T(8,128)(2,1)}, u32[]{:S(2)}) copy-start(bf16[384,512]{1,0:T(8,128)(2,1)} %k_ref.7) | copy-start | bytes 1179652
  1.0 1.0 %copy-start.1 = (bf16[384,512]{1,0:T(8,128)(2,1)S(1)}, bf16[384,512]{1,0:T(8,128)(2,1)}, u32[]{:S(2)}) copy-start(bf16[384,512]{1,0:T(8,128)(2,1)} %v_ref.7) | copy-start | bytes 1179652
  2.0 1.0 %copy-start.2 = (bf16[384,512]{1,0:T(8,128)(2,1)S(1)}, bf16[384,512]{1,0:T(8,128)(2,1)}, u32[]{:S(2)}) copy-start(bf16[384,512]{1,0:T(8,128)(2,1)} %q_ref.7) | copy-start | bytes 1179652
  3.1 11.0 %collective-permute-start = (bf16[3,3,128,128]{3,2,1,0:T(8,128)(2,1)S(1)}, bf16[3,3,128,128]{3,2,1,0:T(8,128)(2,1)S(1)}, u32[]{:S(2)}, u32[]{:S(2)}) collective-permute-start(bf16[3,3,128,128]{3,2,1,0:T(8,128)(2,1)S(1)} %load.5), channel_id=1, source_target_pairs={{0,1},{1,2},{2,3},{3,0},{4,5},{5,6},{6,7},{7,4},{8,9},{9,10},{10,1... | collective-permute-start | bytes 884744 | tf_op jit(solution)/shard_map/ppermute | solution.py:228
  5.4 22.1 %collective-permute-start.1 = (bf16[3,3,128,128]{3,2,1,0:T(8,128)(2,1)S(1)}, bf16[3,3,128,128]{3,2,1,0:T(8,128)(2,1)S(1)}, u32[]{:S(2)}, u32[]{:S(2)}) collective-permute-start(bf16[3,3,128,128]{3,2,1,0:T(8,128)(2,1)S(1)} %load.6), channel_id=1, source_target_pairs={{0,2},{1,3},{2,0},{3,1},{4,6},{5,7},{6,4},{7,5},{8,10},{9,11},{10,... | collective-permute-start | bytes 884744 | tf_op jit(solution)/shard_map/ppermute | solution.py:228
  7.9 19.6 %collective-permute-start.2 = (bf16[3,3,128,128]{3,2,1,0:T(8,128)(2,1)S(1)}, bf16[3,3,128,128]{3,2,1,0:T(8,128)(2,1)S(1)}, u32[]{:S(2)}, u32[]{:S(2)}) collective-permute-start(bf16[3,3,128,128]{3,2,1,0:T(8,128)(2,1)S(1)} %load.7), channel_id=1, source_target_pairs={{0,3},{1,0},{2,1},{3,2},{4,7},{5,4},{6,5},{7,6},{8,11},{9,8},{10,9... | collective-permute-start | bytes 884744 | tf_op jit(solution)/shard_map/ppermute | solution.py:228
  9.1 24.0 %copy-start.4 = (s32[12]{0:T(128)S(1)}, s32[12]{0:T(128)}, u32[]{:S(2)}) copy-start(s32[12]{0:T(128)} %param.9) | copy-start | bytes 148
  9.2 24.1 %copy-start.3 = (s32[12,16]{1,0:T(8,128)S(1)}, s32[12,16]{1,0:T(8,128)}, u32[]{:S(2)}) copy-start(s32[12,16]{1,0:T(8,128)} %lists_ref.1) | copy-start | bytes 2308
  27.6 13.4 %collective-permute-start.3 = (bf16[2,8,128,128]{3,2,1,0:T(8,128)(2,1)S(1)}, bf16[2,8,128,128]{3,2,1,0:T(8,128)(2,1)S(1)}, u32[]{:S(2)}, u32[]{:S(2)}) collective-permute-start(bf16[2,8,128,128]{3,2,1,0:T(8,128)(2,1)S(1)} %slice.6), channel_id=1, source_target_pairs={{0,4},{4,8},{8,12},{1,5},{5,9},{9,13},{2,6},{6,10},{10,14},{3,7},{... | collective-permute-start | bytes 1572872 | tf_op jit(solution)/shard_map/ppermute | solution.py:116
  31.2 9.8 %collective-permute-start.4 = (bf16[2,7,128,128]{3,2,1,0:T(8,128)(2,1)S(1)}, bf16[2,7,128,128]{3,2,1,0:T(8,128)(2,1)S(1)}, u32[]{:S(2)}, u32[]{:S(2)}) collective-permute-start(bf16[2,7,128,128]{3,2,1,0:T(8,128)(2,1)S(1)} %slice.7), channel_id=1, source_target_pairs={{4,0},{8,4},{12,8},{5,1},{9,5},{13,9},{6,2},{10,6},{14,10},{7,3},{... | collective-permute-start | bytes 1376264 | tf_op jit(solution)/shard_map/ppermute | solution.py:117
  42.9 14.3 %collective-permute-start.6 = (bf16[384,128]{1,0:T(8,128)(2,1)S(1)}, bf16[384,128]{1,0:T(8,128)(2,1)S(1)}, u32[]{:S(2)}, u32[]{:S(2)}) collective-permute-start(bf16[384,128]{1,0:T(8,128)(2,1)S(1)} %attend_chunk.4.refs_0_), channel_id=1, source_target_pairs={{0,2},{1,3},{2,0},{3,1},{4,6},{5,7},{6,4},{7,5},{8,10},{9,11},{10,... | collective-permute-start | bytes 294920 | tf_op jit(solution)/shard_map/ppermute | solution.py:228
  50.5 6.7 %collective-permute-start.5 = (bf16[384,128]{1,0:T(8,128)(2,1)S(1)}, bf16[384,128]{1,0:T(8,128)(2,1)S(1)}, u32[]{:S(2)}, u32[]{:S(2)}) collective-permute-start(bf16[384,128]{1,0:T(8,128)(2,1)S(1)} %attend_chunk.5.refs_0_), channel_id=1, source_target_pairs={{0,3},{1,0},{2,1},{3,2},{4,7},{5,4},{6,5},{7,6},{8,11},{9,8},{10,9... | collective-permute-start | bytes 294920 | tf_op jit(solution)/shard_map/ppermute | solution.py:228
  55.4 5.3 %collective-permute-start.7 = (bf16[384,128]{1,0:T(8,128)(2,1)S(1)}, bf16[384,128]{1,0:T(8,128)(2,1)S(1)}, u32[]{:S(2)}, u32[]{:S(2)}) collective-permute-start(bf16[384,128]{1,0:T(8,128)(2,1)S(1)} %attend_chunk.6.refs_0_), channel_id=1, source_target_pairs={{0,1},{1,2},{2,3},{3,0},{4,5},{5,6},{6,7},{7,4},{8,9},{9,10},{10,1... | collective-permute-start | bytes 294920 | tf_op jit(solution)/shard_map/ppermute | solution.py:228

commit v9 on v8

--- a/solution.py
+++ b/solution.py
@@ -172,108 +172,129 @@
     return call(functools.partial(unpack_kernel, heads), "unpack", (back,), [VMEM], (rows, columns))
 
 
-def load_kernel(heads, shift, k_ref, v_ref, q_ref, out_ref):
-    columns = column_of(lax.rem(lax.axis_index("head") + shift, heads))
+def load_kv_kernel(pair, k_ref, v_ref, *refs):
+    out_ref = refs[-1]
+    columns = column_of(lax.axis_index("head") ^ pair)
     for tile in range(BLOCK):
         out_ref[0, tile] = k_ref[rows_of(tile), columns].T
         out_ref[1, tile] = v_ref[rows_of(tile), columns]
-        out_ref[2, tile] = q_ref[rows_of(tile), columns]
+
+
+def load_q_kernel(pair, q_ref, *refs):
+    refs[-1][...] = q_ref[:, column_of(lax.axis_index("head") ^ pair)]
 
 
 def gather_kernel(*refs):
-    *parts, kv_out, q_out = refs
+    *parts, own_ref, odd_ref, even_ref = refs
     me = lax.axis_index("head")
-    for shift, part in enumerate(parts):
-        place = pl.ds(lax.rem(me + len(parts) - shift, len(parts)) * BLOCK, BLOCK)
-        kv_out[:, place] = part[:2]
-        for tile in range(BLOCK):
-            q_out[shift, rows_of(tile), :] = part[2, tile]
-
-
-def join_kernel(*refs):
-    at = 0
-    for ref in refs[:-1]:
-        refs[-1][:, at : at + ref.shape[1]] = ref[...]
-        at += ref.shape[1]
+    for pair, part in enumerate(parts):
+        own_ref[:, pl.ds((me ^ pair) * BLOCK, BLOCK)] = part[...]
+    last = own_ref.shape[1] - EDGE
+    odd = lax.rem(lax.axis_index("ctx"), 2)
+    odd_ref[...] = own_ref[:, pl.ds(odd * last, EDGE)]
+    even_ref[...] = own_ref[:, pl.ds((1 - odd) * last, EDGE)]
+
+
+def join_kernel(own_ref, first_ref, second_ref, out_ref):
+    odd = lax.rem(lax.axis_index("ctx"), 2)
+    tiles = own_ref.shape[1]
+    out_ref[:, EDGE : EDGE + tiles] = own_ref[...]
+
+    def around(low_ref, high_ref):
+        out_ref[:, :EDGE] = low_ref[...]
+        out_ref[:, EDGE + tiles :] = high_ref[:, : EDGE - 1]
+
+    @pl.when(odd == 1)
+    def _():
+        around(second_ref, first_ref)
+
+    @pl.when(odd == 0)
+    def _():
+        around(first_ref, second_ref)
 
 
 def pass_kernel(array_ref, *refs):
     refs[-1][...] = array_ref[...]
 
 
-def attend_chunk_kernel(shift, heads, q_ref, kv_ref, bias_ref, *refs):
+def attend_chunk_kernel(pair, q_ref, kv_ref, bias_ref, *refs):
     out_ref, *scratch = refs[-3:]
-    source = lax.rem(lax.axis_index("head") + heads - shift, heads)
-    attend_block(
-        source * BLOCK, q_ref.at[shift], kv_ref.at[0], kv_ref.at[1], bias_ref, out_ref, *scratch
-    )
-
-
-def spread_kernel(heads, *refs):
-    out_ref = refs[-1]
+    first = (lax.axis_index("head") ^ pair) * BLOCK
+    attend_block(first, q_ref, kv_ref.at[0], kv_ref.at[1], bias_ref, out_ref, *scratch)
+
+
+def spread_kernel(*refs):
+    *parts, out_ref = refs
     me = lax.axis_index("head")
-    for shift in range(heads):
-        out_ref[:, column_of(lax.rem(me + shift, heads))] = refs[shift][...]
-
-
-def by_shifts(queries, keys, values, bias):
-    heads = lax.axis_size("head")
-    order = sorted(range(1, heads), key=lambda shift: -min(shift, heads - shift))
+    for pair, part in enumerate(parts):
+        out_ref[:, column_of(me ^ pair)] = part[...]
+
+
+def in_pairs(queries, keys, values, bias):
+    heads, ctx = lax.axis_size("head"), lax.axis_size("ctx")
     chunk, tiles = (queries.shape[0], HDIM), heads * BLOCK
-
-    def kernel_of(kernel, *settings):
-        return functools.partial(kernel, *settings)
-
-    def send(array, shift):
-        return lax.ppermute(array, "head", [(i, (i + shift) % heads) for i in range(heads)])
-
-    parts = [None] * heads
-    for shift in order + [0]:
+    order = range(heads - 1, 0, -1)
+
+    def exchange(array, pair):
+        return lax.ppermute(array, "head", [(i, i ^ pair) for i in range(heads)])
+
+    def exchange_ctx(array, first):
+        lower = range(first, ctx - 1, 2)
+        return lax.ppermute(array, "ctx", [(i, i + 1) for i in lower] + [(i + 1, i) for i in lower])
+
+    kv_parts, q_parts = [None] * heads, [None] * heads
+    after = ()
+    for pair in [*order, 0]:
+        operands = (keys, values, *after)
         part = call(
-            kernel_of(load_kernel, heads, shift),
-            "load",
-            (keys, values, queries),
-            [VMEM] * 3,
-            (3, BLOCK, TILE, HDIM),
+            functools.partial(load_kv_kernel, pair), "load_kv", operands, [VMEM] * len(operands), (2, BLOCK, TILE, HDIM)
         )
-        parts[shift] = send(part, shift) if shift else part
-    own, local_q = call(
-        gather_kernel, "gather", parts, [VMEM] * heads, [(2, tiles, TILE, HDIM), (heads, *chunk)]
-    )
-    low, high = halo(own, 1, 1)
-    padded = call(join_kernel, "join", (low, own, high), [VMEM] * 3, (2, tiles + LIST - 1, TILE, HDIM))
+        after = (part,)
+        kv_parts[pair] = exchange(part, pair) if pair else part
+    for pair in [*order, 0]:
+        operands = (queries, kv_parts[pair]) if pair else (queries,)
+        part = call(functools.partial(load_q_kernel, pair), "load_q", operands, [VMEM] * len(operands), chunk)
+        q_parts[pair] = exchange(part, pair) if pair else part
+    edge = (2, EDGE, TILE, HDIM)
+    own, odd_edge, even_edge = call(
+        gather_kernel, "gather", kv_parts, [VMEM] * heads, [(2, tiles, TILE, HDIM), edge, edge]
+    )
+    first, second = exchange_ctx(odd_edge, 1), exchange_ctx(even_edge, 0)
+    padded = call(
+        join_kernel, "join", (own, first, second), [VMEM] * 3, (2, tiles + LIST - 1, TILE, HDIM)
+    )
     outs = [None] * heads
     after = ()
-    for shift in order + [0]:
-        operands = (local_q, padded, bias, *after)
-        outs[shift] = call(
-            kernel_of(attend_chunk_kernel, shift, heads),
+    for pair in [*order, 0]:
+        operands = (q_parts[pair], padded, bias, *after)
+        outs[pair] = call(
+            functools.partial(attend_chunk_kernel, pair),
             "attend_chunk",
             operands,
             [VMEM] * len(operands),
             chunk,
             block_scratch(),
             16,
-            cost(BLOCK * LIST // 2 if shift else 1),
+            cost(BLOCK * LIST // 2 if pair else 1),
         )
-        after = (outs[shift],)
-        if shift:
-            outs[shift] = send(outs[shift], -shift)
+        after = (outs[pair],)
+        if pair:
+            outs[pair] = exchange(outs[pair], pair)
     after = ()
-    for shift in order:
-        operands = (outs[shift], *after)
-        outs[shift] = call(
+    for pair in order:
+        operands = (outs[pair], *after)
+        outs[pair] = call(
             pass_kernel, "landed", operands, [VMEM] * len(operands), chunk, cost=cost(BLOCK * LIST // 2)
         )
-        after = (outs[shift],)
-    return call(kernel_of(spread_kernel, heads), "spread", outs, [VMEM] * heads, queries.shape)
+        after = (outs[pair],)
+    return call(spread_kernel, "spread", outs, [VMEM] * heads, queries.shape)
 
 
 def on_device(queries, keys, values, tile_lists, live_counts):
-    bias = mask_bias(tile_lists, live_counts, tile_lists.shape[0] * lax.axis_size("ctx"))
-    heads = lax.axis_size("head")
-    in_chunks = queries.shape[0] == BLOCK * TILE and heads <= 8 and heads % 2 == 0
-    form = by_shifts if in_chunks and heads * BLOCK >= EDGE else whole_range
+    ctx, heads = lax.axis_size("ctx"), lax.axis_size("head")
+    bias = mask_bias(tile_lists, live_counts, tile_lists.shape[0] * ctx)
+    in_chunks = queries.shape[0] == BLOCK * TILE and heads * BLOCK >= EDGE
+    form = in_pairs if in_chunks and heads in (4, 8) and ctx % 2 == 0 else whole_range
     return form(queries, keys, values, bias)
 
 

time: 61.8 us -> 51.5 us (0.83)
  the two profiles are of different devices: /device:TPU:1 before, /device:TPU:0 now
where the time goes in v9:
time: 51.5 us; the launch traced here: 51.3 us
  starting transfers between devices  20.1 us (39%)
  waiting for transfers between devices  19.1 us (37%)
  Pallas kernels  9.85 us (19%)
  local copies, waits for them, and re-layouts  2.1 us (4%)
    ppermute x9, waiting for transfers between devices, exchange(): return lax.ppermute(array, 'head', [(i, i ^ pair) for i in range(heads)])  19.1 us
    ppermute x9, starting transfers between devices, exchange(): return lax.ppermute(array, 'head', [(i, i ^ pair) for i in range(heads)])  16.5 us
    pallas_call x19, Pallas kernels, call(): pl.pallas_call(kernel, out_shape=out_shape, in_specs=in_specs, out_specs=...  9.85 us
    ppermute x2, starting transfers between devices, exchange_ctx(): lax.ppermute(array, 'ctx', [(i, i + 1) for i in lower] + [(i + 1, i) for...  3.57 us
    unnamed x10, local copies, waits for them, and re-layouts  2.01 us
  transfers between devices with their start and end apart: 11, of which 6 were waited for; matrix products, arithmetic and copies ran while one was open for 0% of the time, Pallas kernels for 15%

profile of v9, /device:TPU:0, one launch (start us, length us, event | category | flops | bytes accessed | tf_op | source)
XLA Modules:
  0.0 51.3 jit_solution(12243199975523214378)
XLA Ops:
  0.0 0.0 copy-start
  0.0 1.0 %copy-done = bf16[384,512]{1,0:T(8,128)(2,1)S(1)} copy-done((bf16[384,512]{1,0:T(8,128)(2,1)S(1)}, bf16[384,512]{1,0:T(8,128)(2,1)}, u32[]{:S(2)}) %copy-start) | copy-done | bytes 393240
  1.0 0.0 copy-start.1
  1.0 1.0 %copy-done.1 = bf16[384,512]{1,0:T(8,128)(2,1)S(1)} copy-done((bf16[384,512]{1,0:T(8,128)(2,1)S(1)}, bf16[384,512]{1,0:T(8,128)(2,1)}, u32[]{:S(2)}) %copy-start.1) | copy-done | bytes 393240
  2.0 0.1 load_kv.4.refs_0_
  2.1 0.1 load_kv.5.refs_0_
  2.2 0.0 copy-start.2
  2.2 0.1 load_kv.6.refs_0_
  2.3 0.0 copy-start.4
  2.3 0.0 copy-start.3
  2.4 3.1 %collective-permute-start = (bf16[2,3,128,128]{3,2,1,0:T(8,128)(2,1)S(1)}, bf16[2,3,128,128]{3,2,1,0:T(8,128)(2,1)S(1)}, u32[]{:S(2)}, u32[]{:S(2)}) collective-permute-start(bf16[2,3,128,128]{3,2,1,0:T(8,128)(2,1)S(1)} %load_kv.6.refs_0_), channel_id=1, source_target_pairs={{0,1},{1,0},{2,3},{3,2},{4,5},{5,4},{6,7},{7,6},{8,9},{9,8},{10,11... | collective-permute-start | bytes 589832 | tf_op jit(solution)/shard_map/ppermute | solution.py:239
  5.4 2.6 %collective-permute-start.1 = (bf16[2,3,128,128]{3,2,1,0:T(8,128)(2,1)S(1)}, bf16[2,3,128,128]{3,2,1,0:T(8,128)(2,1)S(1)}, u32[]{:S(2)}, u32[]{:S(2)}) collective-permute-start(bf16[2,3,128,128]{3,2,1,0:T(8,128)(2,1)S(1)} %load_kv.5.refs_0_), channel_id=1, source_target_pairs={{0,2},{1,3},{2,0},{3,1},{4,6},{5,7},{6,4},{7,5},{8,10},{9,11},{10,... | collective-permute-start | bytes 589832 | tf_op jit(solution)/shard_map/ppermute | solution.py:239
  8.0 0.0 collective-permute-start.2
  8.0 0.1 load_kv.7.refs_0_
  8.1 5.6 %collective-permute-done.refs_1_.refs_0_ = bf16[2,3,128,128]{3,2,1,0:T(8,128)(2,1)S(1)} collective-permute-done((bf16[2,3,128,128]{3,2,1,0:T(8,128)(2,1)S(1)}, bf16[2,3,128,128]{3,2,1,0:T(8,128)(2,1)S(1)}, u32[]{:S(2)}, u32[]{:S(2)}) %collective-permute-start) | collective-permute-done | bytes 196640 | tf_op jit(solution)/shard_map/ppermute | solution.py:239
  13.8 8.8 %collective-permute-done.1.refs_2_.refs_0_ = bf16[2,3,128,128]{3,2,1,0:T(8,128)(2,1)S(1)} collective-permute-done((bf16[2,3,128,128]{3,2,1,0:T(8,128)(2,1)S(1)}, bf16[2,3,128,128]{3,2,1,0:T(8,128)(2,1)S(1)}, u32[]{:S(2)}, u32[]{:S(2)}) %collective-permute-start.1) | collective-permute-done | bytes 196640 | tf_op jit(solution)/shard_map/ppermute | solution.py:239
  22.6 0.0 collective-permute-done.2.refs_3_.refs_0_
  22.6 0.9 %gather.1 = (bf16[2,12,128,128]{3,2,1,0:T(8,128)(2,1)S(1)}, bf16[2,8,128,128]{3,2,1,0:T(8,128)(2,1)}, bf16[2,8,128,128]{3,2,1,0:T(8,128)(2,1)S(1)}) custom-call(bf16[2,3,128,128]{3,2,1,0:T(8,128)(2,1)S(1)} %load_kv.7.refs_0_, bf16[2,3,128,128]{3,2,1,0:T(8,128)(2,1)S(1)} %collective-permute-done.refs_1_.refs_0_, ...), custom_call_target="tpu_custom_call" | custom-call | tf_op jit(solution)/shard_map/gather/pallas_call | solution.py:29
  23.5 0.7 %collective-permute-start.3 = (bf16[2,8,128,128]{3,2,1,0:T(8,128)(2,1)}, bf16[2,8,128,128]{3,2,1,0:T(8,128)(2,1)S(1)}, u32[]{:S(2)}, u32[]{:S(2)}) collective-permute-start(bf16[2,8,128,128]{3,2,1,0:T(8,128)(2,1)} %get-tuple-element.9), channel_id=1, source_target_pairs={{4,8},{8,4},{5,9},{9,5},{6,10},{10,6},{7,11},{11,7},{20,24},{24,20... | collective-permute-start | bytes 1572872 | tf_op jit(solution)/shard_map/ppermute | solution.py:243
  24.2 2.9 %collective-permute-start.4 = (bf16[2,8,128,128]{3,2,1,0:T(8,128)(2,1)S(1)}, bf16[2,8,128,128]{3,2,1,0:T(8,128)(2,1)S(1)}, u32[]{:S(2)}, u32[]{:S(2)}) collective-permute-start(bf16[2,8,128,128]{3,2,1,0:T(8,128)(2,1)S(1)} %get-tuple-element.10), channel_id=1, source_target_pairs={{0,4},{8,12},{4,0},{12,8},{1,5},{9,13},{5,1},{13,9},{2,6},{10,14},... | collective-permute-start | bytes 1572872 | tf_op jit(solution)/shard_map/ppermute | solution.py:243
  27.1 0.0 copy-done.2
  27.1 2.5 %collective-permute-start.7 = (bf16[384,128]{1,0:T(8,128)(2,1)S(1)}, bf16[384,128]{1,0:T(8,128)(2,1)S(1)}, u32[]{:S(2)}, u32[]{:S(2)}) collective-permute-start(bf16[384,128]{1,0:T(8,128)(2,1)S(1)} %load_q.7), channel_id=1, source_target_pairs={{0,3},{1,2},{2,1},{3,0},{4,7},{5,6},{6,5},{7,4},{8,11},{9,10},{10,... | collective-permute-start | bytes 294920 | tf_op jit(solution)/shard_map/ppermute | solution.py:239
  29.7 2.4 %collective-permute-start.6 = (bf16[384,128]{1,0:T(8,128)(2,1)S(1)}, bf16[384,128]{1,0:T(8,128)(2,1)S(1)}, u32[]{:S(2)}, u32[]{:S(2)}) collective-permute-start(bf16[384,128]{1,0:T(8,128)(2,1)S(1)} %load_q.6), channel_id=1, source_target_pairs={{0,2},{1,3},{2,0},{3,1},{4,6},{5,7},{6,4},{7,5},{8,10},{9,11},{10,... | collective-permute-start | bytes 294920 | tf_op jit(solution)/shard_map/ppermute | solution.py:239
  32.1 0.2 collective-permute-start.5
  32.3 0.0 copy-done.4
  32.3 0.1 copy.6.counts_ref
  32.4 0.0 copy-done.3
  32.4 0.6 %mask_bias.1.bias_ref = f32[27,12,128]{2,1,0:T(8,128)S(1)} custom-call(s32[12,16]{1,0:T(8,128)S(1)} %copy-done.3, s32[12,1]{1,0:T(8,128)S(1)} %copy.6.counts_ref), custom_call_target="tpu_custom_call" | custom-call | tf_op jit(solution)/shard_map/mask_bias/pallas_call | solution.py:29
  33.0 0.0 collective-permute-done.3.first_ref
  33.0 0.0 collective-permute-done.4.second_ref
  33.0 0.1 join.1.kv_ref
  33.1 0.7 %collective-permute-done.7.q_ref = bf16[384,128]{1,0:T(8,128)(2,1)S(1)} collective-permute-done((bf16[384,128]{1,0:T(8,128)(2,1)S(1)}, bf16[384,128]{1,0:T(8,128)(2,1)S(1)}, u32[]{:S(2)}, u32[]{:S(2)}) %collective-permute-start.7) | collective-permute-done | bytes 98336 | tf_op jit(solution)/shard_map/ppermute | solution.py:239
  33.8 1.7 %attend_chunk.4.refs_0_ = bf16[384,128]{1,0:T(8,128)(2,1)S(1)} custom-call(bf16[384,128]{1,0:T(8,128)(2,1)S(1)} %collective-permute-done.7.q_ref, bf16[2,27,128,128]{3,2,1,0:T(8,128)(2,1)S(1)} %join.1.kv_ref, f32[27,12,128]{2,1,0:T(8,128)S(1)} %mask_bias.1.bias_ref), custom_call_target="tpu_custom_call" | custom-call | flops 201326592 | bytes 393216 | tf_op jit(solution)/shard_map/attend_chunk/pallas_call | solution.py:29
  35.6 2.5 %collective-permute-start.10 = (bf16[384,128]{1,0:T(8,128)(2,1)S(1)}, bf16[384,128]{1,0:T(8,128)(2,1)S(1)}, u32[]{:S(2)}, u32[]{:S(2)}) collective-permute-start(bf16[384,128]{1,0:T(8,128)(2,1)S(1)} %attend_chunk.4.refs_0_), channel_id=1, source_target_pairs={{0,3},{1,2},{2,1},{3,0},{4,7},{5,6},{6,5},{7,4},{8,11},{9,10},{10,... | collective-permute-start | bytes 294920 | tf_op jit(solution)/shard_map/ppermute | solution.py:239
  38.1 2.0 %collective-permute-done.6.q_ref = bf16[384,128]{1,0:T(8,128)(2,1)S(1)} collective-permute-done((bf16[384,128]{1,0:T(8,128)(2,1)S(1)}, bf16[384,128]{1,0:T(8,128)(2,1)S(1)}, u32[]{:S(2)}, u32[]{:S(2)}) %collective-permute-start.6) | collective-permute-done | bytes 98336 | tf_op jit(solution)/shard_map/ppermute | solution.py:239
  40.1 1.7 %attend_chunk.5.refs_0_ = bf16[384,128]{1,0:T(8,128)(2,1)S(1)} custom-call(bf16[384,128]{1,0:T(8,128)(2,1)S(1)} %collective-permute-done.6.q_ref, bf16[2,27,128,128]{3,2,1,0:T(8,128)(2,1)S(1)} %join.1.kv_ref, f32[27,12,128]{2,1,0:T(8,128)S(1)} %mask_bias.1.bias_ref, bf16[384,128]{1,0:T(8,128)(2,1)S(1)} %attend_chunk.4.refs_0_), custom_call_target="tpu_custom_call" | custom-call | flops 201326592 | bytes 393216 | tf_op jit(solution)/shard_map/attend_chunk/pallas_call | solution.py:29
  41.8 1.6 %collective-permute-start.9 = (bf16[384,128]{1,0:T(8,128)(2,1)S(1)}, bf16[384,128]{1,0:T(8,128)(2,1)S(1)}, u32[]{:S(2)}, u32[]{:S(2)}) collective-permute-start(bf16[384,128]{1,0:T(8,128)(2,1)S(1)} %attend_chunk.5.refs_0_), channel_id=1, source_target_pairs={{0,2},{1,3},{2,0},{3,1},{4,6},{5,7},{6,4},{7,5},{8,10},{9,11},{10,... | collective-permute-start | bytes 294920 | tf_op jit(solution)/shard_map/ppermute | solution.py:239
  43.4 0.0 collective-permute-done.5.q_ref
  43.4 1.7 %attend_chunk.6.refs_0_ = bf16[384,128]{1,0:T(8,128)(2,1)S(1)} custom-call(bf16[384,128]{1,0:T(8,128)(2,1)S(1)} %collective-permute-done.5.q_ref, bf16[2,27,128,128]{3,2,1,0:T(8,128)(2,1)S(1)} %join.1.kv_ref, f32[27,12,128]{2,1,0:T(8,128)S(1)} %mask_bias.1.bias_ref, bf16[384,128]{1,0:T(8,128)(2,1)S(1)} %attend_chunk.5.refs_0_), custom_call_target="tpu_custom_call" | custom-call | flops 201326592 | bytes 393216 | tf_op jit(solution)/shard_map/attend_chunk/pallas_call | solution.py:29
  45.1 1.5 %collective-permute-start.8 = (bf16[384,128]{1,0:T(8,128)(2,1)S(1)}, bf16[384,128]{1,0:T(8,128)(2,1)S(1)}, u32[]{:S(2)}, u32[]{:S(2)}) collective-permute-start(bf16[384,128]{1,0:T(8,128)(2,1)S(1)} %attend_chunk.6.refs_0_), channel_id=1, source_target_pairs={{0,1},{1,0},{2,3},{3,2},{4,5},{5,4},{6,7},{7,6},{8,9},{9,8},{10,11... | collective-permute-start | bytes 294920 | tf_op jit(solution)/shard_map/ppermute | solution.py:239
  46.7 1.7 %attend_chunk.7.refs_0_ = bf16[384,128]{1,0:T(8,128)(2,1)S(1)} custom-call(bf16[384,128]{1,0:T(8,128)(2,1)S(1)} %load_q.4.q_ref, bf16[2,27,128,128]{3,2,1,0:T(8,128)(2,1)S(1)} %join.1.kv_ref, f32[27,12,128]{2,1,0:T(8,128)S(1)} %mask_bias.1.bias_ref, bf16[384,128]{1,0:T(8,128)(2,1)S(1)} %attend_chunk.6.refs_0_), custom_call_target="tpu_custom_call" | custom-call | flops 8388608 | bytes 16384 | tf_op jit(solution)/shard_map/attend_chunk/pallas_call | solution.py:29
  48.4 0.0 collective-permute-done.10.array_ref
  48.5 1.2 %collective-permute-done.9.array_ref = bf16[384,128]{1,0:T(8,128)(2,1)S(1)} collective-permute-done((bf16[384,128]{1,0:T(8,128)(2,1)S(1)}, bf16[384,128]{1,0:T(8,128)(2,1)S(1)}, u32[]{:S(2)}, u32[]{:S(2)}) %collective-permute-start.9) | collective-permute-done | bytes 98336 | tf_op jit(solution)/shard_map/ppermute | solution.py:239
  49.6 0.8 %collective-permute-done.8.array_ref = bf16[384,128]{1,0:T(8,128)(2,1)S(1)} collective-permute-done((bf16[384,128]{1,0:T(8,128)(2,1)S(1)}, bf16[384,128]{1,0:T(8,128)(2,1)S(1)}, u32[]{:S(2)}, u32[]{:S(2)}) %collective-permute-start.8) | collective-permute-done | bytes 98336 | tf_op jit(solution)/shard_map/ppermute | solution.py:239
  50.5 0.8 %spread.1 = bf16[384,512]{1,0:T(8,128)(2,1)} custom-call(bf16[384,128]{1,0:T(8,128)(2,1)S(1)} %attend_chunk.7.refs_0_, bf16[384,128]{1,0:T(8,128)(2,1)S(1)} %landed.5.refs_1_, bf16[384,128]{1,0:T(8,128)(2,1)S(1)} %landed.4.refs_0_.refs_2_, bf16[384,128]{1,0:T(8,128)(2,1)S(1)} %landed.3.refs_0_.refs_3_), custom_call_target="tpu_custom_call" | custom-call | tf_op jit(solution)/shard_map/spread/pallas_call | solution.py:29
  (7 shorter events, 0.1 us)
Async XLA Ops:
  0.0 1.0 %copy-start = (bf16[384,512]{1,0:T(8,128)(2,1)S(1)}, bf16[384,512]{1,0:T(8,128)(2,1)}, u32[]{:S(2)}) copy-start(bf16[384,512]{1,0:T(8,128)(2,1)} %k_ref.7) | copy-start | bytes 1179652
  1.0 1.0 %copy-start.1 = (bf16[384,512]{1,0:T(8,128)(2,1)S(1)}, bf16[384,512]{1,0:T(8,128)(2,1)}, u32[]{:S(2)}) copy-start(bf16[384,512]{1,0:T(8,128)(2,1)} %v_ref.7) | copy-start | bytes 1179652
  2.2 24.9 %copy-start.2 = (bf16[384,512]{1,0:T(8,128)(2,1)S(1)}, bf16[384,512]{1,0:T(8,128)(2,1)}, u32[]{:S(2)}) copy-start(bf16[384,512]{1,0:T(8,128)(2,1)} %q_ref.7) | copy-start | bytes 1179652
  2.3 30.0 %copy-start.4 = (s32[12]{0:T(128)S(1)}, s32[12]{0:T(128)}, u32[]{:S(2)}) copy-start(s32[12]{0:T(128)} %param.9) | copy-start | bytes 148
  2.3 30.1 %copy-start.3 = (s32[12,16]{1,0:T(8,128)S(1)}, s32[12,16]{1,0:T(8,128)}, u32[]{:S(2)}) copy-start(s32[12,16]{1,0:T(8,128)} %lists_ref.1) | copy-start | bytes 2308
  2.4 11.4 %collective-permute-start = (bf16[2,3,128,128]{3,2,1,0:T(8,128)(2,1)S(1)}, bf16[2,3,128,128]{3,2,1,0:T(8,128)(2,1)S(1)}, u32[]{:S(2)}, u32[]{:S(2)}) collective-permute-start(bf16[2,3,128,128]{3,2,1,0:T(8,128)(2,1)S(1)} %load_kv.6.refs_0_), channel_id=1, source_target_pairs={{0,1},{1,0},{2,3},{3,2},{4,5},{5,4},{6,7},{7,6},{8,9},{9,8},{10,11... | collective-permute-start | bytes 589832 | tf_op jit(solution)/shard_map/ppermute | solution.py:239
  5.4 17.2 %collective-permute-start.1 = (bf16[2,3,128,128]{3,2,1,0:T(8,128)(2,1)S(1)}, bf16[2,3,128,128]{3,2,1,0:T(8,128)(2,1)S(1)}, u32[]{:S(2)}, u32[]{:S(2)}) collective-permute-start(bf16[2,3,128,128]{3,2,1,0:T(8,128)(2,1)S(1)} %load_kv.5.refs_0_), channel_id=1, source_target_pairs={{0,2},{1,3},{2,0},{3,1},{4,6},{5,7},{6,4},{7,5},{8,10},{9,11},{10,... | collective-permute-start | bytes 589832 | tf_op jit(solution)/shard_map/ppermute | solution.py:239
  8.0 14.6 %collective-permute-start.2 = (bf16[2,3,128,128]{3,2,1,0:T(8,128)(2,1)S(1)}, bf16[2,3,128,128]{3,2,1,0:T(8,128)(2,1)S(1)}, u32[]{:S(2)}, u32[]{:S(2)}) collective-permute-start(bf16[2,3,128,128]{3,2,1,0:T(8,128)(2,1)S(1)} %load_kv.4.refs_0_), channel_id=1, source_target_pairs={{0,3},{1,2},{2,1},{3,0},{4,7},{5,6},{6,5},{7,4},{8,11},{9,10},{10,... | collective-permute-start | bytes 589832 | tf_op jit(solution)/shard_map/ppermute | solution.py:239
  23.5 9.5 %collective-permute-start.3 = (bf16[2,8,128,128]{3,2,1,0:T(8,128)(2,1)}, bf16[2,8,128,128]{3,2,1,0:T(8,128)(2,1)S(1)}, u32[]{:S(2)}, u32[]{:S(2)}) collective-permute-start(bf16[2,8,128,128]{3,2,1,0:T(8,128)(2,1)} %get-tuple-element.9), channel_id=1, source_target_pairs={{4,8},{8,4},{5,9},{9,5},{6,10},{10,6},{7,11},{11,7},{20,24},{24,20... | collective-permute-start | bytes 1572872 | tf_op jit(solution)/shard_map/ppermute | solution.py:243
  24.2 8.8 %collective-permute-start.4 = (bf16[2,8,128,128]{3,2,1,0:T(8,128)(2,1)S(1)}, bf16[2,8,128,128]{3,2,1,0:T(8,128)(2,1)S(1)}, u32[]{:S(2)}, u32[]{:S(2)}) collective-permute-start(bf16[2,8,128,128]{3,2,1,0:T(8,128)(2,1)S(1)} %get-tuple-element.10), channel_id=1, source_target_pairs={{0,4},{8,12},{4,0},{12,8},{1,5},{9,13},{5,1},{13,9},{2,6},{10,14},... | collective-permute-start | bytes 1572872 | tf_op jit(solution)/shard_map/ppermute | solution.py:243
  27.1 6.7 %collective-permute-start.7 = (bf16[384,128]{1,0:T(8,128)(2,1)S(1)}, bf16[384,128]{1,0:T(8,128)(2,1)S(1)}, u32[]{:S(2)}, u32[]{:S(2)}) collective-permute-start(bf16[384,128]{1,0:T(8,128)(2,1)S(1)} %load_q.7), channel_id=1, source_target_pairs={{0,3},{1,2},{2,1},{3,0},{4,7},{5,6},{6,5},{7,4},{8,11},{9,10},{10,... | collective-permute-start | bytes 294920 | tf_op jit(solution)/shard_map/ppermute | solution.py:239
  29.7 10.4 %collective-permute-start.6 = (bf16[384,128]{1,0:T(8,128)(2,1)S(1)}, bf16[384,128]{1,0:T(8,128)(2,1)S(1)}, u32[]{:S(2)}, u32[]{:S(2)}) collective-permute-start(bf16[384,128]{1,0:T(8,128)(2,1)S(1)} %load_q.6), channel_id=1, source_target_pairs={{0,2},{1,3},{2,0},{3,1},{4,6},{5,7},{6,4},{7,5},{8,10},{9,11},{10,... | collective-permute-start | bytes 294920 | tf_op jit(solution)/shard_map/ppermute | solution.py:239
  32.1 11.3 %collective-permute-start.5 = (bf16[384,128]{1,0:T(8,128)(2,1)S(1)}, bf16[384,128]{1,0:T(8,128)(2,1)S(1)}, u32[]{:S(2)}, u32[]{:S(2)}) collective-permute-start(bf16[384,128]{1,0:T(8,128)(2,1)S(1)} %load_q.5), channel_id=1, source_target_pairs={{0,1},{1,0},{2,3},{3,2},{4,5},{5,4},{6,7},{7,6},{8,9},{9,8},{10,11... | collective-permute-start | bytes 294920 | tf_op jit(solution)/shard_map/ppermute | solution.py:239
  35.6 12.9 %collective-permute-start.10 = (bf16[384,128]{1,0:T(8,128)(2,1)S(1)}, bf16[384,128]{1,0:T(8,128)(2,1)S(1)}, u32[]{:S(2)}, u32[]{:S(2)}) collective-permute-start(bf16[384,128]{1,0:T(8,128)(2,1)S(1)} %attend_chunk.4.refs_0_), channel_id=1, source_target_pairs={{0,3},{1,2},{2,1},{3,0},{4,7},{5,6},{6,5},{7,4},{8,11},{9,10},{10,... | collective-permute-start | bytes 294920 | tf_op jit(solution)/shard_map/ppermute | solution.py:239
  41.8 7.9 %collective-permute-start.9 = (bf16[384,128]{1,0:T(8,128)(2,1)S(1)}, bf16[384,128]{1,0:T(8,128)(2,1)S(1)}, u32[]{:S(2)}, u32[]{:S(2)}) collective-permute-start(bf16[384,128]{1,0:T(8,128)(2,1)S(1)} %attend_chunk.5.refs_0_), channel_id=1, source_target_pairs={{0,2},{1,3},{2,0},{3,1},{4,6},{5,7},{6,4},{7,5},{8,10},{9,11},{10,... | collective-permute-start | bytes 294920 | tf_op jit(solution)/shard_map/ppermute | solution.py:239
  45.1 5.3 %collective-permute-start.8 = (bf16[384,128]{1,0:T(8,128)(2,1)S(1)}, bf16[384,128]{1,0:T(8,128)(2,1)S(1)}, u32[]{:S(2)}, u32[]{:S(2)}) collective-permute-start(bf16[384,128]{1,0:T(8,128)(2,1)S(1)} %attend_chunk.6.refs_0_), channel_id=1, source_target_pairs={{0,1},{1,0},{2,3},{3,2},{4,5},{5,4},{6,7},{7,6},{8,9},{9,8},{10,11... | collective-permute-start | bytes 294920 | tf_op jit(solution)/shard_map/ppermute | solution.py:239

commit v10 on v9

--- a/solution.py
+++ b/solution.py
@@ -172,12 +172,11 @@
     return call(functools.partial(unpack_kernel, heads), "unpack", (back,), [VMEM], (rows, columns))
 
 
-def load_kv_kernel(pair, k_ref, v_ref, *refs):
-    out_ref = refs[-1]
+def load_tiles_kernel(pair, turn, array_ref, *refs):
     columns = column_of(lax.axis_index("head") ^ pair)
     for tile in range(BLOCK):
-        out_ref[0, tile] = k_ref[rows_of(tile), columns].T
-        out_ref[1, tile] = v_ref[rows_of(tile), columns]
+        part = array_ref[rows_of(tile), columns]
+        refs[-1][tile] = part.T if turn else part
 
 
 def load_q_kernel(pair, q_ref, *refs):
@@ -185,24 +184,27 @@
 
 
 def gather_kernel(*refs):
-    *parts, own_ref, odd_ref, even_ref = refs
+    *parts, own_ref = refs
     me = lax.axis_index("head")
     for pair, part in enumerate(parts):
-        own_ref[:, pl.ds((me ^ pair) * BLOCK, BLOCK)] = part[...]
-    last = own_ref.shape[1] - EDGE
+        own_ref[pl.ds((me ^ pair) * BLOCK, BLOCK)] = part[...]
+
+
+def edges_kernel(own_ref, odd_ref, even_ref):
+    last = own_ref.shape[0] - EDGE
     odd = lax.rem(lax.axis_index("ctx"), 2)
-    odd_ref[...] = own_ref[:, pl.ds(odd * last, EDGE)]
-    even_ref[...] = own_ref[:, pl.ds((1 - odd) * last, EDGE)]
+    odd_ref[...] = own_ref[pl.ds(odd * last, EDGE)]
+    even_ref[...] = own_ref[pl.ds((1 - odd) * last, EDGE)]
 
 
 def join_kernel(own_ref, first_ref, second_ref, out_ref):
     odd = lax.rem(lax.axis_index("ctx"), 2)
-    tiles = own_ref.shape[1]
-    out_ref[:, EDGE : EDGE + tiles] = own_ref[...]
+    tiles = own_ref.shape[0]
+    out_ref[EDGE : EDGE + tiles] = own_ref[...]
 
     def around(low_ref, high_ref):
-        out_ref[:, :EDGE] = low_ref[...]
-        out_ref[:, EDGE + tiles :] = high_ref[:, : EDGE - 1]
+        out_ref[:EDGE] = low_ref[...]
+        out_ref[EDGE + tiles :] = high_ref[: EDGE - 1]
 
     @pl.when(odd == 1)
     def _():
@@ -213,14 +215,28 @@
         around(first_ref, second_ref)
 
 
+def with_halo(parts):
+    heads, ctx = len(parts), lax.axis_size("ctx")
+    tiles, edge = heads * BLOCK, (EDGE, TILE, HDIM)
+    own = call(gather_kernel, "gather", parts, [VMEM] * heads, (tiles, TILE, HDIM))
+    odd_edge, even_edge = call(edges_kernel, "edges", (own,), [VMEM], [edge, edge])
+
+    def exchange(array, first):
+        lower = range(first, ctx - 1, 2)
+        return lax.ppermute(array, "ctx", [(i, i + 1) for i in lower] + [(i + 1, i) for i in lower])
+
+    operands = (own, exchange(odd_edge, 1), exchange(even_edge, 0))
+    return call(join_kernel, "join", operands, [VMEM] * 3, (tiles + LIST - 1, TILE, HDIM))
+
+
 def pass_kernel(array_ref, *refs):
     refs[-1][...] = array_ref[...]
 
 
-def attend_chunk_kernel(pair, q_ref, kv_ref, bias_ref, *refs):
+def attend_chunk_kernel(pair, q_ref, kt_ref, v_ref, bias_ref, *refs):
     out_ref, *scratch = refs[-3:]
     first = (lax.axis_index("head") ^ pair) * BLOCK
-    attend_block(first, q_ref, kv_ref.at[0], kv_ref.at[1], bias_ref, out_ref, *scratch)
+    attend_block(first, q_ref, kt_ref, v_ref, bias_ref, out_ref, *scratch)
 
 
 def spread_kernel(*refs):
@@ -231,42 +247,33 @@
 
 
 def in_pairs(queries, keys, values, bias):
-    heads, ctx = lax.axis_size("head"), lax.axis_size("ctx")
-    chunk, tiles = (queries.shape[0], HDIM), heads * BLOCK
+    heads = lax.axis_size("head")
+    chunk, tiles = (queries.shape[0], HDIM), (BLOCK, TILE, HDIM)
     order = range(heads - 1, 0, -1)
 
     def exchange(array, pair):
         return lax.ppermute(array, "head", [(i, i ^ pair) for i in range(heads)])
 
-    def exchange_ctx(array, first):
-        lower = range(first, ctx - 1, 2)
-        return lax.ppermute(array, "ctx", [(i, i + 1) for i in lower] + [(i + 1, i) for i in lower])
-
-    kv_parts, q_parts = [None] * heads, [None] * heads
-    after = ()
+    def call_on(kernel, name, operands, shape):
+        return call(kernel, name, operands, [VMEM] * len(operands), shape)
+
+    v_parts, k_parts, q_parts = [None] * heads, [None] * heads, [None] * heads
     for pair in [*order, 0]:
-        operands = (keys, values, *after)
-        part = call(
-            functools.partial(load_kv_kernel, pair), "load_kv", operands, [VMEM] * len(operands), (2, BLOCK, TILE, HDIM)
-        )
-        after = (part,)
-        kv_parts[pair] = exchange(part, pair) if pair else part
+        part = call_on(functools.partial(load_tiles_kernel, pair, False), "load_v", (values,), tiles)
+        v_parts[pair] = exchange(part, pair) if pair else part
     for pair in [*order, 0]:
-        operands = (queries, kv_parts[pair]) if pair else (queries,)
-        part = call(functools.partial(load_q_kernel, pair), "load_q", operands, [VMEM] * len(operands), chunk)
+        operands = (keys, v_parts[pair]) if pair else (keys,)
+        part = call_on(functools.partial(load_tiles_kernel, pair, True), "load_k", operands, tiles)
+        k_parts[pair] = exchange(part, pair) if pair else part
+    for pair in [*order, 0]:
+        operands = (queries, k_parts[pair]) if pair else (queries,)
+        part = call_on(functools.partial(load_q_kernel, pair), "load_q", operands, chunk)
         q_parts[pair] = exchange(part, pair) if pair else part
-    edge = (2, EDGE, TILE, HDIM)
-    own, odd_edge, even_edge = call(
-        gather_kernel, "gather", kv_parts, [VMEM] * heads, [(2, tiles, TILE, HDIM), edge, edge]
-    )
-    first, second = exchange_ctx(odd_edge, 1), exchange_ctx(even_edge, 0)
-    padded = call(
-        join_kernel, "join", (own, first, second), [VMEM] * 3, (2, tiles + LIST - 1, TILE, HDIM)
-    )
+    all_values, all_keys = with_halo(v_parts), with_halo(k_parts)
     outs = [None] * heads
     after = ()
     for pair in [*order, 0]:
-        operands = (q_parts[pair], padded, bias, *after)
+        operands = (q_parts[pair], all_keys, all_values, bias, *after)
         outs[pair] = call(
             functools.partial(attend_chunk_kernel, pair),
             "attend_chunk",

time: 51.5 us -> 51.5 us (level)
  starting transfers between devices: 20.1 us -> 30.8 us
  waiting for transfers between devices: 19.1 us -> 10 us
  local copies, waits for them, and re-layouts: 2.1 us -> 1.11 us
  Pallas kernels: 9.85 us -> 9.12 us
    ppermute x9 -> x12, waiting for transfers between devices: 19.1 us -> 10 us  [exchange(): return lax.ppermute(array, 'head', [(i, i ^ pair) for i in range(heads)])]
    ppermute x9 -> x12, starting transfers between devices: 16.5 us -> 23.9 us  [exchange(): return lax.ppermute(array, 'head', [(i, i ^ pair) for i in range(heads)])]
    ppermute x2 -> x4, starting transfers between devices: 3.57 us -> 6.92 us  [exchange(): lax.ppermute(array, 'ctx', [(i, i + 1) for i in lower] + [(i + 1, i) for...]
    unnamed x10, local copies, waits for them, and re-layouts: 2.01 us -> 1.02 us
    pallas_call x19 -> x27, Pallas kernels: 9.85 us -> 9.12 us  [call(): pl.pallas_call(kernel, out_shape=out_shape, in_specs=in_specs, out_specs=...]
  transfers between devices with their start and end apart: 11 -> 16, of which waited for: 6 -> 5; matrix products, arithmetic and copies ran while one was open for 0% -> 0% of each run, Pallas kernels for 15% -> 16%
where the time goes in v10:
time: 51.5 us; the launch traced here: 51.3 us
  starting transfers between devices  30.8 us (60%)
  waiting for transfers between devices  10 us (19%)
  Pallas kernels  9.12 us (18%)
  local copies, waits for them, and re-layouts  1.11 us (2%)
    ppermute x12, starting transfers between devices, exchange(): return lax.ppermute(array, 'head', [(i, i ^ pair) for i in range(heads)])  23.9 us
    ppermute x12, waiting for transfers between devices, exchange(): return lax.ppermute(array, 'head', [(i, i ^ pair) for i in range(heads)])  10 us
    pallas_call x27, Pallas kernels, call(): pl.pallas_call(kernel, out_shape=out_shape, in_specs=in_specs, out_specs=...  9.12 us
    ppermute x4, starting transfers between devices, exchange(): lax.ppermute(array, 'ctx', [(i, i + 1) for i in lower] + [(i + 1, i) for...  6.92 us
  transfers between devices with their start and end apart: 16, of which 5 were waited for; matrix products, arithmetic and copies ran while one was open for 0% of the time, Pallas kernels for 16%

profile of v10, /device:TPU:0, one launch (start us, length us, event | category | flops | bytes accessed | tf_op | source)
XLA Modules:
  0.0 51.3 jit_solution(6932994727564095182)
XLA Ops:
  0.0 1.0 %copy-done.2 = bf16[384,512]{1,0:T(8,128)(2,1)S(1)} copy-done((bf16[384,512]{1,0:T(8,128)(2,1)S(1)}, bf16[384,512]{1,0:T(8,128)(2,1)}, u32[]{:S(2)}) %copy-start.2) | copy-done | bytes 393240
  1.0 0.0 copy-start
  1.0 3.1 %collective-permute-start = (bf16[3,128,128]{2,1,0:T(8,128)(2,1)S(1)}, bf16[3,128,128]{2,1,0:T(8,128)(2,1)S(1)}, u32[]{:S(2)}, u32[]{:S(2)}) collective-permute-start(bf16[3,128,128]{2,1,0:T(8,128)(2,1)S(1)} %load_v.4), channel_id=1, source_target_pairs={{0,1},{1,0},{2,3},{3,2},{4,5},{5,4},{6,7},{7,6},{8,9},{9,8},{10,11... | collective-permute-start | bytes 294920 | tf_op jit(solution)/shard_map/ppermute | solution.py:255
  4.1 2.7 %collective-permute-start.2 = (bf16[3,128,128]{2,1,0:T(8,128)(2,1)S(1)}, bf16[3,128,128]{2,1,0:T(8,128)(2,1)S(1)}, u32[]{:S(2)}, u32[]{:S(2)}) collective-permute-start(bf16[3,128,128]{2,1,0:T(8,128)(2,1)S(1)} %load_v.5), channel_id=1, source_target_pairs={{0,2},{1,3},{2,0},{3,1},{4,6},{5,7},{6,4},{7,5},{8,10},{9,11},{10,... | collective-permute-start | bytes 294920 | tf_op jit(solution)/shard_map/ppermute | solution.py:255
  6.8 0.1 collective-permute-start.4
  6.9 0.0 collective-permute-done.refs_0_.refs_1_
  6.9 0.1 load_k.5
  7.0 1.9 %collective-permute-start.1 = (bf16[3,128,128]{2,1,0:T(8,128)(2,1)S(1)}, bf16[3,128,128]{2,1,0:T(8,128)(2,1)S(1)}, u32[]{:S(2)}, u32[]{:S(2)}) collective-permute-start(bf16[3,128,128]{2,1,0:T(8,128)(2,1)S(1)} %load_k.5), channel_id=1, source_target_pairs={{0,1},{1,0},{2,3},{3,2},{4,5},{5,4},{6,7},{7,6},{8,9},{9,8},{10,11... | collective-permute-start | bytes 294920 | tf_op jit(solution)/shard_map/ppermute | solution.py:255
  8.9 6.1 %collective-permute-done.2.refs_0_.refs_2_ = bf16[3,128,128]{2,1,0:T(8,128)(2,1)S(1)} collective-permute-done((bf16[3,128,128]{2,1,0:T(8,128)(2,1)S(1)}, bf16[3,128,128]{2,1,0:T(8,128)(2,1)S(1)}, u32[]{:S(2)}, u32[]{:S(2)}) %collective-permute-start.2) | collective-permute-done | bytes 98336 | tf_op jit(solution)/shard_map/ppermute | solution.py:255
  15.0 0.1 load_k.6
  15.1 0.1 collective-permute-start.3
  15.2 0.0 collective-permute-done.4.refs_0_.refs_3_
  15.2 0.1 load_k.7
  15.3 4.4 %collective-permute-start.5 = (bf16[3,128,128]{2,1,0:T(8,128)(2,1)S(1)}, bf16[3,128,128]{2,1,0:T(8,128)(2,1)S(1)}, u32[]{:S(2)}, u32[]{:S(2)}) collective-permute-start(bf16[3,128,128]{2,1,0:T(8,128)(2,1)S(1)} %load_k.7), channel_id=1, source_target_pairs={{0,3},{1,2},{2,1},{3,0},{4,7},{5,6},{6,5},{7,4},{8,11},{9,10},{10,... | collective-permute-start | bytes 294920 | tf_op jit(solution)/shard_map/ppermute | solution.py:255
  19.8 0.7 %collective-permute-start.8 = (bf16[8,128,128]{2,1,0:T(8,128)(2,1)S(1)}, bf16[8,128,128]{2,1,0:T(8,128)(2,1)S(1)}, u32[]{:S(2)}, u32[]{:S(2)}) collective-permute-start(bf16[8,128,128]{2,1,0:T(8,128)(2,1)S(1)} %get-tuple-element.11), channel_id=1, source_target_pairs={{4,8},{8,4},{5,9},{9,5},{6,10},{10,6},{7,11},{11,7},{20,24},{24,20... | collective-permute-start | bytes 786440 | tf_op jit(solution)/shard_map/ppermute | solution.py:226
  20.5 2.9 %collective-permute-start.9 = (bf16[8,128,128]{2,1,0:T(8,128)(2,1)S(1)}, bf16[8,128,128]{2,1,0:T(8,128)(2,1)S(1)}, u32[]{:S(2)}, u32[]{:S(2)}) collective-permute-start(bf16[8,128,128]{2,1,0:T(8,128)(2,1)S(1)} %get-tuple-element.12), channel_id=1, source_target_pairs={{0,4},{8,12},{4,0},{12,8},{1,5},{9,13},{5,1},{13,9},{2,6},{10,14},... | collective-permute-start | bytes 786440 | tf_op jit(solution)/shard_map/ppermute | solution.py:226
  23.4 0.1 load_k.4.refs_0_
  23.5 0.0 collective-permute-done.1.refs_1_.refs_0_
  23.5 0.0 collective-permute-done.3.refs_2_.refs_0_
  23.5 0.0 collective-permute-done.5.refs_3_.refs_0_
  23.5 0.0 copy-start.1
  23.6 0.8 %collective-permute-start.6 = (bf16[8,128,128]{2,1,0:T(8,128)(2,1)S(1)}, bf16[8,128,128]{2,1,0:T(8,128)(2,1)S(1)}, u32[]{:S(2)}, u32[]{:S(2)}) collective-permute-start(bf16[8,128,128]{2,1,0:T(8,128)(2,1)S(1)} %get-tuple-element.9), channel_id=1, source_target_pairs={{4,8},{8,4},{5,9},{9,5},{6,10},{10,6},{7,11},{11,7},{20,24},{24,20... | collective-permute-start | bytes 786440 | tf_op jit(solution)/shard_map/ppermute | solution.py:226
  24.4 2.5 %collective-permute-start.7 = (bf16[8,128,128]{2,1,0:T(8,128)(2,1)S(1)}, bf16[8,128,128]{2,1,0:T(8,128)(2,1)S(1)}, u32[]{:S(2)}, u32[]{:S(2)}) collective-permute-start(bf16[8,128,128]{2,1,0:T(8,128)(2,1)S(1)} %get-tuple-element.10), channel_id=1, source_target_pairs={{0,4},{8,12},{4,0},{12,8},{1,5},{9,13},{5,1},{13,9},{2,6},{10,14},... | collective-permute-start | bytes 786440 | tf_op jit(solution)/shard_map/ppermute | solution.py:226
  27.0 3.0 %collective-permute-start.12 = (bf16[384,128]{1,0:T(8,128)(2,1)S(1)}, bf16[384,128]{1,0:T(8,128)(2,1)S(1)}, u32[]{:S(2)}, u32[]{:S(2)}) collective-permute-start(bf16[384,128]{1,0:T(8,128)(2,1)S(1)} %load_q.7), channel_id=1, source_target_pairs={{0,3},{1,2},{2,1},{3,0},{4,7},{5,6},{6,5},{7,4},{8,11},{9,10},{10,... | collective-permute-start | bytes 294920 | tf_op jit(solution)/shard_map/ppermute | solution.py:255
  30.0 0.0 collective-permute-done.8.first_ref
  30.0 0.4 collective-permute-start.11
  30.4 0.0 copy-start.3
  30.4 0.0 collective-permute-done.9.second_ref
  30.4 1.2 %collective-permute-start.10 = (bf16[384,128]{1,0:T(8,128)(2,1)S(1)}, bf16[384,128]{1,0:T(8,128)(2,1)S(1)}, u32[]{:S(2)}, u32[]{:S(2)}) collective-permute-start(bf16[384,128]{1,0:T(8,128)(2,1)S(1)} %load_q.5), channel_id=1, source_target_pairs={{0,1},{1,0},{2,3},{3,2},{4,5},{5,4},{6,7},{7,6},{8,9},{9,8},{10,11... | collective-permute-start | bytes 294920 | tf_op jit(solution)/shard_map/ppermute | solution.py:255
  31.6 0.1 copy.6.counts_ref
  31.7 0.6 %mask_bias.1.bias_ref = f32[27,12,128]{2,1,0:T(8,128)S(1)} custom-call(s32[12,16]{1,0:T(8,128)S(1)} %copy-done.3, s32[12,1]{1,0:T(8,128)S(1)} %copy.6.counts_ref), custom_call_target="tpu_custom_call" | custom-call | tf_op jit(solution)/shard_map/mask_bias/pallas_call | solution.py:29
  32.3 0.1 join.3.v_ref
  32.4 0.0 collective-permute-done.6.first_ref
  32.4 0.0 collective-permute-done.7.second_ref
  32.4 0.1 join.2.kt_ref
  32.5 1.3 %collective-permute-done.12.q_ref = bf16[384,128]{1,0:T(8,128)(2,1)S(1)} collective-permute-done((bf16[384,128]{1,0:T(8,128)(2,1)S(1)}, bf16[384,128]{1,0:T(8,128)(2,1)S(1)}, u32[]{:S(2)}, u32[]{:S(2)}) %collective-permute-start.12) | collective-permute-done | bytes 98336 | tf_op jit(solution)/shard_map/ppermute | solution.py:255
  33.8 1.7 %attend_chunk.4.refs_0_ = bf16[384,128]{1,0:T(8,128)(2,1)S(1)} custom-call(bf16[384,128]{1,0:T(8,128)(2,1)S(1)} %collective-permute-done.12.q_ref, bf16[27,128,128]{2,1,0:T(8,128)(2,1)S(1)} %join.2.kt_ref, bf16[27,128,128]{2,1,0:T(8,128)(2,1)S(1)} %join.3.v_ref, f32[27,12,128]{2,1,0:T(8,128)S(1)} %mask_bias.1.bias_ref), custom_call_target="tpu_custom_call" | custom-call | flops 201326592 | bytes 393216 | tf_op jit(solution)/shard_map/attend_chunk/pallas_call | solution.py:29
  35.5 3.8 %collective-permute-start.15 = (bf16[384,128]{1,0:T(8,128)(2,1)S(1)}, bf16[384,128]{1,0:T(8,128)(2,1)S(1)}, u32[]{:S(2)}, u32[]{:S(2)}) collective-permute-start(bf16[384,128]{1,0:T(8,128)(2,1)S(1)} %attend_chunk.4.refs_0_), channel_id=1, source_target_pairs={{0,3},{1,2},{2,1},{3,0},{4,7},{5,6},{6,5},{7,4},{8,11},{9,10},{10,... | collective-permute-start | bytes 294920 | tf_op jit(solution)/shard_map/ppermute | solution.py:255
  39.3 1.3 %collective-permute-done.11.q_ref = bf16[384,128]{1,0:T(8,128)(2,1)S(1)} collective-permute-done((bf16[384,128]{1,0:T(8,128)(2,1)S(1)}, bf16[384,128]{1,0:T(8,128)(2,1)S(1)}, u32[]{:S(2)}, u32[]{:S(2)}) %collective-permute-start.11) | collective-permute-done | bytes 98336 | tf_op jit(solution)/shard_map/ppermute | solution.py:255
  40.6 1.7 %attend_chunk.5.refs_0_ = bf16[384,128]{1,0:T(8,128)(2,1)S(1)} custom-call(bf16[384,128]{1,0:T(8,128)(2,1)S(1)} %collective-permute-done.11.q_ref, bf16[27,128,128]{2,1,0:T(8,128)(2,1)S(1)} %join.2.kt_ref, bf16[27,128,128]{2,1,0:T(8,128)(2,1)S(1)} %join.3.v_ref, f32[27,12,128]{2,1,0:T(8,128)S(1)} %mask_bias.1.bias_ref, bf16[384,128]{1,0:T(8,128)(2,1)S(1)} %attend_chunk.4.refs_0_), custom_call_target="tpu_custom_call" | custom-call | flops 201326592 | bytes 393216 | tf_op jit(solution)/shard_map/attend_chunk/pallas_call | solution.py:29
  42.4 1.2 %collective-permute-start.14 = (bf16[384,128]{1,0:T(8,128)(2,1)S(1)}, bf16[384,128]{1,0:T(8,128)(2,1)S(1)}, u32[]{:S(2)}, u32[]{:S(2)}) collective-permute-start(bf16[384,128]{1,0:T(8,128)(2,1)S(1)} %attend_chunk.5.refs_0_), channel_id=1, source_target_pairs={{0,2},{1,3},{2,0},{3,1},{4,6},{5,7},{6,4},{7,5},{8,10},{9,11},{10,... | collective-permute-start | bytes 294920 | tf_op jit(solution)/shard_map/ppermute | solution.py:255
  43.5 0.0 collective-permute-done.10.q_ref
  43.5 1.7 %attend_chunk.6.refs_0_ = bf16[384,128]{1,0:T(8,128)(2,1)S(1)} custom-call(bf16[384,128]{1,0:T(8,128)(2,1)S(1)} %collective-permute-done.10.q_ref, bf16[27,128,128]{2,1,0:T(8,128)(2,1)S(1)} %join.2.kt_ref, bf16[27,128,128]{2,1,0:T(8,128)(2,1)S(1)} %join.3.v_ref, f32[27,12,128]{2,1,0:T(8,128)S(1)} %mask_bias.1.bias_ref, bf16[384,128]{1,0:T(8,128)(2,1)S(1)} %attend_chunk.5.refs_0_), custom_call_target="tpu_custom_call" | custom-call | flops 201326592 | bytes 393216 | tf_op jit(solution)/shard_map/attend_chunk/pallas_call | solution.py:29
  45.3 2.2 %collective-permute-start.13 = (bf16[384,128]{1,0:T(8,128)(2,1)S(1)}, bf16[384,128]{1,0:T(8,128)(2,1)S(1)}, u32[]{:S(2)}, u32[]{:S(2)}) collective-permute-start(bf16[384,128]{1,0:T(8,128)(2,1)S(1)} %attend_chunk.6.refs_0_), channel_id=1, source_target_pairs={{0,1},{1,0},{2,3},{3,2},{4,5},{5,4},{6,7},{7,6},{8,9},{9,8},{10,11... | collective-permute-start | bytes 294920 | tf_op jit(solution)/shard_map/ppermute | solution.py:255
  47.4 1.7 %attend_chunk.7.refs_0_ = bf16[384,128]{1,0:T(8,128)(2,1)S(1)} custom-call(bf16[384,128]{1,0:T(8,128)(2,1)S(1)} %load_q.4.q_ref, bf16[27,128,128]{2,1,0:T(8,128)(2,1)S(1)} %join.2.kt_ref, bf16[27,128,128]{2,1,0:T(8,128)(2,1)S(1)} %join.3.v_ref, f32[27,12,128]{2,1,0:T(8,128)S(1)} %mask_bias.1.bias_ref, bf16[384,128]{1,0:T(8,128)(2,1)S(1)} %attend_chunk.6.refs_0_), custom_call_target="tpu_custom_call" | custom-call | flops 8388608 | bytes 16384 | tf_op jit(solution)/shard_map/attend_chunk/pallas_call | solution.py:29
  49.2 0.2 collective-permute-done.14.array_ref
  49.4 1.1 %collective-permute-done.13.array_ref = bf16[384,128]{1,0:T(8,128)(2,1)S(1)} collective-permute-done((bf16[384,128]{1,0:T(8,128)(2,1)S(1)}, bf16[384,128]{1,0:T(8,128)(2,1)S(1)}, u32[]{:S(2)}, u32[]{:S(2)}) %collective-permute-start.13) | collective-permute-done | bytes 98336 | tf_op jit(solution)/shard_map/ppermute | solution.py:255
  50.5 0.8 %spread.1 = bf16[384,512]{1,0:T(8,128)(2,1)} custom-call(bf16[384,128]{1,0:T(8,128)(2,1)S(1)} %attend_chunk.7.refs_0_, bf16[384,128]{1,0:T(8,128)(2,1)S(1)} %landed.5.refs_1_, bf16[384,128]{1,0:T(8,128)(2,1)S(1)} %landed.4.refs_0_.refs_2_, bf16[384,128]{1,0:T(8,128)(2,1)S(1)} %landed.3.refs_0_.refs_3_), custom_call_target="tpu_custom_call" | custom-call | tf_op jit(solution)/shard_map/spread/pallas_call | solution.py:29
  (22 shorter events, 0.4 us)
Async XLA Ops:
  0.0 1.0 %copy-start.2 = (bf16[384,512]{1,0:T(8,128)(2,1)S(1)}, bf16[384,512]{1,0:T(8,128)(2,1)}, u32[]{:S(2)}) copy-start(bf16[384,512]{1,0:T(8,128)(2,1)} %array_ref.15) | copy-start | bytes 1179652
  1.0 5.9 %copy-start = (bf16[384,512]{1,0:T(8,128)(2,1)S(1)}, bf16[384,512]{1,0:T(8,128)(2,1)}, u32[]{:S(2)}) copy-start(bf16[384,512]{1,0:T(8,128)(2,1)} %array_ref.14) | copy-start | bytes 1179652
  1.0 5.9 %collective-permute-start = (bf16[3,128,128]{2,1,0:T(8,128)(2,1)S(1)}, bf16[3,128,128]{2,1,0:T(8,128)(2,1)S(1)}, u32[]{:S(2)}, u32[]{:S(2)}) collective-permute-start(bf16[3,128,128]{2,1,0:T(8,128)(2,1)S(1)} %load_v.4), channel_id=1, source_target_pairs={{0,1},{1,0},{2,3},{3,2},{4,5},{5,4},{6,7},{7,6},{8,9},{9,8},{10,11... | collective-permute-start | bytes 294920 | tf_op jit(solution)/shard_map/ppermute | solution.py:255
  4.1 10.9 %collective-permute-start.2 = (bf16[3,128,128]{2,1,0:T(8,128)(2,1)S(1)}, bf16[3,128,128]{2,1,0:T(8,128)(2,1)S(1)}, u32[]{:S(2)}, u32[]{:S(2)}) collective-permute-start(bf16[3,128,128]{2,1,0:T(8,128)(2,1)S(1)} %load_v.5), channel_id=1, source_target_pairs={{0,2},{1,3},{2,0},{3,1},{4,6},{5,7},{6,4},{7,5},{8,10},{9,11},{10,... | collective-permute-start | bytes 294920 | tf_op jit(solution)/shard_map/ppermute | solution.py:255
  6.8 8.4 %collective-permute-start.4 = (bf16[3,128,128]{2,1,0:T(8,128)(2,1)S(1)}, bf16[3,128,128]{2,1,0:T(8,128)(2,1)S(1)}, u32[]{:S(2)}, u32[]{:S(2)}) collective-permute-start(bf16[3,128,128]{2,1,0:T(8,128)(2,1)S(1)} %load_v.6), channel_id=1, source_target_pairs={{0,3},{1,2},{2,1},{3,0},{4,7},{5,6},{6,5},{7,4},{8,11},{9,10},{10,... | collective-permute-start | bytes 294920 | tf_op jit(solution)/shard_map/ppermute | solution.py:255
  7.0 16.4 %collective-permute-start.1 = (bf16[3,128,128]{2,1,0:T(8,128)(2,1)S(1)}, bf16[3,128,128]{2,1,0:T(8,128)(2,1)S(1)}, u32[]{:S(2)}, u32[]{:S(2)}) collective-permute-start(bf16[3,128,128]{2,1,0:T(8,128)(2,1)S(1)} %load_k.5), channel_id=1, source_target_pairs={{0,1},{1,0},{2,3},{3,2},{4,5},{5,4},{6,7},{7,6},{8,9},{9,8},{10,11... | collective-permute-start | bytes 294920 | tf_op jit(solution)/shard_map/ppermute | solution.py:255
  15.1 8.4 %collective-permute-start.3 = (bf16[3,128,128]{2,1,0:T(8,128)(2,1)S(1)}, bf16[3,128,128]{2,1,0:T(8,128)(2,1)S(1)}, u32[]{:S(2)}, u32[]{:S(2)}) collective-permute-start(bf16[3,128,128]{2,1,0:T(8,128)(2,1)S(1)} %load_k.6), channel_id=1, source_target_pairs={{0,2},{1,3},{2,0},{3,1},{4,6},{5,7},{6,4},{7,5},{8,10},{9,11},{10,... | collective-permute-start | bytes 294920 | tf_op jit(solution)/shard_map/ppermute | solution.py:255
  15.3 8.2 %collective-permute-start.5 = (bf16[3,128,128]{2,1,0:T(8,128)(2,1)S(1)}, bf16[3,128,128]{2,1,0:T(8,128)(2,1)S(1)}, u32[]{:S(2)}, u32[]{:S(2)}) collective-permute-start(bf16[3,128,128]{2,1,0:T(8,128)(2,1)S(1)} %load_k.7), channel_id=1, source_target_pairs={{0,3},{1,2},{2,1},{3,0},{4,7},{5,6},{6,5},{7,4},{8,11},{9,10},{10,... | collective-permute-start | bytes 294920 | tf_op jit(solution)/shard_map/ppermute | solution.py:255
  19.8 10.2 %collective-permute-start.8 = (bf16[8,128,128]{2,1,0:T(8,128)(2,1)S(1)}, bf16[8,128,128]{2,1,0:T(8,128)(2,1)S(1)}, u32[]{:S(2)}, u32[]{:S(2)}) collective-permute-start(bf16[8,128,128]{2,1,0:T(8,128)(2,1)S(1)} %get-tuple-element.11), channel_id=1, source_target_pairs={{4,8},{8,4},{5,9},{9,5},{6,10},{10,6},{7,11},{11,7},{20,24},{24,20... | collective-permute-start | bytes 786440 | tf_op jit(solution)/shard_map/ppermute | solution.py:226
  20.5 10.0 %collective-permute-start.9 = (bf16[8,128,128]{2,1,0:T(8,128)(2,1)S(1)}, bf16[8,128,128]{2,1,0:T(8,128)(2,1)S(1)}, u32[]{:S(2)}, u32[]{:S(2)}) collective-permute-start(bf16[8,128,128]{2,1,0:T(8,128)(2,1)S(1)} %get-tuple-element.12), channel_id=1, source_target_pairs={{0,4},{8,12},{4,0},{12,8},{1,5},{9,13},{5,1},{13,9},{2,6},{10,14},... | collective-permute-start | bytes 786440 | tf_op jit(solution)/shard_map/ppermute | solution.py:226
  23.5 3.4 %copy-start.1 = (bf16[384,512]{1,0:T(8,128)(2,1)S(1)}, bf16[384,512]{1,0:T(8,128)(2,1)}, u32[]{:S(2)}) copy-start(bf16[384,512]{1,0:T(8,128)(2,1)} %q_ref.7) | copy-start | bytes 1179652
  23.6 8.8 %collective-permute-start.6 = (bf16[8,128,128]{2,1,0:T(8,128)(2,1)S(1)}, bf16[8,128,128]{2,1,0:T(8,128)(2,1)S(1)}, u32[]{:S(2)}, u32[]{:S(2)}) collective-permute-start(bf16[8,128,128]{2,1,0:T(8,128)(2,1)S(1)} %get-tuple-element.9), channel_id=1, source_target_pairs={{4,8},{8,4},{5,9},{9,5},{6,10},{10,6},{7,11},{11,7},{20,24},{24,20... | collective-permute-start | bytes 786440 | tf_op jit(solution)/shard_map/ppermute | solution.py:226
  24.4 8.0 %collective-permute-start.7 = (bf16[8,128,128]{2,1,0:T(8,128)(2,1)S(1)}, bf16[8,128,128]{2,1,0:T(8,128)(2,1)S(1)}, u32[]{:S(2)}, u32[]{:S(2)}) collective-permute-start(bf16[8,128,128]{2,1,0:T(8,128)(2,1)S(1)} %get-tuple-element.10), channel_id=1, source_target_pairs={{0,4},{8,12},{4,0},{12,8},{1,5},{9,13},{5,1},{13,9},{2,6},{10,14},... | collective-permute-start | bytes 786440 | tf_op jit(solution)/shard_map/ppermute | solution.py:226
  27.0 6.8 %collective-permute-start.12 = (bf16[384,128]{1,0:T(8,128)(2,1)S(1)}, bf16[384,128]{1,0:T(8,128)(2,1)S(1)}, u32[]{:S(2)}, u32[]{:S(2)}) collective-permute-start(bf16[384,128]{1,0:T(8,128)(2,1)S(1)} %load_q.7), channel_id=1, source_target_pairs={{0,3},{1,2},{2,1},{3,0},{4,7},{5,6},{6,5},{7,4},{8,11},{9,10},{10,... | collective-permute-start | bytes 294920 | tf_op jit(solution)/shard_map/ppermute | solution.py:255
  30.0 10.6 %collective-permute-start.11 = (bf16[384,128]{1,0:T(8,128)(2,1)S(1)}, bf16[384,128]{1,0:T(8,128)(2,1)S(1)}, u32[]{:S(2)}, u32[]{:S(2)}) collective-permute-start(bf16[384,128]{1,0:T(8,128)(2,1)S(1)} %load_q.6), channel_id=1, source_target_pairs={{0,2},{1,3},{2,0},{3,1},{4,6},{5,7},{6,4},{7,5},{8,10},{9,11},{10,... | collective-permute-start | bytes 294920 | tf_op jit(solution)/shard_map/ppermute | solution.py:255
  30.4 1.2 %copy-start.4 = (s32[12]{0:T(128)S(1)}, s32[12]{0:T(128)}, u32[]{:S(2)}) copy-start(s32[12]{0:T(128)} %param.9) | copy-start | bytes 148
  30.4 1.3 %copy-start.3 = (s32[12,16]{1,0:T(8,128)S(1)}, s32[12,16]{1,0:T(8,128)}, u32[]{:S(2)}) copy-start(s32[12,16]{1,0:T(8,128)} %lists_ref.1) | copy-start | bytes 2308
  30.4 13.1 %collective-permute-start.10 = (bf16[384,128]{1,0:T(8,128)(2,1)S(1)}, bf16[384,128]{1,0:T(8,128)(2,1)S(1)}, u32[]{:S(2)}, u32[]{:S(2)}) collective-permute-start(bf16[384,128]{1,0:T(8,128)(2,1)S(1)} %load_q.5), channel_id=1, source_target_pairs={{0,1},{1,0},{2,3},{3,2},{4,5},{5,4},{6,7},{7,6},{8,9},{9,8},{10,11... | collective-permute-start | bytes 294920 | tf_op jit(solution)/shard_map/ppermute | solution.py:255
  35.5 13.7 %collective-permute-start.15 = (bf16[384,128]{1,0:T(8,128)(2,1)S(1)}, bf16[384,128]{1,0:T(8,128)(2,1)S(1)}, u32[]{:S(2)}, u32[]{:S(2)}) collective-permute-start(bf16[384,128]{1,0:T(8,128)(2,1)S(1)} %attend_chunk.4.refs_0_), channel_id=1, source_target_pairs={{0,3},{1,2},{2,1},{3,0},{4,7},{5,6},{6,5},{7,4},{8,11},{9,10},{10,... | collective-permute-start | bytes 294920 | tf_op jit(solution)/shard_map/ppermute | solution.py:255
  42.4 7.0 %collective-permute-start.14 = (bf16[384,128]{1,0:T(8,128)(2,1)S(1)}, bf16[384,128]{1,0:T(8,128)(2,1)S(1)}, u32[]{:S(2)}, u32[]{:S(2)}) collective-permute-start(bf16[384,128]{1,0:T(8,128)(2,1)S(1)} %attend_chunk.5.refs_0_), channel_id=1, source_target_pairs={{0,2},{1,3},{2,0},{3,1},{4,6},{5,7},{6,4},{7,5},{8,10},{9,11},{10,... | collective-permute-start | bytes 294920 | tf_op jit(solution)/shard_map/ppermute | solution.py:255
  45.3 5.2 %collective-permute-start.13 = (bf16[384,128]{1,0:T(8,128)(2,1)S(1)}, bf16[384,128]{1,0:T(8,128)(2,1)S(1)}, u32[]{:S(2)}, u32[]{:S(2)}) collective-permute-start(bf16[384,128]{1,0:T(8,128)(2,1)S(1)} %attend_chunk.6.refs_0_), channel_id=1, source_target_pairs={{0,1},{1,0},{2,3},{3,2},{4,5},{5,4},{6,7},{7,6},{8,9},{9,8},{10,11... | collective-permute-start | bytes 294920 | tf_op jit(solution)/shard_map/ppermute | solution.py:255

commit v11 on v9

--- a/solution.py
+++ b/solution.py
@@ -185,10 +185,13 @@
 
 
 def gather_kernel(*refs):
-    *parts, own_ref, odd_ref, even_ref = refs
+    *parts, own_ref = refs
     me = lax.axis_index("head")
     for pair, part in enumerate(parts):
         own_ref[:, pl.ds((me ^ pair) * BLOCK, BLOCK)] = part[...]
+
+
+def edges_kernel(own_ref, odd_ref, even_ref):
     last = own_ref.shape[1] - EDGE
     odd = lax.rem(lax.axis_index("ctx"), 2)
     odd_ref[...] = own_ref[:, pl.ds(odd * last, EDGE)]
@@ -213,6 +216,11 @@
         around(first_ref, second_ref)
 
 
+def stack_kernel(*refs):
+    for at, ref in enumerate(refs[:-1]):
+        refs[-1][at] = ref[...]
+
+
 def pass_kernel(array_ref, *refs):
     refs[-1][...] = array_ref[...]
 
@@ -220,7 +228,7 @@
 def attend_chunk_kernel(pair, q_ref, kv_ref, bias_ref, *refs):
     out_ref, *scratch = refs[-3:]
     first = (lax.axis_index("head") ^ pair) * BLOCK
-    attend_block(first, q_ref, kv_ref.at[0], kv_ref.at[1], bias_ref, out_ref, *scratch)
+    attend_block(first, q_ref.at[pair], kv_ref.at[0], kv_ref.at[1], bias_ref, out_ref, *scratch)
 
 
 def spread_kernel(*refs):
@@ -256,9 +264,9 @@
         part = call(functools.partial(load_q_kernel, pair), "load_q", operands, [VMEM] * len(operands), chunk)
         q_parts[pair] = exchange(part, pair) if pair else part
     edge = (2, EDGE, TILE, HDIM)
-    own, odd_edge, even_edge = call(
-        gather_kernel, "gather", kv_parts, [VMEM] * heads, [(2, tiles, TILE, HDIM), edge, edge]
-    )
+    own = call(gather_kernel, "gather", kv_parts, [VMEM] * heads, (2, tiles, TILE, HDIM))
+    odd_edge, even_edge = call(edges_kernel, "edges", (own,), [VMEM], [edge, edge])
+    local_q = call(stack_kernel, "stack", q_parts, [VMEM] * heads, (heads, *chunk), cost=cost(1 << 14))
     first, second = exchange_ctx(odd_edge, 1), exchange_ctx(even_edge, 0)
     padded = call(
         join_kernel, "join", (own, first, second), [VMEM] * 3, (2, tiles + LIST - 1, TILE, HDIM)
@@ -266,7 +274,7 @@
     outs = [None] * heads
     after = ()
     for pair in [*order, 0]:
-        operands = (q_parts[pair], padded, bias, *after)
+        operands = (local_q, padded, bias, *after)
         outs[pair] = call(
             functools.partial(attend_chunk_kernel, pair),
             "attend_chunk",

time: 51.5 us -> 54.9 us (1.066)
  the two profiles are of different devices: /device:TPU:0 before, /device:TPU:2 now
where the time goes in v11:
time: 54.9 us; the launch traced here: 54.8 us
  waiting for transfers between devices  26.2 us (48%)
  starting transfers between devices  17.1 us (31%)
  Pallas kernels  9.12 us (17%)
  local copies, waits for them, and re-layouts  2.16 us (4%)
    ppermute x9, waiting for transfers between devices, exchange(): return lax.ppermute(array, 'head', [(i, i ^ pair) for i in range(heads)])  19.7 us
    ppermute x9, starting transfers between devices, exchange(): return lax.ppermute(array, 'head', [(i, i ^ pair) for i in range(heads)])  15.1 us
    pallas_call x21, Pallas kernels, call(): pl.pallas_call(kernel, out_shape=out_shape, in_specs=in_specs, out_specs=...  9.12 us
    ppermute x2, waiting for transfers between devices, exchange_ctx(): lax.ppermute(array, 'ctx', [(i, i + 1) for i in lower] + [(i + 1, i) for...  6.46 us
    unnamed x12, local copies, waits for them, and re-layouts  2.06 us
    ppermute x2, starting transfers between devices, exchange_ctx(): lax.ppermute(array, 'ctx', [(i, i + 1) for i in lower] + [(i + 1, i) for...  1.99 us
  transfers between devices with their start and end apart: 11, of which 6 were waited for; matrix products, arithmetic and copies ran while one was open for 0% of the time, Pallas kernels for 11%

profile of v11, /device:TPU:2, one launch (start us, length us, event | category | flops | bytes accessed | tf_op | source)
XLA Modules:
  0.0 54.8 jit_solution(13522649930051292964)
XLA Ops:
  0.0 0.0 copy-start
  0.0 0.0 copy-start.1
  0.0 1.0 %copy-done.1 = bf16[384,512]{1,0:T(8,128)(2,1)S(1)} copy-done((bf16[384,512]{1,0:T(8,128)(2,1)S(1)}, bf16[384,512]{1,0:T(8,128)(2,1)}, u32[]{:S(2)}) %copy-start.1) | copy-done | bytes 393240
  1.1 0.0 copy-start.2
  1.1 1.0 %copy-done.2 = bf16[384,512]{1,0:T(8,128)(2,1)S(1)} copy-done((bf16[384,512]{1,0:T(8,128)(2,1)S(1)}, bf16[384,512]{1,0:T(8,128)(2,1)}, u32[]{:S(2)}) %copy-start.2) | copy-done | bytes 393240
  2.0 0.1 load_kv.4.refs_0_
  2.1 0.1 load_kv.5.refs_0_
  2.3 0.0 copy-start.3
  2.3 0.1 load_kv.6.refs_0_
  2.4 0.0 copy-start.5
  2.4 0.0 copy-start.4
  2.4 1.6 %collective-permute-start = (bf16[2,3,128,128]{3,2,1,0:T(8,128)(2,1)S(1)}, bf16[2,3,128,128]{3,2,1,0:T(8,128)(2,1)S(1)}, u32[]{:S(2)}, u32[]{:S(2)}) collective-permute-start(bf16[2,3,128,128]{3,2,1,0:T(8,128)(2,1)S(1)} %load_kv.6.refs_0_), channel_id=1, source_target_pairs={{0,1},{1,0},{2,3},{3,2},{4,5},{5,4},{6,7},{7,6},{8,9},{9,8},{10,11... | collective-permute-start | bytes 589832 | tf_op jit(solution)/shard_map/ppermute | solution.py:247
  4.1 2.6 %collective-permute-start.2 = (bf16[2,3,128,128]{3,2,1,0:T(8,128)(2,1)S(1)}, bf16[2,3,128,128]{3,2,1,0:T(8,128)(2,1)S(1)}, u32[]{:S(2)}, u32[]{:S(2)}) collective-permute-start(bf16[2,3,128,128]{3,2,1,0:T(8,128)(2,1)S(1)} %load_kv.5.refs_0_), channel_id=1, source_target_pairs={{0,2},{1,3},{2,0},{3,1},{4,6},{5,7},{6,4},{7,5},{8,10},{9,11},{10,... | collective-permute-start | bytes 589832 | tf_op jit(solution)/shard_map/ppermute | solution.py:247
  6.6 0.2 collective-permute-start.4
  6.9 5.7 %collective-permute-done.refs_0_.refs_1_ = bf16[2,3,128,128]{3,2,1,0:T(8,128)(2,1)S(1)} collective-permute-done((bf16[2,3,128,128]{3,2,1,0:T(8,128)(2,1)S(1)}, bf16[2,3,128,128]{3,2,1,0:T(8,128)(2,1)S(1)}, u32[]{:S(2)}, u32[]{:S(2)}) %collective-permute-start) | collective-permute-done | bytes 196640 | tf_op jit(solution)/shard_map/ppermute | solution.py:247
  12.6 0.0 copy-done
  12.6 0.1 collective-permute-start.1
  12.7 9.2 %collective-permute-done.2.refs_0_.refs_2_ = bf16[2,3,128,128]{3,2,1,0:T(8,128)(2,1)S(1)} collective-permute-done((bf16[2,3,128,128]{3,2,1,0:T(8,128)(2,1)S(1)}, bf16[2,3,128,128]{3,2,1,0:T(8,128)(2,1)S(1)}, u32[]{:S(2)}, u32[]{:S(2)}) %collective-permute-start.2) | collective-permute-done | bytes 196640 | tf_op jit(solution)/shard_map/ppermute | solution.py:247
  21.9 0.1 collective-permute-start.3
  22.0 0.0 collective-permute-done.4.refs_0_.refs_3_
  22.0 4.0 %collective-permute-start.5 = (bf16[384,128]{1,0:T(8,128)(2,1)S(1)}, bf16[384,128]{1,0:T(8,128)(2,1)S(1)}, u32[]{:S(2)}, u32[]{:S(2)}) collective-permute-start(bf16[384,128]{1,0:T(8,128)(2,1)S(1)} %load_q.7), channel_id=1, source_target_pairs={{0,3},{1,2},{2,1},{3,0},{4,7},{5,6},{6,5},{7,4},{8,11},{9,10},{10,... | collective-permute-start | bytes 294920 | tf_op jit(solution)/shard_map/ppermute | solution.py:247
  26.1 0.0 copy-done.3
  26.1 0.1 load_kv.7.refs_0_
  26.2 0.0 copy-done.5
  26.2 0.1 copy.6.counts_ref
  26.3 0.0 copy-done.4
  26.3 0.6 %mask_bias.1.bias_ref = f32[27,12,128]{2,1,0:T(8,128)S(1)} custom-call(s32[12,16]{1,0:T(8,128)S(1)} %copy-done.4, s32[12,1]{1,0:T(8,128)S(1)} %copy.6.counts_ref), custom_call_target="tpu_custom_call" | custom-call | tf_op jit(solution)/shard_map/mask_bias/pallas_call | solution.py:29
  26.9 0.1 gather.1.own_ref
  26.9 0.1 edges.1
  27.0 1.9 %collective-permute-start.6 = (bf16[2,8,128,128]{3,2,1,0:T(8,128)(2,1)S(1)}, bf16[2,8,128,128]{3,2,1,0:T(8,128)(2,1)S(1)}, u32[]{:S(2)}, u32[]{:S(2)}) collective-permute-start(bf16[2,8,128,128]{3,2,1,0:T(8,128)(2,1)S(1)} %get-tuple-element.7), channel_id=1, source_target_pairs={{4,8},{8,4},{5,9},{9,5},{6,10},{10,6},{7,11},{11,7},{20,24},{24,20... | collective-permute-start | bytes 1572872 | tf_op jit(solution)/shard_map/ppermute | solution.py:251
  29.0 0.1 collective-permute-start.7
  29.0 0.0 collective-permute-done.1.refs_1_
  29.1 2.0 %collective-permute-done.3.refs_2_ = bf16[384,128]{1,0:T(8,128)(2,1)S(1)} collective-permute-done((bf16[384,128]{1,0:T(8,128)(2,1)S(1)}, bf16[384,128]{1,0:T(8,128)(2,1)S(1)}, u32[]{:S(2)}, u32[]{:S(2)}) %collective-permute-start.3) | collective-permute-done | bytes 98336 | tf_op jit(solution)/shard_map/ppermute | solution.py:247
  31.0 0.0 collective-permute-done.5.refs_3_
  31.1 6.5 %collective-permute-done.6.first_ref = bf16[2,8,128,128]{3,2,1,0:T(8,128)(2,1)S(1)} collective-permute-done((bf16[2,8,128,128]{3,2,1,0:T(8,128)(2,1)S(1)}, bf16[2,8,128,128]{3,2,1,0:T(8,128)(2,1)S(1)}, u32[]{:S(2)}, u32[]{:S(2)}) %collective-permute-start.6) | collective-permute-done | bytes 524320 | tf_op jit(solution)/shard_map/ppermute | solution.py:251
  37.5 0.0 collective-permute-done.7.second_ref
  37.5 0.1 join.1.kv_ref
  37.7 1.7 %attend_chunk.4.refs_0_ = bf16[384,128]{1,0:T(8,128)(2,1)S(1)} custom-call(bf16[4,384,128]{2,1,0:T(8,128)(2,1)S(1)} %stack.1.q_ref, bf16[2,27,128,128]{3,2,1,0:T(8,128)(2,1)S(1)} %join.1.kv_ref, f32[27,12,128]{2,1,0:T(8,128)S(1)} %mask_bias.1.bias_ref), custom_call_target="tpu_custom_call" | custom-call | flops 201326592 | bytes 393216 | tf_op jit(solution)/shard_map/attend_chunk/pallas_call | solution.py:29
  39.4 0.1 collective-permute-start.10
  39.5 1.7 %attend_chunk.5.refs_0_ = bf16[384,128]{1,0:T(8,128)(2,1)S(1)} custom-call(bf16[4,384,128]{2,1,0:T(8,128)(2,1)S(1)} %stack.1.q_ref, bf16[2,27,128,128]{3,2,1,0:T(8,128)(2,1)S(1)} %join.1.kv_ref, f32[27,12,128]{2,1,0:T(8,128)S(1)} %mask_bias.1.bias_ref, bf16[384,128]{1,0:T(8,128)(2,1)S(1)} %attend_chunk.4.refs_0_), custom_call_target="tpu_custom_call" | custom-call | flops 201326592 | bytes 393216 | tf_op jit(solution)/shard_map/attend_chunk/pallas_call | solution.py:29
  41.2 6.3 %collective-permute-start.9 = (bf16[384,128]{1,0:T(8,128)(2,1)S(1)}, bf16[384,128]{1,0:T(8,128)(2,1)S(1)}, u32[]{:S(2)}, u32[]{:S(2)}) collective-permute-start(bf16[384,128]{1,0:T(8,128)(2,1)S(1)} %attend_chunk.5.refs_0_), channel_id=1, source_target_pairs={{0,2},{1,3},{2,0},{3,1},{4,6},{5,7},{6,4},{7,5},{8,10},{9,11},{10,... | collective-permute-start | bytes 294920 | tf_op jit(solution)/shard_map/ppermute | solution.py:247
  47.5 1.7 %attend_chunk.6.refs_0_ = bf16[384,128]{1,0:T(8,128)(2,1)S(1)} custom-call(bf16[4,384,128]{2,1,0:T(8,128)(2,1)S(1)} %stack.1.q_ref, bf16[2,27,128,128]{3,2,1,0:T(8,128)(2,1)S(1)} %join.1.kv_ref, f32[27,12,128]{2,1,0:T(8,128)S(1)} %mask_bias.1.bias_ref, bf16[384,128]{1,0:T(8,128)(2,1)S(1)} %attend_chunk.5.refs_0_), custom_call_target="tpu_custom_call" | custom-call | flops 201326592 | bytes 393216 | tf_op jit(solution)/shard_map/attend_chunk/pallas_call | solution.py:29
  49.2 0.1 collective-permute-start.8
  49.3 1.7 %attend_chunk.7.refs_0_ = bf16[384,128]{1,0:T(8,128)(2,1)S(1)} custom-call(bf16[4,384,128]{2,1,0:T(8,128)(2,1)S(1)} %stack.1.q_ref, bf16[2,27,128,128]{3,2,1,0:T(8,128)(2,1)S(1)} %join.1.kv_ref, f32[27,12,128]{2,1,0:T(8,128)S(1)} %mask_bias.1.bias_ref, bf16[384,128]{1,0:T(8,128)(2,1)S(1)} %attend_chunk.6.refs_0_), custom_call_target="tpu_custom_call" | custom-call | flops 8388608 | bytes 16384 | tf_op jit(solution)/shard_map/attend_chunk/pallas_call | solution.py:29
  51.1 0.0 collective-permute-done.10.array_ref
  51.1 0.1 collective-permute-done.9.array_ref
  51.2 2.8 %collective-permute-done.8.array_ref = bf16[384,128]{1,0:T(8,128)(2,1)S(1)} collective-permute-done((bf16[384,128]{1,0:T(8,128)(2,1)S(1)}, bf16[384,128]{1,0:T(8,128)(2,1)S(1)}, u32[]{:S(2)}, u32[]{:S(2)}) %collective-permute-start.8) | collective-permute-done | bytes 98336 | tf_op jit(solution)/shard_map/ppermute | solution.py:247
  53.9 0.8 %spread.1 = bf16[384,512]{1,0:T(8,128)(2,1)} custom-call(bf16[384,128]{1,0:T(8,128)(2,1)S(1)} %attend_chunk.7.refs_0_, bf16[384,128]{1,0:T(8,128)(2,1)S(1)} %landed.5.refs_1_, bf16[384,128]{1,0:T(8,128)(2,1)S(1)} %landed.4.refs_0_.refs_2_, bf16[384,128]{1,0:T(8,128)(2,1)S(1)} %landed.3.refs_0_.refs_3_), custom_call_target="tpu_custom_call" | custom-call | tf_op jit(solution)/shard_map/spread/pallas_call | solution.py:29
  (8 shorter events, 0.1 us)
Async XLA Ops:
  0.0 12.6 %copy-start = (bf16[384,512]{1,0:T(8,128)(2,1)S(1)}, bf16[384,512]{1,0:T(8,128)(2,1)}, u32[]{:S(2)}) copy-start(bf16[384,512]{1,0:T(8,128)(2,1)} %q_ref.7) | copy-start | bytes 1179652
  0.0 1.0 %copy-start.1 = (bf16[384,512]{1,0:T(8,128)(2,1)S(1)}, bf16[384,512]{1,0:T(8,128)(2,1)}, u32[]{:S(2)}) copy-start(bf16[384,512]{1,0:T(8,128)(2,1)} %k_ref.7) | copy-start | bytes 1179652
  1.1 1.0 %copy-start.2 = (bf16[384,512]{1,0:T(8,128)(2,1)S(1)}, bf16[384,512]{1,0:T(8,128)(2,1)}, u32[]{:S(2)}) copy-start(bf16[384,512]{1,0:T(8,128)(2,1)} %v_ref.7) | copy-start | bytes 1179652
  2.3 23.8 %copy-start.3 = (bf16[384,512]{1,0:T(8,128)(2,1)S(1)}, bf16[384,512]{1,0:T(8,128)(2,1)}, u32[]{:S(2)}) copy-start(bf16[384,512]{1,0:T(8,128)(2,1)} %v_ref.7) | copy-start | bytes 1179652
  2.4 23.8 %copy-start.5 = (s32[12]{0:T(128)S(1)}, s32[12]{0:T(128)}, u32[]{:S(2)}) copy-start(s32[12]{0:T(128)} %param.9) | copy-start | bytes 148
  2.4 23.9 %copy-start.4 = (s32[12,16]{1,0:T(8,128)S(1)}, s32[12,16]{1,0:T(8,128)}, u32[]{:S(2)}) copy-start(s32[12,16]{1,0:T(8,128)} %lists_ref.1) | copy-start | bytes 2308
  2.4 10.2 %collective-permute-start = (bf16[2,3,128,128]{3,2,1,0:T(8,128)(2,1)S(1)}, bf16[2,3,128,128]{3,2,1,0:T(8,128)(2,1)S(1)}, u32[]{:S(2)}, u32[]{:S(2)}) collective-permute-start(bf16[2,3,128,128]{3,2,1,0:T(8,128)(2,1)S(1)} %load_kv.6.refs_0_), channel_id=1, source_target_pairs={{0,1},{1,0},{2,3},{3,2},{4,5},{5,4},{6,7},{7,6},{8,9},{9,8},{10,11... | collective-permute-start | bytes 589832 | tf_op jit(solution)/shard_map/ppermute | solution.py:247
  4.1 17.8 %collective-permute-start.2 = (bf16[2,3,128,128]{3,2,1,0:T(8,128)(2,1)S(1)}, bf16[2,3,128,128]{3,2,1,0:T(8,128)(2,1)S(1)}, u32[]{:S(2)}, u32[]{:S(2)}) collective-permute-start(bf16[2,3,128,128]{3,2,1,0:T(8,128)(2,1)S(1)} %load_kv.5.refs_0_), channel_id=1, source_target_pairs={{0,2},{1,3},{2,0},{3,1},{4,6},{5,7},{6,4},{7,5},{8,10},{9,11},{10,... | collective-permute-start | bytes 589832 | tf_op jit(solution)/shard_map/ppermute | solution.py:247
  6.6 15.3 %collective-permute-start.4 = (bf16[2,3,128,128]{3,2,1,0:T(8,128)(2,1)S(1)}, bf16[2,3,128,128]{3,2,1,0:T(8,128)(2,1)S(1)}, u32[]{:S(2)}, u32[]{:S(2)}) collective-permute-start(bf16[2,3,128,128]{3,2,1,0:T(8,128)(2,1)S(1)} %load_kv.4.refs_0_), channel_id=1, source_target_pairs={{0,3},{1,2},{2,1},{3,0},{4,7},{5,6},{6,5},{7,4},{8,11},{9,10},{10,... | collective-permute-start | bytes 589832 | tf_op jit(solution)/shard_map/ppermute | solution.py:247
  12.6 16.5 %collective-permute-start.1 = (bf16[384,128]{1,0:T(8,128)(2,1)S(1)}, bf16[384,128]{1,0:T(8,128)(2,1)S(1)}, u32[]{:S(2)}, u32[]{:S(2)}) collective-permute-start(bf16[384,128]{1,0:T(8,128)(2,1)S(1)} %load_q.5), channel_id=1, source_target_pairs={{0,1},{1,0},{2,3},{3,2},{4,5},{5,4},{6,7},{7,6},{8,9},{9,8},{10,11... | collective-permute-start | bytes 294920 | tf_op jit(solution)/shard_map/ppermute | solution.py:247
  21.9 9.1 %collective-permute-start.3 = (bf16[384,128]{1,0:T(8,128)(2,1)S(1)}, bf16[384,128]{1,0:T(8,128)(2,1)S(1)}, u32[]{:S(2)}, u32[]{:S(2)}) collective-permute-start(bf16[384,128]{1,0:T(8,128)(2,1)S(1)} %load_q.6), channel_id=1, source_target_pairs={{0,2},{1,3},{2,0},{3,1},{4,6},{5,7},{6,4},{7,5},{8,10},{9,11},{10,... | collective-permute-start | bytes 294920 | tf_op jit(solution)/shard_map/ppermute | solution.py:247
  22.0 9.0 %collective-permute-start.5 = (bf16[384,128]{1,0:T(8,128)(2,1)S(1)}, bf16[384,128]{1,0:T(8,128)(2,1)S(1)}, u32[]{:S(2)}, u32[]{:S(2)}) collective-permute-start(bf16[384,128]{1,0:T(8,128)(2,1)S(1)} %load_q.7), channel_id=1, source_target_pairs={{0,3},{1,2},{2,1},{3,0},{4,7},{5,6},{6,5},{7,4},{8,11},{9,10},{10,... | collective-permute-start | bytes 294920 | tf_op jit(solution)/shard_map/ppermute | solution.py:247
  27.0 10.5 %collective-permute-start.6 = (bf16[2,8,128,128]{3,2,1,0:T(8,128)(2,1)S(1)}, bf16[2,8,128,128]{3,2,1,0:T(8,128)(2,1)S(1)}, u32[]{:S(2)}, u32[]{:S(2)}) collective-permute-start(bf16[2,8,128,128]{3,2,1,0:T(8,128)(2,1)S(1)} %get-tuple-element.7), channel_id=1, source_target_pairs={{4,8},{8,4},{5,9},{9,5},{6,10},{10,6},{7,11},{11,7},{20,24},{24,20... | collective-permute-start | bytes 1572872 | tf_op jit(solution)/shard_map/ppermute | solution.py:251
  29.0 8.6 %collective-permute-start.7 = (bf16[2,8,128,128]{3,2,1,0:T(8,128)(2,1)S(1)}, bf16[2,8,128,128]{3,2,1,0:T(8,128)(2,1)S(1)}, u32[]{:S(2)}, u32[]{:S(2)}) collective-permute-start(bf16[2,8,128,128]{3,2,1,0:T(8,128)(2,1)S(1)} %get-tuple-element.8), channel_id=1, source_target_pairs={{0,4},{8,12},{4,0},{12,8},{1,5},{9,13},{5,1},{13,9},{2,6},{10,14},... | collective-permute-start | bytes 1572872 | tf_op jit(solution)/shard_map/ppermute | solution.py:251
  39.4 11.7 %collective-permute-start.10 = (bf16[384,128]{1,0:T(8,128)(2,1)S(1)}, bf16[384,128]{1,0:T(8,128)(2,1)S(1)}, u32[]{:S(2)}, u32[]{:S(2)}) collective-permute-start(bf16[384,128]{1,0:T(8,128)(2,1)S(1)} %attend_chunk.4.refs_0_), channel_id=1, source_target_pairs={{0,3},{1,2},{2,1},{3,0},{4,7},{5,6},{6,5},{7,4},{8,11},{9,10},{10,... | collective-permute-start | bytes 294920 | tf_op jit(solution)/shard_map/ppermute | solution.py:247
  41.2 10.0 %collective-permute-start.9 = (bf16[384,128]{1,0:T(8,128)(2,1)S(1)}, bf16[384,128]{1,0:T(8,128)(2,1)S(1)}, u32[]{:S(2)}, u32[]{:S(2)}) collective-permute-start(bf16[384,128]{1,0:T(8,128)(2,1)S(1)} %attend_chunk.5.refs_0_), channel_id=1, source_target_pairs={{0,2},{1,3},{2,0},{3,1},{4,6},{5,7},{6,4},{7,5},{8,10},{9,11},{10,... | collective-permute-start | bytes 294920 | tf_op jit(solution)/shard_map/ppermute | solution.py:247
  49.2 4.7 %collective-permute-start.8 = (bf16[384,128]{1,0:T(8,128)(2,1)S(1)}, bf16[384,128]{1,0:T(8,128)(2,1)S(1)}, u32[]{:S(2)}, u32[]{:S(2)}) collective-permute-start(bf16[384,128]{1,0:T(8,128)(2,1)S(1)} %attend_chunk.6.refs_0_), channel_id=1, source_target_pairs={{0,1},{1,0},{2,3},{3,2},{4,5},{5,4},{6,7},{7,6},{8,9},{9,8},{10,11... | collective-permute-start | bytes 294920 | tf_op jit(solution)/shard_map/ppermute | solution.py:247

commit v12 on v10

--- a/solution.py
+++ b/solution.py
@@ -172,13 +172,20 @@
     return call(functools.partial(unpack_kernel, heads), "unpack", (back,), [VMEM], (rows, columns))
 
 
-def load_tiles_kernel(pair, turn, array_ref, *refs):
+def load_tiles_kernel(pair, array_ref, *refs, turn):
     columns = column_of(lax.axis_index("head") ^ pair)
     for tile in range(BLOCK):
         part = array_ref[rows_of(tile), columns]
         refs[-1][tile] = part.T if turn else part
 
 
+def load_kq_kernel(pair, k_ref, q_ref, *refs):
+    columns = column_of(lax.axis_index("head") ^ pair)
+    for tile in range(BLOCK):
+        refs[-1][tile] = k_ref[rows_of(tile), columns].T
+        refs[-1][BLOCK + tile] = q_ref[rows_of(tile), columns]
+
+
 def load_q_kernel(pair, q_ref, *refs):
     refs[-1][...] = q_ref[:, column_of(lax.axis_index("head") ^ pair)]
 
@@ -187,7 +194,7 @@
     *parts, own_ref = refs
     me = lax.axis_index("head")
     for pair, part in enumerate(parts):
-        own_ref[pl.ds((me ^ pair) * BLOCK, BLOCK)] = part[...]
+        own_ref[pl.ds((me ^ pair) * BLOCK, BLOCK)] = part[:BLOCK]
 
 
 def edges_kernel(own_ref, odd_ref, even_ref):
@@ -229,6 +236,16 @@
     return call(join_kernel, "join", operands, [VMEM] * 3, (tiles + LIST - 1, TILE, HDIM))
 
 
+def stack_kernel(*refs):
+    *q_refs, out_ref = refs
+    for at, ref in enumerate(q_refs):
+        if len(ref.shape) == 2:
+            out_ref[at] = ref[...]
+        else:
+            for tile in range(BLOCK):
+                out_ref[at, rows_of(tile), :] = ref[BLOCK + tile]
+
+
 def pass_kernel(array_ref, *refs):
     refs[-1][...] = array_ref[...]
 
@@ -236,7 +253,7 @@
 def attend_chunk_kernel(pair, q_ref, kt_ref, v_ref, bias_ref, *refs):
     out_ref, *scratch = refs[-3:]
     first = (lax.axis_index("head") ^ pair) * BLOCK
-    attend_block(first, q_ref, kt_ref, v_ref, bias_ref, out_ref, *scratch)
+    attend_block(first, q_ref.at[pair], kt_ref, v_ref, bias_ref, out_ref, *scratch)
 
 
 def spread_kernel(*refs):
@@ -259,21 +276,29 @@
 
     v_parts, k_parts, q_parts = [None] * heads, [None] * heads, [None] * heads
     for pair in [*order, 0]:
-        part = call_on(functools.partial(load_tiles_kernel, pair, False), "load_v", (values,), tiles)
+        part = call_on(functools.partial(load_tiles_kernel, pair, turn=False), "load_v", (values,), tiles)
         v_parts[pair] = exchange(part, pair) if pair else part
     for pair in [*order, 0]:
-        operands = (keys, v_parts[pair]) if pair else (keys,)
-        part = call_on(functools.partial(load_tiles_kernel, pair, True), "load_k", operands, tiles)
+        operands = (keys, queries) if pair == 1 else (keys,)
+        kernel = load_kq_kernel if pair == 1 else functools.partial(load_tiles_kernel, turn=True)
+        shape = (len(operands) * BLOCK, TILE, HDIM)
+        after = (v_parts[pair],) if pair else ()
+        part = call_on(functools.partial(kernel, pair), "load_k", (*operands, *after), shape)
         k_parts[pair] = exchange(part, pair) if pair else part
-    for pair in [*order, 0]:
+    q_parts[1] = k_parts[1]
+    for pair in [*order[:-1], 0]:
         operands = (queries, k_parts[pair]) if pair else (queries,)
         part = call_on(functools.partial(load_q_kernel, pair), "load_q", operands, chunk)
         q_parts[pair] = exchange(part, pair) if pair else part
     all_values, all_keys = with_halo(v_parts), with_halo(k_parts)
+    local_q = call(stack_kernel, "stack", q_parts, [VMEM] * heads, (heads, *chunk), cost=cost(100))
+    all_values = call(
+        pass_kernel, "values", (all_values, local_q), [VMEM] * 2, all_values.shape, cost=cost(16384)
+    )
     outs = [None] * heads
     after = ()
     for pair in [*order, 0]:
-        operands = (q_parts[pair], all_keys, all_values, bias, *after)
+        operands = (local_q, all_keys, all_values, bias, *after)
         outs[pair] = call(
             functools.partial(attend_chunk_kernel, pair),
             "attend_chunk",

time: 51.5 us -> 51.5 us (level)
  starting transfers between devices: 30.8 us -> 24.4 us
  waiting for transfers between devices: 10 us -> 15.8 us
  local copies, waits for them, and re-layouts: 1.11 us -> 1.7 us
    ppermute x12 -> x11, waiting for transfers between devices: 10 us -> 14.5 us  [exchange(): return lax.ppermute(array, 'head', [(i, i ^ pair) for i in range(heads)])]
    ppermute x12 -> x11, starting transfers between devices: 23.9 us -> 20.2 us  [exchange(): return lax.ppermute(array, 'head', [(i, i ^ pair) for i in range(heads)])]
    ppermute x4, starting transfers between devices: 6.92 us -> 4.26 us  [exchange(): lax.ppermute(array, 'ctx', [(i, i + 1) for i in lower] + [(i + 1, i) for...]
    ppermute x4, waiting for transfers between devices: 0.01 us -> 1.34 us  [exchange(): lax.ppermute(array, 'ctx', [(i, i + 1) for i in lower] + [(i + 1, i) for...]
    unnamed x10, local copies, waits for them, and re-layouts: 1.02 us -> 1.61 us
    pallas_call x27 -> x28, Pallas kernels: 9.12 us -> 9.04 us  [call(): pl.pallas_call(kernel, out_shape=out_shape, in_specs=in_specs, out_specs=...]
  transfers between devices with their start and end apart: 16 -> 15, of which waited for: 5 -> 6; matrix products, arithmetic and copies ran while one was open for 0% -> 0% of each run, Pallas kernels for 16% -> 13%
where the time goes in v12:
time: 51.5 us; the launch traced here: 51.2 us
  starting transfers between devices  24.4 us (47%)
  waiting for transfers between devices  15.8 us (31%)
  Pallas kernels  9.04 us (18%)
  local copies, waits for them, and re-layouts  1.7 us (3%)
    ppermute x11, starting transfers between devices, exchange(): return lax.ppermute(array, 'head', [(i, i ^ pair) for i in range(heads)])  20.2 us
    ppermute x11, waiting for transfers between devices, exchange(): return lax.ppermute(array, 'head', [(i, i ^ pair) for i in range(heads)])  14.5 us
    pallas_call x28, Pallas kernels, call(): pl.pallas_call(kernel, out_shape=out_shape, in_specs=in_specs, out_specs=...  9.04 us
    ppermute x4, starting transfers between devices, exchange(): lax.ppermute(array, 'ctx', [(i, i + 1) for i in lower] + [(i + 1, i) for...  4.26 us
    unnamed x10, local copies, waits for them, and re-layouts  1.61 us
    ppermute x4, waiting for transfers between devices, exchange(): lax.ppermute(array, 'ctx', [(i, i + 1) for i in lower] + [(i + 1, i) for...  1.34 us
  transfers between devices with their start and end apart: 15, of which 6 were waited for; matrix products, arithmetic and copies ran while one was open for 0% of the time, Pallas kernels for 13%

profile of v12, /device:TPU:0, one launch (start us, length us, event | category | flops | bytes accessed | tf_op | source)
XLA Modules:
  0.0 51.2 jit_solution(403851841994930110)
XLA Ops:
  0.0 1.0 %copy-done.2 = bf16[384,512]{1,0:T(8,128)(2,1)S(1)} copy-done((bf16[384,512]{1,0:T(8,128)(2,1)S(1)}, bf16[384,512]{1,0:T(8,128)(2,1)}, u32[]{:S(2)}) %copy-start.2) | copy-done | bytes 393240
  1.0 0.0 copy-start
  1.0 0.0 copy-start.1
  1.0 3.1 %collective-permute-start = (bf16[3,128,128]{2,1,0:T(8,128)(2,1)S(1)}, bf16[3,128,128]{2,1,0:T(8,128)(2,1)S(1)}, u32[]{:S(2)}, u32[]{:S(2)}) collective-permute-start(bf16[3,128,128]{2,1,0:T(8,128)(2,1)S(1)} %load_v.4), channel_id=1, source_target_pairs={{0,1},{1,0},{2,3},{3,2},{4,5},{5,4},{6,7},{7,6},{8,9},{9,8},{10,11... | collective-permute-start | bytes 294920 | tf_op jit(solution)/shard_map/ppermute | solution.py:272
  4.2 2.7 %collective-permute-start.2 = (bf16[3,128,128]{2,1,0:T(8,128)(2,1)S(1)}, bf16[3,128,128]{2,1,0:T(8,128)(2,1)S(1)}, u32[]{:S(2)}, u32[]{:S(2)}) collective-permute-start(bf16[3,128,128]{2,1,0:T(8,128)(2,1)S(1)} %load_v.5), channel_id=1, source_target_pairs={{0,2},{1,3},{2,0},{3,1},{4,6},{5,7},{6,4},{7,5},{8,10},{9,11},{10,... | collective-permute-start | bytes 294920 | tf_op jit(solution)/shard_map/ppermute | solution.py:272
  6.8 0.1 collective-permute-start.5
  6.9 0.0 collective-permute-done.refs_0_.refs_1_
  6.9 0.1 load_k.4
  7.1 1.9 %collective-permute-start.1 = (bf16[6,128,128]{2,1,0:T(8,128)(2,1)S(1)}, bf16[6,128,128]{2,1,0:T(8,128)(2,1)S(1)}, u32[]{:S(2)}, u32[]{:S(2)}) collective-permute-start(bf16[6,128,128]{2,1,0:T(8,128)(2,1)S(1)} %load_k.4), channel_id=1, source_target_pairs={{0,1},{1,0},{2,3},{3,2},{4,5},{5,4},{6,7},{7,6},{8,9},{9,8},{10,11... | collective-permute-start | bytes 589832 | tf_op jit(solution)/shard_map/ppermute | solution.py:272
  8.9 5.8 %collective-permute-done.2.refs_0_.refs_2_ = bf16[3,128,128]{2,1,0:T(8,128)(2,1)S(1)} collective-permute-done((bf16[3,128,128]{2,1,0:T(8,128)(2,1)S(1)}, bf16[3,128,128]{2,1,0:T(8,128)(2,1)S(1)}, u32[]{:S(2)}, u32[]{:S(2)}) %collective-permute-start.2) | collective-permute-done | bytes 98336 | tf_op jit(solution)/shard_map/ppermute | solution.py:272
  14.7 0.1 load_k.5
  14.8 0.1 collective-permute-start.3
  14.9 0.0 collective-permute-done.5.refs_0_.refs_3_
  14.9 0.1 load_k.6
  15.0 2.6 %collective-permute-start.6 = (bf16[3,128,128]{2,1,0:T(8,128)(2,1)S(1)}, bf16[3,128,128]{2,1,0:T(8,128)(2,1)S(1)}, u32[]{:S(2)}, u32[]{:S(2)}) collective-permute-start(bf16[3,128,128]{2,1,0:T(8,128)(2,1)S(1)} %load_k.6), channel_id=1, source_target_pairs={{0,3},{1,2},{2,1},{3,0},{4,7},{5,6},{6,5},{7,4},{8,11},{9,10},{10,... | collective-permute-start | bytes 294920 | tf_op jit(solution)/shard_map/ppermute | solution.py:272
  17.7 0.7 %collective-permute-start.10 = (bf16[8,128,128]{2,1,0:T(8,128)(2,1)S(1)}, bf16[8,128,128]{2,1,0:T(8,128)(2,1)S(1)}, u32[]{:S(2)}, u32[]{:S(2)}) collective-permute-start(bf16[8,128,128]{2,1,0:T(8,128)(2,1)S(1)} %get-tuple-element.11), channel_id=1, source_target_pairs={{4,8},{8,4},{5,9},{9,5},{6,10},{10,6},{7,11},{11,7},{20,24},{24,20... | collective-permute-start | bytes 786440 | tf_op jit(solution)/shard_map/ppermute | solution.py:233
  18.4 2.9 %collective-permute-start.11 = (bf16[8,128,128]{2,1,0:T(8,128)(2,1)S(1)}, bf16[8,128,128]{2,1,0:T(8,128)(2,1)S(1)}, u32[]{:S(2)}, u32[]{:S(2)}) collective-permute-start(bf16[8,128,128]{2,1,0:T(8,128)(2,1)S(1)} %get-tuple-element.12), channel_id=1, source_target_pairs={{0,4},{8,12},{4,0},{12,8},{1,5},{9,13},{5,1},{13,9},{2,6},{10,14},... | collective-permute-start | bytes 786440 | tf_op jit(solution)/shard_map/ppermute | solution.py:233
  21.3 2.0 %collective-permute-done.3.refs_0_.refs_2_ = bf16[3,128,128]{2,1,0:T(8,128)(2,1)S(1)} collective-permute-done((bf16[3,128,128]{2,1,0:T(8,128)(2,1)S(1)}, bf16[3,128,128]{2,1,0:T(8,128)(2,1)S(1)}, u32[]{:S(2)}, u32[]{:S(2)}) %collective-permute-start.3) | collective-permute-done | bytes 98336 | tf_op jit(solution)/shard_map/ppermute | solution.py:272
  23.3 2.3 %collective-permute-start.4 = (bf16[384,128]{1,0:T(8,128)(2,1)S(1)}, bf16[384,128]{1,0:T(8,128)(2,1)S(1)}, u32[]{:S(2)}, u32[]{:S(2)}) collective-permute-start(bf16[384,128]{1,0:T(8,128)(2,1)S(1)} %load_q.4), channel_id=1, source_target_pairs={{0,2},{1,3},{2,0},{3,1},{4,6},{5,7},{6,4},{7,5},{8,10},{9,11},{10,... | collective-permute-start | bytes 294920 | tf_op jit(solution)/shard_map/ppermute | solution.py:272
  25.6 0.0 collective-permute-done.6.refs_0_.refs_3_
  25.6 3.0 %collective-permute-start.7 = (bf16[384,128]{1,0:T(8,128)(2,1)S(1)}, bf16[384,128]{1,0:T(8,128)(2,1)S(1)}, u32[]{:S(2)}, u32[]{:S(2)}) collective-permute-start(bf16[384,128]{1,0:T(8,128)(2,1)S(1)} %load_q.5), channel_id=1, source_target_pairs={{0,3},{1,2},{2,1},{3,0},{4,7},{5,6},{6,5},{7,4},{8,11},{9,10},{10,... | collective-permute-start | bytes 294920 | tf_op jit(solution)/shard_map/ppermute | solution.py:272
  28.6 0.0 copy-start.4
  28.6 0.1 load_k.7.refs_0_
  28.7 0.0 copy-start.3
  28.7 0.5 %copy-done.4 = s32[12]{0:T(128)S(1)} copy-done((s32[12]{0:T(128)S(1)}, s32[12]{0:T(128)}, u32[]{:S(2)}) %copy-start.4) | copy-done | bytes 72
  29.2 0.1 copy.6.counts_ref
  29.3 0.1 copy-done.3
  29.4 0.6 %mask_bias.1.bias_ref = f32[27,12,128]{2,1,0:T(8,128)S(1)} custom-call(s32[12,16]{1,0:T(8,128)S(1)} %copy-done.3, s32[12,1]{1,0:T(8,128)S(1)} %copy.6.counts_ref), custom_call_target="tpu_custom_call" | custom-call | tf_op jit(solution)/shard_map/mask_bias/pallas_call | solution.py:29
  30.0 0.0 collective-permute-done.1.refs_1_
  30.1 0.7 %collective-permute-start.8 = (bf16[8,128,128]{2,1,0:T(8,128)(2,1)S(1)}, bf16[8,128,128]{2,1,0:T(8,128)(2,1)S(1)}, u32[]{:S(2)}, u32[]{:S(2)}) collective-permute-start(bf16[8,128,128]{2,1,0:T(8,128)(2,1)S(1)} %get-tuple-element.9), channel_id=1, source_target_pairs={{4,8},{8,4},{5,9},{9,5},{6,10},{10,6},{7,11},{11,7},{20,24},{24,20... | collective-permute-start | bytes 786440 | tf_op jit(solution)/shard_map/ppermute | solution.py:233
  30.8 3.0 %collective-permute-done.4.refs_2_ = bf16[384,128]{1,0:T(8,128)(2,1)S(1)} collective-permute-done((bf16[384,128]{1,0:T(8,128)(2,1)S(1)}, bf16[384,128]{1,0:T(8,128)(2,1)S(1)}, u32[]{:S(2)}, u32[]{:S(2)}) %collective-permute-start.4) | collective-permute-done | bytes 98336 | tf_op jit(solution)/shard_map/ppermute | solution.py:272
  33.7 0.0 collective-permute-start.9
  33.7 0.0 collective-permute-done.7.refs_3_
  33.8 0.0 collective-permute-done.10.first_ref
  33.8 0.1 join.3.array_ref
  33.8 0.1 values.1.v_ref
  33.9 1.3 %collective-permute-done.9.second_ref = bf16[8,128,128]{2,1,0:T(8,128)(2,1)S(1)} collective-permute-done((bf16[8,128,128]{2,1,0:T(8,128)(2,1)S(1)}, bf16[8,128,128]{2,1,0:T(8,128)(2,1)S(1)}, u32[]{:S(2)}, u32[]{:S(2)}) %collective-permute-start.9) | collective-permute-done | bytes 262176 | tf_op jit(solution)/shard_map/ppermute | solution.py:233
  35.3 0.1 join.2.kt_ref
  35.3 1.7 %attend_chunk.4.refs_0_ = bf16[384,128]{1,0:T(8,128)(2,1)S(1)} custom-call(bf16[4,384,128]{2,1,0:T(8,128)(2,1)S(1)} %stack.1.refs_0_.q_ref, bf16[27,128,128]{2,1,0:T(8,128)(2,1)S(1)} %join.2.kt_ref, bf16[27,128,128]{2,1,0:T(8,128)(2,1)S(1)} %values.1.v_ref, f32[27,12,128]{2,1,0:T(8,128)S(1)} %mask_bias.1.bias_ref), custom_call_target="tpu_custom_call" | custom-call | flops 201326592 | bytes 393216 | tf_op jit(solution)/shard_map/attend_chunk/pallas_call | solution.py:29
  37.0 2.7 %collective-permute-start.14 = (bf16[384,128]{1,0:T(8,128)(2,1)S(1)}, bf16[384,128]{1,0:T(8,128)(2,1)S(1)}, u32[]{:S(2)}, u32[]{:S(2)}) collective-permute-start(bf16[384,128]{1,0:T(8,128)(2,1)S(1)} %attend_chunk.4.refs_0_), channel_id=1, source_target_pairs={{0,3},{1,2},{2,1},{3,0},{4,7},{5,6},{6,5},{7,4},{8,11},{9,10},{10,... | collective-permute-start | bytes 294920 | tf_op jit(solution)/shard_map/ppermute | solution.py:272
  39.7 1.7 %attend_chunk.5.refs_0_ = bf16[384,128]{1,0:T(8,128)(2,1)S(1)} custom-call(bf16[4,384,128]{2,1,0:T(8,128)(2,1)S(1)} %stack.1.refs_0_.q_ref, bf16[27,128,128]{2,1,0:T(8,128)(2,1)S(1)} %join.2.kt_ref, bf16[27,128,128]{2,1,0:T(8,128)(2,1)S(1)} %values.1.v_ref, f32[27,12,128]{2,1,0:T(8,128)S(1)} %mask_bias.1.bias_ref, bf16[384,128]{1,0:T(8,128)(2,1)S(1)} %attend_chunk.4.refs_0_), custom_call_target="tpu_custom_call" | custom-call | flops 201326592 | bytes 393216 | tf_op jit(solution)/shard_map/attend_chunk/pallas_call | solution.py:29
  41.4 0.1 collective-permute-start.13
  41.5 1.7 %attend_chunk.6.refs_0_ = bf16[384,128]{1,0:T(8,128)(2,1)S(1)} custom-call(bf16[4,384,128]{2,1,0:T(8,128)(2,1)S(1)} %stack.1.refs_0_.q_ref, bf16[27,128,128]{2,1,0:T(8,128)(2,1)S(1)} %join.2.kt_ref, bf16[27,128,128]{2,1,0:T(8,128)(2,1)S(1)} %values.1.v_ref, f32[27,12,128]{2,1,0:T(8,128)S(1)} %mask_bias.1.bias_ref, bf16[384,128]{1,0:T(8,128)(2,1)S(1)} %attend_chunk.5.refs_0_), custom_call_target="tpu_custom_call" | custom-call | flops 201326592 | bytes 393216 | tf_op jit(solution)/shard_map/attend_chunk/pallas_call | solution.py:29
  43.2 1.8 %collective-permute-start.12 = (bf16[384,128]{1,0:T(8,128)(2,1)S(1)}, bf16[384,128]{1,0:T(8,128)(2,1)S(1)}, u32[]{:S(2)}, u32[]{:S(2)}) collective-permute-start(bf16[384,128]{1,0:T(8,128)(2,1)S(1)} %attend_chunk.6.refs_0_), channel_id=1, source_target_pairs={{0,1},{1,0},{2,3},{3,2},{4,5},{5,4},{6,7},{7,6},{8,9},{9,8},{10,11... | collective-permute-start | bytes 294920 | tf_op jit(solution)/shard_map/ppermute | solution.py:272
  45.0 1.7 %attend_chunk.7.refs_0_ = bf16[384,128]{1,0:T(8,128)(2,1)S(1)} custom-call(bf16[4,384,128]{2,1,0:T(8,128)(2,1)S(1)} %stack.1.refs_0_.q_ref, bf16[27,128,128]{2,1,0:T(8,128)(2,1)S(1)} %join.2.kt_ref, bf16[27,128,128]{2,1,0:T(8,128)(2,1)S(1)} %values.1.v_ref, f32[27,12,128]{2,1,0:T(8,128)S(1)} %mask_bias.1.bias_ref, bf16[384,128]{1,0:T(8,128)(2,1)S(1)} %attend_chunk.6.refs_0_), custom_call_target="tpu_custom_call" | custom-call | flops 8388608 | bytes 16384 | tf_op jit(solution)/shard_map/attend_chunk/pallas_call | solution.py:29
  46.7 2.6 %collective-permute-done.13.array_ref = bf16[384,128]{1,0:T(8,128)(2,1)S(1)} collective-permute-done((bf16[384,128]{1,0:T(8,128)(2,1)S(1)}, bf16[384,128]{1,0:T(8,128)(2,1)S(1)}, u32[]{:S(2)}, u32[]{:S(2)}) %collective-permute-start.13) | collective-permute-done | bytes 98336 | tf_op jit(solution)/shard_map/ppermute | solution.py:272
  49.3 1.1 %collective-permute-done.12.array_ref = bf16[384,128]{1,0:T(8,128)(2,1)S(1)} collective-permute-done((bf16[384,128]{1,0:T(8,128)(2,1)S(1)}, bf16[384,128]{1,0:T(8,128)(2,1)S(1)}, u32[]{:S(2)}, u32[]{:S(2)}) %collective-permute-start.12) | collective-permute-done | bytes 98336 | tf_op jit(solution)/shard_map/ppermute | solution.py:272
  50.4 0.8 %spread.1 = bf16[384,512]{1,0:T(8,128)(2,1)} custom-call(bf16[384,128]{1,0:T(8,128)(2,1)S(1)} %attend_chunk.7.refs_0_, bf16[384,128]{1,0:T(8,128)(2,1)S(1)} %landed.5.refs_1_, bf16[384,128]{1,0:T(8,128)(2,1)S(1)} %landed.4.refs_0_.refs_2_, bf16[384,128]{1,0:T(8,128)(2,1)S(1)} %landed.3.refs_0_.refs_3_), custom_call_target="tpu_custom_call" | custom-call | tf_op jit(solution)/shard_map/spread/pallas_call | solution.py:29
  (21 shorter events, 0.4 us)
Async XLA Ops:
  0.0 1.0 %copy-start.2 = (bf16[384,512]{1,0:T(8,128)(2,1)S(1)}, bf16[384,512]{1,0:T(8,128)(2,1)}, u32[]{:S(2)}) copy-start(bf16[384,512]{1,0:T(8,128)(2,1)} %array_ref.13) | copy-start | bytes 1179652
  1.0 5.9 %copy-start = (bf16[384,512]{1,0:T(8,128)(2,1)S(1)}, bf16[384,512]{1,0:T(8,128)(2,1)}, u32[]{:S(2)}) copy-start(bf16[384,512]{1,0:T(8,128)(2,1)} %q_ref.7) | copy-start | bytes 1179652
  1.0 5.9 %copy-start.1 = (bf16[384,512]{1,0:T(8,128)(2,1)S(1)}, bf16[384,512]{1,0:T(8,128)(2,1)}, u32[]{:S(2)}) copy-start(bf16[384,512]{1,0:T(8,128)(2,1)} %array_ref.12) | copy-start | bytes 1179652
  1.0 5.9 %collective-permute-start = (bf16[3,128,128]{2,1,0:T(8,128)(2,1)S(1)}, bf16[3,128,128]{2,1,0:T(8,128)(2,1)S(1)}, u32[]{:S(2)}, u32[]{:S(2)}) collective-permute-start(bf16[3,128,128]{2,1,0:T(8,128)(2,1)S(1)} %load_v.4), channel_id=1, source_target_pairs={{0,1},{1,0},{2,3},{3,2},{4,5},{5,4},{6,7},{7,6},{8,9},{9,8},{10,11... | collective-permute-start | bytes 294920 | tf_op jit(solution)/shard_map/ppermute | solution.py:272
  4.2 10.6 %collective-permute-start.2 = (bf16[3,128,128]{2,1,0:T(8,128)(2,1)S(1)}, bf16[3,128,128]{2,1,0:T(8,128)(2,1)S(1)}, u32[]{:S(2)}, u32[]{:S(2)}) collective-permute-start(bf16[3,128,128]{2,1,0:T(8,128)(2,1)S(1)} %load_v.5), channel_id=1, source_target_pairs={{0,2},{1,3},{2,0},{3,1},{4,6},{5,7},{6,4},{7,5},{8,10},{9,11},{10,... | collective-permute-start | bytes 294920 | tf_op jit(solution)/shard_map/ppermute | solution.py:272
  6.8 8.0 %collective-permute-start.5 = (bf16[3,128,128]{2,1,0:T(8,128)(2,1)S(1)}, bf16[3,128,128]{2,1,0:T(8,128)(2,1)S(1)}, u32[]{:S(2)}, u32[]{:S(2)}) collective-permute-start(bf16[3,128,128]{2,1,0:T(8,128)(2,1)S(1)} %load_v.6), channel_id=1, source_target_pairs={{0,3},{1,2},{2,1},{3,0},{4,7},{5,6},{6,5},{7,4},{8,11},{9,10},{10,... | collective-permute-start | bytes 294920 | tf_op jit(solution)/shard_map/ppermute | solution.py:272
  7.1 22.9 %collective-permute-start.1 = (bf16[6,128,128]{2,1,0:T(8,128)(2,1)S(1)}, bf16[6,128,128]{2,1,0:T(8,128)(2,1)S(1)}, u32[]{:S(2)}, u32[]{:S(2)}) collective-permute-start(bf16[6,128,128]{2,1,0:T(8,128)(2,1)S(1)} %load_k.4), channel_id=1, source_target_pairs={{0,1},{1,0},{2,3},{3,2},{4,5},{5,4},{6,7},{7,6},{8,9},{9,8},{10,11... | collective-permute-start | bytes 589832 | tf_op jit(solution)/shard_map/ppermute | solution.py:272
  14.8 8.5 %collective-permute-start.3 = (bf16[3,128,128]{2,1,0:T(8,128)(2,1)S(1)}, bf16[3,128,128]{2,1,0:T(8,128)(2,1)S(1)}, u32[]{:S(2)}, u32[]{:S(2)}) collective-permute-start(bf16[3,128,128]{2,1,0:T(8,128)(2,1)S(1)} %load_k.5), channel_id=1, source_target_pairs={{0,2},{1,3},{2,0},{3,1},{4,6},{5,7},{6,4},{7,5},{8,10},{9,11},{10,... | collective-permute-start | bytes 294920 | tf_op jit(solution)/shard_map/ppermute | solution.py:272
  15.0 10.6 %collective-permute-start.6 = (bf16[3,128,128]{2,1,0:T(8,128)(2,1)S(1)}, bf16[3,128,128]{2,1,0:T(8,128)(2,1)S(1)}, u32[]{:S(2)}, u32[]{:S(2)}) collective-permute-start(bf16[3,128,128]{2,1,0:T(8,128)(2,1)S(1)} %load_k.6), channel_id=1, source_target_pairs={{0,3},{1,2},{2,1},{3,0},{4,7},{5,6},{6,5},{7,4},{8,11},{9,10},{10,... | collective-permute-start | bytes 294920 | tf_op jit(solution)/shard_map/ppermute | solution.py:272
  17.7 16.1 %collective-permute-start.10 = (bf16[8,128,128]{2,1,0:T(8,128)(2,1)S(1)}, bf16[8,128,128]{2,1,0:T(8,128)(2,1)S(1)}, u32[]{:S(2)}, u32[]{:S(2)}) collective-permute-start(bf16[8,128,128]{2,1,0:T(8,128)(2,1)S(1)} %get-tuple-element.11), channel_id=1, source_target_pairs={{4,8},{8,4},{5,9},{9,5},{6,10},{10,6},{7,11},{11,7},{20,24},{24,20... | collective-permute-start | bytes 786440 | tf_op jit(solution)/shard_map/ppermute | solution.py:233
  18.4 15.4 %collective-permute-start.11 = (bf16[8,128,128]{2,1,0:T(8,128)(2,1)S(1)}, bf16[8,128,128]{2,1,0:T(8,128)(2,1)S(1)}, u32[]{:S(2)}, u32[]{:S(2)}) collective-permute-start(bf16[8,128,128]{2,1,0:T(8,128)(2,1)S(1)} %get-tuple-element.12), channel_id=1, source_target_pairs={{0,4},{8,12},{4,0},{12,8},{1,5},{9,13},{5,1},{13,9},{2,6},{10,14},... | collective-permute-start | bytes 786440 | tf_op jit(solution)/shard_map/ppermute | solution.py:233
  23.3 10.4 %collective-permute-start.4 = (bf16[384,128]{1,0:T(8,128)(2,1)S(1)}, bf16[384,128]{1,0:T(8,128)(2,1)S(1)}, u32[]{:S(2)}, u32[]{:S(2)}) collective-permute-start(bf16[384,128]{1,0:T(8,128)(2,1)S(1)} %load_q.4), channel_id=1, source_target_pairs={{0,2},{1,3},{2,0},{3,1},{4,6},{5,7},{6,4},{7,5},{8,10},{9,11},{10,... | collective-permute-start | bytes 294920 | tf_op jit(solution)/shard_map/ppermute | solution.py:272
  25.6 8.1 %collective-permute-start.7 = (bf16[384,128]{1,0:T(8,128)(2,1)S(1)}, bf16[384,128]{1,0:T(8,128)(2,1)S(1)}, u32[]{:S(2)}, u32[]{:S(2)}) collective-permute-start(bf16[384,128]{1,0:T(8,128)(2,1)S(1)} %load_q.5), channel_id=1, source_target_pairs={{0,3},{1,2},{2,1},{3,0},{4,7},{5,6},{6,5},{7,4},{8,11},{9,10},{10,... | collective-permute-start | bytes 294920 | tf_op jit(solution)/shard_map/ppermute | solution.py:272
  28.6 0.7 %copy-start.4 = (s32[12]{0:T(128)S(1)}, s32[12]{0:T(128)}, u32[]{:S(2)}) copy-start(s32[12]{0:T(128)} %param.9) | copy-start | bytes 148
  28.7 0.7 %copy-start.3 = (s32[12,16]{1,0:T(8,128)S(1)}, s32[12,16]{1,0:T(8,128)}, u32[]{:S(2)}) copy-start(s32[12,16]{1,0:T(8,128)} %lists_ref.1) | copy-start | bytes 2308
  30.1 3.8 %collective-permute-start.8 = (bf16[8,128,128]{2,1,0:T(8,128)(2,1)S(1)}, bf16[8,128,128]{2,1,0:T(8,128)(2,1)S(1)}, u32[]{:S(2)}, u32[]{:S(2)}) collective-permute-start(bf16[8,128,128]{2,1,0:T(8,128)(2,1)S(1)} %get-tuple-element.9), channel_id=1, source_target_pairs={{4,8},{8,4},{5,9},{9,5},{6,10},{10,6},{7,11},{11,7},{20,24},{24,20... | collective-permute-start | bytes 786440 | tf_op jit(solution)/shard_map/ppermute | solution.py:233
  33.7 1.5 %collective-permute-start.9 = (bf16[8,128,128]{2,1,0:T(8,128)(2,1)S(1)}, bf16[8,128,128]{2,1,0:T(8,128)(2,1)S(1)}, u32[]{:S(2)}, u32[]{:S(2)}) collective-permute-start(bf16[8,128,128]{2,1,0:T(8,128)(2,1)S(1)} %get-tuple-element.10), channel_id=1, source_target_pairs={{0,4},{8,12},{4,0},{12,8},{1,5},{9,13},{5,1},{13,9},{2,6},{10,14},... | collective-permute-start | bytes 786440 | tf_op jit(solution)/shard_map/ppermute | solution.py:233
  37.0 9.6 %collective-permute-start.14 = (bf16[384,128]{1,0:T(8,128)(2,1)S(1)}, bf16[384,128]{1,0:T(8,128)(2,1)S(1)}, u32[]{:S(2)}, u32[]{:S(2)}) collective-permute-start(bf16[384,128]{1,0:T(8,128)(2,1)S(1)} %attend_chunk.4.refs_0_), channel_id=1, source_target_pairs={{0,3},{1,2},{2,1},{3,0},{4,7},{5,6},{6,5},{7,4},{8,11},{9,10},{10,... | collective-permute-start | bytes 294920 | tf_op jit(solution)/shard_map/ppermute | solution.py:272
  41.4 7.9 %collective-permute-start.13 = (bf16[384,128]{1,0:T(8,128)(2,1)S(1)}, bf16[384,128]{1,0:T(8,128)(2,1)S(1)}, u32[]{:S(2)}, u32[]{:S(2)}) collective-permute-start(bf16[384,128]{1,0:T(8,128)(2,1)S(1)} %attend_chunk.5.refs_0_), channel_id=1, source_target_pairs={{0,2},{1,3},{2,0},{3,1},{4,6},{5,7},{6,4},{7,5},{8,10},{9,11},{10,... | collective-permute-start | bytes 294920 | tf_op jit(solution)/shard_map/ppermute | solution.py:272
  43.2 7.2 %collective-permute-start.12 = (bf16[384,128]{1,0:T(8,128)(2,1)S(1)}, bf16[384,128]{1,0:T(8,128)(2,1)S(1)}, u32[]{:S(2)}, u32[]{:S(2)}) collective-permute-start(bf16[384,128]{1,0:T(8,128)(2,1)S(1)} %attend_chunk.6.refs_0_), channel_id=1, source_target_pairs={{0,1},{1,0},{2,3},{3,2},{4,5},{5,4},{6,7},{7,6},{8,9},{9,8},{10,11... | collective-permute-start | bytes 294920 | tf_op jit(solution)/shard_map/ppermute | solution.py:272

commit v13 on v12

--- a/solution.py
+++ b/solution.py
@@ -283,6 +283,8 @@
         kernel = load_kq_kernel if pair == 1 else functools.partial(load_tiles_kernel, turn=True)
         shape = (len(operands) * BLOCK, TILE, HDIM)
         after = (v_parts[pair],) if pair else ()
+        if pair == order[0]:
+            after += (bias,)
         part = call_on(functools.partial(kernel, pair), "load_k", (*operands, *after), shape)
         k_parts[pair] = exchange(part, pair) if pair else part
     q_parts[1] = k_parts[1]

time: 51.5 us -> 51.3 us (level)
  starting transfers between devices: 24.4 us -> 23.2 us
  waiting for transfers between devices: 15.8 us -> 16.7 us
    ppermute x11, starting transfers between devices: 20.2 us -> 19 us  [exchange(): return lax.ppermute(array, 'head', [(i, i ^ pair) for i in range(heads)])]
    ppermute x11, waiting for transfers between devices: 14.5 us -> 15.3 us  [exchange(): return lax.ppermute(array, 'head', [(i, i ^ pair) for i in range(heads)])]
    unnamed x10 -> x12, local copies, waits for them, and re-layouts: 1.61 us -> 1.56 us
where the time goes in v13:
time: 51.3 us; the launch traced here: 51 us
  starting transfers between devices  23.2 us (45%)
  waiting for transfers between devices  16.7 us (33%)
  Pallas kernels  9.21 us (18%)
  local copies, waits for them, and re-layouts  1.65 us (3%)
    ppermute x11, starting transfers between devices, exchange(): return lax.ppermute(array, 'head', [(i, i ^ pair) for i in range(heads)])  19 us
    ppermute x11, waiting for transfers between devices, exchange(): return lax.ppermute(array, 'head', [(i, i ^ pair) for i in range(heads)])  15.3 us
    pallas_call x28, Pallas kernels, call(): pl.pallas_call(kernel, out_shape=out_shape, in_specs=in_specs, out_specs=...  9.21 us
    ppermute x4, starting transfers between devices, exchange(): lax.ppermute(array, 'ctx', [(i, i + 1) for i in lower] + [(i + 1, i) for...  4.26 us
    unnamed x12, local copies, waits for them, and re-layouts  1.56 us
    ppermute x4, waiting for transfers between devices, exchange(): lax.ppermute(array, 'ctx', [(i, i + 1) for i in lower] + [(i + 1, i) for...  1.34 us
  transfers between devices with their start and end apart: 15, of which 6 were waited for; matrix products, arithmetic and copies ran while one was open for 0% of the time, Pallas kernels for 13%

profile of v13, /device:TPU:0, one launch (start us, length us, event | category | flops | bytes accessed | tf_op | source)
XLA Modules:
  0.0 51.0 jit_solution(13255063171582556434)
XLA Ops:
  0.0 1.0 %copy-done.2 = bf16[384,512]{1,0:T(8,128)(2,1)S(1)} copy-done((bf16[384,512]{1,0:T(8,128)(2,1)S(1)}, bf16[384,512]{1,0:T(8,128)(2,1)}, u32[]{:S(2)}) %copy-start.2) | copy-done | bytes 393240
  1.0 3.1 %collective-permute-start = (bf16[3,128,128]{2,1,0:T(8,128)(2,1)S(1)}, bf16[3,128,128]{2,1,0:T(8,128)(2,1)S(1)}, u32[]{:S(2)}, u32[]{:S(2)}) collective-permute-start(bf16[3,128,128]{2,1,0:T(8,128)(2,1)S(1)} %load_v.4), channel_id=1, source_target_pairs={{0,1},{1,0},{2,3},{3,2},{4,5},{5,4},{6,7},{7,6},{8,9},{9,8},{10,11... | collective-permute-start | bytes 294920 | tf_op jit(solution)/shard_map/ppermute | solution.py:272
  4.1 0.0 copy-start
  4.1 2.7 %collective-permute-start.2 = (bf16[3,128,128]{2,1,0:T(8,128)(2,1)S(1)}, bf16[3,128,128]{2,1,0:T(8,128)(2,1)S(1)}, u32[]{:S(2)}, u32[]{:S(2)}) collective-permute-start(bf16[3,128,128]{2,1,0:T(8,128)(2,1)S(1)} %load_v.5), channel_id=1, source_target_pairs={{0,2},{1,3},{2,0},{3,1},{4,6},{5,7},{6,4},{7,5},{8,10},{9,11},{10,... | collective-permute-start | bytes 294920 | tf_op jit(solution)/shard_map/ppermute | solution.py:272
  6.8 0.0 copy-start.4
  6.8 0.1 collective-permute-start.5
  6.9 0.5 %copy-done.5 = s32[12]{0:T(128)S(1)} copy-done((s32[12]{0:T(128)S(1)}, s32[12]{0:T(128)}, u32[]{:S(2)}) %copy-start.5) | copy-done | bytes 72
  7.5 0.1 copy.6.counts_ref
  7.6 0.6 %mask_bias.1.refs_1_.bias_ref = f32[27,12,128]{2,1,0:T(8,128)S(1)} custom-call(s32[12,16]{1,0:T(8,128)S(1)} %copy-done.4, s32[12,1]{1,0:T(8,128)S(1)} %copy.6.counts_ref), custom_call_target="tpu_custom_call" | custom-call | tf_op jit(solution)/shard_map/mask_bias/pallas_call | solution.py:29
  8.1 0.0 collective-permute-done.refs_0_.refs_1_
  8.2 0.1 load_k.4
  8.3 0.6 %collective-permute-start.1 = (bf16[6,128,128]{2,1,0:T(8,128)(2,1)S(1)}, bf16[6,128,128]{2,1,0:T(8,128)(2,1)S(1)}, u32[]{:S(2)}, u32[]{:S(2)}) collective-permute-start(bf16[6,128,128]{2,1,0:T(8,128)(2,1)S(1)} %load_k.4), channel_id=1, source_target_pairs={{0,1},{1,0},{2,3},{3,2},{4,5},{5,4},{6,7},{7,6},{8,9},{9,8},{10,11... | collective-permute-start | bytes 589832 | tf_op jit(solution)/shard_map/ppermute | solution.py:272
  8.9 5.8 %collective-permute-done.2.refs_0_.refs_2_ = bf16[3,128,128]{2,1,0:T(8,128)(2,1)S(1)} collective-permute-done((bf16[3,128,128]{2,1,0:T(8,128)(2,1)S(1)}, bf16[3,128,128]{2,1,0:T(8,128)(2,1)S(1)}, u32[]{:S(2)}, u32[]{:S(2)}) %collective-permute-start.2) | collective-permute-done | bytes 98336 | tf_op jit(solution)/shard_map/ppermute | solution.py:272
  14.7 0.1 load_k.5
  14.8 0.0 copy-start.3
  14.8 0.1 collective-permute-start.3
  14.9 0.0 collective-permute-done.5.refs_0_.refs_3_
  14.9 0.1 load_k.6
  15.0 2.6 %collective-permute-start.6 = (bf16[3,128,128]{2,1,0:T(8,128)(2,1)S(1)}, bf16[3,128,128]{2,1,0:T(8,128)(2,1)S(1)}, u32[]{:S(2)}, u32[]{:S(2)}) collective-permute-start(bf16[3,128,128]{2,1,0:T(8,128)(2,1)S(1)} %load_k.6), channel_id=1, source_target_pairs={{0,3},{1,2},{2,1},{3,0},{4,7},{5,6},{6,5},{7,4},{8,11},{9,10},{10,... | collective-permute-start | bytes 294920 | tf_op jit(solution)/shard_map/ppermute | solution.py:272
  17.7 0.7 %collective-permute-start.10 = (bf16[8,128,128]{2,1,0:T(8,128)(2,1)S(1)}, bf16[8,128,128]{2,1,0:T(8,128)(2,1)S(1)}, u32[]{:S(2)}, u32[]{:S(2)}) collective-permute-start(bf16[8,128,128]{2,1,0:T(8,128)(2,1)S(1)} %get-tuple-element.11), channel_id=1, source_target_pairs={{4,8},{8,4},{5,9},{9,5},{6,10},{10,6},{7,11},{11,7},{20,24},{24,20... | collective-permute-start | bytes 786440 | tf_op jit(solution)/shard_map/ppermute | solution.py:233
  18.4 2.9 %collective-permute-start.11 = (bf16[8,128,128]{2,1,0:T(8,128)(2,1)S(1)}, bf16[8,128,128]{2,1,0:T(8,128)(2,1)S(1)}, u32[]{:S(2)}, u32[]{:S(2)}) collective-permute-start(bf16[8,128,128]{2,1,0:T(8,128)(2,1)S(1)} %get-tuple-element.12), channel_id=1, source_target_pairs={{0,4},{8,12},{4,0},{12,8},{1,5},{9,13},{5,1},{13,9},{2,6},{10,14},... | collective-permute-start | bytes 786440 | tf_op jit(solution)/shard_map/ppermute | solution.py:233
  21.3 1.9 %collective-permute-done.3.refs_0_.refs_2_ = bf16[3,128,128]{2,1,0:T(8,128)(2,1)S(1)} collective-permute-done((bf16[3,128,128]{2,1,0:T(8,128)(2,1)S(1)}, bf16[3,128,128]{2,1,0:T(8,128)(2,1)S(1)}, u32[]{:S(2)}, u32[]{:S(2)}) %collective-permute-start.3) | collective-permute-done | bytes 98336 | tf_op jit(solution)/shard_map/ppermute | solution.py:272
  23.3 2.3 %collective-permute-start.4 = (bf16[384,128]{1,0:T(8,128)(2,1)S(1)}, bf16[384,128]{1,0:T(8,128)(2,1)S(1)}, u32[]{:S(2)}, u32[]{:S(2)}) collective-permute-start(bf16[384,128]{1,0:T(8,128)(2,1)S(1)} %load_q.4), channel_id=1, source_target_pairs={{0,2},{1,3},{2,0},{3,1},{4,6},{5,7},{6,4},{7,5},{8,10},{9,11},{10,... | collective-permute-start | bytes 294920 | tf_op jit(solution)/shard_map/ppermute | solution.py:272
  25.6 3.0 %collective-permute-start.7 = (bf16[384,128]{1,0:T(8,128)(2,1)S(1)}, bf16[384,128]{1,0:T(8,128)(2,1)S(1)}, u32[]{:S(2)}, u32[]{:S(2)}) collective-permute-start(bf16[384,128]{1,0:T(8,128)(2,1)S(1)} %load_q.5), channel_id=1, source_target_pairs={{0,3},{1,2},{2,1},{3,0},{4,7},{5,6},{6,5},{7,4},{8,11},{9,10},{10,... | collective-permute-start | bytes 294920 | tf_op jit(solution)/shard_map/ppermute | solution.py:272
  28.6 0.1 load_k.7.refs_0_
  28.7 0.0 collective-permute-done.1.refs_1_
  28.8 0.7 %collective-permute-start.8 = (bf16[8,128,128]{2,1,0:T(8,128)(2,1)S(1)}, bf16[8,128,128]{2,1,0:T(8,128)(2,1)S(1)}, u32[]{:S(2)}, u32[]{:S(2)}) collective-permute-start(bf16[8,128,128]{2,1,0:T(8,128)(2,1)S(1)} %get-tuple-element.9), channel_id=1, source_target_pairs={{4,8},{8,4},{5,9},{9,5},{6,10},{10,6},{7,11},{11,7},{20,24},{24,20... | collective-permute-start | bytes 786440 | tf_op jit(solution)/shard_map/ppermute | solution.py:233
  29.5 4.2 %collective-permute-done.4.refs_2_ = bf16[384,128]{1,0:T(8,128)(2,1)S(1)} collective-permute-done((bf16[384,128]{1,0:T(8,128)(2,1)S(1)}, bf16[384,128]{1,0:T(8,128)(2,1)S(1)}, u32[]{:S(2)}, u32[]{:S(2)}) %collective-permute-start.4) | collective-permute-done | bytes 98336 | tf_op jit(solution)/shard_map/ppermute | solution.py:272
  33.7 0.0 collective-permute-start.9
  33.7 0.0 collective-permute-done.7.refs_3_
  33.7 0.0 collective-permute-done.10.first_ref
  33.7 0.0 collective-permute-done.11.second_ref
  33.7 0.1 join.3.array_ref
  33.8 0.1 values.1.v_ref
  33.9 0.0 collective-permute-done.8.first_ref
  33.9 1.3 %collective-permute-done.9.second_ref = bf16[8,128,128]{2,1,0:T(8,128)(2,1)S(1)} collective-permute-done((bf16[8,128,128]{2,1,0:T(8,128)(2,1)S(1)}, bf16[8,128,128]{2,1,0:T(8,128)(2,1)S(1)}, u32[]{:S(2)}, u32[]{:S(2)}) %collective-permute-start.9) | collective-permute-done | bytes 262176 | tf_op jit(solution)/shard_map/ppermute | solution.py:233
  35.2 0.1 join.2.kt_ref
  35.3 1.7 %attend_chunk.4.refs_0_ = bf16[384,128]{1,0:T(8,128)(2,1)S(1)} custom-call(bf16[4,384,128]{2,1,0:T(8,128)(2,1)S(1)} %stack.1.refs_0_.q_ref, bf16[27,128,128]{2,1,0:T(8,128)(2,1)S(1)} %join.2.kt_ref, bf16[27,128,128]{2,1,0:T(8,128)(2,1)S(1)} %values.1.v_ref, f32[27,12,128]{2,1,0:T(8,128)S(1)} %mask_bias.1.refs_1_.bias_ref), custom_call_target="tpu_custom_call" | custom-call | flops 201326592 | bytes 393216 | tf_op jit(solution)/shard_map/attend_chunk/pallas_call | solution.py:29
  37.0 2.8 %collective-permute-start.14 = (bf16[384,128]{1,0:T(8,128)(2,1)S(1)}, bf16[384,128]{1,0:T(8,128)(2,1)S(1)}, u32[]{:S(2)}, u32[]{:S(2)}) collective-permute-start(bf16[384,128]{1,0:T(8,128)(2,1)S(1)} %attend_chunk.4.refs_0_), channel_id=1, source_target_pairs={{0,3},{1,2},{2,1},{3,0},{4,7},{5,6},{6,5},{7,4},{8,11},{9,10},{10,... | collective-permute-start | bytes 294920 | tf_op jit(solution)/shard_map/ppermute | solution.py:272
  39.8 1.7 %attend_chunk.5.refs_0_ = bf16[384,128]{1,0:T(8,128)(2,1)S(1)} custom-call(bf16[4,384,128]{2,1,0:T(8,128)(2,1)S(1)} %stack.1.refs_0_.q_ref, bf16[27,128,128]{2,1,0:T(8,128)(2,1)S(1)} %join.2.kt_ref, bf16[27,128,128]{2,1,0:T(8,128)(2,1)S(1)} %values.1.v_ref, f32[27,12,128]{2,1,0:T(8,128)S(1)} %mask_bias.1.refs_1_.bias_ref, ...), custom_call_target="tpu_custom_call" | custom-call | flops 201326592 | bytes 393216 | tf_op jit(solution)/shard_map/attend_chunk/pallas_call | solution.py:29
  41.5 0.1 collective-permute-start.13
  41.6 1.7 %attend_chunk.6.refs_0_ = bf16[384,128]{1,0:T(8,128)(2,1)S(1)} custom-call(bf16[4,384,128]{2,1,0:T(8,128)(2,1)S(1)} %stack.1.refs_0_.q_ref, bf16[27,128,128]{2,1,0:T(8,128)(2,1)S(1)} %join.2.kt_ref, bf16[27,128,128]{2,1,0:T(8,128)(2,1)S(1)} %values.1.v_ref, f32[27,12,128]{2,1,0:T(8,128)S(1)} %mask_bias.1.refs_1_.bias_ref, ...), custom_call_target="tpu_custom_call" | custom-call | flops 201326592 | bytes 393216 | tf_op jit(solution)/shard_map/attend_chunk/pallas_call | solution.py:29
  43.3 1.7 %collective-permute-start.12 = (bf16[384,128]{1,0:T(8,128)(2,1)S(1)}, bf16[384,128]{1,0:T(8,128)(2,1)S(1)}, u32[]{:S(2)}, u32[]{:S(2)}) collective-permute-start(bf16[384,128]{1,0:T(8,128)(2,1)S(1)} %attend_chunk.6.refs_0_), channel_id=1, source_target_pairs={{0,1},{1,0},{2,3},{3,2},{4,5},{5,4},{6,7},{7,6},{8,9},{9,8},{10,11... | collective-permute-start | bytes 294920 | tf_op jit(solution)/shard_map/ppermute | solution.py:272
  45.0 1.7 %attend_chunk.7.refs_0_ = bf16[384,128]{1,0:T(8,128)(2,1)S(1)} custom-call(bf16[4,384,128]{2,1,0:T(8,128)(2,1)S(1)} %stack.1.refs_0_.q_ref, bf16[27,128,128]{2,1,0:T(8,128)(2,1)S(1)} %join.2.kt_ref, bf16[27,128,128]{2,1,0:T(8,128)(2,1)S(1)} %values.1.v_ref, f32[27,12,128]{2,1,0:T(8,128)S(1)} %mask_bias.1.refs_1_.bias_ref, ...), custom_call_target="tpu_custom_call" | custom-call | flops 8388608 | bytes 16384 | tf_op jit(solution)/shard_map/attend_chunk/pallas_call | solution.py:29
  46.8 0.0 collective-permute-done.14.array_ref
  46.8 1.9 %collective-permute-done.13.array_ref = bf16[384,128]{1,0:T(8,128)(2,1)S(1)} collective-permute-done((bf16[384,128]{1,0:T(8,128)(2,1)S(1)}, bf16[384,128]{1,0:T(8,128)(2,1)S(1)}, u32[]{:S(2)}, u32[]{:S(2)}) %collective-permute-start.13) | collective-permute-done | bytes 98336 | tf_op jit(solution)/shard_map/ppermute | solution.py:272
  48.6 1.5 %collective-permute-done.12.array_ref = bf16[384,128]{1,0:T(8,128)(2,1)S(1)} collective-permute-done((bf16[384,128]{1,0:T(8,128)(2,1)S(1)}, bf16[384,128]{1,0:T(8,128)(2,1)S(1)}, u32[]{:S(2)}, u32[]{:S(2)}) %collective-permute-start.12) | collective-permute-done | bytes 98336 | tf_op jit(solution)/shard_map/ppermute | solution.py:272
  50.2 0.8 %spread.1 = bf16[384,512]{1,0:T(8,128)(2,1)} custom-call(bf16[384,128]{1,0:T(8,128)(2,1)S(1)} %attend_chunk.7.refs_0_, bf16[384,128]{1,0:T(8,128)(2,1)S(1)} %landed.5.refs_1_, bf16[384,128]{1,0:T(8,128)(2,1)S(1)} %landed.4.refs_0_.refs_2_, bf16[384,128]{1,0:T(8,128)(2,1)S(1)} %landed.3.refs_0_.refs_3_), custom_call_target="tpu_custom_call" | custom-call | tf_op jit(solution)/shard_map/spread/pallas_call | solution.py:29
  (23 shorter events, 0.4 us)
Async XLA Ops:
  0.0 1.0 %copy-start.2 = (bf16[384,512]{1,0:T(8,128)(2,1)S(1)}, bf16[384,512]{1,0:T(8,128)(2,1)}, u32[]{:S(2)}) copy-start(bf16[384,512]{1,0:T(8,128)(2,1)} %array_ref.13) | copy-start | bytes 1179652
  1.0 7.1 %collective-permute-start = (bf16[3,128,128]{2,1,0:T(8,128)(2,1)S(1)}, bf16[3,128,128]{2,1,0:T(8,128)(2,1)S(1)}, u32[]{:S(2)}, u32[]{:S(2)}) collective-permute-start(bf16[3,128,128]{2,1,0:T(8,128)(2,1)S(1)} %load_v.4), channel_id=1, source_target_pairs={{0,1},{1,0},{2,3},{3,2},{4,5},{5,4},{6,7},{7,6},{8,9},{9,8},{10,11... | collective-permute-start | bytes 294920 | tf_op jit(solution)/shard_map/ppermute | solution.py:272
  4.1 4.0 %copy-start.1 = (bf16[384,512]{1,0:T(8,128)(2,1)S(1)}, bf16[384,512]{1,0:T(8,128)(2,1)}, u32[]{:S(2)}) copy-start(bf16[384,512]{1,0:T(8,128)(2,1)} %array_ref.12) | copy-start | bytes 1179652
  4.1 4.0 %copy-start = (bf16[384,512]{1,0:T(8,128)(2,1)S(1)}, bf16[384,512]{1,0:T(8,128)(2,1)}, u32[]{:S(2)}) copy-start(bf16[384,512]{1,0:T(8,128)(2,1)} %q_ref.7) | copy-start | bytes 1179652
  4.1 10.6 %collective-permute-start.2 = (bf16[3,128,128]{2,1,0:T(8,128)(2,1)S(1)}, bf16[3,128,128]{2,1,0:T(8,128)(2,1)S(1)}, u32[]{:S(2)}, u32[]{:S(2)}) collective-permute-start(bf16[3,128,128]{2,1,0:T(8,128)(2,1)S(1)} %load_v.5), channel_id=1, source_target_pairs={{0,2},{1,3},{2,0},{3,1},{4,6},{5,7},{6,4},{7,5},{8,10},{9,11},{10,... | collective-permute-start | bytes 294920 | tf_op jit(solution)/shard_map/ppermute | solution.py:272
  6.8 0.7 %copy-start.5 = (s32[12]{0:T(128)S(1)}, s32[12]{0:T(128)}, u32[]{:S(2)}) copy-start(s32[12]{0:T(128)} %param.9) | copy-start | bytes 148
  6.8 0.7 %copy-start.4 = (s32[12,16]{1,0:T(8,128)S(1)}, s32[12,16]{1,0:T(8,128)}, u32[]{:S(2)}) copy-start(s32[12,16]{1,0:T(8,128)} %lists_ref.1) | copy-start | bytes 2308
  6.8 8.0 %collective-permute-start.5 = (bf16[3,128,128]{2,1,0:T(8,128)(2,1)S(1)}, bf16[3,128,128]{2,1,0:T(8,128)(2,1)S(1)}, u32[]{:S(2)}, u32[]{:S(2)}) collective-permute-start(bf16[3,128,128]{2,1,0:T(8,128)(2,1)S(1)} %load_v.6), channel_id=1, source_target_pairs={{0,3},{1,2},{2,1},{3,0},{4,7},{5,6},{6,5},{7,4},{8,11},{9,10},{10,... | collective-permute-start | bytes 294920 | tf_op jit(solution)/shard_map/ppermute | solution.py:272
  8.3 20.4 %collective-permute-start.1 = (bf16[6,128,128]{2,1,0:T(8,128)(2,1)S(1)}, bf16[6,128,128]{2,1,0:T(8,128)(2,1)S(1)}, u32[]{:S(2)}, u32[]{:S(2)}) collective-permute-start(bf16[6,128,128]{2,1,0:T(8,128)(2,1)S(1)} %load_k.4), channel_id=1, source_target_pairs={{0,1},{1,0},{2,3},{3,2},{4,5},{5,4},{6,7},{7,6},{8,9},{9,8},{10,11... | collective-permute-start | bytes 589832 | tf_op jit(solution)/shard_map/ppermute | solution.py:272
  14.8 2.8 %copy-start.3 = (bf16[384,512]{1,0:T(8,128)(2,1)S(1)}, bf16[384,512]{1,0:T(8,128)(2,1)}, u32[]{:S(2)}) copy-start(bf16[384,512]{1,0:T(8,128)(2,1)} %array_ref.13) | copy-start | bytes 1179652
  14.8 8.4 %collective-permute-start.3 = (bf16[3,128,128]{2,1,0:T(8,128)(2,1)S(1)}, bf16[3,128,128]{2,1,0:T(8,128)(2,1)S(1)}, u32[]{:S(2)}, u32[]{:S(2)}) collective-permute-start(bf16[3,128,128]{2,1,0:T(8,128)(2,1)S(1)} %load_k.5), channel_id=1, source_target_pairs={{0,2},{1,3},{2,0},{3,1},{4,6},{5,7},{6,4},{7,5},{8,10},{9,11},{10,... | collective-permute-start | bytes 294920 | tf_op jit(solution)/shard_map/ppermute | solution.py:272
  15.0 10.6 %collective-permute-start.6 = (bf16[3,128,128]{2,1,0:T(8,128)(2,1)S(1)}, bf16[3,128,128]{2,1,0:T(8,128)(2,1)S(1)}, u32[]{:S(2)}, u32[]{:S(2)}) collective-permute-start(bf16[3,128,128]{2,1,0:T(8,128)(2,1)S(1)} %load_k.6), channel_id=1, source_target_pairs={{0,3},{1,2},{2,1},{3,0},{4,7},{5,6},{6,5},{7,4},{8,11},{9,10},{10,... | collective-permute-start | bytes 294920 | tf_op jit(solution)/shard_map/ppermute | solution.py:272
  17.7 16.0 %collective-permute-start.10 = (bf16[8,128,128]{2,1,0:T(8,128)(2,1)S(1)}, bf16[8,128,128]{2,1,0:T(8,128)(2,1)S(1)}, u32[]{:S(2)}, u32[]{:S(2)}) collective-permute-start(bf16[8,128,128]{2,1,0:T(8,128)(2,1)S(1)} %get-tuple-element.11), channel_id=1, source_target_pairs={{4,8},{8,4},{5,9},{9,5},{6,10},{10,6},{7,11},{11,7},{20,24},{24,20... | collective-permute-start | bytes 786440 | tf_op jit(solution)/shard_map/ppermute | solution.py:233
  18.4 15.3 %collective-permute-start.11 = (bf16[8,128,128]{2,1,0:T(8,128)(2,1)S(1)}, bf16[8,128,128]{2,1,0:T(8,128)(2,1)S(1)}, u32[]{:S(2)}, u32[]{:S(2)}) collective-permute-start(bf16[8,128,128]{2,1,0:T(8,128)(2,1)S(1)} %get-tuple-element.12), channel_id=1, source_target_pairs={{0,4},{8,12},{4,0},{12,8},{1,5},{9,13},{5,1},{13,9},{2,6},{10,14},... | collective-permute-start | bytes 786440 | tf_op jit(solution)/shard_map/ppermute | solution.py:233
  23.3 10.4 %collective-permute-start.4 = (bf16[384,128]{1,0:T(8,128)(2,1)S(1)}, bf16[384,128]{1,0:T(8,128)(2,1)S(1)}, u32[]{:S(2)}, u32[]{:S(2)}) collective-permute-start(bf16[384,128]{1,0:T(8,128)(2,1)S(1)} %load_q.4), channel_id=1, source_target_pairs={{0,2},{1,3},{2,0},{3,1},{4,6},{5,7},{6,4},{7,5},{8,10},{9,11},{10,... | collective-permute-start | bytes 294920 | tf_op jit(solution)/shard_map/ppermute | solution.py:272
  25.6 8.1 %collective-permute-start.7 = (bf16[384,128]{1,0:T(8,128)(2,1)S(1)}, bf16[384,128]{1,0:T(8,128)(2,1)S(1)}, u32[]{:S(2)}, u32[]{:S(2)}) collective-permute-start(bf16[384,128]{1,0:T(8,128)(2,1)S(1)} %load_q.5), channel_id=1, source_target_pairs={{0,3},{1,2},{2,1},{3,0},{4,7},{5,6},{6,5},{7,4},{8,11},{9,10},{10,... | collective-permute-start | bytes 294920 | tf_op jit(solution)/shard_map/ppermute | solution.py:272
  28.8 5.1 %collective-permute-start.8 = (bf16[8,128,128]{2,1,0:T(8,128)(2,1)S(1)}, bf16[8,128,128]{2,1,0:T(8,128)(2,1)S(1)}, u32[]{:S(2)}, u32[]{:S(2)}) collective-permute-start(bf16[8,128,128]{2,1,0:T(8,128)(2,1)S(1)} %get-tuple-element.9), channel_id=1, source_target_pairs={{4,8},{8,4},{5,9},{9,5},{6,10},{10,6},{7,11},{11,7},{20,24},{24,20... | collective-permute-start | bytes 786440 | tf_op jit(solution)/shard_map/ppermute | solution.py:233
  33.7 1.5 %collective-permute-start.9 = (bf16[8,128,128]{2,1,0:T(8,128)(2,1)S(1)}, bf16[8,128,128]{2,1,0:T(8,128)(2,1)S(1)}, u32[]{:S(2)}, u32[]{:S(2)}) collective-permute-start(bf16[8,128,128]{2,1,0:T(8,128)(2,1)S(1)} %get-tuple-element.10), channel_id=1, source_target_pairs={{0,4},{8,12},{4,0},{12,8},{1,5},{9,13},{5,1},{13,9},{2,6},{10,14},... | collective-permute-start | bytes 786440 | tf_op jit(solution)/shard_map/ppermute | solution.py:233
  37.0 9.8 %collective-permute-start.14 = (bf16[384,128]{1,0:T(8,128)(2,1)S(1)}, bf16[384,128]{1,0:T(8,128)(2,1)S(1)}, u32[]{:S(2)}, u32[]{:S(2)}) collective-permute-start(bf16[384,128]{1,0:T(8,128)(2,1)S(1)} %attend_chunk.4.refs_0_), channel_id=1, source_target_pairs={{0,3},{1,2},{2,1},{3,0},{4,7},{5,6},{6,5},{7,4},{8,11},{9,10},{10,... | collective-permute-start | bytes 294920 | tf_op jit(solution)/shard_map/ppermute | solution.py:272
  41.5 7.1 %collective-permute-start.13 = (bf16[384,128]{1,0:T(8,128)(2,1)S(1)}, bf16[384,128]{1,0:T(8,128)(2,1)S(1)}, u32[]{:S(2)}, u32[]{:S(2)}) collective-permute-start(bf16[384,128]{1,0:T(8,128)(2,1)S(1)} %attend_chunk.5.refs_0_), channel_id=1, source_target_pairs={{0,2},{1,3},{2,0},{3,1},{4,6},{5,7},{6,4},{7,5},{8,10},{9,11},{10,... | collective-permute-start | bytes 294920 | tf_op jit(solution)/shard_map/ppermute | solution.py:272
  43.3 6.9 %collective-permute-start.12 = (bf16[384,128]{1,0:T(8,128)(2,1)S(1)}, bf16[384,128]{1,0:T(8,128)(2,1)S(1)}, u32[]{:S(2)}, u32[]{:S(2)}) collective-permute-start(bf16[384,128]{1,0:T(8,128)(2,1)S(1)} %attend_chunk.6.refs_0_), channel_id=1, source_target_pairs={{0,1},{1,0},{2,3},{3,2},{4,5},{5,4},{6,7},{7,6},{8,9},{9,8},{10,11... | collective-permute-start | bytes 294920 | tf_op jit(solution)/shard_map/ppermute | solution.py:272

commit v14 on v13

--- a/solution.py
+++ b/solution.py
@@ -69,28 +69,26 @@
 
 
 def attend_block(first, q_ref, kt_ref, v_ref, bias_ref, out_ref, scores, probs):
-    for pair in range(WINDOW // 2):
-        low = max(0, 2 * pair - LIST + 1)
-        high = min(BLOCK - 1, 2 * pair + 1)
-        at = first + 2 * pair
-        keys = jnp.concatenate([kt_ref[at], kt_ref[at + 1]], axis=1)
-        part = jnp.dot(
-            q_ref[low * TILE : (high + 1) * TILE, :], keys, preferred_element_type=jnp.float32
-        )
-        for half in range(2):
-            for tile in range(low, high + 1):
-                offset = 2 * pair + half - tile
-                if 0 <= offset < LIST:
-                    bias = bias_ref[at + half, pl.ds(first + tile, 1), :]
-                    scores[tile, :, rows_of(offset)] = part[rows_of(tile - low), rows_of(half)] + bias
+    def score(tile):
+        row = first + tile
+        highest = jnp.full((TILE, TILE), HIDDEN, jnp.float32)
+        for offset in range(0, LIST, 2):
+            at = row + offset
+            keys = jnp.concatenate([kt_ref[at], kt_ref[at + 1]], axis=1)
+            part = jnp.dot(q_ref[rows_of(tile), :], keys, preferred_element_type=jnp.float32)
+            for half in range(2):
+                masked = part[:, rows_of(half)] + bias_ref[at + half, pl.ds(row, 1), :]
+                scores[tile, :, rows_of(offset + half)] = masked
+                highest = jnp.maximum(highest, masked)
+        return jnp.broadcast_to(jnp.max(highest, axis=1, keepdims=True), (TILE, TILE))
+
+    maxima = [score(0)]
     for tile in range(BLOCK):
-        highest = scores[tile, :, rows_of(0)]
-        for offset in range(1, LIST):
-            highest = jnp.maximum(highest, scores[tile, :, rows_of(offset)])
-        highest = jnp.broadcast_to(jnp.max(highest, axis=1, keepdims=True), (TILE, TILE))
+        if tile + 1 < BLOCK:
+            maxima.append(score(tile + 1))
         total = jnp.zeros((TILE, TILE), jnp.float32)
         for offset in range(LIST):
-            weights = jnp.exp2((scores[tile, :, rows_of(offset)] - highest) * EXPONENT_SCALE)
+            weights = jnp.exp2((scores[tile, :, rows_of(offset)] - maxima[tile]) * EXPONENT_SCALE)
             total += weights
             probs[tile, :, rows_of(offset)] = weights.astype(jnp.bfloat16)
         values = v_ref[pl.ds(first + tile, LIST)].reshape(LIST * TILE, HDIM)

time: 51.3 us -> 51 us (level)
  transfers between devices with their start and end apart: 15 -> 15, of which waited for: 6 -> 6; matrix products, arithmetic and copies ran while one was open for 0% -> 0% of each run, Pallas kernels for 13% -> 12%
where the time goes in v14:
time: 51 us; the launch traced here: 50.7 us
  starting transfers between devices  23.2 us (45%)
  waiting for transfers between devices  16.8 us (33%)
  Pallas kernels  8.8 us (17%)
  local copies, waits for them, and re-layouts  1.65 us (3%)
    ppermute x11, starting transfers between devices, exchange(): return lax.ppermute(array, 'head', [(i, i ^ pair) for i in range(heads)])  19 us
    ppermute x11, waiting for transfers between devices, exchange(): return lax.ppermute(array, 'head', [(i, i ^ pair) for i in range(heads)])  15.4 us
    pallas_call x28, Pallas kernels, call(): pl.pallas_call(kernel, out_shape=out_shape, in_specs=in_specs, out_specs=...  8.8 us
    ppermute x4, starting transfers between devices, exchange(): lax.ppermute(array, 'ctx', [(i, i + 1) for i in lower] + [(i + 1, i) for...  4.26 us
    unnamed x12, local copies, waits for them, and re-layouts  1.56 us
    ppermute x4, waiting for transfers between devices, exchange(): lax.ppermute(array, 'ctx', [(i, i + 1) for i in lower] + [(i + 1, i) for...  1.34 us
  transfers between devices with their start and end apart: 15, of which 6 were waited for; matrix products, arithmetic and copies ran while one was open for 0% of the time, Pallas kernels for 12%

profile of v14, /device:TPU:0, one launch (start us, length us, event | category | flops | bytes accessed | tf_op | source)
XLA Modules:
  0.0 50.7 jit_solution(15875112711998296549)
XLA Ops:
  0.0 1.0 %copy-done.2 = bf16[384,512]{1,0:T(8,128)(2,1)S(1)} copy-done((bf16[384,512]{1,0:T(8,128)(2,1)S(1)}, bf16[384,512]{1,0:T(8,128)(2,1)}, u32[]{:S(2)}) %copy-start.2) | copy-done | bytes 393240
  1.0 3.1 %collective-permute-start = (bf16[3,128,128]{2,1,0:T(8,128)(2,1)S(1)}, bf16[3,128,128]{2,1,0:T(8,128)(2,1)S(1)}, u32[]{:S(2)}, u32[]{:S(2)}) collective-permute-start(bf16[3,128,128]{2,1,0:T(8,128)(2,1)S(1)} %load_v.4), channel_id=1, source_target_pairs={{0,1},{1,0},{2,3},{3,2},{4,5},{5,4},{6,7},{7,6},{8,9},{9,8},{10,11... | collective-permute-start | bytes 294920 | tf_op jit(solution)/shard_map/ppermute | solution.py:270
  4.1 0.0 copy-start
  4.1 2.7 %collective-permute-start.2 = (bf16[3,128,128]{2,1,0:T(8,128)(2,1)S(1)}, bf16[3,128,128]{2,1,0:T(8,128)(2,1)S(1)}, u32[]{:S(2)}, u32[]{:S(2)}) collective-permute-start(bf16[3,128,128]{2,1,0:T(8,128)(2,1)S(1)} %load_v.5), channel_id=1, source_target_pairs={{0,2},{1,3},{2,0},{3,1},{4,6},{5,7},{6,4},{7,5},{8,10},{9,11},{10,... | collective-permute-start | bytes 294920 | tf_op jit(solution)/shard_map/ppermute | solution.py:270
  6.8 0.0 copy-start.4
  6.8 0.1 collective-permute-start.5
  6.9 0.5 %copy-done.5 = s32[12]{0:T(128)S(1)} copy-done((s32[12]{0:T(128)S(1)}, s32[12]{0:T(128)}, u32[]{:S(2)}) %copy-start.5) | copy-done | bytes 72
  7.5 0.1 copy.6.counts_ref
  7.6 0.6 %mask_bias.1.refs_1_.bias_ref = f32[27,12,128]{2,1,0:T(8,128)S(1)} custom-call(s32[12,16]{1,0:T(8,128)S(1)} %copy-done.4, s32[12,1]{1,0:T(8,128)S(1)} %copy.6.counts_ref), custom_call_target="tpu_custom_call" | custom-call | tf_op jit(solution)/shard_map/mask_bias/pallas_call | solution.py:29
  8.1 0.0 collective-permute-done.refs_0_.refs_1_
  8.2 0.1 load_k.4
  8.3 0.6 %collective-permute-start.1 = (bf16[6,128,128]{2,1,0:T(8,128)(2,1)S(1)}, bf16[6,128,128]{2,1,0:T(8,128)(2,1)S(1)}, u32[]{:S(2)}, u32[]{:S(2)}) collective-permute-start(bf16[6,128,128]{2,1,0:T(8,128)(2,1)S(1)} %load_k.4), channel_id=1, source_target_pairs={{0,1},{1,0},{2,3},{3,2},{4,5},{5,4},{6,7},{7,6},{8,9},{9,8},{10,11... | collective-permute-start | bytes 589832 | tf_op jit(solution)/shard_map/ppermute | solution.py:270
  8.9 5.8 %collective-permute-done.2.refs_0_.refs_2_ = bf16[3,128,128]{2,1,0:T(8,128)(2,1)S(1)} collective-permute-done((bf16[3,128,128]{2,1,0:T(8,128)(2,1)S(1)}, bf16[3,128,128]{2,1,0:T(8,128)(2,1)S(1)}, u32[]{:S(2)}, u32[]{:S(2)}) %collective-permute-start.2) | collective-permute-done | bytes 98336 | tf_op jit(solution)/shard_map/ppermute | solution.py:270
  14.7 0.1 load_k.5
  14.8 0.0 copy-start.3
  14.8 0.1 collective-permute-start.3
  14.9 0.0 collective-permute-done.5.refs_0_.refs_3_
  14.9 0.1 load_k.6
  15.0 2.6 %collective-permute-start.6 = (bf16[3,128,128]{2,1,0:T(8,128)(2,1)S(1)}, bf16[3,128,128]{2,1,0:T(8,128)(2,1)S(1)}, u32[]{:S(2)}, u32[]{:S(2)}) collective-permute-start(bf16[3,128,128]{2,1,0:T(8,128)(2,1)S(1)} %load_k.6), channel_id=1, source_target_pairs={{0,3},{1,2},{2,1},{3,0},{4,7},{5,6},{6,5},{7,4},{8,11},{9,10},{10,... | collective-permute-start | bytes 294920 | tf_op jit(solution)/shard_map/ppermute | solution.py:270
  17.7 0.7 %collective-permute-start.10 = (bf16[8,128,128]{2,1,0:T(8,128)(2,1)S(1)}, bf16[8,128,128]{2,1,0:T(8,128)(2,1)S(1)}, u32[]{:S(2)}, u32[]{:S(2)}) collective-permute-start(bf16[8,128,128]{2,1,0:T(8,128)(2,1)S(1)} %get-tuple-element.11), channel_id=1, source_target_pairs={{4,8},{8,4},{5,9},{9,5},{6,10},{10,6},{7,11},{11,7},{20,24},{24,20... | collective-permute-start | bytes 786440 | tf_op jit(solution)/shard_map/ppermute | solution.py:231
  18.4 2.9 %collective-permute-start.11 = (bf16[8,128,128]{2,1,0:T(8,128)(2,1)S(1)}, bf16[8,128,128]{2,1,0:T(8,128)(2,1)S(1)}, u32[]{:S(2)}, u32[]{:S(2)}) collective-permute-start(bf16[8,128,128]{2,1,0:T(8,128)(2,1)S(1)} %get-tuple-element.12), channel_id=1, source_target_pairs={{0,4},{8,12},{4,0},{12,8},{1,5},{9,13},{5,1},{13,9},{2,6},{10,14},... | collective-permute-start | bytes 786440 | tf_op jit(solution)/shard_map/ppermute | solution.py:231
  21.3 1.9 %collective-permute-done.3.refs_0_.refs_2_ = bf16[3,128,128]{2,1,0:T(8,128)(2,1)S(1)} collective-permute-done((bf16[3,128,128]{2,1,0:T(8,128)(2,1)S(1)}, bf16[3,128,128]{2,1,0:T(8,128)(2,1)S(1)}, u32[]{:S(2)}, u32[]{:S(2)}) %collective-permute-start.3) | collective-permute-done | bytes 98336 | tf_op jit(solution)/shard_map/ppermute | solution.py:270
  23.3 2.3 %collective-permute-start.4 = (bf16[384,128]{1,0:T(8,128)(2,1)S(1)}, bf16[384,128]{1,0:T(8,128)(2,1)S(1)}, u32[]{:S(2)}, u32[]{:S(2)}) collective-permute-start(bf16[384,128]{1,0:T(8,128)(2,1)S(1)} %load_q.4), channel_id=1, source_target_pairs={{0,2},{1,3},{2,0},{3,1},{4,6},{5,7},{6,4},{7,5},{8,10},{9,11},{10,... | collective-permute-start | bytes 294920 | tf_op jit(solution)/shard_map/ppermute | solution.py:270
  25.6 0.0 collective-permute-done.6.refs_0_.refs_3_
  25.6 3.0 %collective-permute-start.7 = (bf16[384,128]{1,0:T(8,128)(2,1)S(1)}, bf16[384,128]{1,0:T(8,128)(2,1)S(1)}, u32[]{:S(2)}, u32[]{:S(2)}) collective-permute-start(bf16[384,128]{1,0:T(8,128)(2,1)S(1)} %load_q.5), channel_id=1, source_target_pairs={{0,3},{1,2},{2,1},{3,0},{4,7},{5,6},{6,5},{7,4},{8,11},{9,10},{10,... | collective-permute-start | bytes 294920 | tf_op jit(solution)/shard_map/ppermute | solution.py:270
  28.6 0.1 load_k.7.refs_0_
  28.7 0.0 collective-permute-done.1.refs_1_
  28.8 0.7 %collective-permute-start.8 = (bf16[8,128,128]{2,1,0:T(8,128)(2,1)S(1)}, bf16[8,128,128]{2,1,0:T(8,128)(2,1)S(1)}, u32[]{:S(2)}, u32[]{:S(2)}) collective-permute-start(bf16[8,128,128]{2,1,0:T(8,128)(2,1)S(1)} %get-tuple-element.9), channel_id=1, source_target_pairs={{4,8},{8,4},{5,9},{9,5},{6,10},{10,6},{7,11},{11,7},{20,24},{24,20... | collective-permute-start | bytes 786440 | tf_op jit(solution)/shard_map/ppermute | solution.py:231
  29.5 4.2 %collective-permute-done.4.refs_2_ = bf16[384,128]{1,0:T(8,128)(2,1)S(1)} collective-permute-done((bf16[384,128]{1,0:T(8,128)(2,1)S(1)}, bf16[384,128]{1,0:T(8,128)(2,1)S(1)}, u32[]{:S(2)}, u32[]{:S(2)}) %collective-permute-start.4) | collective-permute-done | bytes 98336 | tf_op jit(solution)/shard_map/ppermute | solution.py:270
  33.7 0.0 collective-permute-start.9
  33.7 0.0 collective-permute-done.7.refs_3_
  33.7 0.0 collective-permute-done.11.second_ref
  33.7 0.1 join.3.array_ref
  33.8 0.1 values.1.v_ref
  33.9 0.0 collective-permute-done.8.first_ref
  33.9 1.3 %collective-permute-done.9.second_ref = bf16[8,128,128]{2,1,0:T(8,128)(2,1)S(1)} collective-permute-done((bf16[8,128,128]{2,1,0:T(8,128)(2,1)S(1)}, bf16[8,128,128]{2,1,0:T(8,128)(2,1)S(1)}, u32[]{:S(2)}, u32[]{:S(2)}) %collective-permute-start.9) | collective-permute-done | bytes 262176 | tf_op jit(solution)/shard_map/ppermute | solution.py:231
  35.2 0.1 join.2.kt_ref
  35.3 1.6 %attend_chunk.4.refs_0_ = bf16[384,128]{1,0:T(8,128)(2,1)S(1)} custom-call(bf16[4,384,128]{2,1,0:T(8,128)(2,1)S(1)} %stack.1.refs_0_.q_ref, bf16[27,128,128]{2,1,0:T(8,128)(2,1)S(1)} %join.2.kt_ref, bf16[27,128,128]{2,1,0:T(8,128)(2,1)S(1)} %values.1.v_ref, f32[27,12,128]{2,1,0:T(8,128)S(1)} %mask_bias.1.refs_1_.bias_ref), custom_call_target="tpu_custom_call" | custom-call | flops 201326592 | bytes 393216 | tf_op jit(solution)/shard_map/attend_chunk/pallas_call | solution.py:29
  36.9 2.8 %collective-permute-start.14 = (bf16[384,128]{1,0:T(8,128)(2,1)S(1)}, bf16[384,128]{1,0:T(8,128)(2,1)S(1)}, u32[]{:S(2)}, u32[]{:S(2)}) collective-permute-start(bf16[384,128]{1,0:T(8,128)(2,1)S(1)} %attend_chunk.4.refs_0_), channel_id=1, source_target_pairs={{0,3},{1,2},{2,1},{3,0},{4,7},{5,6},{6,5},{7,4},{8,11},{9,10},{10,... | collective-permute-start | bytes 294920 | tf_op jit(solution)/shard_map/ppermute | solution.py:270
  39.7 1.6 %attend_chunk.5.refs_0_ = bf16[384,128]{1,0:T(8,128)(2,1)S(1)} custom-call(bf16[4,384,128]{2,1,0:T(8,128)(2,1)S(1)} %stack.1.refs_0_.q_ref, bf16[27,128,128]{2,1,0:T(8,128)(2,1)S(1)} %join.2.kt_ref, bf16[27,128,128]{2,1,0:T(8,128)(2,1)S(1)} %values.1.v_ref, f32[27,12,128]{2,1,0:T(8,128)S(1)} %mask_bias.1.refs_1_.bias_ref, ...), custom_call_target="tpu_custom_call" | custom-call | flops 201326592 | bytes 393216 | tf_op jit(solution)/shard_map/attend_chunk/pallas_call | solution.py:29
  41.3 0.1 collective-permute-start.13
  41.4 1.6 %attend_chunk.6.refs_0_ = bf16[384,128]{1,0:T(8,128)(2,1)S(1)} custom-call(bf16[4,384,128]{2,1,0:T(8,128)(2,1)S(1)} %stack.1.refs_0_.q_ref, bf16[27,128,128]{2,1,0:T(8,128)(2,1)S(1)} %join.2.kt_ref, bf16[27,128,128]{2,1,0:T(8,128)(2,1)S(1)} %values.1.v_ref, f32[27,12,128]{2,1,0:T(8,128)S(1)} %mask_bias.1.refs_1_.bias_ref, ...), custom_call_target="tpu_custom_call" | custom-call | flops 201326592 | bytes 393216 | tf_op jit(solution)/shard_map/attend_chunk/pallas_call | solution.py:29
  43.0 1.7 %collective-permute-start.12 = (bf16[384,128]{1,0:T(8,128)(2,1)S(1)}, bf16[384,128]{1,0:T(8,128)(2,1)S(1)}, u32[]{:S(2)}, u32[]{:S(2)}) collective-permute-start(bf16[384,128]{1,0:T(8,128)(2,1)S(1)} %attend_chunk.6.refs_0_), channel_id=1, source_target_pairs={{0,1},{1,0},{2,3},{3,2},{4,5},{5,4},{6,7},{7,6},{8,9},{9,8},{10,11... | collective-permute-start | bytes 294920 | tf_op jit(solution)/shard_map/ppermute | solution.py:270
  44.7 1.6 %attend_chunk.7.refs_0_ = bf16[384,128]{1,0:T(8,128)(2,1)S(1)} custom-call(bf16[4,384,128]{2,1,0:T(8,128)(2,1)S(1)} %stack.1.refs_0_.q_ref, bf16[27,128,128]{2,1,0:T(8,128)(2,1)S(1)} %join.2.kt_ref, bf16[27,128,128]{2,1,0:T(8,128)(2,1)S(1)} %values.1.v_ref, f32[27,12,128]{2,1,0:T(8,128)S(1)} %mask_bias.1.refs_1_.bias_ref, ...), custom_call_target="tpu_custom_call" | custom-call | flops 8388608 | bytes 16384 | tf_op jit(solution)/shard_map/attend_chunk/pallas_call | solution.py:29
  46.4 0.0 collective-permute-done.14.array_ref
  46.4 2.2 %collective-permute-done.13.array_ref = bf16[384,128]{1,0:T(8,128)(2,1)S(1)} collective-permute-done((bf16[384,128]{1,0:T(8,128)(2,1)S(1)}, bf16[384,128]{1,0:T(8,128)(2,1)S(1)}, u32[]{:S(2)}, u32[]{:S(2)}) %collective-permute-start.13) | collective-permute-done | bytes 98336 | tf_op jit(solution)/shard_map/ppermute | solution.py:270
  48.6 1.3 %collective-permute-done.12.array_ref = bf16[384,128]{1,0:T(8,128)(2,1)S(1)} collective-permute-done((bf16[384,128]{1,0:T(8,128)(2,1)S(1)}, bf16[384,128]{1,0:T(8,128)(2,1)S(1)}, u32[]{:S(2)}, u32[]{:S(2)}) %collective-permute-start.12) | collective-permute-done | bytes 98336 | tf_op jit(solution)/shard_map/ppermute | solution.py:270
  49.9 0.8 %spread.1 = bf16[384,512]{1,0:T(8,128)(2,1)} custom-call(bf16[384,128]{1,0:T(8,128)(2,1)S(1)} %attend_chunk.7.refs_0_, bf16[384,128]{1,0:T(8,128)(2,1)S(1)} %landed.5.refs_1_, bf16[384,128]{1,0:T(8,128)(2,1)S(1)} %landed.4.refs_0_.refs_2_, bf16[384,128]{1,0:T(8,128)(2,1)S(1)} %landed.3.refs_0_.refs_3_), custom_call_target="tpu_custom_call" | custom-call | tf_op jit(solution)/shard_map/spread/pallas_call | solution.py:29
  (23 shorter events, 0.4 us)
Async XLA Ops:
  0.0 1.0 %copy-start.2 = (bf16[384,512]{1,0:T(8,128)(2,1)S(1)}, bf16[384,512]{1,0:T(8,128)(2,1)}, u32[]{:S(2)}) copy-start(bf16[384,512]{1,0:T(8,128)(2,1)} %array_ref.13) | copy-start | bytes 1179652
  1.0 7.1 %collective-permute-start = (bf16[3,128,128]{2,1,0:T(8,128)(2,1)S(1)}, bf16[3,128,128]{2,1,0:T(8,128)(2,1)S(1)}, u32[]{:S(2)}, u32[]{:S(2)}) collective-permute-start(bf16[3,128,128]{2,1,0:T(8,128)(2,1)S(1)} %load_v.4), channel_id=1, source_target_pairs={{0,1},{1,0},{2,3},{3,2},{4,5},{5,4},{6,7},{7,6},{8,9},{9,8},{10,11... | collective-permute-start | bytes 294920 | tf_op jit(solution)/shard_map/ppermute | solution.py:270
  4.1 4.0 %copy-start.1 = (bf16[384,512]{1,0:T(8,128)(2,1)S(1)}, bf16[384,512]{1,0:T(8,128)(2,1)}, u32[]{:S(2)}) copy-start(bf16[384,512]{1,0:T(8,128)(2,1)} %array_ref.12) | copy-start | bytes 1179652
  4.1 4.0 %copy-start = (bf16[384,512]{1,0:T(8,128)(2,1)S(1)}, bf16[384,512]{1,0:T(8,128)(2,1)}, u32[]{:S(2)}) copy-start(bf16[384,512]{1,0:T(8,128)(2,1)} %q_ref.7) | copy-start | bytes 1179652
  4.1 10.6 %collective-permute-start.2 = (bf16[3,128,128]{2,1,0:T(8,128)(2,1)S(1)}, bf16[3,128,128]{2,1,0:T(8,128)(2,1)S(1)}, u32[]{:S(2)}, u32[]{:S(2)}) collective-permute-start(bf16[3,128,128]{2,1,0:T(8,128)(2,1)S(1)} %load_v.5), channel_id=1, source_target_pairs={{0,2},{1,3},{2,0},{3,1},{4,6},{5,7},{6,4},{7,5},{8,10},{9,11},{10,... | collective-permute-start | bytes 294920 | tf_op jit(solution)/shard_map/ppermute | solution.py:270
  6.8 0.7 %copy-start.5 = (s32[12]{0:T(128)S(1)}, s32[12]{0:T(128)}, u32[]{:S(2)}) copy-start(s32[12]{0:T(128)} %param.9) | copy-start | bytes 148
  6.8 0.7 %copy-start.4 = (s32[12,16]{1,0:T(8,128)S(1)}, s32[12,16]{1,0:T(8,128)}, u32[]{:S(2)}) copy-start(s32[12,16]{1,0:T(8,128)} %lists_ref.1) | copy-start | bytes 2308
  6.8 8.0 %collective-permute-start.5 = (bf16[3,128,128]{2,1,0:T(8,128)(2,1)S(1)}, bf16[3,128,128]{2,1,0:T(8,128)(2,1)S(1)}, u32[]{:S(2)}, u32[]{:S(2)}) collective-permute-start(bf16[3,128,128]{2,1,0:T(8,128)(2,1)S(1)} %load_v.6), channel_id=1, source_target_pairs={{0,3},{1,2},{2,1},{3,0},{4,7},{5,6},{6,5},{7,4},{8,11},{9,10},{10,... | collective-permute-start | bytes 294920 | tf_op jit(solution)/shard_map/ppermute | solution.py:270
  8.3 20.4 %collective-permute-start.1 = (bf16[6,128,128]{2,1,0:T(8,128)(2,1)S(1)}, bf16[6,128,128]{2,1,0:T(8,128)(2,1)S(1)}, u32[]{:S(2)}, u32[]{:S(2)}) collective-permute-start(bf16[6,128,128]{2,1,0:T(8,128)(2,1)S(1)} %load_k.4), channel_id=1, source_target_pairs={{0,1},{1,0},{2,3},{3,2},{4,5},{5,4},{6,7},{7,6},{8,9},{9,8},{10,11... | collective-permute-start | bytes 589832 | tf_op jit(solution)/shard_map/ppermute | solution.py:270
  14.8 2.8 %copy-start.3 = (bf16[384,512]{1,0:T(8,128)(2,1)S(1)}, bf16[384,512]{1,0:T(8,128)(2,1)}, u32[]{:S(2)}) copy-start(bf16[384,512]{1,0:T(8,128)(2,1)} %array_ref.13) | copy-start | bytes 1179652
  14.8 8.4 %collective-permute-start.3 = (bf16[3,128,128]{2,1,0:T(8,128)(2,1)S(1)}, bf16[3,128,128]{2,1,0:T(8,128)(2,1)S(1)}, u32[]{:S(2)}, u32[]{:S(2)}) collective-permute-start(bf16[3,128,128]{2,1,0:T(8,128)(2,1)S(1)} %load_k.5), channel_id=1, source_target_pairs={{0,2},{1,3},{2,0},{3,1},{4,6},{5,7},{6,4},{7,5},{8,10},{9,11},{10,... | collective-permute-start | bytes 294920 | tf_op jit(solution)/shard_map/ppermute | solution.py:270
  15.0 10.6 %collective-permute-start.6 = (bf16[3,128,128]{2,1,0:T(8,128)(2,1)S(1)}, bf16[3,128,128]{2,1,0:T(8,128)(2,1)S(1)}, u32[]{:S(2)}, u32[]{:S(2)}) collective-permute-start(bf16[3,128,128]{2,1,0:T(8,128)(2,1)S(1)} %load_k.6), channel_id=1, source_target_pairs={{0,3},{1,2},{2,1},{3,0},{4,7},{5,6},{6,5},{7,4},{8,11},{9,10},{10,... | collective-permute-start | bytes 294920 | tf_op jit(solution)/shard_map/ppermute | solution.py:270
  17.7 16.0 %collective-permute-start.10 = (bf16[8,128,128]{2,1,0:T(8,128)(2,1)S(1)}, bf16[8,128,128]{2,1,0:T(8,128)(2,1)S(1)}, u32[]{:S(2)}, u32[]{:S(2)}) collective-permute-start(bf16[8,128,128]{2,1,0:T(8,128)(2,1)S(1)} %get-tuple-element.11), channel_id=1, source_target_pairs={{4,8},{8,4},{5,9},{9,5},{6,10},{10,6},{7,11},{11,7},{20,24},{24,20... | collective-permute-start | bytes 786440 | tf_op jit(solution)/shard_map/ppermute | solution.py:231
  18.4 15.3 %collective-permute-start.11 = (bf16[8,128,128]{2,1,0:T(8,128)(2,1)S(1)}, bf16[8,128,128]{2,1,0:T(8,128)(2,1)S(1)}, u32[]{:S(2)}, u32[]{:S(2)}) collective-permute-start(bf16[8,128,128]{2,1,0:T(8,128)(2,1)S(1)} %get-tuple-element.12), channel_id=1, source_target_pairs={{0,4},{8,12},{4,0},{12,8},{1,5},{9,13},{5,1},{13,9},{2,6},{10,14},... | collective-permute-start | bytes 786440 | tf_op jit(solution)/shard_map/ppermute | solution.py:231
  23.3 10.4 %collective-permute-start.4 = (bf16[384,128]{1,0:T(8,128)(2,1)S(1)}, bf16[384,128]{1,0:T(8,128)(2,1)S(1)}, u32[]{:S(2)}, u32[]{:S(2)}) collective-permute-start(bf16[384,128]{1,0:T(8,128)(2,1)S(1)} %load_q.4), channel_id=1, source_target_pairs={{0,2},{1,3},{2,0},{3,1},{4,6},{5,7},{6,4},{7,5},{8,10},{9,11},{10,... | collective-permute-start | bytes 294920 | tf_op jit(solution)/shard_map/ppermute | solution.py:270
  25.6 8.1 %collective-permute-start.7 = (bf16[384,128]{1,0:T(8,128)(2,1)S(1)}, bf16[384,128]{1,0:T(8,128)(2,1)S(1)}, u32[]{:S(2)}, u32[]{:S(2)}) collective-permute-start(bf16[384,128]{1,0:T(8,128)(2,1)S(1)} %load_q.5), channel_id=1, source_target_pairs={{0,3},{1,2},{2,1},{3,0},{4,7},{5,6},{6,5},{7,4},{8,11},{9,10},{10,... | collective-permute-start | bytes 294920 | tf_op jit(solution)/shard_map/ppermute | solution.py:270
  28.8 5.1 %collective-permute-start.8 = (bf16[8,128,128]{2,1,0:T(8,128)(2,1)S(1)}, bf16[8,128,128]{2,1,0:T(8,128)(2,1)S(1)}, u32[]{:S(2)}, u32[]{:S(2)}) collective-permute-start(bf16[8,128,128]{2,1,0:T(8,128)(2,1)S(1)} %get-tuple-element.9), channel_id=1, source_target_pairs={{4,8},{8,4},{5,9},{9,5},{6,10},{10,6},{7,11},{11,7},{20,24},{24,20... | collective-permute-start | bytes 786440 | tf_op jit(solution)/shard_map/ppermute | solution.py:231
  33.7 1.5 %collective-permute-start.9 = (bf16[8,128,128]{2,1,0:T(8,128)(2,1)S(1)}, bf16[8,128,128]{2,1,0:T(8,128)(2,1)S(1)}, u32[]{:S(2)}, u32[]{:S(2)}) collective-permute-start(bf16[8,128,128]{2,1,0:T(8,128)(2,1)S(1)} %get-tuple-element.10), channel_id=1, source_target_pairs={{0,4},{8,12},{4,0},{12,8},{1,5},{9,13},{5,1},{13,9},{2,6},{10,14},... | collective-permute-start | bytes 786440 | tf_op jit(solution)/shard_map/ppermute | solution.py:231
  36.9 9.5 %collective-permute-start.14 = (bf16[384,128]{1,0:T(8,128)(2,1)S(1)}, bf16[384,128]{1,0:T(8,128)(2,1)S(1)}, u32[]{:S(2)}, u32[]{:S(2)}) collective-permute-start(bf16[384,128]{1,0:T(8,128)(2,1)S(1)} %attend_chunk.4.refs_0_), channel_id=1, source_target_pairs={{0,3},{1,2},{2,1},{3,0},{4,7},{5,6},{6,5},{7,4},{8,11},{9,10},{10,... | collective-permute-start | bytes 294920 | tf_op jit(solution)/shard_map/ppermute | solution.py:270
  41.3 7.2 %collective-permute-start.13 = (bf16[384,128]{1,0:T(8,128)(2,1)S(1)}, bf16[384,128]{1,0:T(8,128)(2,1)S(1)}, u32[]{:S(2)}, u32[]{:S(2)}) collective-permute-start(bf16[384,128]{1,0:T(8,128)(2,1)S(1)} %attend_chunk.5.refs_0_), channel_id=1, source_target_pairs={{0,2},{1,3},{2,0},{3,1},{4,6},{5,7},{6,4},{7,5},{8,10},{9,11},{10,... | collective-permute-start | bytes 294920 | tf_op jit(solution)/shard_map/ppermute | solution.py:270
  43.0 6.9 %collective-permute-start.12 = (bf16[384,128]{1,0:T(8,128)(2,1)S(1)}, bf16[384,128]{1,0:T(8,128)(2,1)S(1)}, u32[]{:S(2)}, u32[]{:S(2)}) collective-permute-start(bf16[384,128]{1,0:T(8,128)(2,1)S(1)} %attend_chunk.6.refs_0_), channel_id=1, source_target_pairs={{0,1},{1,0},{2,3},{3,2},{4,5},{5,4},{6,7},{7,6},{8,9},{9,8},{10,11... | collective-permute-start | bytes 294920 | tf_op jit(solution)/shard_map/ppermute | solution.py:270

commit v15 on v14

--- a/solution.py
+++ b/solution.py
@@ -280,7 +280,7 @@
         operands = (keys, queries) if pair == 1 else (keys,)
         kernel = load_kq_kernel if pair == 1 else functools.partial(load_tiles_kernel, turn=True)
         shape = (len(operands) * BLOCK, TILE, HDIM)
-        after = (v_parts[pair],) if pair else ()
+        after = (v_parts[1],) if pair else ()
         if pair == order[0]:
             after += (bias,)
         part = call_on(functools.partial(kernel, pair), "load_k", (*operands, *after), shape)

time: 51 us -> 50.7 us (level)
  waiting for transfers between devices: 16.8 us -> 15 us
  local copies, waits for them, and re-layouts: 1.65 us -> 2.49 us
  starting transfers between devices: 23.2 us -> 24 us
    ppermute x4, waiting for transfers between devices: 1.34 us -> 0.01 us  [exchange(): lax.ppermute(array, 'ctx', [(i, i + 1) for i in lower] + [(i + 1, i) for...]
    unnamed x12, local copies, waits for them, and re-layouts: 1.56 us -> 2.4 us
    ppermute x11, starting transfers between devices: 19 us -> 19.7 us  [exchange(): return lax.ppermute(array, 'head', [(i, i ^ pair) for i in range(heads)])]
where the time goes in v15:
time: 50.7 us; the launch traced here: 50.5 us
  starting transfers between devices  24 us (47%)
  waiting for transfers between devices  15 us (30%)
  Pallas kernels  8.81 us (17%)
  local copies, waits for them, and re-layouts  2.49 us (5%)
    ppermute x11, starting transfers between devices, exchange(): return lax.ppermute(array, 'head', [(i, i ^ pair) for i in range(heads)])  19.7 us
    ppermute x11, waiting for transfers between devices, exchange(): return lax.ppermute(array, 'head', [(i, i ^ pair) for i in range(heads)])  14.9 us
    pallas_call x28, Pallas kernels, call(): pl.pallas_call(kernel, out_shape=out_shape, in_specs=in_specs, out_specs=...  8.81 us
    ppermute x4, starting transfers between devices, exchange(): lax.ppermute(array, 'ctx', [(i, i + 1) for i in lower] + [(i + 1, i) for...  4.26 us
    unnamed x12, local copies, waits for them, and re-layouts  2.4 us
  transfers between devices with their start and end apart: 15, of which 6 were waited for; matrix products, arithmetic and copies ran while one was open for 0% of the time, Pallas kernels for 12%

profile of v15, /device:TPU:0, one launch (start us, length us, event | category | flops | bytes accessed | tf_op | source)
XLA Modules:
  0.0 50.5 jit_solution(18405822156873290716)
XLA Ops:
  0.0 1.0 %copy-done.2 = bf16[384,512]{1,0:T(8,128)(2,1)S(1)} copy-done((bf16[384,512]{1,0:T(8,128)(2,1)S(1)}, bf16[384,512]{1,0:T(8,128)(2,1)}, u32[]{:S(2)}) %copy-start.2) | copy-done | bytes 393240
  1.0 0.0 copy-start
  1.0 0.0 copy-start.1
  1.0 3.1 %collective-permute-start = (bf16[3,128,128]{2,1,0:T(8,128)(2,1)S(1)}, bf16[3,128,128]{2,1,0:T(8,128)(2,1)S(1)}, u32[]{:S(2)}, u32[]{:S(2)}) collective-permute-start(bf16[3,128,128]{2,1,0:T(8,128)(2,1)S(1)} %load_v.4), channel_id=1, source_target_pairs={{0,1},{1,0},{2,3},{3,2},{4,5},{5,4},{6,7},{7,6},{8,9},{9,8},{10,11... | collective-permute-start | bytes 294920 | tf_op jit(solution)/shard_map/ppermute | solution.py:270
  4.2 2.7 %collective-permute-start.8 = (bf16[3,128,128]{2,1,0:T(8,128)(2,1)S(1)}, bf16[3,128,128]{2,1,0:T(8,128)(2,1)S(1)}, u32[]{:S(2)}, u32[]{:S(2)}) collective-permute-start(bf16[3,128,128]{2,1,0:T(8,128)(2,1)S(1)} %load_v.6), channel_id=1, source_target_pairs={{0,2},{1,3},{2,0},{3,1},{4,6},{5,7},{6,4},{7,5},{8,10},{9,11},{10,... | collective-permute-start | bytes 294920 | tf_op jit(solution)/shard_map/ppermute | solution.py:270
  6.8 0.0 copy-start.5
  6.8 0.1 collective-permute-start.9
  6.9 0.6 %copy-done.5 = s32[12]{0:T(128)S(1)} copy-done((s32[12]{0:T(128)S(1)}, s32[12]{0:T(128)}, u32[]{:S(2)}) %copy-start.5) | copy-done | bytes 72
  7.5 0.1 copy.6.counts_ref
  7.6 0.0 collective-permute-done.refs_0_.refs_1_
  7.6 0.1 load_k.4
  7.7 0.0 copy-start.4
  7.7 1.2 %collective-permute-start.1 = (bf16[6,128,128]{2,1,0:T(8,128)(2,1)S(1)}, bf16[6,128,128]{2,1,0:T(8,128)(2,1)S(1)}, u32[]{:S(2)}, u32[]{:S(2)}) collective-permute-start(bf16[6,128,128]{2,1,0:T(8,128)(2,1)S(1)} %load_k.4), channel_id=1, source_target_pairs={{0,1},{1,0},{2,3},{3,2},{4,5},{5,4},{6,7},{7,6},{8,9},{9,8},{10,11... | collective-permute-start | bytes 589832 | tf_op jit(solution)/shard_map/ppermute | solution.py:270
  8.9 0.1 load_k.5
  9.0 3.7 %collective-permute-start.2 = (bf16[3,128,128]{2,1,0:T(8,128)(2,1)S(1)}, bf16[3,128,128]{2,1,0:T(8,128)(2,1)S(1)}, u32[]{:S(2)}, u32[]{:S(2)}) collective-permute-start(bf16[3,128,128]{2,1,0:T(8,128)(2,1)S(1)} %load_k.5), channel_id=1, source_target_pairs={{0,2},{1,3},{2,0},{3,1},{4,6},{5,7},{6,4},{7,5},{8,10},{9,11},{10,... | collective-permute-start | bytes 294920 | tf_op jit(solution)/shard_map/ppermute | solution.py:270
  12.7 0.6 %mask_bias.1.refs_1_.bias_ref = f32[27,12,128]{2,1,0:T(8,128)S(1)} custom-call(s32[12,16]{1,0:T(8,128)S(1)} %copy-done.4, s32[12,1]{1,0:T(8,128)S(1)} %copy.6.counts_ref), custom_call_target="tpu_custom_call" | custom-call | tf_op jit(solution)/shard_map/mask_bias/pallas_call | solution.py:29
  13.3 0.0 copy-start.3
  13.3 0.1 load_k.6
  13.4 0.1 collective-permute-start.4
  13.5 0.8 %copy-done.3 = bf16[384,512]{1,0:T(8,128)(2,1)S(1)} copy-done((bf16[384,512]{1,0:T(8,128)(2,1)S(1)}, bf16[384,512]{1,0:T(8,128)(2,1)}, u32[]{:S(2)}) %copy-start.3) | copy-done | bytes 393240
  14.3 0.4 collective-permute-done.8.refs_2_
  14.7 0.0 collective-permute-done.9.refs_3_
  14.8 0.7 %collective-permute-start.10 = (bf16[8,128,128]{2,1,0:T(8,128)(2,1)S(1)}, bf16[8,128,128]{2,1,0:T(8,128)(2,1)S(1)}, u32[]{:S(2)}, u32[]{:S(2)}) collective-permute-start(bf16[8,128,128]{2,1,0:T(8,128)(2,1)S(1)} %get-tuple-element.11), channel_id=1, source_target_pairs={{4,8},{8,4},{5,9},{9,5},{6,10},{10,6},{7,11},{11,7},{20,24},{24,20... | collective-permute-start | bytes 786440 | tf_op jit(solution)/shard_map/ppermute | solution.py:231
  15.5 2.9 %collective-permute-start.11 = (bf16[8,128,128]{2,1,0:T(8,128)(2,1)S(1)}, bf16[8,128,128]{2,1,0:T(8,128)(2,1)S(1)}, u32[]{:S(2)}, u32[]{:S(2)}) collective-permute-start(bf16[8,128,128]{2,1,0:T(8,128)(2,1)S(1)} %get-tuple-element.12), channel_id=1, source_target_pairs={{0,4},{8,12},{4,0},{12,8},{1,5},{9,13},{5,1},{13,9},{2,6},{10,14},... | collective-permute-start | bytes 786440 | tf_op jit(solution)/shard_map/ppermute | solution.py:231
  18.4 4.7 %collective-permute-done.2.refs_0_.refs_2_ = bf16[3,128,128]{2,1,0:T(8,128)(2,1)S(1)} collective-permute-done((bf16[3,128,128]{2,1,0:T(8,128)(2,1)S(1)}, bf16[3,128,128]{2,1,0:T(8,128)(2,1)S(1)}, u32[]{:S(2)}, u32[]{:S(2)}) %collective-permute-start.2) | collective-permute-done | bytes 98336 | tf_op jit(solution)/shard_map/ppermute | solution.py:270
  23.1 3.3 %collective-permute-start.3 = (bf16[384,128]{1,0:T(8,128)(2,1)S(1)}, bf16[384,128]{1,0:T(8,128)(2,1)S(1)}, u32[]{:S(2)}, u32[]{:S(2)}) collective-permute-start(bf16[384,128]{1,0:T(8,128)(2,1)S(1)} %load_q.4), channel_id=1, source_target_pairs={{0,2},{1,3},{2,0},{3,1},{4,6},{5,7},{6,4},{7,5},{8,10},{9,11},{10,... | collective-permute-start | bytes 294920 | tf_op jit(solution)/shard_map/ppermute | solution.py:270
  26.4 0.0 collective-permute-done.4.refs_0_.refs_3_
  26.4 0.1 collective-permute-start.5
  26.6 0.1 load_k.7.refs_0_
  26.7 0.0 collective-permute-done.1.refs_1_
  26.8 0.7 %collective-permute-start.6 = (bf16[8,128,128]{2,1,0:T(8,128)(2,1)S(1)}, bf16[8,128,128]{2,1,0:T(8,128)(2,1)S(1)}, u32[]{:S(2)}, u32[]{:S(2)}) collective-permute-start(bf16[8,128,128]{2,1,0:T(8,128)(2,1)S(1)} %get-tuple-element.9), channel_id=1, source_target_pairs={{4,8},{8,4},{5,9},{9,5},{6,10},{10,6},{7,11},{11,7},{20,24},{24,20... | collective-permute-start | bytes 786440 | tf_op jit(solution)/shard_map/ppermute | solution.py:231
  27.4 3.0 %collective-permute-done.3.refs_2_ = bf16[384,128]{1,0:T(8,128)(2,1)S(1)} collective-permute-done((bf16[384,128]{1,0:T(8,128)(2,1)S(1)}, bf16[384,128]{1,0:T(8,128)(2,1)S(1)}, u32[]{:S(2)}, u32[]{:S(2)}) %collective-permute-start.3) | collective-permute-done | bytes 98336 | tf_op jit(solution)/shard_map/ppermute | solution.py:270
  30.5 2.5 %collective-permute-done.5.refs_3_ = bf16[384,128]{1,0:T(8,128)(2,1)S(1)} collective-permute-done((bf16[384,128]{1,0:T(8,128)(2,1)S(1)}, bf16[384,128]{1,0:T(8,128)(2,1)S(1)}, u32[]{:S(2)}, u32[]{:S(2)}) %collective-permute-start.5) | collective-permute-done | bytes 98336 | tf_op jit(solution)/shard_map/ppermute | solution.py:270
  33.0 0.0 collective-permute-done.10.first_ref
  33.0 0.1 join.3.array_ref
  33.1 0.1 values.1.v_ref
  33.2 0.0 collective-permute-done.7.second_ref
  33.2 0.1 join.2.kt_ref
  33.3 1.6 %attend_chunk.4.refs_0_ = bf16[384,128]{1,0:T(8,128)(2,1)S(1)} custom-call(bf16[4,384,128]{2,1,0:T(8,128)(2,1)S(1)} %stack.1.refs_0_.q_ref, bf16[27,128,128]{2,1,0:T(8,128)(2,1)S(1)} %join.2.kt_ref, bf16[27,128,128]{2,1,0:T(8,128)(2,1)S(1)} %values.1.v_ref, f32[27,12,128]{2,1,0:T(8,128)S(1)} %mask_bias.1.refs_1_.bias_ref), custom_call_target="tpu_custom_call" | custom-call | flops 201326592 | bytes 393216 | tf_op jit(solution)/shard_map/attend_chunk/pallas_call | solution.py:29
  34.9 4.8 %collective-permute-start.14 = (bf16[384,128]{1,0:T(8,128)(2,1)S(1)}, bf16[384,128]{1,0:T(8,128)(2,1)S(1)}, u32[]{:S(2)}, u32[]{:S(2)}) collective-permute-start(bf16[384,128]{1,0:T(8,128)(2,1)S(1)} %attend_chunk.4.refs_0_), channel_id=1, source_target_pairs={{0,3},{1,2},{2,1},{3,0},{4,7},{5,6},{6,5},{7,4},{8,11},{9,10},{10,... | collective-permute-start | bytes 294920 | tf_op jit(solution)/shard_map/ppermute | solution.py:270
  39.7 1.6 %attend_chunk.5.refs_0_ = bf16[384,128]{1,0:T(8,128)(2,1)S(1)} custom-call(bf16[4,384,128]{2,1,0:T(8,128)(2,1)S(1)} %stack.1.refs_0_.q_ref, bf16[27,128,128]{2,1,0:T(8,128)(2,1)S(1)} %join.2.kt_ref, bf16[27,128,128]{2,1,0:T(8,128)(2,1)S(1)} %values.1.v_ref, f32[27,12,128]{2,1,0:T(8,128)S(1)} %mask_bias.1.refs_1_.bias_ref, ...), custom_call_target="tpu_custom_call" | custom-call | flops 201326592 | bytes 393216 | tf_op jit(solution)/shard_map/attend_chunk/pallas_call | solution.py:29
  41.3 0.1 collective-permute-start.13
  41.4 1.6 %attend_chunk.6.refs_0_ = bf16[384,128]{1,0:T(8,128)(2,1)S(1)} custom-call(bf16[4,384,128]{2,1,0:T(8,128)(2,1)S(1)} %stack.1.refs_0_.q_ref, bf16[27,128,128]{2,1,0:T(8,128)(2,1)S(1)} %join.2.kt_ref, bf16[27,128,128]{2,1,0:T(8,128)(2,1)S(1)} %values.1.v_ref, f32[27,12,128]{2,1,0:T(8,128)S(1)} %mask_bias.1.refs_1_.bias_ref, ...), custom_call_target="tpu_custom_call" | custom-call | flops 201326592 | bytes 393216 | tf_op jit(solution)/shard_map/attend_chunk/pallas_call | solution.py:29
  43.0 0.6 %collective-permute-start.12 = (bf16[384,128]{1,0:T(8,128)(2,1)S(1)}, bf16[384,128]{1,0:T(8,128)(2,1)S(1)}, u32[]{:S(2)}, u32[]{:S(2)}) collective-permute-start(bf16[384,128]{1,0:T(8,128)(2,1)S(1)} %attend_chunk.6.refs_0_), channel_id=1, source_target_pairs={{0,1},{1,0},{2,3},{3,2},{4,5},{5,4},{6,7},{7,6},{8,9},{9,8},{10,11... | collective-permute-start | bytes 294920 | tf_op jit(solution)/shard_map/ppermute | solution.py:270
  43.6 1.6 %attend_chunk.7.refs_0_ = bf16[384,128]{1,0:T(8,128)(2,1)S(1)} custom-call(bf16[4,384,128]{2,1,0:T(8,128)(2,1)S(1)} %stack.1.refs_0_.q_ref, bf16[27,128,128]{2,1,0:T(8,128)(2,1)S(1)} %join.2.kt_ref, bf16[27,128,128]{2,1,0:T(8,128)(2,1)S(1)} %values.1.v_ref, f32[27,12,128]{2,1,0:T(8,128)S(1)} %mask_bias.1.refs_1_.bias_ref, ...), custom_call_target="tpu_custom_call" | custom-call | flops 8388608 | bytes 16384 | tf_op jit(solution)/shard_map/attend_chunk/pallas_call | solution.py:29
  45.3 2.6 %collective-permute-done.13.array_ref = bf16[384,128]{1,0:T(8,128)(2,1)S(1)} collective-permute-done((bf16[384,128]{1,0:T(8,128)(2,1)S(1)}, bf16[384,128]{1,0:T(8,128)(2,1)S(1)}, u32[]{:S(2)}, u32[]{:S(2)}) %collective-permute-start.13) | collective-permute-done | bytes 98336 | tf_op jit(solution)/shard_map/ppermute | solution.py:270
  47.9 1.7 %collective-permute-done.12.array_ref = bf16[384,128]{1,0:T(8,128)(2,1)S(1)} collective-permute-done((bf16[384,128]{1,0:T(8,128)(2,1)S(1)}, bf16[384,128]{1,0:T(8,128)(2,1)S(1)}, u32[]{:S(2)}, u32[]{:S(2)}) %collective-permute-start.12) | collective-permute-done | bytes 98336 | tf_op jit(solution)/shard_map/ppermute | solution.py:270
  49.7 0.8 %spread.1 = bf16[384,512]{1,0:T(8,128)(2,1)} custom-call(bf16[384,128]{1,0:T(8,128)(2,1)S(1)} %attend_chunk.7.refs_0_, bf16[384,128]{1,0:T(8,128)(2,1)S(1)} %landed.5.refs_1_, bf16[384,128]{1,0:T(8,128)(2,1)S(1)} %landed.4.refs_0_.refs_2_, bf16[384,128]{1,0:T(8,128)(2,1)S(1)} %landed.3.refs_0_.refs_3_), custom_call_target="tpu_custom_call" | custom-call | tf_op jit(solution)/shard_map/spread/pallas_call | solution.py:29
  (23 shorter events, 0.4 us)
Async XLA Ops:
  0.0 1.0 %copy-start.2 = (bf16[384,512]{1,0:T(8,128)(2,1)S(1)}, bf16[384,512]{1,0:T(8,128)(2,1)}, u32[]{:S(2)}) copy-start(bf16[384,512]{1,0:T(8,128)(2,1)} %array_ref.13) | copy-start | bytes 1179652
  1.0 6.6 %copy-start = (bf16[384,512]{1,0:T(8,128)(2,1)S(1)}, bf16[384,512]{1,0:T(8,128)(2,1)}, u32[]{:S(2)}) copy-start(bf16[384,512]{1,0:T(8,128)(2,1)} %q_ref.7) | copy-start | bytes 1179652
  1.0 6.6 %copy-start.1 = (bf16[384,512]{1,0:T(8,128)(2,1)S(1)}, bf16[384,512]{1,0:T(8,128)(2,1)}, u32[]{:S(2)}) copy-start(bf16[384,512]{1,0:T(8,128)(2,1)} %array_ref.10) | copy-start | bytes 1179652
  1.0 6.5 %collective-permute-start = (bf16[3,128,128]{2,1,0:T(8,128)(2,1)S(1)}, bf16[3,128,128]{2,1,0:T(8,128)(2,1)S(1)}, u32[]{:S(2)}, u32[]{:S(2)}) collective-permute-start(bf16[3,128,128]{2,1,0:T(8,128)(2,1)S(1)} %load_v.4), channel_id=1, source_target_pairs={{0,1},{1,0},{2,3},{3,2},{4,5},{5,4},{6,7},{7,6},{8,9},{9,8},{10,11... | collective-permute-start | bytes 294920 | tf_op jit(solution)/shard_map/ppermute | solution.py:270
  4.2 10.6 %collective-permute-start.8 = (bf16[3,128,128]{2,1,0:T(8,128)(2,1)S(1)}, bf16[3,128,128]{2,1,0:T(8,128)(2,1)S(1)}, u32[]{:S(2)}, u32[]{:S(2)}) collective-permute-start(bf16[3,128,128]{2,1,0:T(8,128)(2,1)S(1)} %load_v.6), channel_id=1, source_target_pairs={{0,2},{1,3},{2,0},{3,1},{4,6},{5,7},{6,4},{7,5},{8,10},{9,11},{10,... | collective-permute-start | bytes 294920 | tf_op jit(solution)/shard_map/ppermute | solution.py:270
  6.8 0.7 %copy-start.5 = (s32[12]{0:T(128)S(1)}, s32[12]{0:T(128)}, u32[]{:S(2)}) copy-start(s32[12]{0:T(128)} %param.9) | copy-start | bytes 148
  6.8 7.9 %collective-permute-start.9 = (bf16[3,128,128]{2,1,0:T(8,128)(2,1)S(1)}, bf16[3,128,128]{2,1,0:T(8,128)(2,1)S(1)}, u32[]{:S(2)}, u32[]{:S(2)}) collective-permute-start(bf16[3,128,128]{2,1,0:T(8,128)(2,1)S(1)} %load_v.7), channel_id=1, source_target_pairs={{0,3},{1,2},{2,1},{3,0},{4,7},{5,6},{6,5},{7,4},{8,11},{9,10},{10,... | collective-permute-start | bytes 294920 | tf_op jit(solution)/shard_map/ppermute | solution.py:270
  7.7 5.0 %copy-start.4 = (s32[12,16]{1,0:T(8,128)S(1)}, s32[12,16]{1,0:T(8,128)}, u32[]{:S(2)}) copy-start(s32[12,16]{1,0:T(8,128)} %lists_ref.1) | copy-start | bytes 2308
  7.7 18.9 %collective-permute-start.1 = (bf16[6,128,128]{2,1,0:T(8,128)(2,1)S(1)}, bf16[6,128,128]{2,1,0:T(8,128)(2,1)S(1)}, u32[]{:S(2)}, u32[]{:S(2)}) collective-permute-start(bf16[6,128,128]{2,1,0:T(8,128)(2,1)S(1)} %load_k.4), channel_id=1, source_target_pairs={{0,1},{1,0},{2,3},{3,2},{4,5},{5,4},{6,7},{7,6},{8,9},{9,8},{10,11... | collective-permute-start | bytes 589832 | tf_op jit(solution)/shard_map/ppermute | solution.py:270
  9.0 14.0 %collective-permute-start.2 = (bf16[3,128,128]{2,1,0:T(8,128)(2,1)S(1)}, bf16[3,128,128]{2,1,0:T(8,128)(2,1)S(1)}, u32[]{:S(2)}, u32[]{:S(2)}) collective-permute-start(bf16[3,128,128]{2,1,0:T(8,128)(2,1)S(1)} %load_k.5), channel_id=1, source_target_pairs={{0,2},{1,3},{2,0},{3,1},{4,6},{5,7},{6,4},{7,5},{8,10},{9,11},{10,... | collective-permute-start | bytes 294920 | tf_op jit(solution)/shard_map/ppermute | solution.py:270
  13.3 1.0 %copy-start.3 = (bf16[384,512]{1,0:T(8,128)(2,1)S(1)}, bf16[384,512]{1,0:T(8,128)(2,1)}, u32[]{:S(2)}) copy-start(bf16[384,512]{1,0:T(8,128)(2,1)} %array_ref.13) | copy-start | bytes 1179652
  13.4 13.0 %collective-permute-start.4 = (bf16[3,128,128]{2,1,0:T(8,128)(2,1)S(1)}, bf16[3,128,128]{2,1,0:T(8,128)(2,1)S(1)}, u32[]{:S(2)}, u32[]{:S(2)}) collective-permute-start(bf16[3,128,128]{2,1,0:T(8,128)(2,1)S(1)} %load_k.6), channel_id=1, source_target_pairs={{0,3},{1,2},{2,1},{3,0},{4,7},{5,6},{6,5},{7,4},{8,11},{9,10},{10,... | collective-permute-start | bytes 294920 | tf_op jit(solution)/shard_map/ppermute | solution.py:270
  14.8 18.2 %collective-permute-start.10 = (bf16[8,128,128]{2,1,0:T(8,128)(2,1)S(1)}, bf16[8,128,128]{2,1,0:T(8,128)(2,1)S(1)}, u32[]{:S(2)}, u32[]{:S(2)}) collective-permute-start(bf16[8,128,128]{2,1,0:T(8,128)(2,1)S(1)} %get-tuple-element.11), channel_id=1, source_target_pairs={{4,8},{8,4},{5,9},{9,5},{6,10},{10,6},{7,11},{11,7},{20,24},{24,20... | collective-permute-start | bytes 786440 | tf_op jit(solution)/shard_map/ppermute | solution.py:231
  15.5 17.5 %collective-permute-start.11 = (bf16[8,128,128]{2,1,0:T(8,128)(2,1)S(1)}, bf16[8,128,128]{2,1,0:T(8,128)(2,1)S(1)}, u32[]{:S(2)}, u32[]{:S(2)}) collective-permute-start(bf16[8,128,128]{2,1,0:T(8,128)(2,1)S(1)} %get-tuple-element.12), channel_id=1, source_target_pairs={{0,4},{8,12},{4,0},{12,8},{1,5},{9,13},{5,1},{13,9},{2,6},{10,14},... | collective-permute-start | bytes 786440 | tf_op jit(solution)/shard_map/ppermute | solution.py:231
  23.1 7.4 %collective-permute-start.3 = (bf16[384,128]{1,0:T(8,128)(2,1)S(1)}, bf16[384,128]{1,0:T(8,128)(2,1)S(1)}, u32[]{:S(2)}, u32[]{:S(2)}) collective-permute-start(bf16[384,128]{1,0:T(8,128)(2,1)S(1)} %load_q.4), channel_id=1, source_target_pairs={{0,2},{1,3},{2,0},{3,1},{4,6},{5,7},{6,4},{7,5},{8,10},{9,11},{10,... | collective-permute-start | bytes 294920 | tf_op jit(solution)/shard_map/ppermute | solution.py:270
  26.4 6.5 %collective-permute-start.5 = (bf16[384,128]{1,0:T(8,128)(2,1)S(1)}, bf16[384,128]{1,0:T(8,128)(2,1)S(1)}, u32[]{:S(2)}, u32[]{:S(2)}) collective-permute-start(bf16[384,128]{1,0:T(8,128)(2,1)S(1)} %load_q.5), channel_id=1, source_target_pairs={{0,3},{1,2},{2,1},{3,0},{4,7},{5,6},{6,5},{7,4},{8,11},{9,10},{10,... | collective-permute-start | bytes 294920 | tf_op jit(solution)/shard_map/ppermute | solution.py:270
  26.8 6.4 %collective-permute-start.6 = (bf16[8,128,128]{2,1,0:T(8,128)(2,1)S(1)}, bf16[8,128,128]{2,1,0:T(8,128)(2,1)S(1)}, u32[]{:S(2)}, u32[]{:S(2)}) collective-permute-start(bf16[8,128,128]{2,1,0:T(8,128)(2,1)S(1)} %get-tuple-element.9), channel_id=1, source_target_pairs={{4,8},{8,4},{5,9},{9,5},{6,10},{10,6},{7,11},{11,7},{20,24},{24,20... | collective-permute-start | bytes 786440 | tf_op jit(solution)/shard_map/ppermute | solution.py:231
  30.5 2.7 %collective-permute-start.7 = (bf16[8,128,128]{2,1,0:T(8,128)(2,1)S(1)}, bf16[8,128,128]{2,1,0:T(8,128)(2,1)S(1)}, u32[]{:S(2)}, u32[]{:S(2)}) collective-permute-start(bf16[8,128,128]{2,1,0:T(8,128)(2,1)S(1)} %get-tuple-element.10), channel_id=1, source_target_pairs={{0,4},{8,12},{4,0},{12,8},{1,5},{9,13},{5,1},{13,9},{2,6},{10,14},... | collective-permute-start | bytes 786440 | tf_op jit(solution)/shard_map/ppermute | solution.py:231
  34.9 10.4 %collective-permute-start.14 = (bf16[384,128]{1,0:T(8,128)(2,1)S(1)}, bf16[384,128]{1,0:T(8,128)(2,1)S(1)}, u32[]{:S(2)}, u32[]{:S(2)}) collective-permute-start(bf16[384,128]{1,0:T(8,128)(2,1)S(1)} %attend_chunk.4.refs_0_), channel_id=1, source_target_pairs={{0,3},{1,2},{2,1},{3,0},{4,7},{5,6},{6,5},{7,4},{8,11},{9,10},{10,... | collective-permute-start | bytes 294920 | tf_op jit(solution)/shard_map/ppermute | solution.py:270
  41.3 6.6 %collective-permute-start.13 = (bf16[384,128]{1,0:T(8,128)(2,1)S(1)}, bf16[384,128]{1,0:T(8,128)(2,1)S(1)}, u32[]{:S(2)}, u32[]{:S(2)}) collective-permute-start(bf16[384,128]{1,0:T(8,128)(2,1)S(1)} %attend_chunk.5.refs_0_), channel_id=1, source_target_pairs={{0,2},{1,3},{2,0},{3,1},{4,6},{5,7},{6,4},{7,5},{8,10},{9,11},{10,... | collective-permute-start | bytes 294920 | tf_op jit(solution)/shard_map/ppermute | solution.py:270
  43.0 6.7 %collective-permute-start.12 = (bf16[384,128]{1,0:T(8,128)(2,1)S(1)}, bf16[384,128]{1,0:T(8,128)(2,1)S(1)}, u32[]{:S(2)}, u32[]{:S(2)}) collective-permute-start(bf16[384,128]{1,0:T(8,128)(2,1)S(1)} %attend_chunk.6.refs_0_), channel_id=1, source_target_pairs={{0,1},{1,0},{2,3},{3,2},{4,5},{5,4},{6,7},{7,6},{8,9},{9,8},{10,11... | collective-permute-start | bytes 294920 | tf_op jit(solution)/shard_map/ppermute | solution.py:270

commit v16 on v15

--- a/solution.py
+++ b/solution.py
@@ -254,11 +254,31 @@
     attend_block(first, q_ref.at[pair], kt_ref, v_ref, bias_ref, out_ref, *scratch)
 
 
-def spread_kernel(*refs):
-    *parts, out_ref = refs
+def spread_kernel(pairs, *refs):
+    out_ref, sems = refs[-2:]
     me = lax.axis_index("head")
-    for pair, part in enumerate(parts):
-        out_ref[:, column_of(me ^ pair)] = part[...]
+    copies = [
+        pltpu.make_async_copy(part, out_ref.at[:, column_of(me ^ pair)], sems.at[at])
+        for at, (pair, part) in enumerate(zip(pairs, refs))
+    ]
+    for copy in copies:
+        copy.start()
+    for copy in copies:
+        copy.wait()
+
+
+def spread(outs, pairs, shape, *before):
+    anywhere = pl.BlockSpec(memory_space=pl.ANY)
+    return pl.pallas_call(
+        functools.partial(spread_kernel, pairs),
+        out_shape=jax.ShapeDtypeStruct(shape, jnp.bfloat16),
+        in_specs=[VMEM] * len(pairs) + [anywhere] * len(before),
+        out_specs=anywhere,
+        scratch_shapes=[pltpu.SemaphoreType.DMA((len(pairs),))],
+        input_output_aliases={len(pairs): 0} if before else {},
+        compiler_params=pltpu.CompilerParams(vmem_limit_bytes=8 << 20),
+        name="spread",
+    )(*(outs[pair] for pair in pairs), *before)
 
 
 def in_pairs(queries, keys, values, bias):
@@ -274,7 +294,8 @@
 
     v_parts, k_parts, q_parts = [None] * heads, [None] * heads, [None] * heads
     for pair in [*order, 0]:
-        part = call_on(functools.partial(load_tiles_kernel, pair, turn=False), "load_v", (values,), tiles)
+        column = (lax.axis_index("head") ^ pair) * HDIM
+        part = lax.dynamic_slice_in_dim(values, column, HDIM, axis=1).reshape(tiles)
         v_parts[pair] = exchange(part, pair) if pair else part
     for pair in [*order, 0]:
         operands = (keys, queries) if pair == 1 else (keys,)
@@ -319,7 +340,9 @@
             pass_kernel, "landed", operands, [VMEM] * len(operands), chunk, cost=cost(BLOCK * LIST // 2)
         )
         after = (outs[pair],)
-    return call(spread_kernel, "spread", outs, [VMEM] * heads, queries.shape)
+    last = order[-1]
+    early = [pair for pair in range(heads) if pair != last]
+    return spread(outs, [last], queries.shape, spread(outs, early, queries.shape))
 
 
 def on_device(queries, keys, values, tile_lists, live_counts):

time: 50.7 us -> 50.1 us (0.988)
  waiting for transfers between devices: 15 us -> 10.7 us
  starting transfers between devices: 24 us -> 27.9 us
  local copies, waits for them, and re-layouts: 2.49 us -> 1.79 us
    ppermute x11, waiting for transfers between devices: 14.9 us -> 10.7 us  [exchange(): return lax.ppermute(array, 'head', [(i, i ^ pair) for i in range(heads)])]
    ppermute x4, starting transfers between devices: 4.26 us -> 6.63 us  [exchange(): lax.ppermute(array, 'ctx', [(i, i + 1) for i in lower] + [(i + 1, i) for...]
    unnamed x12 -> x8, local copies, waits for them, and re-layouts: 2.4 us -> 0.55 us
    ppermute x11, starting transfers between devices: 19.7 us -> 21.2 us  [exchange(): return lax.ppermute(array, 'head', [(i, i ^ pair) for i in range(heads)])]
    pallas_call x0 -> x2, Pallas kernels: none -> 1.4 us  [spread(): pl.pallas_call(functools.partial(spread_kernel, pairs), out_shape=jax.Sha...]
    dynamic_slice x0 -> x1, local copies, waits for them, and re-layouts: none -> 1.14 us  [in_pairs(): part = lax.dynamic_slice_in_dim(values, column, HDIM, axis=1).reshape(tiles)]
    pallas_call x28 -> x23, Pallas kernels: 8.81 us -> 7.9 us  [call(): pl.pallas_call(kernel, out_shape=out_shape, in_specs=in_specs, out_specs=...]
  transfers between devices with their start and end apart: 15 -> 15, of which waited for: 6 -> 5; matrix products, arithmetic and copies ran while one was open for 0% -> 0% of each run, Pallas kernels for 12% -> 14%
where the time goes in v16:
time: 50.1 us; the launch traced here: 49.9 us
  starting transfers between devices  27.9 us (56%)
  waiting for transfers between devices  10.7 us (21%)
  Pallas kernels  9.3 us (19%)
  local copies, waits for them, and re-layouts  1.79 us (4%)
    ppermute x11, starting transfers between devices, exchange(): return lax.ppermute(array, 'head', [(i, i ^ pair) for i in range(heads)])  21.2 us
    ppermute x11, waiting for transfers between devices, exchange(): return lax.ppermute(array, 'head', [(i, i ^ pair) for i in range(heads)])  10.7 us
    pallas_call x23, Pallas kernels, call(): pl.pallas_call(kernel, out_shape=out_shape, in_specs=in_specs, out_specs=...  7.9 us
    ppermute x4, starting transfers between devices, exchange(): lax.ppermute(array, 'ctx', [(i, i + 1) for i in lower] + [(i + 1, i) for...  6.63 us
    pallas_call x2, Pallas kernels, spread(): pl.pallas_call(functools.partial(spread_kernel, pairs), out_shape=jax.Sha...  1.4 us
    dynamic_slice x1, local copies, waits for them, and re-layouts, in_pairs(): part = lax.dynamic_slice_in_dim(values, column, HDIM, axis=1).reshape(tiles)  1.14 us
  transfers between devices with their start and end apart: 15, of which 5 were waited for; matrix products, arithmetic and copies ran while one was open for 0% of the time, Pallas kernels for 14%

profile of v16, /device:TPU:0, one launch (start us, length us, event | category | flops | bytes accessed | tf_op | source)
XLA Modules:
  0.0 49.9 jit_solution(7796828269871990275)
XLA Ops:
  0.0 1.1 %constant_dynamic-slice_fusion = (bf16[384,128]{1,0:T(8,128)(2,1)S(1)}, bf16[384,128]{1,0:T(8,128)(2,1)S(1)}, bf16[384,128]{1,0:T(8,128)(2,1)S(1)}, bf16[384,128]{1,0:T(8,128)(2,1)S(1)}) fusion(bf16[384,512]{1,0:T(8,128)(2,1)} %param.7, s32[]{:T(128)S(6)} %select_n.15, s32[]{:T(128)S(6)} %select_n.13, s32[]{:T(128)S(6)} %select_n.12, s32[]{:T(128)S(6)} %select_n.14), kind=kLoop, calls=%fused_computation | loop fusion | bytes 786448 | tf_op jit(solution)/shard_map/dynamic_slice | solution.py:298
  1.2 3.1 %collective-permute-start = (bf16[3,128,128]{2,1,0:T(8,128)(2,1)S(1)}, bf16[3,128,128]{2,1,0:T(8,128)(2,1)S(1)}, u32[]{:S(2)}, u32[]{:S(2)}) collective-permute-start(bf16[3,128,128]{2,1,0:T(8,128)(2,1)S(1)} %bitcast.8), channel_id=1, source_target_pairs={{0,1},{1,0},{2,3},{3,2},{4,5},{5,4},{6,7},{7,6},{8,9},{9,8},{10,11... | collective-permute-start | bytes 294920 | tf_op jit(solution)/shard_map/ppermute | solution.py:290
  4.2 2.5 %collective-permute-start.9 = (bf16[3,128,128]{2,1,0:T(8,128)(2,1)S(1)}, bf16[3,128,128]{2,1,0:T(8,128)(2,1)S(1)}, u32[]{:S(2)}, u32[]{:S(2)}) collective-permute-start(bf16[3,128,128]{2,1,0:T(8,128)(2,1)S(1)} %bitcast.7), channel_id=1, source_target_pairs={{0,3},{1,2},{2,1},{3,0},{4,7},{5,6},{6,5},{7,4},{8,11},{9,10},{10,... | collective-permute-start | bytes 294920 | tf_op jit(solution)/shard_map/ppermute | solution.py:290
  6.7 0.1 collective-permute-start.8
  6.8 0.5 %copy-done.3 = s32[12]{0:T(128)S(1)} copy-done((s32[12]{0:T(128)S(1)}, s32[12]{0:T(128)}, u32[]{:S(2)}) %copy-start.3) | copy-done | bytes 72
  7.4 0.1 copy.7.counts_ref
  7.5 0.0 collective-permute-done.refs_0_.refs_1_
  7.5 0.1 load_k.4
  7.6 0.0 copy-start.2
  7.6 1.4 %collective-permute-start.1 = (bf16[6,128,128]{2,1,0:T(8,128)(2,1)S(1)}, bf16[6,128,128]{2,1,0:T(8,128)(2,1)S(1)}, u32[]{:S(2)}, u32[]{:S(2)}) collective-permute-start(bf16[6,128,128]{2,1,0:T(8,128)(2,1)S(1)} %load_k.4), channel_id=1, source_target_pairs={{0,1},{1,0},{2,3},{3,2},{4,5},{5,4},{6,7},{7,6},{8,9},{9,8},{10,11... | collective-permute-start | bytes 589832 | tf_op jit(solution)/shard_map/ppermute | solution.py:290
  9.0 0.1 load_k.5
  9.1 3.7 %collective-permute-start.2 = (bf16[3,128,128]{2,1,0:T(8,128)(2,1)S(1)}, bf16[3,128,128]{2,1,0:T(8,128)(2,1)S(1)}, u32[]{:S(2)}, u32[]{:S(2)}) collective-permute-start(bf16[3,128,128]{2,1,0:T(8,128)(2,1)S(1)} %load_k.5), channel_id=1, source_target_pairs={{0,2},{1,3},{2,0},{3,1},{4,6},{5,7},{6,4},{7,5},{8,10},{9,11},{10,... | collective-permute-start | bytes 294920 | tf_op jit(solution)/shard_map/ppermute | solution.py:290
  12.8 0.6 %mask_bias.1.refs_1_.bias_ref = f32[27,12,128]{2,1,0:T(8,128)S(1)} custom-call(s32[12,16]{1,0:T(8,128)S(1)} %copy-done.2, s32[12,1]{1,0:T(8,128)S(1)} %copy.7.counts_ref), custom_call_target="tpu_custom_call" | custom-call | tf_op jit(solution)/shard_map/mask_bias/pallas_call | solution.py:29
  13.4 0.1 load_k.6
  13.5 0.1 collective-permute-start.4
  13.6 0.0 collective-permute-done.9.refs_3_
  13.6 2.6 %collective-permute-done.8.refs_2_ = bf16[3,128,128]{2,1,0:T(8,128)(2,1)S(1)} collective-permute-done((bf16[3,128,128]{2,1,0:T(8,128)(2,1)S(1)}, bf16[3,128,128]{2,1,0:T(8,128)(2,1)S(1)}, u32[]{:S(2)}, u32[]{:S(2)}) %collective-permute-start.8) | collective-permute-done | bytes 98336 | tf_op jit(solution)/shard_map/ppermute | solution.py:290
  16.3 0.7 %collective-permute-start.10 = (bf16[8,128,128]{2,1,0:T(8,128)(2,1)S(1)}, bf16[8,128,128]{2,1,0:T(8,128)(2,1)S(1)}, u32[]{:S(2)}, u32[]{:S(2)}) collective-permute-start(bf16[8,128,128]{2,1,0:T(8,128)(2,1)S(1)} %get-tuple-element.11), channel_id=1, source_target_pairs={{4,8},{8,4},{5,9},{9,5},{6,10},{10,6},{7,11},{11,7},{20,24},{24,20... | collective-permute-start | bytes 786440 | tf_op jit(solution)/shard_map/ppermute | solution.py:231
  17.0 2.9 %collective-permute-start.11 = (bf16[8,128,128]{2,1,0:T(8,128)(2,1)S(1)}, bf16[8,128,128]{2,1,0:T(8,128)(2,1)S(1)}, u32[]{:S(2)}, u32[]{:S(2)}) collective-permute-start(bf16[8,128,128]{2,1,0:T(8,128)(2,1)S(1)} %get-tuple-element.12), channel_id=1, source_target_pairs={{0,4},{8,12},{4,0},{12,8},{1,5},{9,13},{5,1},{13,9},{2,6},{10,14},... | collective-permute-start | bytes 786440 | tf_op jit(solution)/shard_map/ppermute | solution.py:231
  19.9 2.6 %collective-permute-done.2.refs_0_.refs_2_ = bf16[3,128,128]{2,1,0:T(8,128)(2,1)S(1)} collective-permute-done((bf16[3,128,128]{2,1,0:T(8,128)(2,1)S(1)}, bf16[3,128,128]{2,1,0:T(8,128)(2,1)S(1)}, u32[]{:S(2)}, u32[]{:S(2)}) %collective-permute-start.2) | collective-permute-done | bytes 98336 | tf_op jit(solution)/shard_map/ppermute | solution.py:290
  22.5 0.1 collective-permute-start.3
  22.6 0.0 collective-permute-done.4.refs_0_.refs_3_
  22.6 4.7 %collective-permute-start.5 = (bf16[384,128]{1,0:T(8,128)(2,1)S(1)}, bf16[384,128]{1,0:T(8,128)(2,1)S(1)}, u32[]{:S(2)}, u32[]{:S(2)}) collective-permute-start(bf16[384,128]{1,0:T(8,128)(2,1)S(1)} %load_q.5), channel_id=1, source_target_pairs={{0,3},{1,2},{2,1},{3,0},{4,7},{5,6},{6,5},{7,4},{8,11},{9,10},{10,... | collective-permute-start | bytes 294920 | tf_op jit(solution)/shard_map/ppermute | solution.py:290
  27.4 0.1 load_k.7.refs_0_
  27.5 0.0 collective-permute-done.1.refs_1_
  27.6 0.7 %collective-permute-start.6 = (bf16[8,128,128]{2,1,0:T(8,128)(2,1)S(1)}, bf16[8,128,128]{2,1,0:T(8,128)(2,1)S(1)}, u32[]{:S(2)}, u32[]{:S(2)}) collective-permute-start(bf16[8,128,128]{2,1,0:T(8,128)(2,1)S(1)} %get-tuple-element.9), channel_id=1, source_target_pairs={{4,8},{8,4},{5,9},{9,5},{6,10},{10,6},{7,11},{11,7},{20,24},{24,20... | collective-permute-start | bytes 786440 | tf_op jit(solution)/shard_map/ppermute | solution.py:231
  28.3 0.0 collective-permute-done.3.refs_2_
  28.3 2.4 %collective-permute-start.7 = (bf16[8,128,128]{2,1,0:T(8,128)(2,1)S(1)}, bf16[8,128,128]{2,1,0:T(8,128)(2,1)S(1)}, u32[]{:S(2)}, u32[]{:S(2)}) collective-permute-start(bf16[8,128,128]{2,1,0:T(8,128)(2,1)S(1)} %get-tuple-element.10), channel_id=1, source_target_pairs={{0,4},{8,12},{4,0},{12,8},{1,5},{9,13},{5,1},{13,9},{2,6},{10,14},... | collective-permute-start | bytes 786440 | tf_op jit(solution)/shard_map/ppermute | solution.py:231
  30.7 1.8 %collective-permute-done.5.refs_3_ = bf16[384,128]{1,0:T(8,128)(2,1)S(1)} collective-permute-done((bf16[384,128]{1,0:T(8,128)(2,1)S(1)}, bf16[384,128]{1,0:T(8,128)(2,1)S(1)}, u32[]{:S(2)}, u32[]{:S(2)}) %collective-permute-start.5) | collective-permute-done | bytes 98336 | tf_op jit(solution)/shard_map/ppermute | solution.py:290
  32.5 0.0 collective-permute-done.10.first_ref
  32.5 0.0 collective-permute-done.11.second_ref
  32.5 0.1 join.3.array_ref
  32.6 0.1 values.1.v_ref
  32.6 0.0 collective-permute-done.6.first_ref
  32.6 0.0 collective-permute-done.7.second_ref
  32.6 0.1 join.2.kt_ref
  32.7 1.6 %attend_chunk.4.refs_0_ = bf16[384,128]{1,0:T(8,128)(2,1)S(1)} custom-call(bf16[4,384,128]{2,1,0:T(8,128)(2,1)S(1)} %stack.1.refs_0_.q_ref, bf16[27,128,128]{2,1,0:T(8,128)(2,1)S(1)} %join.2.kt_ref, bf16[27,128,128]{2,1,0:T(8,128)(2,1)S(1)} %values.1.v_ref, f32[27,12,128]{2,1,0:T(8,128)S(1)} %mask_bias.1.refs_1_.bias_ref), custom_call_target="tpu_custom_call" | custom-call | flops 201326592 | bytes 393216 | tf_op jit(solution)/shard_map/attend_chunk/pallas_call | solution.py:29
  34.3 4.8 %collective-permute-start.14 = (bf16[384,128]{1,0:T(8,128)(2,1)S(1)}, bf16[384,128]{1,0:T(8,128)(2,1)S(1)}, u32[]{:S(2)}, u32[]{:S(2)}) collective-permute-start(bf16[384,128]{1,0:T(8,128)(2,1)S(1)} %attend_chunk.4.refs_0_), channel_id=1, source_target_pairs={{0,3},{1,2},{2,1},{3,0},{4,7},{5,6},{6,5},{7,4},{8,11},{9,10},{10,... | collective-permute-start | bytes 294920 | tf_op jit(solution)/shard_map/ppermute | solution.py:290
  39.2 1.6 %attend_chunk.5.refs_0_ = bf16[384,128]{1,0:T(8,128)(2,1)S(1)} custom-call(bf16[4,384,128]{2,1,0:T(8,128)(2,1)S(1)} %stack.1.refs_0_.q_ref, bf16[27,128,128]{2,1,0:T(8,128)(2,1)S(1)} %join.2.kt_ref, bf16[27,128,128]{2,1,0:T(8,128)(2,1)S(1)} %values.1.v_ref, f32[27,12,128]{2,1,0:T(8,128)S(1)} %mask_bias.1.refs_1_.bias_ref, ...), custom_call_target="tpu_custom_call" | custom-call | flops 201326592 | bytes 393216 | tf_op jit(solution)/shard_map/attend_chunk/pallas_call | solution.py:29
  40.8 0.1 collective-permute-start.13
  40.9 1.6 %attend_chunk.6.refs_0_ = bf16[384,128]{1,0:T(8,128)(2,1)S(1)} custom-call(bf16[4,384,128]{2,1,0:T(8,128)(2,1)S(1)} %stack.1.refs_0_.q_ref, bf16[27,128,128]{2,1,0:T(8,128)(2,1)S(1)} %join.2.kt_ref, bf16[27,128,128]{2,1,0:T(8,128)(2,1)S(1)} %values.1.v_ref, f32[27,12,128]{2,1,0:T(8,128)S(1)} %mask_bias.1.refs_1_.bias_ref, ...), custom_call_target="tpu_custom_call" | custom-call | flops 201326592 | bytes 393216 | tf_op jit(solution)/shard_map/attend_chunk/pallas_call | solution.py:29
  42.5 0.6 %collective-permute-start.12 = (bf16[384,128]{1,0:T(8,128)(2,1)S(1)}, bf16[384,128]{1,0:T(8,128)(2,1)S(1)}, u32[]{:S(2)}, u32[]{:S(2)}) collective-permute-start(bf16[384,128]{1,0:T(8,128)(2,1)S(1)} %attend_chunk.6.refs_0_), channel_id=1, source_target_pairs={{0,1},{1,0},{2,3},{3,2},{4,5},{5,4},{6,7},{7,6},{8,9},{9,8},{10,11... | collective-permute-start | bytes 294920 | tf_op jit(solution)/shard_map/ppermute | solution.py:290
  43.2 1.6 %attend_chunk.7.refs_0_ = bf16[384,128]{1,0:T(8,128)(2,1)S(1)} custom-call(bf16[4,384,128]{2,1,0:T(8,128)(2,1)S(1)} %stack.1.refs_0_.q_ref, bf16[27,128,128]{2,1,0:T(8,128)(2,1)S(1)} %join.2.kt_ref, bf16[27,128,128]{2,1,0:T(8,128)(2,1)S(1)} %values.1.v_ref, f32[27,12,128]{2,1,0:T(8,128)S(1)} %mask_bias.1.refs_1_.bias_ref, ...), custom_call_target="tpu_custom_call" | custom-call | flops 8388608 | bytes 16384 | tf_op jit(solution)/shard_map/attend_chunk/pallas_call | solution.py:29
  44.8 0.0 collective-permute-done.14.array_ref
  44.8 3.1 %collective-permute-done.13.array_ref = bf16[384,128]{1,0:T(8,128)(2,1)S(1)} collective-permute-done((bf16[384,128]{1,0:T(8,128)(2,1)S(1)}, bf16[384,128]{1,0:T(8,128)(2,1)S(1)}, u32[]{:S(2)}, u32[]{:S(2)}) %collective-permute-start.13) | collective-permute-done | bytes 98336 | tf_op jit(solution)/shard_map/ppermute | solution.py:290
  47.9 0.7 %spread.2.refs_1_ = bf16[384,512]{1,0:T(8,128)(2,1)} custom-call(bf16[384,128]{1,0:T(8,128)(2,1)S(1)} %attend_chunk.7.refs_0_, bf16[384,128]{1,0:T(8,128)(2,1)S(1)} %landed.4.refs_0_.refs_1_, bf16[384,128]{1,0:T(8,128)(2,1)S(1)} %landed.3.refs_0_.refs_2_), custom_call_target="tpu_custom_call" | custom-call | tf_op jit(solution)/shard_map/spread/pallas_call | solution.py:272
  48.7 0.6 %collective-permute-done.12.array_ref = bf16[384,128]{1,0:T(8,128)(2,1)S(1)} collective-permute-done((bf16[384,128]{1,0:T(8,128)(2,1)S(1)}, bf16[384,128]{1,0:T(8,128)(2,1)S(1)}, u32[]{:S(2)}, u32[]{:S(2)}) %collective-permute-start.12) | collective-permute-done | bytes 98336 | tf_op jit(solution)/shard_map/ppermute | solution.py:290
  49.3 0.7 %spread.3 = bf16[384,512]{1,0:T(8,128)(2,1)} custom-call(bf16[384,128]{1,0:T(8,128)(2,1)S(1)} %landed.5.refs_0_, bf16[384,512]{1,0:T(8,128)(2,1)} %spread.2.refs_1_), custom_call_target="tpu_custom_call", output_to_operand_aliasing={{}: (1, {})} | custom-call | tf_op jit(solution)/shard_map/spread/pallas_call | solution.py:272
  (17 shorter events, 0.3 us)
Async XLA Ops:
  0.0 7.5 %copy-start = (bf16[384,512]{1,0:T(8,128)(2,1)S(1)}, bf16[384,512]{1,0:T(8,128)(2,1)}, u32[]{:S(2)}) copy-start(bf16[384,512]{1,0:T(8,128)(2,1)} %q_ref.7) | copy-start | bytes 1179652
  0.0 7.5 %copy-start.1 = (bf16[384,512]{1,0:T(8,128)(2,1)S(1)}, bf16[384,512]{1,0:T(8,128)(2,1)}, u32[]{:S(2)}) copy-start(bf16[384,512]{1,0:T(8,128)(2,1)} %array_ref.5) | copy-start | bytes 1179652
  1.2 6.3 %collective-permute-start = (bf16[3,128,128]{2,1,0:T(8,128)(2,1)S(1)}, bf16[3,128,128]{2,1,0:T(8,128)(2,1)S(1)}, u32[]{:S(2)}, u32[]{:S(2)}) collective-permute-start(bf16[3,128,128]{2,1,0:T(8,128)(2,1)S(1)} %bitcast.8), channel_id=1, source_target_pairs={{0,1},{1,0},{2,3},{3,2},{4,5},{5,4},{6,7},{7,6},{8,9},{9,8},{10,11... | collective-permute-start | bytes 294920 | tf_op jit(solution)/shard_map/ppermute | solution.py:290
  4.2 9.4 %collective-permute-start.9 = (bf16[3,128,128]{2,1,0:T(8,128)(2,1)S(1)}, bf16[3,128,128]{2,1,0:T(8,128)(2,1)S(1)}, u32[]{:S(2)}, u32[]{:S(2)}) collective-permute-start(bf16[3,128,128]{2,1,0:T(8,128)(2,1)S(1)} %bitcast.7), channel_id=1, source_target_pairs={{0,3},{1,2},{2,1},{3,0},{4,7},{5,6},{6,5},{7,4},{8,11},{9,10},{10,... | collective-permute-start | bytes 294920 | tf_op jit(solution)/shard_map/ppermute | solution.py:290
  6.7 0.7 %copy-start.3 = (s32[12]{0:T(128)S(1)}, s32[12]{0:T(128)}, u32[]{:S(2)}) copy-start(s32[12]{0:T(128)} %param.9) | copy-start | bytes 148
  6.7 9.5 %collective-permute-start.8 = (bf16[3,128,128]{2,1,0:T(8,128)(2,1)S(1)}, bf16[3,128,128]{2,1,0:T(8,128)(2,1)S(1)}, u32[]{:S(2)}, u32[]{:S(2)}) collective-permute-start(bf16[3,128,128]{2,1,0:T(8,128)(2,1)S(1)} %bitcast.6), channel_id=1, source_target_pairs={{0,2},{1,3},{2,0},{3,1},{4,6},{5,7},{6,4},{7,5},{8,10},{9,11},{10,... | collective-permute-start | bytes 294920 | tf_op jit(solution)/shard_map/ppermute | solution.py:290
  7.6 5.3 %copy-start.2 = (s32[12,16]{1,0:T(8,128)S(1)}, s32[12,16]{1,0:T(8,128)}, u32[]{:S(2)}) copy-start(s32[12,16]{1,0:T(8,128)} %lists_ref.1) | copy-start | bytes 2308
  7.6 19.9 %collective-permute-start.1 = (bf16[6,128,128]{2,1,0:T(8,128)(2,1)S(1)}, bf16[6,128,128]{2,1,0:T(8,128)(2,1)S(1)}, u32[]{:S(2)}, u32[]{:S(2)}) collective-permute-start(bf16[6,128,128]{2,1,0:T(8,128)(2,1)S(1)} %load_k.4), channel_id=1, source_target_pairs={{0,1},{1,0},{2,3},{3,2},{4,5},{5,4},{6,7},{7,6},{8,9},{9,8},{10,11... | collective-permute-start | bytes 589832 | tf_op jit(solution)/shard_map/ppermute | solution.py:290
  9.1 13.4 %collective-permute-start.2 = (bf16[3,128,128]{2,1,0:T(8,128)(2,1)S(1)}, bf16[3,128,128]{2,1,0:T(8,128)(2,1)S(1)}, u32[]{:S(2)}, u32[]{:S(2)}) collective-permute-start(bf16[3,128,128]{2,1,0:T(8,128)(2,1)S(1)} %load_k.5), channel_id=1, source_target_pairs={{0,2},{1,3},{2,0},{3,1},{4,6},{5,7},{6,4},{7,5},{8,10},{9,11},{10,... | collective-permute-start | bytes 294920 | tf_op jit(solution)/shard_map/ppermute | solution.py:290
  13.5 9.1 %collective-permute-start.4 = (bf16[3,128,128]{2,1,0:T(8,128)(2,1)S(1)}, bf16[3,128,128]{2,1,0:T(8,128)(2,1)S(1)}, u32[]{:S(2)}, u32[]{:S(2)}) collective-permute-start(bf16[3,128,128]{2,1,0:T(8,128)(2,1)S(1)} %load_k.6), channel_id=1, source_target_pairs={{0,3},{1,2},{2,1},{3,0},{4,7},{5,6},{6,5},{7,4},{8,11},{9,10},{10,... | collective-permute-start | bytes 294920 | tf_op jit(solution)/shard_map/ppermute | solution.py:290
  16.3 16.1 %collective-permute-start.10 = (bf16[8,128,128]{2,1,0:T(8,128)(2,1)S(1)}, bf16[8,128,128]{2,1,0:T(8,128)(2,1)S(1)}, u32[]{:S(2)}, u32[]{:S(2)}) collective-permute-start(bf16[8,128,128]{2,1,0:T(8,128)(2,1)S(1)} %get-tuple-element.11), channel_id=1, source_target_pairs={{4,8},{8,4},{5,9},{9,5},{6,10},{10,6},{7,11},{11,7},{20,24},{24,20... | collective-permute-start | bytes 786440 | tf_op jit(solution)/shard_map/ppermute | solution.py:231
  17.0 15.5 %collective-permute-start.11 = (bf16[8,128,128]{2,1,0:T(8,128)(2,1)S(1)}, bf16[8,128,128]{2,1,0:T(8,128)(2,1)S(1)}, u32[]{:S(2)}, u32[]{:S(2)}) collective-permute-start(bf16[8,128,128]{2,1,0:T(8,128)(2,1)S(1)} %get-tuple-element.12), channel_id=1, source_target_pairs={{0,4},{8,12},{4,0},{12,8},{1,5},{9,13},{5,1},{13,9},{2,6},{10,14},... | collective-permute-start | bytes 786440 | tf_op jit(solution)/shard_map/ppermute | solution.py:231
  22.5 5.8 %collective-permute-start.3 = (bf16[384,128]{1,0:T(8,128)(2,1)S(1)}, bf16[384,128]{1,0:T(8,128)(2,1)S(1)}, u32[]{:S(2)}, u32[]{:S(2)}) collective-permute-start(bf16[384,128]{1,0:T(8,128)(2,1)S(1)} %load_q.4), channel_id=1, source_target_pairs={{0,2},{1,3},{2,0},{3,1},{4,6},{5,7},{6,4},{7,5},{8,10},{9,11},{10,... | collective-permute-start | bytes 294920 | tf_op jit(solution)/shard_map/ppermute | solution.py:290
  22.6 9.8 %collective-permute-start.5 = (bf16[384,128]{1,0:T(8,128)(2,1)S(1)}, bf16[384,128]{1,0:T(8,128)(2,1)S(1)}, u32[]{:S(2)}, u32[]{:S(2)}) collective-permute-start(bf16[384,128]{1,0:T(8,128)(2,1)S(1)} %load_q.5), channel_id=1, source_target_pairs={{0,3},{1,2},{2,1},{3,0},{4,7},{5,6},{6,5},{7,4},{8,11},{9,10},{10,... | collective-permute-start | bytes 294920 | tf_op jit(solution)/shard_map/ppermute | solution.py:290
  27.6 5.0 %collective-permute-start.6 = (bf16[8,128,128]{2,1,0:T(8,128)(2,1)S(1)}, bf16[8,128,128]{2,1,0:T(8,128)(2,1)S(1)}, u32[]{:S(2)}, u32[]{:S(2)}) collective-permute-start(bf16[8,128,128]{2,1,0:T(8,128)(2,1)S(1)} %get-tuple-element.9), channel_id=1, source_target_pairs={{4,8},{8,4},{5,9},{9,5},{6,10},{10,6},{7,11},{11,7},{20,24},{24,20... | collective-permute-start | bytes 786440 | tf_op jit(solution)/shard_map/ppermute | solution.py:231
  28.3 4.4 %collective-permute-start.7 = (bf16[8,128,128]{2,1,0:T(8,128)(2,1)S(1)}, bf16[8,128,128]{2,1,0:T(8,128)(2,1)S(1)}, u32[]{:S(2)}, u32[]{:S(2)}) collective-permute-start(bf16[8,128,128]{2,1,0:T(8,128)(2,1)S(1)} %get-tuple-element.10), channel_id=1, source_target_pairs={{0,4},{8,12},{4,0},{12,8},{1,5},{9,13},{5,1},{13,9},{2,6},{10,14},... | collective-permute-start | bytes 786440 | tf_op jit(solution)/shard_map/ppermute | solution.py:231
  34.3 10.4 %collective-permute-start.14 = (bf16[384,128]{1,0:T(8,128)(2,1)S(1)}, bf16[384,128]{1,0:T(8,128)(2,1)S(1)}, u32[]{:S(2)}, u32[]{:S(2)}) collective-permute-start(bf16[384,128]{1,0:T(8,128)(2,1)S(1)} %attend_chunk.4.refs_0_), channel_id=1, source_target_pairs={{0,3},{1,2},{2,1},{3,0},{4,7},{5,6},{6,5},{7,4},{8,11},{9,10},{10,... | collective-permute-start | bytes 294920 | tf_op jit(solution)/shard_map/ppermute | solution.py:290
  40.8 7.1 %collective-permute-start.13 = (bf16[384,128]{1,0:T(8,128)(2,1)S(1)}, bf16[384,128]{1,0:T(8,128)(2,1)S(1)}, u32[]{:S(2)}, u32[]{:S(2)}) collective-permute-start(bf16[384,128]{1,0:T(8,128)(2,1)S(1)} %attend_chunk.5.refs_0_), channel_id=1, source_target_pairs={{0,2},{1,3},{2,0},{3,1},{4,6},{5,7},{6,4},{7,5},{8,10},{9,11},{10,... | collective-permute-start | bytes 294920 | tf_op jit(solution)/shard_map/ppermute | solution.py:290
  42.5 6.7 %collective-permute-start.12 = (bf16[384,128]{1,0:T(8,128)(2,1)S(1)}, bf16[384,128]{1,0:T(8,128)(2,1)S(1)}, u32[]{:S(2)}, u32[]{:S(2)}) collective-permute-start(bf16[384,128]{1,0:T(8,128)(2,1)S(1)} %attend_chunk.6.refs_0_), channel_id=1, source_target_pairs={{0,1},{1,0},{2,3},{3,2},{4,5},{5,4},{6,7},{7,6},{8,9},{9,8},{10,11... | collective-permute-start | bytes 294920 | tf_op jit(solution)/shard_map/ppermute | solution.py:290

commit v17 on v16

--- a/solution.py
+++ b/solution.py
@@ -294,8 +294,7 @@
 
     v_parts, k_parts, q_parts = [None] * heads, [None] * heads, [None] * heads
     for pair in [*order, 0]:
-        column = (lax.axis_index("head") ^ pair) * HDIM
-        part = lax.dynamic_slice_in_dim(values, column, HDIM, axis=1).reshape(tiles)
+        part = call_on(functools.partial(load_tiles_kernel, pair, turn=False), "load_v", (values,), tiles)
         v_parts[pair] = exchange(part, pair) if pair else part
     for pair in [*order, 0]:
         operands = (keys, queries) if pair == 1 else (keys,)
@@ -340,9 +339,9 @@
             pass_kernel, "landed", operands, [VMEM] * len(operands), chunk, cost=cost(BLOCK * LIST // 2)
         )
         after = (outs[pair],)
-    last = order[-1]
-    early = [pair for pair in range(heads) if pair != last]
-    return spread(outs, [last], queries.shape, spread(outs, early, queries.shape))
+    last = list(order[-2:])
+    early = [pair for pair in range(heads) if pair not in last]
+    return spread(outs, last, queries.shape, spread(outs, early, queries.shape))
 
 
 def on_device(queries, keys, values, tile_lists, live_counts):

time: 50.1 us -> 50.6 us (level)
  starting transfers between devices: 27.9 us -> 24 us
  waiting for transfers between devices: 10.7 us -> 14.3 us
  local copies, waits for them, and re-layouts: 1.79 us -> 2.49 us
    ppermute x11, waiting for transfers between devices: 10.7 us -> 14.2 us  [exchange(): return lax.ppermute(array, 'head', [(i, i ^ pair) for i in range(heads)])]
    ppermute x4, starting transfers between devices: 6.63 us -> 4.26 us  [exchange(): lax.ppermute(array, 'ctx', [(i, i + 1) for i in lower] + [(i + 1, i) for...]
    unnamed x8 -> x12, local copies, waits for them, and re-layouts: 0.55 us -> 2.4 us
    ppermute x11, starting transfers between devices: 21.2 us -> 19.7 us  [exchange(): return lax.ppermute(array, 'head', [(i, i ^ pair) for i in range(heads)])]
    dynamic_slice x1 -> x0, local copies, waits for them, and re-layouts: 1.14 us -> none  [in_pairs(): part = lax.dynamic_slice_in_dim(values, column, HDIM, axis=1).reshape(tiles)]
    pallas_call x23 -> x27, Pallas kernels: 7.9 us -> 7.97 us  [call(): pl.pallas_call(kernel, out_shape=out_shape, in_specs=in_specs, out_specs=...]
  transfers between devices with their start and end apart: 15 -> 15, of which waited for: 5 -> 6; matrix products, arithmetic and copies ran while one was open for 0% -> 0% of each run, Pallas kernels for 14% -> 14%
where the time goes in v17:
time: 50.6 us; the launch traced here: 50.4 us
  starting transfers between devices  24 us (47%)
  waiting for transfers between devices  14.3 us (28%)
  Pallas kernels  9.38 us (19%)
  local copies, waits for them, and re-layouts  2.49 us (5%)
    ppermute x11, starting transfers between devices, exchange(): return lax.ppermute(array, 'head', [(i, i ^ pair) for i in range(heads)])  19.7 us
    ppermute x11, waiting for transfers between devices, exchange(): return lax.ppermute(array, 'head', [(i, i ^ pair) for i in range(heads)])  14.2 us
    pallas_call x27, Pallas kernels, call(): pl.pallas_call(kernel, out_shape=out_shape, in_specs=in_specs, out_specs=...  7.97 us
    ppermute x4, starting transfers between devices, exchange(): lax.ppermute(array, 'ctx', [(i, i + 1) for i in lower] + [(i + 1, i) for...  4.26 us
    unnamed x12, local copies, waits for them, and re-layouts  2.4 us
    pallas_call x2, Pallas kernels, spread(): pl.pallas_call(functools.partial(spread_kernel, pairs), out_shape=jax.Sha...  1.4 us
  transfers between devices with their start and end apart: 15, of which 6 were waited for; matrix products, arithmetic and copies ran while one was open for 0% of the time, Pallas kernels for 14%

profile of v17, /device:TPU:0, one launch (start us, length us, event | category | flops | bytes accessed | tf_op | source)
XLA Modules:
  0.0 50.4 jit_solution(15604378880002186695)
XLA Ops:
  0.0 1.0 %copy-done.2 = bf16[384,512]{1,0:T(8,128)(2,1)S(1)} copy-done((bf16[384,512]{1,0:T(8,128)(2,1)S(1)}, bf16[384,512]{1,0:T(8,128)(2,1)}, u32[]{:S(2)}) %copy-start.2) | copy-done | bytes 393240
  1.0 0.0 copy-start
  1.0 0.0 copy-start.1
  1.0 3.1 %collective-permute-start = (bf16[3,128,128]{2,1,0:T(8,128)(2,1)S(1)}, bf16[3,128,128]{2,1,0:T(8,128)(2,1)S(1)}, u32[]{:S(2)}, u32[]{:S(2)}) collective-permute-start(bf16[3,128,128]{2,1,0:T(8,128)(2,1)S(1)} %load_v.4), channel_id=1, source_target_pairs={{0,1},{1,0},{2,3},{3,2},{4,5},{5,4},{6,7},{7,6},{8,9},{9,8},{10,11... | collective-permute-start | bytes 294920 | tf_op jit(solution)/shard_map/ppermute | solution.py:290
  4.2 2.7 %collective-permute-start.8 = (bf16[3,128,128]{2,1,0:T(8,128)(2,1)S(1)}, bf16[3,128,128]{2,1,0:T(8,128)(2,1)S(1)}, u32[]{:S(2)}, u32[]{:S(2)}) collective-permute-start(bf16[3,128,128]{2,1,0:T(8,128)(2,1)S(1)} %load_v.6), channel_id=1, source_target_pairs={{0,2},{1,3},{2,0},{3,1},{4,6},{5,7},{6,4},{7,5},{8,10},{9,11},{10,... | collective-permute-start | bytes 294920 | tf_op jit(solution)/shard_map/ppermute | solution.py:290
  6.8 0.0 copy-start.5
  6.8 0.1 collective-permute-start.9
  6.9 0.6 %copy-done.5 = s32[12]{0:T(128)S(1)} copy-done((s32[12]{0:T(128)S(1)}, s32[12]{0:T(128)}, u32[]{:S(2)}) %copy-start.5) | copy-done | bytes 72
  7.5 0.1 copy.7.counts_ref
  7.6 0.0 collective-permute-done.refs_0_.refs_1_
  7.6 0.1 load_k.4
  7.7 0.0 copy-start.4
  7.7 1.2 %collective-permute-start.1 = (bf16[6,128,128]{2,1,0:T(8,128)(2,1)S(1)}, bf16[6,128,128]{2,1,0:T(8,128)(2,1)S(1)}, u32[]{:S(2)}, u32[]{:S(2)}) collective-permute-start(bf16[6,128,128]{2,1,0:T(8,128)(2,1)S(1)} %load_k.4), channel_id=1, source_target_pairs={{0,1},{1,0},{2,3},{3,2},{4,5},{5,4},{6,7},{7,6},{8,9},{9,8},{10,11... | collective-permute-start | bytes 589832 | tf_op jit(solution)/shard_map/ppermute | solution.py:290
  8.9 0.1 load_k.5
  9.0 3.7 %collective-permute-start.2 = (bf16[3,128,128]{2,1,0:T(8,128)(2,1)S(1)}, bf16[3,128,128]{2,1,0:T(8,128)(2,1)S(1)}, u32[]{:S(2)}, u32[]{:S(2)}) collective-permute-start(bf16[3,128,128]{2,1,0:T(8,128)(2,1)S(1)} %load_k.5), channel_id=1, source_target_pairs={{0,2},{1,3},{2,0},{3,1},{4,6},{5,7},{6,4},{7,5},{8,10},{9,11},{10,... | collective-permute-start | bytes 294920 | tf_op jit(solution)/shard_map/ppermute | solution.py:290
  12.7 0.6 %mask_bias.1.refs_1_.bias_ref = f32[27,12,128]{2,1,0:T(8,128)S(1)} custom-call(s32[12,16]{1,0:T(8,128)S(1)} %copy-done.4, s32[12,1]{1,0:T(8,128)S(1)} %copy.7.counts_ref), custom_call_target="tpu_custom_call" | custom-call | tf_op jit(solution)/shard_map/mask_bias/pallas_call | solution.py:29
  13.3 0.0 copy-start.3
  13.3 0.1 load_k.6
  13.4 0.1 collective-permute-start.4
  13.5 0.8 %copy-done.3 = bf16[384,512]{1,0:T(8,128)(2,1)S(1)} copy-done((bf16[384,512]{1,0:T(8,128)(2,1)S(1)}, bf16[384,512]{1,0:T(8,128)(2,1)}, u32[]{:S(2)}) %copy-start.3) | copy-done | bytes 393240
  14.3 0.4 collective-permute-done.8.refs_2_
  14.7 0.0 collective-permute-done.9.refs_3_
  14.8 0.7 %collective-permute-start.10 = (bf16[8,128,128]{2,1,0:T(8,128)(2,1)S(1)}, bf16[8,128,128]{2,1,0:T(8,128)(2,1)S(1)}, u32[]{:S(2)}, u32[]{:S(2)}) collective-permute-start(bf16[8,128,128]{2,1,0:T(8,128)(2,1)S(1)} %get-tuple-element.11), channel_id=1, source_target_pairs={{4,8},{8,4},{5,9},{9,5},{6,10},{10,6},{7,11},{11,7},{20,24},{24,20... | collective-permute-start | bytes 786440 | tf_op jit(solution)/shard_map/ppermute | solution.py:231
  15.5 2.9 %collective-permute-start.11 = (bf16[8,128,128]{2,1,0:T(8,128)(2,1)S(1)}, bf16[8,128,128]{2,1,0:T(8,128)(2,1)S(1)}, u32[]{:S(2)}, u32[]{:S(2)}) collective-permute-start(bf16[8,128,128]{2,1,0:T(8,128)(2,1)S(1)} %get-tuple-element.12), channel_id=1, source_target_pairs={{0,4},{8,12},{4,0},{12,8},{1,5},{9,13},{5,1},{13,9},{2,6},{10,14},... | collective-permute-start | bytes 786440 | tf_op jit(solution)/shard_map/ppermute | solution.py:231
  18.4 4.7 %collective-permute-done.2.refs_0_.refs_2_ = bf16[3,128,128]{2,1,0:T(8,128)(2,1)S(1)} collective-permute-done((bf16[3,128,128]{2,1,0:T(8,128)(2,1)S(1)}, bf16[3,128,128]{2,1,0:T(8,128)(2,1)S(1)}, u32[]{:S(2)}, u32[]{:S(2)}) %collective-permute-start.2) | collective-permute-done | bytes 98336 | tf_op jit(solution)/shard_map/ppermute | solution.py:290
  23.1 3.3 %collective-permute-start.3 = (bf16[384,128]{1,0:T(8,128)(2,1)S(1)}, bf16[384,128]{1,0:T(8,128)(2,1)S(1)}, u32[]{:S(2)}, u32[]{:S(2)}) collective-permute-start(bf16[384,128]{1,0:T(8,128)(2,1)S(1)} %load_q.4), channel_id=1, source_target_pairs={{0,2},{1,3},{2,0},{3,1},{4,6},{5,7},{6,4},{7,5},{8,10},{9,11},{10,... | collective-permute-start | bytes 294920 | tf_op jit(solution)/shard_map/ppermute | solution.py:290
  26.4 0.1 collective-permute-start.5
  26.6 0.1 load_k.7.refs_0_
  26.7 0.0 collective-permute-done.1.refs_1_
  26.8 0.7 %collective-permute-start.6 = (bf16[8,128,128]{2,1,0:T(8,128)(2,1)S(1)}, bf16[8,128,128]{2,1,0:T(8,128)(2,1)S(1)}, u32[]{:S(2)}, u32[]{:S(2)}) collective-permute-start(bf16[8,128,128]{2,1,0:T(8,128)(2,1)S(1)} %get-tuple-element.9), channel_id=1, source_target_pairs={{4,8},{8,4},{5,9},{9,5},{6,10},{10,6},{7,11},{11,7},{20,24},{24,20... | collective-permute-start | bytes 786440 | tf_op jit(solution)/shard_map/ppermute | solution.py:231
  27.4 3.0 %collective-permute-done.3.refs_2_ = bf16[384,128]{1,0:T(8,128)(2,1)S(1)} collective-permute-done((bf16[384,128]{1,0:T(8,128)(2,1)S(1)}, bf16[384,128]{1,0:T(8,128)(2,1)S(1)}, u32[]{:S(2)}, u32[]{:S(2)}) %collective-permute-start.3) | collective-permute-done | bytes 98336 | tf_op jit(solution)/shard_map/ppermute | solution.py:290
  30.5 0.0 collective-permute-start.7
  30.5 2.5 %collective-permute-done.5.refs_3_ = bf16[384,128]{1,0:T(8,128)(2,1)S(1)} collective-permute-done((bf16[384,128]{1,0:T(8,128)(2,1)S(1)}, bf16[384,128]{1,0:T(8,128)(2,1)S(1)}, u32[]{:S(2)}, u32[]{:S(2)}) %collective-permute-start.5) | collective-permute-done | bytes 98336 | tf_op jit(solution)/shard_map/ppermute | solution.py:290
  33.0 0.0 collective-permute-done.10.first_ref
  33.0 0.1 join.3.array_ref
  33.1 0.1 values.1.v_ref
  33.2 0.1 join.2.kt_ref
  33.3 1.6 %attend_chunk.4.refs_0_ = bf16[384,128]{1,0:T(8,128)(2,1)S(1)} custom-call(bf16[4,384,128]{2,1,0:T(8,128)(2,1)S(1)} %stack.1.refs_0_.q_ref, bf16[27,128,128]{2,1,0:T(8,128)(2,1)S(1)} %join.2.kt_ref, bf16[27,128,128]{2,1,0:T(8,128)(2,1)S(1)} %values.1.v_ref, f32[27,12,128]{2,1,0:T(8,128)S(1)} %mask_bias.1.refs_1_.bias_ref), custom_call_target="tpu_custom_call" | custom-call | flops 201326592 | bytes 393216 | tf_op jit(solution)/shard_map/attend_chunk/pallas_call | solution.py:29
  34.9 4.8 %collective-permute-start.13 = (bf16[384,128]{1,0:T(8,128)(2,1)S(1)}, bf16[384,128]{1,0:T(8,128)(2,1)S(1)}, u32[]{:S(2)}, u32[]{:S(2)}) collective-permute-start(bf16[384,128]{1,0:T(8,128)(2,1)S(1)} %attend_chunk.4.refs_0_), channel_id=1, source_target_pairs={{0,3},{1,2},{2,1},{3,0},{4,7},{5,6},{6,5},{7,4},{8,11},{9,10},{10,... | collective-permute-start | bytes 294920 | tf_op jit(solution)/shard_map/ppermute | solution.py:290
  39.7 1.6 %attend_chunk.5.refs_0_ = bf16[384,128]{1,0:T(8,128)(2,1)S(1)} custom-call(bf16[4,384,128]{2,1,0:T(8,128)(2,1)S(1)} %stack.1.refs_0_.q_ref, bf16[27,128,128]{2,1,0:T(8,128)(2,1)S(1)} %join.2.kt_ref, bf16[27,128,128]{2,1,0:T(8,128)(2,1)S(1)} %values.1.v_ref, f32[27,12,128]{2,1,0:T(8,128)S(1)} %mask_bias.1.refs_1_.bias_ref, ...), custom_call_target="tpu_custom_call" | custom-call | flops 201326592 | bytes 393216 | tf_op jit(solution)/shard_map/attend_chunk/pallas_call | solution.py:29
  41.3 0.1 collective-permute-start.12
  41.4 1.6 %attend_chunk.6.refs_0_ = bf16[384,128]{1,0:T(8,128)(2,1)S(1)} custom-call(bf16[4,384,128]{2,1,0:T(8,128)(2,1)S(1)} %stack.1.refs_0_.q_ref, bf16[27,128,128]{2,1,0:T(8,128)(2,1)S(1)} %join.2.kt_ref, bf16[27,128,128]{2,1,0:T(8,128)(2,1)S(1)} %values.1.v_ref, f32[27,12,128]{2,1,0:T(8,128)S(1)} %mask_bias.1.refs_1_.bias_ref, ...), custom_call_target="tpu_custom_call" | custom-call | flops 201326592 | bytes 393216 | tf_op jit(solution)/shard_map/attend_chunk/pallas_call | solution.py:29
  43.0 0.6 %collective-permute-start.14 = (bf16[384,128]{1,0:T(8,128)(2,1)S(1)}, bf16[384,128]{1,0:T(8,128)(2,1)S(1)}, u32[]{:S(2)}, u32[]{:S(2)}) collective-permute-start(bf16[384,128]{1,0:T(8,128)(2,1)S(1)} %attend_chunk.6.refs_0_), channel_id=1, source_target_pairs={{0,1},{1,0},{2,3},{3,2},{4,5},{5,4},{6,7},{7,6},{8,9},{9,8},{10,11... | collective-permute-start | bytes 294920 | tf_op jit(solution)/shard_map/ppermute | solution.py:290
  43.6 1.6 %attend_chunk.7.refs_0_ = bf16[384,128]{1,0:T(8,128)(2,1)S(1)} custom-call(bf16[4,384,128]{2,1,0:T(8,128)(2,1)S(1)} %stack.1.refs_0_.q_ref, bf16[27,128,128]{2,1,0:T(8,128)(2,1)S(1)} %join.2.kt_ref, bf16[27,128,128]{2,1,0:T(8,128)(2,1)S(1)} %values.1.v_ref, f32[27,12,128]{2,1,0:T(8,128)S(1)} %mask_bias.1.refs_1_.bias_ref, ...), custom_call_target="tpu_custom_call" | custom-call | flops 8388608 | bytes 16384 | tf_op jit(solution)/shard_map/attend_chunk/pallas_call | solution.py:29
  45.3 0.7 %spread.2.refs_2_ = bf16[384,512]{1,0:T(8,128)(2,1)} custom-call(bf16[384,128]{1,0:T(8,128)(2,1)S(1)} %attend_chunk.7.refs_0_, bf16[384,128]{1,0:T(8,128)(2,1)S(1)} %landed.3.refs_0_.refs_1_), custom_call_target="tpu_custom_call" | custom-call | tf_op jit(solution)/shard_map/spread/pallas_call | solution.py:272
  46.0 1.9 %collective-permute-done.12.array_ref = bf16[384,128]{1,0:T(8,128)(2,1)S(1)} collective-permute-done((bf16[384,128]{1,0:T(8,128)(2,1)S(1)}, bf16[384,128]{1,0:T(8,128)(2,1)S(1)}, u32[]{:S(2)}, u32[]{:S(2)}) %collective-permute-start.12) | collective-permute-done | bytes 98336 | tf_op jit(solution)/shard_map/ppermute | solution.py:290
  47.9 1.7 %collective-permute-done.14.array_ref = bf16[384,128]{1,0:T(8,128)(2,1)S(1)} collective-permute-done((bf16[384,128]{1,0:T(8,128)(2,1)S(1)}, bf16[384,128]{1,0:T(8,128)(2,1)S(1)}, u32[]{:S(2)}, u32[]{:S(2)}) %collective-permute-start.14) | collective-permute-done | bytes 98336 | tf_op jit(solution)/shard_map/ppermute | solution.py:290
  49.7 0.7 %spread.3 = bf16[384,512]{1,0:T(8,128)(2,1)} custom-call(bf16[384,128]{1,0:T(8,128)(2,1)S(1)} %landed.4.refs_0_, bf16[384,128]{1,0:T(8,128)(2,1)S(1)} %landed.5.refs_1_, bf16[384,512]{1,0:T(8,128)(2,1)} %spread.2.refs_2_), custom_call_target="tpu_custom_call", output_to_operand_aliasing={{}: (2, {})} | custom-call | tf_op jit(solution)/shard_map/spread/pallas_call | solution.py:272
  (24 shorter events, 0.4 us)
Async XLA Ops:
  0.0 1.0 %copy-start.2 = (bf16[384,512]{1,0:T(8,128)(2,1)S(1)}, bf16[384,512]{1,0:T(8,128)(2,1)}, u32[]{:S(2)}) copy-start(bf16[384,512]{1,0:T(8,128)(2,1)} %array_ref.13) | copy-start | bytes 1179652
  1.0 6.6 %copy-start = (bf16[384,512]{1,0:T(8,128)(2,1)S(1)}, bf16[384,512]{1,0:T(8,128)(2,1)}, u32[]{:S(2)}) copy-start(bf16[384,512]{1,0:T(8,128)(2,1)} %q_ref.7) | copy-start | bytes 1179652
  1.0 6.6 %copy-start.1 = (bf16[384,512]{1,0:T(8,128)(2,1)S(1)}, bf16[384,512]{1,0:T(8,128)(2,1)}, u32[]{:S(2)}) copy-start(bf16[384,512]{1,0:T(8,128)(2,1)} %array_ref.10) | copy-start | bytes 1179652
  1.0 6.5 %collective-permute-start = (bf16[3,128,128]{2,1,0:T(8,128)(2,1)S(1)}, bf16[3,128,128]{2,1,0:T(8,128)(2,1)S(1)}, u32[]{:S(2)}, u32[]{:S(2)}) collective-permute-start(bf16[3,128,128]{2,1,0:T(8,128)(2,1)S(1)} %load_v.4), channel_id=1, source_target_pairs={{0,1},{1,0},{2,3},{3,2},{4,5},{5,4},{6,7},{7,6},{8,9},{9,8},{10,11... | collective-permute-start | bytes 294920 | tf_op jit(solution)/shard_map/ppermute | solution.py:290
  4.2 10.6 %collective-permute-start.8 = (bf16[3,128,128]{2,1,0:T(8,128)(2,1)S(1)}, bf16[3,128,128]{2,1,0:T(8,128)(2,1)S(1)}, u32[]{:S(2)}, u32[]{:S(2)}) collective-permute-start(bf16[3,128,128]{2,1,0:T(8,128)(2,1)S(1)} %load_v.6), channel_id=1, source_target_pairs={{0,2},{1,3},{2,0},{3,1},{4,6},{5,7},{6,4},{7,5},{8,10},{9,11},{10,... | collective-permute-start | bytes 294920 | tf_op jit(solution)/shard_map/ppermute | solution.py:290
  6.8 0.7 %copy-start.5 = (s32[12]{0:T(128)S(1)}, s32[12]{0:T(128)}, u32[]{:S(2)}) copy-start(s32[12]{0:T(128)} %param.9) | copy-start | bytes 148
  6.8 7.9 %collective-permute-start.9 = (bf16[3,128,128]{2,1,0:T(8,128)(2,1)S(1)}, bf16[3,128,128]{2,1,0:T(8,128)(2,1)S(1)}, u32[]{:S(2)}, u32[]{:S(2)}) collective-permute-start(bf16[3,128,128]{2,1,0:T(8,128)(2,1)S(1)} %load_v.7), channel_id=1, source_target_pairs={{0,3},{1,2},{2,1},{3,0},{4,7},{5,6},{6,5},{7,4},{8,11},{9,10},{10,... | collective-permute-start | bytes 294920 | tf_op jit(solution)/shard_map/ppermute | solution.py:290
  7.7 5.0 %copy-start.4 = (s32[12,16]{1,0:T(8,128)S(1)}, s32[12,16]{1,0:T(8,128)}, u32[]{:S(2)}) copy-start(s32[12,16]{1,0:T(8,128)} %lists_ref.1) | copy-start | bytes 2308
  7.7 18.9 %collective-permute-start.1 = (bf16[6,128,128]{2,1,0:T(8,128)(2,1)S(1)}, bf16[6,128,128]{2,1,0:T(8,128)(2,1)S(1)}, u32[]{:S(2)}, u32[]{:S(2)}) collective-permute-start(bf16[6,128,128]{2,1,0:T(8,128)(2,1)S(1)} %load_k.4), channel_id=1, source_target_pairs={{0,1},{1,0},{2,3},{3,2},{4,5},{5,4},{6,7},{7,6},{8,9},{9,8},{10,11... | collective-permute-start | bytes 589832 | tf_op jit(solution)/shard_map/ppermute | solution.py:290
  9.0 14.0 %collective-permute-start.2 = (bf16[3,128,128]{2,1,0:T(8,128)(2,1)S(1)}, bf16[3,128,128]{2,1,0:T(8,128)(2,1)S(1)}, u32[]{:S(2)}, u32[]{:S(2)}) collective-permute-start(bf16[3,128,128]{2,1,0:T(8,128)(2,1)S(1)} %load_k.5), channel_id=1, source_target_pairs={{0,2},{1,3},{2,0},{3,1},{4,6},{5,7},{6,4},{7,5},{8,10},{9,11},{10,... | collective-permute-start | bytes 294920 | tf_op jit(solution)/shard_map/ppermute | solution.py:290
  13.3 1.0 %copy-start.3 = (bf16[384,512]{1,0:T(8,128)(2,1)S(1)}, bf16[384,512]{1,0:T(8,128)(2,1)}, u32[]{:S(2)}) copy-start(bf16[384,512]{1,0:T(8,128)(2,1)} %array_ref.13) | copy-start | bytes 1179652
  13.4 13.0 %collective-permute-start.4 = (bf16[3,128,128]{2,1,0:T(8,128)(2,1)S(1)}, bf16[3,128,128]{2,1,0:T(8,128)(2,1)S(1)}, u32[]{:S(2)}, u32[]{:S(2)}) collective-permute-start(bf16[3,128,128]{2,1,0:T(8,128)(2,1)S(1)} %load_k.6), channel_id=1, source_target_pairs={{0,3},{1,2},{2,1},{3,0},{4,7},{5,6},{6,5},{7,4},{8,11},{9,10},{10,... | collective-permute-start | bytes 294920 | tf_op jit(solution)/shard_map/ppermute | solution.py:290
  14.8 18.2 %collective-permute-start.10 = (bf16[8,128,128]{2,1,0:T(8,128)(2,1)S(1)}, bf16[8,128,128]{2,1,0:T(8,128)(2,1)S(1)}, u32[]{:S(2)}, u32[]{:S(2)}) collective-permute-start(bf16[8,128,128]{2,1,0:T(8,128)(2,1)S(1)} %get-tuple-element.11), channel_id=1, source_target_pairs={{4,8},{8,4},{5,9},{9,5},{6,10},{10,6},{7,11},{11,7},{20,24},{24,20... | collective-permute-start | bytes 786440 | tf_op jit(solution)/shard_map/ppermute | solution.py:231
  15.5 17.5 %collective-permute-start.11 = (bf16[8,128,128]{2,1,0:T(8,128)(2,1)S(1)}, bf16[8,128,128]{2,1,0:T(8,128)(2,1)S(1)}, u32[]{:S(2)}, u32[]{:S(2)}) collective-permute-start(bf16[8,128,128]{2,1,0:T(8,128)(2,1)S(1)} %get-tuple-element.12), channel_id=1, source_target_pairs={{0,4},{8,12},{4,0},{12,8},{1,5},{9,13},{5,1},{13,9},{2,6},{10,14},... | collective-permute-start | bytes 786440 | tf_op jit(solution)/shard_map/ppermute | solution.py:231
  23.1 7.4 %collective-permute-start.3 = (bf16[384,128]{1,0:T(8,128)(2,1)S(1)}, bf16[384,128]{1,0:T(8,128)(2,1)S(1)}, u32[]{:S(2)}, u32[]{:S(2)}) collective-permute-start(bf16[384,128]{1,0:T(8,128)(2,1)S(1)} %load_q.4), channel_id=1, source_target_pairs={{0,2},{1,3},{2,0},{3,1},{4,6},{5,7},{6,4},{7,5},{8,10},{9,11},{10,... | collective-permute-start | bytes 294920 | tf_op jit(solution)/shard_map/ppermute | solution.py:290
  26.4 6.5 %collective-permute-start.5 = (bf16[384,128]{1,0:T(8,128)(2,1)S(1)}, bf16[384,128]{1,0:T(8,128)(2,1)S(1)}, u32[]{:S(2)}, u32[]{:S(2)}) collective-permute-start(bf16[384,128]{1,0:T(8,128)(2,1)S(1)} %load_q.5), channel_id=1, source_target_pairs={{0,3},{1,2},{2,1},{3,0},{4,7},{5,6},{6,5},{7,4},{8,11},{9,10},{10,... | collective-permute-start | bytes 294920 | tf_op jit(solution)/shard_map/ppermute | solution.py:290
  26.8 6.4 %collective-permute-start.6 = (bf16[8,128,128]{2,1,0:T(8,128)(2,1)S(1)}, bf16[8,128,128]{2,1,0:T(8,128)(2,1)S(1)}, u32[]{:S(2)}, u32[]{:S(2)}) collective-permute-start(bf16[8,128,128]{2,1,0:T(8,128)(2,1)S(1)} %get-tuple-element.9), channel_id=1, source_target_pairs={{4,8},{8,4},{5,9},{9,5},{6,10},{10,6},{7,11},{11,7},{20,24},{24,20... | collective-permute-start | bytes 786440 | tf_op jit(solution)/shard_map/ppermute | solution.py:231
  30.5 2.7 %collective-permute-start.7 = (bf16[8,128,128]{2,1,0:T(8,128)(2,1)S(1)}, bf16[8,128,128]{2,1,0:T(8,128)(2,1)S(1)}, u32[]{:S(2)}, u32[]{:S(2)}) collective-permute-start(bf16[8,128,128]{2,1,0:T(8,128)(2,1)S(1)} %get-tuple-element.10), channel_id=1, source_target_pairs={{0,4},{8,12},{4,0},{12,8},{1,5},{9,13},{5,1},{13,9},{2,6},{10,14},... | collective-permute-start | bytes 786440 | tf_op jit(solution)/shard_map/ppermute | solution.py:231
  34.9 10.4 %collective-permute-start.13 = (bf16[384,128]{1,0:T(8,128)(2,1)S(1)}, bf16[384,128]{1,0:T(8,128)(2,1)S(1)}, u32[]{:S(2)}, u32[]{:S(2)}) collective-permute-start(bf16[384,128]{1,0:T(8,128)(2,1)S(1)} %attend_chunk.4.refs_0_), channel_id=1, source_target_pairs={{0,3},{1,2},{2,1},{3,0},{4,7},{5,6},{6,5},{7,4},{8,11},{9,10},{10,... | collective-permute-start | bytes 294920 | tf_op jit(solution)/shard_map/ppermute | solution.py:290
  41.3 6.6 %collective-permute-start.12 = (bf16[384,128]{1,0:T(8,128)(2,1)S(1)}, bf16[384,128]{1,0:T(8,128)(2,1)S(1)}, u32[]{:S(2)}, u32[]{:S(2)}) collective-permute-start(bf16[384,128]{1,0:T(8,128)(2,1)S(1)} %attend_chunk.5.refs_0_), channel_id=1, source_target_pairs={{0,2},{1,3},{2,0},{3,1},{4,6},{5,7},{6,4},{7,5},{8,10},{9,11},{10,... | collective-permute-start | bytes 294920 | tf_op jit(solution)/shard_map/ppermute | solution.py:290
  43.0 6.7 %collective-permute-start.14 = (bf16[384,128]{1,0:T(8,128)(2,1)S(1)}, bf16[384,128]{1,0:T(8,128)(2,1)S(1)}, u32[]{:S(2)}, u32[]{:S(2)}) collective-permute-start(bf16[384,128]{1,0:T(8,128)(2,1)S(1)} %attend_chunk.6.refs_0_), channel_id=1, source_target_pairs={{0,1},{1,0},{2,3},{3,2},{4,5},{5,4},{6,7},{7,6},{8,9},{9,8},{10,11... | collective-permute-start | bytes 294920 | tf_op jit(solution)/shard_map/ppermute | solution.py:290

commit v18 on v16

--- a/solution.py
+++ b/solution.py
@@ -302,7 +302,7 @@
         kernel = load_kq_kernel if pair == 1 else functools.partial(load_tiles_kernel, turn=True)
         shape = (len(operands) * BLOCK, TILE, HDIM)
         after = (v_parts[1],) if pair else ()
-        if pair == order[0]:
+        if pair == 1:
             after += (bias,)
         part = call_on(functools.partial(kernel, pair), "load_k", (*operands, *after), shape)
         k_parts[pair] = exchange(part, pair) if pair else part

time: 50.1 us -> 50.1 us (level)
  waiting for transfers between devices: 10.7 us -> 11.3 us
  local copies, waits for them, and re-layouts: 1.79 us -> 1.26 us
    ppermute x11, waiting for transfers between devices: 10.7 us -> 11.3 us  [exchange(): return lax.ppermute(array, 'head', [(i, i ^ pair) for i in range(heads)])]
    unnamed x8, local copies, waits for them, and re-layouts: 0.55 us -> 0.02 us
where the time goes in v18:
time: 50.1 us; the launch traced here: 49.9 us
  starting transfers between devices  27.8 us (55%)
  waiting for transfers between devices  11.3 us (23%)
  Pallas kernels  9.3 us (19%)
  local copies, waits for them, and re-layouts  1.26 us (3%)
    ppermute x11, starting transfers between devices, exchange(): return lax.ppermute(array, 'head', [(i, i ^ pair) for i in range(heads)])  21.1 us
    ppermute x11, waiting for transfers between devices, exchange(): return lax.ppermute(array, 'head', [(i, i ^ pair) for i in range(heads)])  11.3 us
    pallas_call x23, Pallas kernels, call(): pl.pallas_call(kernel, out_shape=out_shape, in_specs=in_specs, out_specs=...  7.89 us
    ppermute x4, starting transfers between devices, exchange(): lax.ppermute(array, 'ctx', [(i, i + 1) for i in lower] + [(i + 1, i) for...  6.63 us
    pallas_call x2, Pallas kernels, spread(): pl.pallas_call(functools.partial(spread_kernel, pairs), out_shape=jax.Sha...  1.4 us
    dynamic_slice x1, local copies, waits for them, and re-layouts, in_pairs(): part = lax.dynamic_slice_in_dim(values, column, HDIM, axis=1).reshape(tiles)  1.14 us
  transfers between devices with their start and end apart: 15, of which 5 were waited for; matrix products, arithmetic and copies ran while one was open for 0% of the time, Pallas kernels for 14%

profile of v18, /device:TPU:0, one launch (start us, length us, event | category | flops | bytes accessed | tf_op | source)
XLA Modules:
  0.0 49.9 jit_solution(6744396865427935055)
XLA Ops:
  0.0 1.1 %constant_dynamic-slice_fusion = (bf16[384,128]{1,0:T(8,128)(2,1)S(1)}, bf16[384,128]{1,0:T(8,128)(2,1)S(1)}, bf16[384,128]{1,0:T(8,128)(2,1)S(1)}, bf16[384,128]{1,0:T(8,128)(2,1)S(1)}) fusion(bf16[384,512]{1,0:T(8,128)(2,1)} %param.7, s32[]{:T(128)S(6)} %select_n.15, s32[]{:T(128)S(6)} %select_n.13, s32[]{:T(128)S(6)} %select_n.12, s32[]{:T(128)S(6)} %select_n.14), kind=kLoop, calls=%fused_computation | loop fusion | bytes 786448 | tf_op jit(solution)/shard_map/dynamic_slice | solution.py:298
  1.2 0.0 copy-start.3
  1.2 3.1 %collective-permute-start = (bf16[3,128,128]{2,1,0:T(8,128)(2,1)S(1)}, bf16[3,128,128]{2,1,0:T(8,128)(2,1)S(1)}, u32[]{:S(2)}, u32[]{:S(2)}) collective-permute-start(bf16[3,128,128]{2,1,0:T(8,128)(2,1)S(1)} %bitcast.8), channel_id=1, source_target_pairs={{0,1},{1,0},{2,3},{3,2},{4,5},{5,4},{6,7},{7,6},{8,9},{9,8},{10,11... | collective-permute-start | bytes 294920 | tf_op jit(solution)/shard_map/ppermute | solution.py:290
  4.3 2.5 %collective-permute-start.9 = (bf16[3,128,128]{2,1,0:T(8,128)(2,1)S(1)}, bf16[3,128,128]{2,1,0:T(8,128)(2,1)S(1)}, u32[]{:S(2)}, u32[]{:S(2)}) collective-permute-start(bf16[3,128,128]{2,1,0:T(8,128)(2,1)S(1)} %bitcast.7), channel_id=1, source_target_pairs={{0,3},{1,2},{2,1},{3,0},{4,7},{5,6},{6,5},{7,4},{8,11},{9,10},{10,... | collective-permute-start | bytes 294920 | tf_op jit(solution)/shard_map/ppermute | solution.py:290
  6.7 0.1 collective-permute-start.8
  6.8 0.0 copy-done.3
  6.9 0.1 copy.7.counts_ref
  6.9 0.6 %mask_bias.1.refs_1_.bias_ref = f32[27,12,128]{2,1,0:T(8,128)S(1)} custom-call(s32[12,16]{1,0:T(8,128)S(1)} %copy-done.2, s32[12,1]{1,0:T(8,128)S(1)} %copy.7.counts_ref), custom_call_target="tpu_custom_call" | custom-call | tf_op jit(solution)/shard_map/mask_bias/pallas_call | solution.py:29
  7.5 0.0 collective-permute-done.refs_0_.refs_1_
  7.6 0.1 load_k.4
  7.7 1.9 %collective-permute-start.1 = (bf16[6,128,128]{2,1,0:T(8,128)(2,1)S(1)}, bf16[6,128,128]{2,1,0:T(8,128)(2,1)S(1)}, u32[]{:S(2)}, u32[]{:S(2)}) collective-permute-start(bf16[6,128,128]{2,1,0:T(8,128)(2,1)S(1)} %load_k.4), channel_id=1, source_target_pairs={{0,1},{1,0},{2,3},{3,2},{4,5},{5,4},{6,7},{7,6},{8,9},{9,8},{10,11... | collective-permute-start | bytes 589832 | tf_op jit(solution)/shard_map/ppermute | solution.py:290
  9.5 0.1 load_k.5
  9.6 3.2 %collective-permute-start.2 = (bf16[3,128,128]{2,1,0:T(8,128)(2,1)S(1)}, bf16[3,128,128]{2,1,0:T(8,128)(2,1)S(1)}, u32[]{:S(2)}, u32[]{:S(2)}) collective-permute-start(bf16[3,128,128]{2,1,0:T(8,128)(2,1)S(1)} %load_k.5), channel_id=1, source_target_pairs={{0,2},{1,3},{2,0},{3,1},{4,6},{5,7},{6,4},{7,5},{8,10},{9,11},{10,... | collective-permute-start | bytes 294920 | tf_op jit(solution)/shard_map/ppermute | solution.py:290
  12.8 0.1 load_k.6
  12.9 0.1 collective-permute-start.4
  13.0 0.0 collective-permute-done.9.refs_3_
  13.0 3.2 %collective-permute-done.8.refs_2_ = bf16[3,128,128]{2,1,0:T(8,128)(2,1)S(1)} collective-permute-done((bf16[3,128,128]{2,1,0:T(8,128)(2,1)S(1)}, bf16[3,128,128]{2,1,0:T(8,128)(2,1)S(1)}, u32[]{:S(2)}, u32[]{:S(2)}) %collective-permute-start.8) | collective-permute-done | bytes 98336 | tf_op jit(solution)/shard_map/ppermute | solution.py:290
  16.4 0.7 %collective-permute-start.10 = (bf16[8,128,128]{2,1,0:T(8,128)(2,1)S(1)}, bf16[8,128,128]{2,1,0:T(8,128)(2,1)S(1)}, u32[]{:S(2)}, u32[]{:S(2)}) collective-permute-start(bf16[8,128,128]{2,1,0:T(8,128)(2,1)S(1)} %get-tuple-element.11), channel_id=1, source_target_pairs={{4,8},{8,4},{5,9},{9,5},{6,10},{10,6},{7,11},{11,7},{20,24},{24,20... | collective-permute-start | bytes 786440 | tf_op jit(solution)/shard_map/ppermute | solution.py:231
  17.0 2.9 %collective-permute-start.11 = (bf16[8,128,128]{2,1,0:T(8,128)(2,1)S(1)}, bf16[8,128,128]{2,1,0:T(8,128)(2,1)S(1)}, u32[]{:S(2)}, u32[]{:S(2)}) collective-permute-start(bf16[8,128,128]{2,1,0:T(8,128)(2,1)S(1)} %get-tuple-element.12), channel_id=1, source_target_pairs={{0,4},{8,12},{4,0},{12,8},{1,5},{9,13},{5,1},{13,9},{2,6},{10,14},... | collective-permute-start | bytes 786440 | tf_op jit(solution)/shard_map/ppermute | solution.py:231
  19.9 2.6 %collective-permute-done.2.refs_0_.refs_2_ = bf16[3,128,128]{2,1,0:T(8,128)(2,1)S(1)} collective-permute-done((bf16[3,128,128]{2,1,0:T(8,128)(2,1)S(1)}, bf16[3,128,128]{2,1,0:T(8,128)(2,1)S(1)}, u32[]{:S(2)}, u32[]{:S(2)}) %collective-permute-start.2) | collective-permute-done | bytes 98336 | tf_op jit(solution)/shard_map/ppermute | solution.py:290
  22.5 0.1 collective-permute-start.3
  22.6 0.0 collective-permute-done.4.refs_0_.refs_3_
  22.7 4.7 %collective-permute-start.5 = (bf16[384,128]{1,0:T(8,128)(2,1)S(1)}, bf16[384,128]{1,0:T(8,128)(2,1)S(1)}, u32[]{:S(2)}, u32[]{:S(2)}) collective-permute-start(bf16[384,128]{1,0:T(8,128)(2,1)S(1)} %load_q.5), channel_id=1, source_target_pairs={{0,3},{1,2},{2,1},{3,0},{4,7},{5,6},{6,5},{7,4},{8,11},{9,10},{10,... | collective-permute-start | bytes 294920 | tf_op jit(solution)/shard_map/ppermute | solution.py:290
  27.4 0.1 load_k.7.refs_0_
  27.5 0.0 collective-permute-done.1.refs_1_
  27.6 0.7 %collective-permute-start.6 = (bf16[8,128,128]{2,1,0:T(8,128)(2,1)S(1)}, bf16[8,128,128]{2,1,0:T(8,128)(2,1)S(1)}, u32[]{:S(2)}, u32[]{:S(2)}) collective-permute-start(bf16[8,128,128]{2,1,0:T(8,128)(2,1)S(1)} %get-tuple-element.9), channel_id=1, source_target_pairs={{4,8},{8,4},{5,9},{9,5},{6,10},{10,6},{7,11},{11,7},{20,24},{24,20... | collective-permute-start | bytes 786440 | tf_op jit(solution)/shard_map/ppermute | solution.py:231
  28.3 0.0 collective-permute-done.3.refs_2_
  28.3 2.4 %collective-permute-start.7 = (bf16[8,128,128]{2,1,0:T(8,128)(2,1)S(1)}, bf16[8,128,128]{2,1,0:T(8,128)(2,1)S(1)}, u32[]{:S(2)}, u32[]{:S(2)}) collective-permute-start(bf16[8,128,128]{2,1,0:T(8,128)(2,1)S(1)} %get-tuple-element.10), channel_id=1, source_target_pairs={{0,4},{8,12},{4,0},{12,8},{1,5},{9,13},{5,1},{13,9},{2,6},{10,14},... | collective-permute-start | bytes 786440 | tf_op jit(solution)/shard_map/ppermute | solution.py:231
  30.7 1.8 %collective-permute-done.5.refs_3_ = bf16[384,128]{1,0:T(8,128)(2,1)S(1)} collective-permute-done((bf16[384,128]{1,0:T(8,128)(2,1)S(1)}, bf16[384,128]{1,0:T(8,128)(2,1)S(1)}, u32[]{:S(2)}, u32[]{:S(2)}) %collective-permute-start.5) | collective-permute-done | bytes 98336 | tf_op jit(solution)/shard_map/ppermute | solution.py:290
  32.5 0.0 collective-permute-done.10.first_ref
  32.5 0.0 collective-permute-done.11.second_ref
  32.5 0.1 join.3.array_ref
  32.6 0.1 values.1.v_ref
  32.6 0.0 collective-permute-done.6.first_ref
  32.6 0.0 collective-permute-done.7.second_ref
  32.7 0.1 join.2.kt_ref
  32.7 1.6 %attend_chunk.4.refs_0_ = bf16[384,128]{1,0:T(8,128)(2,1)S(1)} custom-call(bf16[4,384,128]{2,1,0:T(8,128)(2,1)S(1)} %stack.1.refs_0_.q_ref, bf16[27,128,128]{2,1,0:T(8,128)(2,1)S(1)} %join.2.kt_ref, bf16[27,128,128]{2,1,0:T(8,128)(2,1)S(1)} %values.1.v_ref, f32[27,12,128]{2,1,0:T(8,128)S(1)} %mask_bias.1.refs_1_.bias_ref), custom_call_target="tpu_custom_call" | custom-call | flops 201326592 | bytes 393216 | tf_op jit(solution)/shard_map/attend_chunk/pallas_call | solution.py:29
  34.4 4.8 %collective-permute-start.14 = (bf16[384,128]{1,0:T(8,128)(2,1)S(1)}, bf16[384,128]{1,0:T(8,128)(2,1)S(1)}, u32[]{:S(2)}, u32[]{:S(2)}) collective-permute-start(bf16[384,128]{1,0:T(8,128)(2,1)S(1)} %attend_chunk.4.refs_0_), channel_id=1, source_target_pairs={{0,3},{1,2},{2,1},{3,0},{4,7},{5,6},{6,5},{7,4},{8,11},{9,10},{10,... | collective-permute-start | bytes 294920 | tf_op jit(solution)/shard_map/ppermute | solution.py:290
  39.2 1.6 %attend_chunk.5.refs_0_ = bf16[384,128]{1,0:T(8,128)(2,1)S(1)} custom-call(bf16[4,384,128]{2,1,0:T(8,128)(2,1)S(1)} %stack.1.refs_0_.q_ref, bf16[27,128,128]{2,1,0:T(8,128)(2,1)S(1)} %join.2.kt_ref, bf16[27,128,128]{2,1,0:T(8,128)(2,1)S(1)} %values.1.v_ref, f32[27,12,128]{2,1,0:T(8,128)S(1)} %mask_bias.1.refs_1_.bias_ref, ...), custom_call_target="tpu_custom_call" | custom-call | flops 201326592 | bytes 393216 | tf_op jit(solution)/shard_map/attend_chunk/pallas_call | solution.py:29
  40.8 0.1 collective-permute-start.13
  40.9 1.6 %attend_chunk.6.refs_0_ = bf16[384,128]{1,0:T(8,128)(2,1)S(1)} custom-call(bf16[4,384,128]{2,1,0:T(8,128)(2,1)S(1)} %stack.1.refs_0_.q_ref, bf16[27,128,128]{2,1,0:T(8,128)(2,1)S(1)} %join.2.kt_ref, bf16[27,128,128]{2,1,0:T(8,128)(2,1)S(1)} %values.1.v_ref, f32[27,12,128]{2,1,0:T(8,128)S(1)} %mask_bias.1.refs_1_.bias_ref, ...), custom_call_target="tpu_custom_call" | custom-call | flops 201326592 | bytes 393216 | tf_op jit(solution)/shard_map/attend_chunk/pallas_call | solution.py:29
  42.5 0.6 %collective-permute-start.12 = (bf16[384,128]{1,0:T(8,128)(2,1)S(1)}, bf16[384,128]{1,0:T(8,128)(2,1)S(1)}, u32[]{:S(2)}, u32[]{:S(2)}) collective-permute-start(bf16[384,128]{1,0:T(8,128)(2,1)S(1)} %attend_chunk.6.refs_0_), channel_id=1, source_target_pairs={{0,1},{1,0},{2,3},{3,2},{4,5},{5,4},{6,7},{7,6},{8,9},{9,8},{10,11... | collective-permute-start | bytes 294920 | tf_op jit(solution)/shard_map/ppermute | solution.py:290
  43.2 1.6 %attend_chunk.7.refs_0_ = bf16[384,128]{1,0:T(8,128)(2,1)S(1)} custom-call(bf16[4,384,128]{2,1,0:T(8,128)(2,1)S(1)} %stack.1.refs_0_.q_ref, bf16[27,128,128]{2,1,0:T(8,128)(2,1)S(1)} %join.2.kt_ref, bf16[27,128,128]{2,1,0:T(8,128)(2,1)S(1)} %values.1.v_ref, f32[27,12,128]{2,1,0:T(8,128)S(1)} %mask_bias.1.refs_1_.bias_ref, ...), custom_call_target="tpu_custom_call" | custom-call | flops 8388608 | bytes 16384 | tf_op jit(solution)/shard_map/attend_chunk/pallas_call | solution.py:29
  44.8 0.0 collective-permute-done.14.array_ref
  44.8 3.1 %collective-permute-done.13.array_ref = bf16[384,128]{1,0:T(8,128)(2,1)S(1)} collective-permute-done((bf16[384,128]{1,0:T(8,128)(2,1)S(1)}, bf16[384,128]{1,0:T(8,128)(2,1)S(1)}, u32[]{:S(2)}, u32[]{:S(2)}) %collective-permute-start.13) | collective-permute-done | bytes 98336 | tf_op jit(solution)/shard_map/ppermute | solution.py:290
  47.9 0.7 %spread.2.refs_1_ = bf16[384,512]{1,0:T(8,128)(2,1)} custom-call(bf16[384,128]{1,0:T(8,128)(2,1)S(1)} %attend_chunk.7.refs_0_, bf16[384,128]{1,0:T(8,128)(2,1)S(1)} %landed.4.refs_0_.refs_1_, bf16[384,128]{1,0:T(8,128)(2,1)S(1)} %landed.3.refs_0_.refs_2_), custom_call_target="tpu_custom_call" | custom-call | tf_op jit(solution)/shard_map/spread/pallas_call | solution.py:272
  48.7 0.6 %collective-permute-done.12.array_ref = bf16[384,128]{1,0:T(8,128)(2,1)S(1)} collective-permute-done((bf16[384,128]{1,0:T(8,128)(2,1)S(1)}, bf16[384,128]{1,0:T(8,128)(2,1)S(1)}, u32[]{:S(2)}, u32[]{:S(2)}) %collective-permute-start.12) | collective-permute-done | bytes 98336 | tf_op jit(solution)/shard_map/ppermute | solution.py:290
  49.3 0.7 %spread.3 = bf16[384,512]{1,0:T(8,128)(2,1)} custom-call(bf16[384,128]{1,0:T(8,128)(2,1)S(1)} %landed.5.refs_0_, bf16[384,512]{1,0:T(8,128)(2,1)} %spread.2.refs_1_), custom_call_target="tpu_custom_call", output_to_operand_aliasing={{}: (1, {})} | custom-call | tf_op jit(solution)/shard_map/spread/pallas_call | solution.py:272
  (17 shorter events, 0.3 us)
Async XLA Ops:
  0.0 7.5 %copy-start = (bf16[384,512]{1,0:T(8,128)(2,1)S(1)}, bf16[384,512]{1,0:T(8,128)(2,1)}, u32[]{:S(2)}) copy-start(bf16[384,512]{1,0:T(8,128)(2,1)} %q_ref.7) | copy-start | bytes 1179652
  0.0 7.5 %copy-start.1 = (bf16[384,512]{1,0:T(8,128)(2,1)S(1)}, bf16[384,512]{1,0:T(8,128)(2,1)}, u32[]{:S(2)}) copy-start(bf16[384,512]{1,0:T(8,128)(2,1)} %array_ref.5) | copy-start | bytes 1179652
  1.2 5.7 %copy-start.3 = (s32[12]{0:T(128)S(1)}, s32[12]{0:T(128)}, u32[]{:S(2)}) copy-start(s32[12]{0:T(128)} %param.9) | copy-start | bytes 148
  1.2 6.4 %collective-permute-start = (bf16[3,128,128]{2,1,0:T(8,128)(2,1)S(1)}, bf16[3,128,128]{2,1,0:T(8,128)(2,1)S(1)}, u32[]{:S(2)}, u32[]{:S(2)}) collective-permute-start(bf16[3,128,128]{2,1,0:T(8,128)(2,1)S(1)} %bitcast.8), channel_id=1, source_target_pairs={{0,1},{1,0},{2,3},{3,2},{4,5},{5,4},{6,7},{7,6},{8,9},{9,8},{10,11... | collective-permute-start | bytes 294920 | tf_op jit(solution)/shard_map/ppermute | solution.py:290
  4.3 2.7 %copy-start.2 = (s32[12,16]{1,0:T(8,128)S(1)}, s32[12,16]{1,0:T(8,128)}, u32[]{:S(2)}) copy-start(s32[12,16]{1,0:T(8,128)} %lists_ref.1) | copy-start | bytes 2308
  4.3 8.8 %collective-permute-start.9 = (bf16[3,128,128]{2,1,0:T(8,128)(2,1)S(1)}, bf16[3,128,128]{2,1,0:T(8,128)(2,1)S(1)}, u32[]{:S(2)}, u32[]{:S(2)}) collective-permute-start(bf16[3,128,128]{2,1,0:T(8,128)(2,1)S(1)} %bitcast.7), channel_id=1, source_target_pairs={{0,3},{1,2},{2,1},{3,0},{4,7},{5,6},{6,5},{7,4},{8,11},{9,10},{10,... | collective-permute-start | bytes 294920 | tf_op jit(solution)/shard_map/ppermute | solution.py:290
  6.7 9.5 %collective-permute-start.8 = (bf16[3,128,128]{2,1,0:T(8,128)(2,1)S(1)}, bf16[3,128,128]{2,1,0:T(8,128)(2,1)S(1)}, u32[]{:S(2)}, u32[]{:S(2)}) collective-permute-start(bf16[3,128,128]{2,1,0:T(8,128)(2,1)S(1)} %bitcast.6), channel_id=1, source_target_pairs={{0,2},{1,3},{2,0},{3,1},{4,6},{5,7},{6,4},{7,5},{8,10},{9,11},{10,... | collective-permute-start | bytes 294920 | tf_op jit(solution)/shard_map/ppermute | solution.py:290
  7.7 19.8 %collective-permute-start.1 = (bf16[6,128,128]{2,1,0:T(8,128)(2,1)S(1)}, bf16[6,128,128]{2,1,0:T(8,128)(2,1)S(1)}, u32[]{:S(2)}, u32[]{:S(2)}) collective-permute-start(bf16[6,128,128]{2,1,0:T(8,128)(2,1)S(1)} %load_k.4), channel_id=1, source_target_pairs={{0,1},{1,0},{2,3},{3,2},{4,5},{5,4},{6,7},{7,6},{8,9},{9,8},{10,11... | collective-permute-start | bytes 589832 | tf_op jit(solution)/shard_map/ppermute | solution.py:290
  9.6 12.9 %collective-permute-start.2 = (bf16[3,128,128]{2,1,0:T(8,128)(2,1)S(1)}, bf16[3,128,128]{2,1,0:T(8,128)(2,1)S(1)}, u32[]{:S(2)}, u32[]{:S(2)}) collective-permute-start(bf16[3,128,128]{2,1,0:T(8,128)(2,1)S(1)} %load_k.5), channel_id=1, source_target_pairs={{0,2},{1,3},{2,0},{3,1},{4,6},{5,7},{6,4},{7,5},{8,10},{9,11},{10,... | collective-permute-start | bytes 294920 | tf_op jit(solution)/shard_map/ppermute | solution.py:290
  12.9 9.7 %collective-permute-start.4 = (bf16[3,128,128]{2,1,0:T(8,128)(2,1)S(1)}, bf16[3,128,128]{2,1,0:T(8,128)(2,1)S(1)}, u32[]{:S(2)}, u32[]{:S(2)}) collective-permute-start(bf16[3,128,128]{2,1,0:T(8,128)(2,1)S(1)} %load_k.6), channel_id=1, source_target_pairs={{0,3},{1,2},{2,1},{3,0},{4,7},{5,6},{6,5},{7,4},{8,11},{9,10},{10,... | collective-permute-start | bytes 294920 | tf_op jit(solution)/shard_map/ppermute | solution.py:290
  16.4 16.1 %collective-permute-start.10 = (bf16[8,128,128]{2,1,0:T(8,128)(2,1)S(1)}, bf16[8,128,128]{2,1,0:T(8,128)(2,1)S(1)}, u32[]{:S(2)}, u32[]{:S(2)}) collective-permute-start(bf16[8,128,128]{2,1,0:T(8,128)(2,1)S(1)} %get-tuple-element.11), channel_id=1, source_target_pairs={{4,8},{8,4},{5,9},{9,5},{6,10},{10,6},{7,11},{11,7},{20,24},{24,20... | collective-permute-start | bytes 786440 | tf_op jit(solution)/shard_map/ppermute | solution.py:231
  17.0 15.5 %collective-permute-start.11 = (bf16[8,128,128]{2,1,0:T(8,128)(2,1)S(1)}, bf16[8,128,128]{2,1,0:T(8,128)(2,1)S(1)}, u32[]{:S(2)}, u32[]{:S(2)}) collective-permute-start(bf16[8,128,128]{2,1,0:T(8,128)(2,1)S(1)} %get-tuple-element.12), channel_id=1, source_target_pairs={{0,4},{8,12},{4,0},{12,8},{1,5},{9,13},{5,1},{13,9},{2,6},{10,14},... | collective-permute-start | bytes 786440 | tf_op jit(solution)/shard_map/ppermute | solution.py:231
  22.5 5.7 %collective-permute-start.3 = (bf16[384,128]{1,0:T(8,128)(2,1)S(1)}, bf16[384,128]{1,0:T(8,128)(2,1)S(1)}, u32[]{:S(2)}, u32[]{:S(2)}) collective-permute-start(bf16[384,128]{1,0:T(8,128)(2,1)S(1)} %load_q.4), channel_id=1, source_target_pairs={{0,2},{1,3},{2,0},{3,1},{4,6},{5,7},{6,4},{7,5},{8,10},{9,11},{10,... | collective-permute-start | bytes 294920 | tf_op jit(solution)/shard_map/ppermute | solution.py:290
  22.7 9.8 %collective-permute-start.5 = (bf16[384,128]{1,0:T(8,128)(2,1)S(1)}, bf16[384,128]{1,0:T(8,128)(2,1)S(1)}, u32[]{:S(2)}, u32[]{:S(2)}) collective-permute-start(bf16[384,128]{1,0:T(8,128)(2,1)S(1)} %load_q.5), channel_id=1, source_target_pairs={{0,3},{1,2},{2,1},{3,0},{4,7},{5,6},{6,5},{7,4},{8,11},{9,10},{10,... | collective-permute-start | bytes 294920 | tf_op jit(solution)/shard_map/ppermute | solution.py:290
  27.6 5.0 %collective-permute-start.6 = (bf16[8,128,128]{2,1,0:T(8,128)(2,1)S(1)}, bf16[8,128,128]{2,1,0:T(8,128)(2,1)S(1)}, u32[]{:S(2)}, u32[]{:S(2)}) collective-permute-start(bf16[8,128,128]{2,1,0:T(8,128)(2,1)S(1)} %get-tuple-element.9), channel_id=1, source_target_pairs={{4,8},{8,4},{5,9},{9,5},{6,10},{10,6},{7,11},{11,7},{20,24},{24,20... | collective-permute-start | bytes 786440 | tf_op jit(solution)/shard_map/ppermute | solution.py:231
  28.3 4.4 %collective-permute-start.7 = (bf16[8,128,128]{2,1,0:T(8,128)(2,1)S(1)}, bf16[8,128,128]{2,1,0:T(8,128)(2,1)S(1)}, u32[]{:S(2)}, u32[]{:S(2)}) collective-permute-start(bf16[8,128,128]{2,1,0:T(8,128)(2,1)S(1)} %get-tuple-element.10), channel_id=1, source_target_pairs={{0,4},{8,12},{4,0},{12,8},{1,5},{9,13},{5,1},{13,9},{2,6},{10,14},... | collective-permute-start | bytes 786440 | tf_op jit(solution)/shard_map/ppermute | solution.py:231
  34.4 10.4 %collective-permute-start.14 = (bf16[384,128]{1,0:T(8,128)(2,1)S(1)}, bf16[384,128]{1,0:T(8,128)(2,1)S(1)}, u32[]{:S(2)}, u32[]{:S(2)}) collective-permute-start(bf16[384,128]{1,0:T(8,128)(2,1)S(1)} %attend_chunk.4.refs_0_), channel_id=1, source_target_pairs={{0,3},{1,2},{2,1},{3,0},{4,7},{5,6},{6,5},{7,4},{8,11},{9,10},{10,... | collective-permute-start | bytes 294920 | tf_op jit(solution)/shard_map/ppermute | solution.py:290
  40.8 7.1 %collective-permute-start.13 = (bf16[384,128]{1,0:T(8,128)(2,1)S(1)}, bf16[384,128]{1,0:T(8,128)(2,1)S(1)}, u32[]{:S(2)}, u32[]{:S(2)}) collective-permute-start(bf16[384,128]{1,0:T(8,128)(2,1)S(1)} %attend_chunk.5.refs_0_), channel_id=1, source_target_pairs={{0,2},{1,3},{2,0},{3,1},{4,6},{5,7},{6,4},{7,5},{8,10},{9,11},{10,... | collective-permute-start | bytes 294920 | tf_op jit(solution)/shard_map/ppermute | solution.py:290
  42.5 6.7 %collective-permute-start.12 = (bf16[384,128]{1,0:T(8,128)(2,1)S(1)}, bf16[384,128]{1,0:T(8,128)(2,1)S(1)}, u32[]{:S(2)}, u32[]{:S(2)}) collective-permute-start(bf16[384,128]{1,0:T(8,128)(2,1)S(1)} %attend_chunk.6.refs_0_), channel_id=1, source_target_pairs={{0,1},{1,0},{2,3},{3,2},{4,5},{5,4},{6,7},{7,6},{8,9},{9,8},{10,11... | collective-permute-start | bytes 294920 | tf_op jit(solution)/shard_map/ppermute | solution.py:290

commit v19 on v18

--- a/solution.py
+++ b/solution.py
@@ -317,6 +317,8 @@
         pass_kernel, "values", (all_values, local_q), [VMEM] * 2, all_values.shape, cost=cost(16384)
     )
     outs = [None] * heads
+    half = heads // 2
+    order = [half, *(pair for pair in order if pair != half)]
     after = ()
     for pair in [*order, 0]:
         operands = (local_q, all_keys, all_values, bias, *after)

time: 50.1 us -> 49.5 us (0.988)
  waiting for transfers between devices: 11.3 us -> 10.7 us
    ppermute x11, waiting for transfers between devices: 11.3 us -> 10.7 us  [exchange(): return lax.ppermute(array, 'head', [(i, i ^ pair) for i in range(heads)])]
where the time goes in v19:
time: 49.5 us; the launch traced here: 49.3 us
  starting transfers between devices  27.8 us (56%)
  waiting for transfers between devices  10.7 us (22%)
  Pallas kernels  9.29 us (19%)
  local copies, waits for them, and re-layouts  1.26 us (3%)
    ppermute x11, starting transfers between devices, exchange(): return lax.ppermute(array, 'head', [(i, i ^ pair) for i in range(heads)])  21.2 us
    ppermute x11, waiting for transfers between devices, exchange(): return lax.ppermute(array, 'head', [(i, i ^ pair) for i in range(heads)])  10.7 us
    pallas_call x23, Pallas kernels, call(): pl.pallas_call(kernel, out_shape=out_shape, in_specs=in_specs, out_specs=...  7.88 us
    ppermute x4, starting transfers between devices, exchange(): lax.ppermute(array, 'ctx', [(i, i + 1) for i in lower] + [(i + 1, i) for...  6.63 us
    pallas_call x2, Pallas kernels, spread(): pl.pallas_call(functools.partial(spread_kernel, pairs), out_shape=jax.Sha...  1.4 us
    dynamic_slice x1, local copies, waits for them, and re-layouts, in_pairs(): part = lax.dynamic_slice_in_dim(values, column, HDIM, axis=1).reshape(tiles)  1.14 us
  transfers between devices with their start and end apart: 15, of which 5 were waited for; matrix products, arithmetic and copies ran while one was open for 0% of the time, Pallas kernels for 14%

profile of v19, /device:TPU:0, one launch (start us, length us, event | category | flops | bytes accessed | tf_op | source)
XLA Modules:
  0.0 49.3 jit_solution(7050582621361115785)
XLA Ops:
  0.0 1.1 %constant_dynamic-slice_fusion = (bf16[384,128]{1,0:T(8,128)(2,1)S(1)}, bf16[384,128]{1,0:T(8,128)(2,1)S(1)}, bf16[384,128]{1,0:T(8,128)(2,1)S(1)}, bf16[384,128]{1,0:T(8,128)(2,1)S(1)}) fusion(bf16[384,512]{1,0:T(8,128)(2,1)} %param.7, s32[]{:T(128)S(6)} %select_n.15, s32[]{:T(128)S(6)} %select_n.13, s32[]{:T(128)S(6)} %select_n.12, s32[]{:T(128)S(6)} %select_n.14), kind=kLoop, calls=%fused_computation | loop fusion | bytes 786448 | tf_op jit(solution)/shard_map/dynamic_slice | solution.py:298
  1.2 0.0 copy-start.3
  1.2 3.1 %collective-permute-start = (bf16[3,128,128]{2,1,0:T(8,128)(2,1)S(1)}, bf16[3,128,128]{2,1,0:T(8,128)(2,1)S(1)}, u32[]{:S(2)}, u32[]{:S(2)}) collective-permute-start(bf16[3,128,128]{2,1,0:T(8,128)(2,1)S(1)} %bitcast.8), channel_id=1, source_target_pairs={{0,1},{1,0},{2,3},{3,2},{4,5},{5,4},{6,7},{7,6},{8,9},{9,8},{10,11... | collective-permute-start | bytes 294920 | tf_op jit(solution)/shard_map/ppermute | solution.py:290
  4.3 2.5 %collective-permute-start.9 = (bf16[3,128,128]{2,1,0:T(8,128)(2,1)S(1)}, bf16[3,128,128]{2,1,0:T(8,128)(2,1)S(1)}, u32[]{:S(2)}, u32[]{:S(2)}) collective-permute-start(bf16[3,128,128]{2,1,0:T(8,128)(2,1)S(1)} %bitcast.7), channel_id=1, source_target_pairs={{0,3},{1,2},{2,1},{3,0},{4,7},{5,6},{6,5},{7,4},{8,11},{9,10},{10,... | collective-permute-start | bytes 294920 | tf_op jit(solution)/shard_map/ppermute | solution.py:290
  6.7 0.1 collective-permute-start.8
  6.8 0.0 copy-done.3
  6.9 0.1 copy.7.counts_ref
  6.9 0.6 %mask_bias.1.refs_1_.bias_ref = f32[27,12,128]{2,1,0:T(8,128)S(1)} custom-call(s32[12,16]{1,0:T(8,128)S(1)} %copy-done.2, s32[12,1]{1,0:T(8,128)S(1)} %copy.7.counts_ref), custom_call_target="tpu_custom_call" | custom-call | tf_op jit(solution)/shard_map/mask_bias/pallas_call | solution.py:29
  7.5 0.0 collective-permute-done.refs_0_.refs_1_
  7.6 0.1 load_k.4
  7.7 1.9 %collective-permute-start.1 = (bf16[6,128,128]{2,1,0:T(8,128)(2,1)S(1)}, bf16[6,128,128]{2,1,0:T(8,128)(2,1)S(1)}, u32[]{:S(2)}, u32[]{:S(2)}) collective-permute-start(bf16[6,128,128]{2,1,0:T(8,128)(2,1)S(1)} %load_k.4), channel_id=1, source_target_pairs={{0,1},{1,0},{2,3},{3,2},{4,5},{5,4},{6,7},{7,6},{8,9},{9,8},{10,11... | collective-permute-start | bytes 589832 | tf_op jit(solution)/shard_map/ppermute | solution.py:290
  9.5 0.1 load_k.5
  9.6 3.2 %collective-permute-start.2 = (bf16[3,128,128]{2,1,0:T(8,128)(2,1)S(1)}, bf16[3,128,128]{2,1,0:T(8,128)(2,1)S(1)}, u32[]{:S(2)}, u32[]{:S(2)}) collective-permute-start(bf16[3,128,128]{2,1,0:T(8,128)(2,1)S(1)} %load_k.5), channel_id=1, source_target_pairs={{0,2},{1,3},{2,0},{3,1},{4,6},{5,7},{6,4},{7,5},{8,10},{9,11},{10,... | collective-permute-start | bytes 294920 | tf_op jit(solution)/shard_map/ppermute | solution.py:290
  12.8 0.1 load_k.6
  12.9 0.1 collective-permute-start.4
  13.0 0.0 collective-permute-done.9.refs_3_
  13.0 3.2 %collective-permute-done.8.refs_2_ = bf16[3,128,128]{2,1,0:T(8,128)(2,1)S(1)} collective-permute-done((bf16[3,128,128]{2,1,0:T(8,128)(2,1)S(1)}, bf16[3,128,128]{2,1,0:T(8,128)(2,1)S(1)}, u32[]{:S(2)}, u32[]{:S(2)}) %collective-permute-start.8) | collective-permute-done | bytes 98336 | tf_op jit(solution)/shard_map/ppermute | solution.py:290
  16.4 0.7 %collective-permute-start.10 = (bf16[8,128,128]{2,1,0:T(8,128)(2,1)S(1)}, bf16[8,128,128]{2,1,0:T(8,128)(2,1)S(1)}, u32[]{:S(2)}, u32[]{:S(2)}) collective-permute-start(bf16[8,128,128]{2,1,0:T(8,128)(2,1)S(1)} %get-tuple-element.11), channel_id=1, source_target_pairs={{4,8},{8,4},{5,9},{9,5},{6,10},{10,6},{7,11},{11,7},{20,24},{24,20... | collective-permute-start | bytes 786440 | tf_op jit(solution)/shard_map/ppermute | solution.py:231
  17.0 2.9 %collective-permute-start.11 = (bf16[8,128,128]{2,1,0:T(8,128)(2,1)S(1)}, bf16[8,128,128]{2,1,0:T(8,128)(2,1)S(1)}, u32[]{:S(2)}, u32[]{:S(2)}) collective-permute-start(bf16[8,128,128]{2,1,0:T(8,128)(2,1)S(1)} %get-tuple-element.12), channel_id=1, source_target_pairs={{0,4},{8,12},{4,0},{12,8},{1,5},{9,13},{5,1},{13,9},{2,6},{10,14},... | collective-permute-start | bytes 786440 | tf_op jit(solution)/shard_map/ppermute | solution.py:231
  19.9 2.6 %collective-permute-done.2.refs_0_.refs_2_ = bf16[3,128,128]{2,1,0:T(8,128)(2,1)S(1)} collective-permute-done((bf16[3,128,128]{2,1,0:T(8,128)(2,1)S(1)}, bf16[3,128,128]{2,1,0:T(8,128)(2,1)S(1)}, u32[]{:S(2)}, u32[]{:S(2)}) %collective-permute-start.2) | collective-permute-done | bytes 98336 | tf_op jit(solution)/shard_map/ppermute | solution.py:290
  22.5 0.1 collective-permute-start.3
  22.6 0.0 collective-permute-done.4.refs_0_.refs_3_
  22.7 4.7 %collective-permute-start.5 = (bf16[384,128]{1,0:T(8,128)(2,1)S(1)}, bf16[384,128]{1,0:T(8,128)(2,1)S(1)}, u32[]{:S(2)}, u32[]{:S(2)}) collective-permute-start(bf16[384,128]{1,0:T(8,128)(2,1)S(1)} %load_q.5), channel_id=1, source_target_pairs={{0,3},{1,2},{2,1},{3,0},{4,7},{5,6},{6,5},{7,4},{8,11},{9,10},{10,... | collective-permute-start | bytes 294920 | tf_op jit(solution)/shard_map/ppermute | solution.py:290
  27.4 0.1 load_k.7.refs_0_
  27.5 0.0 collective-permute-done.1.refs_1_
  27.6 0.7 %collective-permute-start.6 = (bf16[8,128,128]{2,1,0:T(8,128)(2,1)S(1)}, bf16[8,128,128]{2,1,0:T(8,128)(2,1)S(1)}, u32[]{:S(2)}, u32[]{:S(2)}) collective-permute-start(bf16[8,128,128]{2,1,0:T(8,128)(2,1)S(1)} %get-tuple-element.9), channel_id=1, source_target_pairs={{4,8},{8,4},{5,9},{9,5},{6,10},{10,6},{7,11},{11,7},{20,24},{24,20... | collective-permute-start | bytes 786440 | tf_op jit(solution)/shard_map/ppermute | solution.py:231
  28.3 0.0 collective-permute-done.3.refs_2_
  28.3 2.4 %collective-permute-start.7 = (bf16[8,128,128]{2,1,0:T(8,128)(2,1)S(1)}, bf16[8,128,128]{2,1,0:T(8,128)(2,1)S(1)}, u32[]{:S(2)}, u32[]{:S(2)}) collective-permute-start(bf16[8,128,128]{2,1,0:T(8,128)(2,1)S(1)} %get-tuple-element.10), channel_id=1, source_target_pairs={{0,4},{8,12},{4,0},{12,8},{1,5},{9,13},{5,1},{13,9},{2,6},{10,14},... | collective-permute-start | bytes 786440 | tf_op jit(solution)/shard_map/ppermute | solution.py:231
  30.7 1.8 %collective-permute-done.5.refs_3_ = bf16[384,128]{1,0:T(8,128)(2,1)S(1)} collective-permute-done((bf16[384,128]{1,0:T(8,128)(2,1)S(1)}, bf16[384,128]{1,0:T(8,128)(2,1)S(1)}, u32[]{:S(2)}, u32[]{:S(2)}) %collective-permute-start.5) | collective-permute-done | bytes 98336 | tf_op jit(solution)/shard_map/ppermute | solution.py:290
  32.5 0.0 collective-permute-done.10.first_ref
  32.5 0.0 collective-permute-done.11.second_ref
  32.5 0.1 join.3.array_ref
  32.6 0.1 values.1.v_ref
  32.6 0.0 collective-permute-done.6.first_ref
  32.6 0.0 collective-permute-done.7.second_ref
  32.7 0.1 join.2.kt_ref
  32.7 1.6 %attend_chunk.4.refs_0_ = bf16[384,128]{1,0:T(8,128)(2,1)S(1)} custom-call(bf16[4,384,128]{2,1,0:T(8,128)(2,1)S(1)} %stack.1.refs_0_.q_ref, bf16[27,128,128]{2,1,0:T(8,128)(2,1)S(1)} %join.2.kt_ref, bf16[27,128,128]{2,1,0:T(8,128)(2,1)S(1)} %values.1.v_ref, f32[27,12,128]{2,1,0:T(8,128)S(1)} %mask_bias.1.refs_1_.bias_ref), custom_call_target="tpu_custom_call" | custom-call | flops 201326592 | bytes 393216 | tf_op jit(solution)/shard_map/attend_chunk/pallas_call | solution.py:29
  34.4 3.8 %collective-permute-start.14 = (bf16[384,128]{1,0:T(8,128)(2,1)S(1)}, bf16[384,128]{1,0:T(8,128)(2,1)S(1)}, u32[]{:S(2)}, u32[]{:S(2)}) collective-permute-start(bf16[384,128]{1,0:T(8,128)(2,1)S(1)} %attend_chunk.4.refs_0_), channel_id=1, source_target_pairs={{0,2},{1,3},{2,0},{3,1},{4,6},{5,7},{6,4},{7,5},{8,10},{9,11},{10,... | collective-permute-start | bytes 294920 | tf_op jit(solution)/shard_map/ppermute | solution.py:290
  38.2 1.6 %attend_chunk.5.refs_0_ = bf16[384,128]{1,0:T(8,128)(2,1)S(1)} custom-call(bf16[4,384,128]{2,1,0:T(8,128)(2,1)S(1)} %stack.1.refs_0_.q_ref, bf16[27,128,128]{2,1,0:T(8,128)(2,1)S(1)} %join.2.kt_ref, bf16[27,128,128]{2,1,0:T(8,128)(2,1)S(1)} %values.1.v_ref, f32[27,12,128]{2,1,0:T(8,128)S(1)} %mask_bias.1.refs_1_.bias_ref, ...), custom_call_target="tpu_custom_call" | custom-call | flops 201326592 | bytes 393216 | tf_op jit(solution)/shard_map/attend_chunk/pallas_call | solution.py:29
  39.8 1.3 %collective-permute-start.13 = (bf16[384,128]{1,0:T(8,128)(2,1)S(1)}, bf16[384,128]{1,0:T(8,128)(2,1)S(1)}, u32[]{:S(2)}, u32[]{:S(2)}) collective-permute-start(bf16[384,128]{1,0:T(8,128)(2,1)S(1)} %attend_chunk.5.refs_0_), channel_id=1, source_target_pairs={{0,3},{1,2},{2,1},{3,0},{4,7},{5,6},{6,5},{7,4},{8,11},{9,10},{10,... | collective-permute-start | bytes 294920 | tf_op jit(solution)/shard_map/ppermute | solution.py:290
  41.1 1.6 %attend_chunk.6.refs_0_ = bf16[384,128]{1,0:T(8,128)(2,1)S(1)} custom-call(bf16[4,384,128]{2,1,0:T(8,128)(2,1)S(1)} %stack.1.refs_0_.q_ref, bf16[27,128,128]{2,1,0:T(8,128)(2,1)S(1)} %join.2.kt_ref, bf16[27,128,128]{2,1,0:T(8,128)(2,1)S(1)} %values.1.v_ref, f32[27,12,128]{2,1,0:T(8,128)S(1)} %mask_bias.1.refs_1_.bias_ref, ...), custom_call_target="tpu_custom_call" | custom-call | flops 201326592 | bytes 393216 | tf_op jit(solution)/shard_map/attend_chunk/pallas_call | solution.py:29
  42.7 0.5 collective-permute-start.12
  43.2 1.6 %attend_chunk.7.refs_0_ = bf16[384,128]{1,0:T(8,128)(2,1)S(1)} custom-call(bf16[4,384,128]{2,1,0:T(8,128)(2,1)S(1)} %stack.1.refs_0_.q_ref, bf16[27,128,128]{2,1,0:T(8,128)(2,1)S(1)} %join.2.kt_ref, bf16[27,128,128]{2,1,0:T(8,128)(2,1)S(1)} %values.1.v_ref, f32[27,12,128]{2,1,0:T(8,128)S(1)} %mask_bias.1.refs_1_.bias_ref, ...), custom_call_target="tpu_custom_call" | custom-call | flops 8388608 | bytes 16384 | tf_op jit(solution)/shard_map/attend_chunk/pallas_call | solution.py:29
  44.8 0.0 collective-permute-done.14.array_ref
  44.8 1.9 %collective-permute-done.13.array_ref = bf16[384,128]{1,0:T(8,128)(2,1)S(1)} collective-permute-done((bf16[384,128]{1,0:T(8,128)(2,1)S(1)}, bf16[384,128]{1,0:T(8,128)(2,1)S(1)}, u32[]{:S(2)}, u32[]{:S(2)}) %collective-permute-start.13) | collective-permute-done | bytes 98336 | tf_op jit(solution)/shard_map/ppermute | solution.py:290
  46.8 0.7 %spread.2.refs_1_ = bf16[384,512]{1,0:T(8,128)(2,1)} custom-call(bf16[384,128]{1,0:T(8,128)(2,1)S(1)} %attend_chunk.7.refs_0_, bf16[384,128]{1,0:T(8,128)(2,1)S(1)} %landed.3.refs_0_.refs_1_, bf16[384,128]{1,0:T(8,128)(2,1)S(1)} %landed.4.refs_0_.refs_2_), custom_call_target="tpu_custom_call" | custom-call | tf_op jit(solution)/shard_map/spread/pallas_call | solution.py:272
  47.5 1.1 %collective-permute-done.12.array_ref = bf16[384,128]{1,0:T(8,128)(2,1)S(1)} collective-permute-done((bf16[384,128]{1,0:T(8,128)(2,1)S(1)}, bf16[384,128]{1,0:T(8,128)(2,1)S(1)}, u32[]{:S(2)}, u32[]{:S(2)}) %collective-permute-start.12) | collective-permute-done | bytes 98336 | tf_op jit(solution)/shard_map/ppermute | solution.py:290
  48.7 0.7 %spread.3 = bf16[384,512]{1,0:T(8,128)(2,1)} custom-call(bf16[384,128]{1,0:T(8,128)(2,1)S(1)} %landed.5.refs_0_, bf16[384,512]{1,0:T(8,128)(2,1)} %spread.2.refs_1_), custom_call_target="tpu_custom_call", output_to_operand_aliasing={{}: (1, {})} | custom-call | tf_op jit(solution)/shard_map/spread/pallas_call | solution.py:272
  (17 shorter events, 0.3 us)
Async XLA Ops:
  0.0 7.5 %copy-start = (bf16[384,512]{1,0:T(8,128)(2,1)S(1)}, bf16[384,512]{1,0:T(8,128)(2,1)}, u32[]{:S(2)}) copy-start(bf16[384,512]{1,0:T(8,128)(2,1)} %q_ref.7) | copy-start | bytes 1179652
  0.0 7.5 %copy-start.1 = (bf16[384,512]{1,0:T(8,128)(2,1)S(1)}, bf16[384,512]{1,0:T(8,128)(2,1)}, u32[]{:S(2)}) copy-start(bf16[384,512]{1,0:T(8,128)(2,1)} %array_ref.5) | copy-start | bytes 1179652
  1.2 5.7 %copy-start.3 = (s32[12]{0:T(128)S(1)}, s32[12]{0:T(128)}, u32[]{:S(2)}) copy-start(s32[12]{0:T(128)} %param.9) | copy-start | bytes 148
  1.2 6.4 %collective-permute-start = (bf16[3,128,128]{2,1,0:T(8,128)(2,1)S(1)}, bf16[3,128,128]{2,1,0:T(8,128)(2,1)S(1)}, u32[]{:S(2)}, u32[]{:S(2)}) collective-permute-start(bf16[3,128,128]{2,1,0:T(8,128)(2,1)S(1)} %bitcast.8), channel_id=1, source_target_pairs={{0,1},{1,0},{2,3},{3,2},{4,5},{5,4},{6,7},{7,6},{8,9},{9,8},{10,11... | collective-permute-start | bytes 294920 | tf_op jit(solution)/shard_map/ppermute | solution.py:290
  4.3 2.7 %copy-start.2 = (s32[12,16]{1,0:T(8,128)S(1)}, s32[12,16]{1,0:T(8,128)}, u32[]{:S(2)}) copy-start(s32[12,16]{1,0:T(8,128)} %lists_ref.1) | copy-start | bytes 2308
  4.3 8.8 %collective-permute-start.9 = (bf16[3,128,128]{2,1,0:T(8,128)(2,1)S(1)}, bf16[3,128,128]{2,1,0:T(8,128)(2,1)S(1)}, u32[]{:S(2)}, u32[]{:S(2)}) collective-permute-start(bf16[3,128,128]{2,1,0:T(8,128)(2,1)S(1)} %bitcast.7), channel_id=1, source_target_pairs={{0,3},{1,2},{2,1},{3,0},{4,7},{5,6},{6,5},{7,4},{8,11},{9,10},{10,... | collective-permute-start | bytes 294920 | tf_op jit(solution)/shard_map/ppermute | solution.py:290
  6.7 9.5 %collective-permute-start.8 = (bf16[3,128,128]{2,1,0:T(8,128)(2,1)S(1)}, bf16[3,128,128]{2,1,0:T(8,128)(2,1)S(1)}, u32[]{:S(2)}, u32[]{:S(2)}) collective-permute-start(bf16[3,128,128]{2,1,0:T(8,128)(2,1)S(1)} %bitcast.6), channel_id=1, source_target_pairs={{0,2},{1,3},{2,0},{3,1},{4,6},{5,7},{6,4},{7,5},{8,10},{9,11},{10,... | collective-permute-start | bytes 294920 | tf_op jit(solution)/shard_map/ppermute | solution.py:290
  7.7 19.8 %collective-permute-start.1 = (bf16[6,128,128]{2,1,0:T(8,128)(2,1)S(1)}, bf16[6,128,128]{2,1,0:T(8,128)(2,1)S(1)}, u32[]{:S(2)}, u32[]{:S(2)}) collective-permute-start(bf16[6,128,128]{2,1,0:T(8,128)(2,1)S(1)} %load_k.4), channel_id=1, source_target_pairs={{0,1},{1,0},{2,3},{3,2},{4,5},{5,4},{6,7},{7,6},{8,9},{9,8},{10,11... | collective-permute-start | bytes 589832 | tf_op jit(solution)/shard_map/ppermute | solution.py:290
  9.6 12.9 %collective-permute-start.2 = (bf16[3,128,128]{2,1,0:T(8,128)(2,1)S(1)}, bf16[3,128,128]{2,1,0:T(8,128)(2,1)S(1)}, u32[]{:S(2)}, u32[]{:S(2)}) collective-permute-start(bf16[3,128,128]{2,1,0:T(8,128)(2,1)S(1)} %load_k.5), channel_id=1, source_target_pairs={{0,2},{1,3},{2,0},{3,1},{4,6},{5,7},{6,4},{7,5},{8,10},{9,11},{10,... | collective-permute-start | bytes 294920 | tf_op jit(solution)/shard_map/ppermute | solution.py:290
  12.9 9.7 %collective-permute-start.4 = (bf16[3,128,128]{2,1,0:T(8,128)(2,1)S(1)}, bf16[3,128,128]{2,1,0:T(8,128)(2,1)S(1)}, u32[]{:S(2)}, u32[]{:S(2)}) collective-permute-start(bf16[3,128,128]{2,1,0:T(8,128)(2,1)S(1)} %load_k.6), channel_id=1, source_target_pairs={{0,3},{1,2},{2,1},{3,0},{4,7},{5,6},{6,5},{7,4},{8,11},{9,10},{10,... | collective-permute-start | bytes 294920 | tf_op jit(solution)/shard_map/ppermute | solution.py:290
  16.4 16.1 %collective-permute-start.10 = (bf16[8,128,128]{2,1,0:T(8,128)(2,1)S(1)}, bf16[8,128,128]{2,1,0:T(8,128)(2,1)S(1)}, u32[]{:S(2)}, u32[]{:S(2)}) collective-permute-start(bf16[8,128,128]{2,1,0:T(8,128)(2,1)S(1)} %get-tuple-element.11), channel_id=1, source_target_pairs={{4,8},{8,4},{5,9},{9,5},{6,10},{10,6},{7,11},{11,7},{20,24},{24,20... | collective-permute-start | bytes 786440 | tf_op jit(solution)/shard_map/ppermute | solution.py:231
  17.0 15.5 %collective-permute-start.11 = (bf16[8,128,128]{2,1,0:T(8,128)(2,1)S(1)}, bf16[8,128,128]{2,1,0:T(8,128)(2,1)S(1)}, u32[]{:S(2)}, u32[]{:S(2)}) collective-permute-start(bf16[8,128,128]{2,1,0:T(8,128)(2,1)S(1)} %get-tuple-element.12), channel_id=1, source_target_pairs={{0,4},{8,12},{4,0},{12,8},{1,5},{9,13},{5,1},{13,9},{2,6},{10,14},... | collective-permute-start | bytes 786440 | tf_op jit(solution)/shard_map/ppermute | solution.py:231
  22.5 5.7 %collective-permute-start.3 = (bf16[384,128]{1,0:T(8,128)(2,1)S(1)}, bf16[384,128]{1,0:T(8,128)(2,1)S(1)}, u32[]{:S(2)}, u32[]{:S(2)}) collective-permute-start(bf16[384,128]{1,0:T(8,128)(2,1)S(1)} %load_q.4), channel_id=1, source_target_pairs={{0,2},{1,3},{2,0},{3,1},{4,6},{5,7},{6,4},{7,5},{8,10},{9,11},{10,... | collective-permute-start | bytes 294920 | tf_op jit(solution)/shard_map/ppermute | solution.py:290
  22.7 9.8 %collective-permute-start.5 = (bf16[384,128]{1,0:T(8,128)(2,1)S(1)}, bf16[384,128]{1,0:T(8,128)(2,1)S(1)}, u32[]{:S(2)}, u32[]{:S(2)}) collective-permute-start(bf16[384,128]{1,0:T(8,128)(2,1)S(1)} %load_q.5), channel_id=1, source_target_pairs={{0,3},{1,2},{2,1},{3,0},{4,7},{5,6},{6,5},{7,4},{8,11},{9,10},{10,... | collective-permute-start | bytes 294920 | tf_op jit(solution)/shard_map/ppermute | solution.py:290
  27.6 5.0 %collective-permute-start.6 = (bf16[8,128,128]{2,1,0:T(8,128)(2,1)S(1)}, bf16[8,128,128]{2,1,0:T(8,128)(2,1)S(1)}, u32[]{:S(2)}, u32[]{:S(2)}) collective-permute-start(bf16[8,128,128]{2,1,0:T(8,128)(2,1)S(1)} %get-tuple-element.9), channel_id=1, source_target_pairs={{4,8},{8,4},{5,9},{9,5},{6,10},{10,6},{7,11},{11,7},{20,24},{24,20... | collective-permute-start | bytes 786440 | tf_op jit(solution)/shard_map/ppermute | solution.py:231
  28.3 4.4 %collective-permute-start.7 = (bf16[8,128,128]{2,1,0:T(8,128)(2,1)S(1)}, bf16[8,128,128]{2,1,0:T(8,128)(2,1)S(1)}, u32[]{:S(2)}, u32[]{:S(2)}) collective-permute-start(bf16[8,128,128]{2,1,0:T(8,128)(2,1)S(1)} %get-tuple-element.10), channel_id=1, source_target_pairs={{0,4},{8,12},{4,0},{12,8},{1,5},{9,13},{5,1},{13,9},{2,6},{10,14},... | collective-permute-start | bytes 786440 | tf_op jit(solution)/shard_map/ppermute | solution.py:231
  34.4 10.4 %collective-permute-start.14 = (bf16[384,128]{1,0:T(8,128)(2,1)S(1)}, bf16[384,128]{1,0:T(8,128)(2,1)S(1)}, u32[]{:S(2)}, u32[]{:S(2)}) collective-permute-start(bf16[384,128]{1,0:T(8,128)(2,1)S(1)} %attend_chunk.4.refs_0_), channel_id=1, source_target_pairs={{0,2},{1,3},{2,0},{3,1},{4,6},{5,7},{6,4},{7,5},{8,10},{9,11},{10,... | collective-permute-start | bytes 294920 | tf_op jit(solution)/shard_map/ppermute | solution.py:290
  39.8 6.9 %collective-permute-start.13 = (bf16[384,128]{1,0:T(8,128)(2,1)S(1)}, bf16[384,128]{1,0:T(8,128)(2,1)S(1)}, u32[]{:S(2)}, u32[]{:S(2)}) collective-permute-start(bf16[384,128]{1,0:T(8,128)(2,1)S(1)} %attend_chunk.5.refs_0_), channel_id=1, source_target_pairs={{0,3},{1,2},{2,1},{3,0},{4,7},{5,6},{6,5},{7,4},{8,11},{9,10},{10,... | collective-permute-start | bytes 294920 | tf_op jit(solution)/shard_map/ppermute | solution.py:290
  42.7 6.0 %collective-permute-start.12 = (bf16[384,128]{1,0:T(8,128)(2,1)S(1)}, bf16[384,128]{1,0:T(8,128)(2,1)S(1)}, u32[]{:S(2)}, u32[]{:S(2)}) collective-permute-start(bf16[384,128]{1,0:T(8,128)(2,1)S(1)} %attend_chunk.6.refs_0_), channel_id=1, source_target_pairs={{0,1},{1,0},{2,3},{3,2},{4,5},{5,4},{6,7},{7,6},{8,9},{9,8},{10,11... | collective-permute-start | bytes 294920 | tf_op jit(solution)/shard_map/ppermute | solution.py:290
